TPU v7x, 128 devices: a whole 4x4x4 slice. The times are simulated.
128 devices in a mesh: wide: 32 (over z, x, y_lo), rep: 4 (over y_hi, core).
Axes of the slice: x: 4, y: 4 (y_hi: 2, y_lo: 2; y = y_hi * 2 + y_lo), z: 4, core: 2. Of those that a mesh axis runs over, the one named last changes fastest.
Arguments:
- samples: bfloat16 [16384, 49152], P(('wide', 'rep')), may hold values from -6 to 6
- out_grad: bfloat16 [16384, 24576], P(('wide', 'rep')), may hold values from -0.046875 to 0.046875
- row_ids: int32 [16384, 256], P(('wide', 'rep')), may hold values from 0 to 255
- table_owner: int32 [256], replicated, may hold values from 0 to 255, each once
- slot_map: int32 [256, 256], P('wide'), may hold values from 0 to 2047, as said below
- proj: bfloat16 [256, 16], P('wide'), may hold values from -0.375 to 0.375
- gain_flat: bfloat16 [4096], P('wide'), may hold values from 0.25 to 1.75
- w_in: bfloat16 [4096, 128], P('wide'), may hold values from -0.09375 to 0.09375
- w_out: bfloat16 [12288, 128], P('wide'), may hold values from -0.5 to 0.5
- w_lcb: bfloat16 [256, 64], P('wide'), may hold values from -0.375 to 0.375
- table_rows: float32 [65536, 192], P('wide'), may hold values from -0.6 to 0.6
- row_accum: float32 [65536], P('wide'), may hold values from 0.0001 to 0.01
Outputs:
- proj_grad: float32 [256, 16], P('wide')
- gain_grad: float32 [4096], P('wide')
- w_in_grad: float32 [4096, 128], P('wide')
- w_out_grad: float32 [12288, 128], P('wide')
- w_lcb_grad: float32 [256, 64], P('wide')
- new_rows: float32 [65536, 192], P('wide')
- new_accum: float32 [65536], P('wide')
Inputs may be any that keep to these rules, and one draw needn't show every extreme that they name: `table_owner`: each position 0 to 255 once. `slot_map`: within each aligned block of 8 rows every value 0 to 2047 appears once.
All inputs are finite; a program needn't handle non-finite values.
Results may differ from a plain program's by a relative error of at most 0.0065.
Values may be sent and summed in bfloat16 or wider, within the bound.
No kernel may reach another device: no remote copies, remote signals or barrier semaphores. Data moves between devices by JAX's collectives and lax.ppermute only.
A program may use at most 256 MiB of HBM per device.

v0:
```python
import jax
import jax.numpy as jnp
from jax import lax
from jax.sharding import PartitionSpec as P

LEARN = 0.1
EPS = 1e-05
HIGH = lax.Precision.HIGHEST


def body(
    samples,
    out_grad,
    row_ids,
    table_owner,
    slot_map,
    proj,
    gain_flat,
    w_in,
    w_out,
    w_lcb,
    table_rows,
    row_accum,
):
    proj_f, gain_f, w_in_f, w_out_f, w_lcb_f = (
        lax.all_gather(proj, "wide", axis=0, tiled=True),
        lax.all_gather(gain_flat, "wide", axis=0, tiled=True),
        lax.all_gather(w_in, "wide", axis=0, tiled=True),
        lax.all_gather(w_out, "wide", axis=0, tiled=True),
        lax.all_gather(w_lcb, "wide", axis=0, tiled=True),
    )
    count = samples.shape[0]
    n_emb = proj_f.shape[0]
    rank = proj_f.shape[1]
    width = samples.shape[1] // n_emb
    n_feat = w_out_f.shape[0] // width
    x3 = samples.reshape(count, n_emb, width)
    grad3 = out_grad.astype(jnp.float32).reshape(count, -1, width)
    f32 = jnp.float32
    brain_float_half = jnp.bfloat16
    x3_single = x3.astype(f32)
    proj_single = proj_f.astype(f32)
    score = jnp.einsum("bnd,nk->bdk", x3, proj_f, preferred_element_type=f32)
    flat = jnp.einsum("bnd,bdk->bnk", x3_single, score, precision=HIGH).reshape(count, n_emb * rank)
    centered_input = flat - jnp.mean(flat, axis=1, keepdims=True)
    inverse_deviation = 1.0 / jnp.sqrt(
        jnp.mean(centered_input * centered_input, axis=1, keepdims=True) + EPS
    )
    standardized_input = centered_input * inverse_deviation
    gain_single_32 = gain_f.astype(f32)
    normalized_rows = (standardized_input * gain_single_32).astype(brain_float_half)
    pre = jnp.dot(normalized_rows, w_in_f, preferred_element_type=f32)
    hidden = jax.nn.silu(pre).astype(brain_float_half)
    fout = jnp.einsum("bh,jh->bj", hidden, w_out_f, preferred_element_type=f32).reshape(
        count, n_feat, width
    )
    lout = jnp.einsum("bnd,nl->bld", x3, w_lcb_f, preferred_element_type=f32)
    joined = jnp.concatenate([fout, lout], axis=1)
    mid = joined - jnp.mean(joined, axis=2, keepdims=True)
    out_inv = 1.0 / jnp.sqrt(jnp.mean(mid * mid, axis=2, keepdims=True) + EPS)
    chat = mid * out_inv
    dcat = out_inv * (
        grad3
        - jnp.mean(grad3, axis=2, keepdims=True)
        - chat * jnp.mean(grad3 * chat, axis=2, keepdims=True)
    )
    dfeat = dcat[:, :n_feat].reshape(count, n_feat * width).astype(brain_float_half)
    dlin = dcat[:, n_feat:].astype(brain_float_half)
    g_out = jnp.einsum("bj,bh->jh", dfeat, hidden, preferred_element_type=f32)
    g_lcb = jnp.einsum("bnd,bld->nl", x3, dlin, preferred_element_type=f32)
    sig = jax.nn.sigmoid(pre)
    dhidden = jnp.dot(dfeat, w_out_f, preferred_element_type=f32)
    dpre = (dhidden * sig * (1.0 + pre * (1.0 - sig))).astype(brain_float_half)
    g_in = jnp.einsum("bi,bh->ih", normalized_rows, dpre, preferred_element_type=f32)
    norm_gradient = jnp.einsum("bh,ih->bi", dpre, w_in_f, preferred_element_type=f32)
    gain_gradient = jnp.sum(norm_gradient * standardized_input, axis=0)
    boundary_value = norm_gradient * gain_single_32
    flat_gradient = inverse_deviation * (
        boundary_value
        - jnp.mean(boundary_value, axis=1, keepdims=True)
        - standardized_input * jnp.mean(boundary_value * standardized_input, axis=1, keepdims=True)
    )
    dfm = flat_gradient.reshape(count, n_emb, rank).astype(brain_float_half)
    dscore = jnp.einsum("bnd,bnk->bdk", x3, dfm, preferred_element_type=f32)
    g_proj = jnp.einsum("bnd,bdk->nk", x3_single, dscore, precision=HIGH)
    dx3 = jnp.einsum("bnk,bdk->bnd", dfm.astype(f32), score, precision=HIGH)
    dx3 = dx3 + jnp.einsum("nk,bdk->bnd", proj_single, dscore, precision=HIGH)
    dx3 = dx3 + jnp.einsum("nl,bld->bnd", w_lcb_f, dlin, preferred_element_type=f32)
    dx_send = dx3.astype(brain_float_half)
    grads = (g_proj, gain_gradient, g_in, g_out, g_lcb)
    shards = (
        lax.psum_scatter(grads[0], "wide", scatter_dimension=0, tiled=True),
        lax.psum_scatter(grads[1], "wide", scatter_dimension=0, tiled=True),
        lax.psum_scatter(grads[2], "wide", scatter_dimension=0, tiled=True),
        lax.psum_scatter(grads[3], "wide", scatter_dimension=0, tiled=True),
        lax.psum_scatter(grads[4], "wide", scatter_dimension=0, tiled=True),
    )
    proj_grad, gain_grad, w_in_grad, w_out_grad, w_lcb_grad = lax.psum(
        (shards[0], shards[1], shards[2], shards[3], shards[4]), "rep"
    )
    ordering = (
        jnp.zeros((n_emb,), jnp.int32).at[table_owner].set(jnp.arange(n_emb, dtype=jnp.int32))
    )
    dx_owner = jnp.take(dx_send, ordering, axis=1).reshape(count, n_emb * width)
    ids_owner = jnp.take(row_ids, ordering, axis=1)
    recv_grad, recv_ids = (
        lax.all_to_all(dx_owner, "wide", split_axis=1, concat_axis=0, tiled=True),
        lax.all_to_all(ids_owner, "wide", split_axis=1, concat_axis=0, tiled=True),
    )
    tables_here = recv_ids.shape[1]
    rows = slot_map.shape[1]
    row_range = jnp.arange(rows, dtype=jnp.int32)

    def table_rows_grad(position):
        picks = lax.dynamic_slice_in_dim(recv_ids, position, 1, 1)
        onehot = (picks == row_range[None, :]).astype(brain_float_half)
        block = lax.dynamic_slice_in_dim(recv_grad, position * width, width, 1)
        return jnp.einsum("mr,md->rd", onehot, block, preferred_element_type=f32)

    grow = lax.map(table_rows_grad, jnp.arange(tables_here, dtype=jnp.int32))
    state_size = tables_here * rows
    back = (
        jnp.zeros((state_size,), jnp.int32)
        .at[slot_map.reshape(state_size)]
        .set(jnp.arange(state_size, dtype=jnp.int32))
    )
    gstate = jnp.take(grow.reshape(state_size, width), back, axis=0)
    total = lax.psum(gstate, "rep")
    new_accum = row_accum + jnp.mean(total * total, axis=1)
    new_rows = table_rows - LEARN * total / jnp.sqrt(new_accum)[:, None]
    return (proj_grad, gain_grad, w_in_grad, w_out_grad, w_lcb_grad, new_rows, new_accum)


def solution(mesh):
    in_specs = (
        P(("wide", "rep"), None),
        P(("wide", "rep"), None),
        P(("wide", "rep"), None),
        P(),
        P("wide", None),
        P("wide", None),
        P("wide"),
        P("wide", None),
        P("wide", None),
        P("wide", None),
        P("wide", None),
        P("wide"),
    )
    out_specs = (
        P("wide", None),
        P("wide"),
        P("wide", None),
        P("wide", None),
        P("wide", None),
        P("wide", None),
        P("wide"),
    )
    return jax.shard_map(body, mesh=mesh, in_specs=in_specs, out_specs=out_specs, check_vma=False)
```

profile of v0, /device:TPU:1, one launch (start us, length us, event | category | flops | bytes accessed | tf_op | source)
XLA Modules:
  0.0 1266.5 jit_solution(5290281193544643902)
XLA Ops:
  8.7 16.6 %copy.102 = bf16[128,49152]{0,1:T(8,128)(2,1)} copy(bf16[128,49152]{1,0:T(8,128)(2,1)} %param.14) | data formatting | bytes 25165824 | tf_op args[0]
  25.3 18.2 %copy.132 = bf16[128,256,192]{1,2,0:T(8,128)(2,1)} copy(bf16[128,256,192]{0,2,1:T(8,128)(2,1)} %bitcast.112) | data formatting | bytes 25165824 | tf_op jit(solution)/shard_map/reshape | solution.py:37
  43.5 17.0 %copy.109 = bf16[128,256,192]{1,0,2:T(8,128)(2,1)} copy(bf16[128,256,192]{0,2,1:T(8,128)(2,1)} %bitcast.113) | data formatting | bytes 25165824 | tf_op jit(solution)/shard_map/reshape | solution.py:37
  62.0 69.3 %all-gather = bf16[32,1,128]{2,1,0:T(2,128)(2,1)S(1)} all-gather(bf16[1,1,128]{2,1,0:T(2,128)(2,1)S(1)} %bitcast.135), channel_id=1, replica_groups=mesh['wide'=32,'rep'=4] {'wide'}, dimensions={0}, use_global_device_ids=true | all-gather | bytes 8448 | tf_op jit(solution)/shard_map/all_gather | solution.py:27
  132.2 8.5 copy.111
  140.8 9.1 convert.6
  149.9 63.0 %all_gather.15 = bf16[256,16]{1,0:T(8,128)(2,1)S(1)} all-gather(bf16[8,16]{1,0:T(8,128)(2,1)S(1)} %copy-done.17), channel_id=1, replica_groups=mesh['wide'=32,'rep'=4] {'wide'}, dimensions={0}, use_global_device_ids=true | all-gather | bytes 8448 | tf_op jit(solution)/shard_map/all_gather | solution.py:26
  212.9 8.1 fusion.26
  221.1 6.9 fusion.38
  233.4 65.8 %all_gather.19 = bf16[256,64]{1,0:T(8,128)(2,1)S(1)} all-gather(bf16[8,64]{1,0:T(8,128)(2,1)S(1)} %copy-done.18), channel_id=1, replica_groups=mesh['wide'=32,'rep'=4] {'wide'}, dimensions={0}, use_global_device_ids=true | all-gather | bytes 33792 | tf_op jit(solution)/shard_map/all_gather | solution.py:30
  302.6 4.6 convert_reduce_fusion
  307.2 11.1 convolution_bitcast_fusion
  323.7 6.3 copy.110
  333.6 5.5 multiply_reduce_fusion.1
  339.2 13.4 %multiply_reduce_fusion = f32[128,128]{0,1:T(8,128)S(1)} fusion(f32[128,128,192]{0,2,1:T(8,128)} %convert.6, f32[128,128]{0,1:T(8,128)S(1)} %add_rsqrt_fusion, f32[128,128]{0,1:T(8,128)S(1)} %broadcast_multiply_fusion.2, f32[128,64,192]{0,1,2:T(8,128)S(1)} %bitcast.109, f32[128,64,192]{0,1,2:T(8,128)S(1)} %bitcast.111), kind=kLoop, calls=%fused_computation.20 | loop fusion | flops 15712256 | bytes 25362432 | tf_op jit(solution)/shard_map/reduce_sum | solution.py:65
  352.6 16.1 %multiply_convert_fusion = bf16[128,128,192]{0,1,2:T(8,128)(2,1)} fusion(f32[128,128,192]{0,2,1:T(8,128)S(1)} %bitcast.115, f32[128,128]{0,1:T(8,128)S(1)} %broadcast_multiply_fusion, f32[128,128]{0,1:T(8,128)S(1)} %broadcast_multiply_fusion.1, f32[128,128]{0,1:T(8,128)S(1)} %add_rsqrt_fusion, f32[128,128]{0,1:T(8,128)S(1)} %broadcast_multiply_fusion.2, ...), kind=kLoop, calls=%fused_computation.19 | loop fusion | flops 25165824 | bytes 31719424 | tf_op jit(solution)/shard_map/convert.2
  368.8 6.2 fusion.37
  389.9 9.7 fusion.40
  399.7 13.4 %fusion.42 = f32[128,256,192]{1,2,0:T(8,128)} fusion(bf16[128,256,16]{1,2,0:T(8,128)(2,1)S(1)} %copy-done.6, f32[128,192,16]{1,2,0:T(8,128)S(1)} %copy-done.3), kind=kOutput, calls=%fused_computation.84 | convolution fusion | flops 1207959552 | bytes 27787264 | tf_op jit(solution)/shard_map/bnk,bdk->bnd/dot_general | solution.py:86
  413.1 7.5 copy.123
  420.7 16.1 %fusion.14 = f32[128,192,256]{2,1,0:T(8,128)} fusion(f32[128,16,192]{2,1,0:T(8,128)} %fusion.40, bf16[256,16]{1,0:T(8,128)(2,1)S(1)} %all_gather.15), kind=kOutput, calls=%fused_computation.25 | convolution fusion | flops 1207959552 | bytes 26746880 | tf_op jit(solution)/shard_map/nk,bdk->bnd/dot_general | solution.py:87
  436.8 23.0 %fusion.12 = bf16[128,256,192]{1,2,0:T(8,128)(2,1)} fusion(f32[128,256,192]{1,2,0:T(8,128)} %fusion.42, f32[128,192,256]{2,1,0:T(8,128)} %fusion.14, bf16[128,64,192]{2,1,0:T(8,128)(2,1)} %copy.123, bf16[256,64]{1,0:T(8,128)(2,1)S(1)} %all_gather.19), kind=kOutput, calls=%fused_computation.15 | convolution fusion | flops 824180736 | bytes 66093056 | tf_op jit(solution)/shard_map/nl,bld->bnd/dot_general | solution.py:88
  459.9 23.3 %copy.124 = bf16[128,256,192]{2,0,1:T(8,128)(2,1)} copy(bf16[128,256,192]{1,2,0:T(8,128)(2,1)} %fusion.12) | data formatting | bytes 25165824 | tf_op jit(solution)/shard_map/convert_element_type | solution.py:89
  483.2 15.6 %gather_fusion.1 = bf16[256,128,192]{2,1,0:T(8,128)(2,1)} fusion(bf16[128,256,192]{2,0,1:T(8,128)(2,1)} %copy.124, s32[1024]{0:T(1024)S(1)} %pad_clamp_fusion), kind=kCustom, calls=%fused_computation.1 | custom fusion | bytes 25166848 | tf_op jit(solution)/shard_map/jit(_take)/gather | solution.py:104
  498.8 18.9 %copy.125 = bf16[128,256,192]{0,2,1:T(8,128)(2,1)} copy(bf16[128,256,192]{2,0,1:T(8,128)(2,1)} %bitcast.116) | data formatting | bytes 25165824 | tf_op jit(solution)/shard_map/jit(_take)/gather | solution.py:104
  517.7 13.3 %bitcast_select_fusion = bf16[128,32,1536]{0,2,1:T(8,128)(2,1)} fusion(pred[32,1536]{1,0:T(8,128)(4,1)S(1)} %copy-done.10, bf16[128,32,1536]{0,2,1:T(8,128)(2,1)} %bitcast.119), kind=kLoop, calls=%fused_computation.18 | loop fusion | flops 6291456 | bytes 25214976 | tf_op jit(solution)/shard_map/jit(_take)/select_n | solution.py:104
  531.1 5.1 all-to-all-start.1
  541.7 8.3 scatter_custom_fusion
  550.8 158.4 %all-to-all-done.1 = bf16[128,32,1536]{0,2,1:T(8,128)(2,1)} async-done(((bf16[128,32,1536]{0,2,1:T(8,128)(2,1)}), bf16[128,32,1536]{0,2,1:T(8,128)(2,1)}, u32[]{:S(2)}, u32[]{:S(2)}) %all-to-all-start.1) | async-done | bytes 12582944 | tf_op jit(solution)/shard_map/all_to_all | solution.py:107
  709.2 3.9 all-to-all-start
  713.1 8.5 convolution_bitcast_fusion.1
  721.7 16.4 %copy.126 = bf16[32,128,1536]{2,1,0:T(8,128)(2,1)} copy(bf16[32,128,1536]{1,2,0:T(8,128)(2,1)} %bitcast.27) | data formatting | bytes 25165824 | tf_op jit(solution)/shard_map/all_to_all | solution.py:107
  738.1 69.7 %while.11 = (s32[]{:T(128)}, f32[8,256,192]{1,2,0:T(8,128)}, s32[8]{0:T(128)S(1)}, s32[4096,8]{0,1:T(8,128)S(1)}, bf16[4096,1536]{1,0:T(8,128)(2,1)}, /*index=5*...) while((s32[]{:T(128)}, f32[8,256,192]{1,2,0:T(8,128)}, s32[8]{0:T(128)S(1)}, ...), condition=%wide.region_22.23_spmd.clone, body=%wide.region_21.22_spmd.clone.sunk | while | flops 403701760 | bytes 2343125 | solution.py:120
  741.3 5.5 fusion.67
  750.0 5.5 fusion.67
  758.8 5.5 fusion.67
  767.5 5.5 fusion.67
  776.2 5.5 fusion.67
  785.0 5.5 fusion.67
  793.7 5.5 fusion.67
  802.4 5.4 fusion.67
  809.6 8.6 gather_fusion.2
  821.7 71.3 %reduce-scatter.7.cloned.1.call-done = f32[384,128]{1,0:T(8,128)} async-done(((f32[12288,128]{1,0:T(8,128)}), f32[384,128]{1,0:T(8,128)}) %reduce-scatter.7.cloned.1.call-update) | async-done | bytes 196624 | tf_op jit(solution)/shard_map/reduce_scatter | solution.py:95
  897.8 8.0 fusion.20
  905.8 130.4 %all-reduce.3 = (f32[256,16]{0,1:T(8,128)S(1)}, f32[4096]{0:T(1024)S(1)}) all-reduce(f32[256,16]{0,1:T(8,128)S(1)} %fusion.20, f32[4096]{0:T(1024)S(1)} %get-tuple-element.80), channel_id=2, replica_groups=mesh['wide'=32,'rep'=4] {'wide'}, use_global_device_ids=true, to_apply=%region_8.9.clone | all-reduce | flops 8192 | bytes 65536
  1036.4 135.6 %all-reduce.9.cloned.1.call-done = f32[256,64]{0,1:T(8,128)} async-done(((f32[256,64]{0,1:T(8,128)}), f32[256,64]{0,1:T(8,128)}) %all-reduce.9.cloned.1.call-update) | async-done | bytes 65552
  1172.8 29.7 %all-reduce.4 = (f32[8,16]{0,1:T(8,128)S(1)}, f32[128]{0:T(128)}, f32[8,64]{0,1:T(8,128)S(1)}) all-reduce(f32[8,16]{0,1:T(8,128)S(1)} %constant_dynamic-slice_fusion.2, f32[128]{0:T(128)S(1)} %dynamic-slice.3, f32[8,64]{0,1:T(8,128)S(1)} %constant_dynamic-slice_fusion.1), channel_id=1, replica_groups=mesh['wide'=32,'rep'=4] {'rep'}, use_global_device_ids=true, to_apply=%region_9.10 | all-reduce | flops 768 | bytes 6144 | tf_op jit(solution)/shard_map/psum | solution.py:98
  1203.8 47.2 %all-reduce.11.cloned.1.call-done = (f32[128,128]{1,0:T(8,128)}, f32[384,128]{1,0:T(8,128)}, f32[2048,192]{1,0:T(8,128)}) async-done(((f32[128,128]{1,0:T(8,128)}, f32[384,128]{1,0:T(8,128)}, f32[2048,192]{1,0:T(8,128)}), (f32[128,128]{1,0:T(8,128)}, f32[384,128]{1,0:T(8,128)}, f32[2048,192]{1,0:T(8,128)})) %all-reduce.11.cloned.1.call-update) | async-done | bytes 1835024 | tf_op jit(solution)/shard_map/psum | solution.py:98
  (157 shorter events, 67.0 us)
Async XLA Ops:
  7.2 311.5 %all-gather.4.cloned.1.call-start = ((), (), s32[]{:S(2)}) async-start(), calls=%async_computation.4 | async-start | bytes 1081344 | tf_op jit(solution)/shard_map/all_gather | solution.py:28
  7.9 312.8 %all-gather.6.cloned.1.call-start = ((), (), s32[]{:S(2)}) async-start(), calls=%async_computation.5 | async-start | bytes 3244032 | tf_op jit(solution)/shard_map/all_gather | solution.py:29
  8.6 813.1 %reduce-scatter.5.cloned.1.call-start = ((), (), s32[]{:S(2)}) async-start(), calls=%async_computation.6 | async-start | bytes 2162688 | tf_op jit(solution)/shard_map/reduce_scatter | solution.py:94
  43.5 17.0 %copy-start.19 = (s32[256]{0:T(256)S(1)}, s32[256]{0:T(256)}, u32[]{:S(2)}) copy-start(s32[256]{0:T(256)} %param.17) | copy-start | bytes 3076
  43.5 18.5 %copy-start.20 = (bf16[128]{0:T(256)(128)(2,1)S(1)}, bf16[128]{0:T(256)(128)(2,1)}, u32[]{:S(2)}) copy-start(bf16[128]{0:T(256)(128)(2,1)} %param.20) | copy-start | bytes 772
  62.0 78.8 %copy-start.13 = (pred[32,8]{1,0:T(8,128)(4,1)}, pred[32,8]{1,0:T(8,128)(4,1)S(1)}, u32[]{:S(2)}) copy-start(pred[32,8]{1,0:T(8,128)(4,1)S(1)} %broadcast_in_dim.66) | copy-start | bytes 772
  140.8 9.1 copy-start.17
  140.8 80.3 %slice-start = ((s8[12582912]{0:T(1024)(128)(4,1)}), s8[4194304]{0:T(1024)(128)(4,1)S(1)}, s32[]{:S(2)}) async-start(s8[12582912]{0:T(1024)(128)(4,1)} %bitcast.105), calls=%async_computation.10 | async-start | bytes 8388608
  140.8 80.3 %slice-start.1 = ((s8[12582912]{0:T(1024)(128)(4,1)}), s8[4194304]{0:T(1024)(128)(4,1)S(1)}, s32[]{:S(2)}) async-start(s8[12582912]{0:T(1024)(128)(4,1)} %bitcast.105), calls=%async_computation.11 | async-start | bytes 8388608
  212.9 8.2 slice-start.2
  221.1 7.0 copy-start.2
  228.1 5.3 copy-start.18
  233.3 85.0 %copy-start = (f32[128,4096]{1,0:T(8,128)}, f32[128,4096]{1,0:T(8,128)S(1)}, u32[]{:S(2)}) copy-start(f32[128,4096]{1,0:T(8,128)S(1)} %copy.107) | copy-start | bytes 6291460
  318.7 5.0 copy-start.7
  323.6 6.3 slice-start.3
  323.7 6.3 slice-start.4
  333.5 5.6 slice-start.5
  333.6 5.6 slice-start.6
  333.6 19.0 %slice-start.7 = ((s8[12582912]{0:T(1024)(128)(4,1)}), s8[4194304]{0:T(1024)(128)(4,1)S(1)}, s32[]{:S(2)}) async-start(s8[12582912]{0:T(1024)(128)(4,1)} %bitcast.114), calls=%async_computation.17 | async-start | bytes 8388608
  339.1 13.5 %slice-start.8 = ((s8[12582912]{0:T(1024)(128)(4,1)}), s8[4194304]{0:T(1024)(128)(4,1)S(1)}, s32[]{:S(2)}) async-start(s8[12582912]{0:T(1024)(128)(4,1)} %bitcast.114), calls=%async_computation.18 | async-start | bytes 8388608
  339.2 13.4 %slice-start.9 = ((s8[12582912]{0:T(1024)(128)(4,1)}), s8[4194304]{0:T(1024)(128)(4,1)S(1)}, s32[]{:S(2)}) async-start(s8[12582912]{0:T(1024)(128)(4,1)} %bitcast.114), calls=%async_computation.19 | async-start | bytes 8388608
  374.9 2.0 copy-start.5
  377.0 1.2 copy-start.8
  380.0 3.0 copy-start.1
  389.9 9.7 copy-start.3
  389.9 9.7 copy-start.6
  498.8 18.9 %copy-start.10 = (pred[32,1536]{1,0:T(8,128)(4,1)S(1)}, pred[32,1536]{1,0:T(8,128)(4,1)}, u32[]{:S(2)}) copy-start(pred[32,1536]{1,0:T(8,128)(4,1)} %broadcast_in_dim.71) | copy-start | bytes 147460
  531.1 178.1 %all-to-all-start.1 = ((bf16[128,32,1536]{0,2,1:T(8,128)(2,1)}), bf16[128,32,1536]{0,2,1:T(8,128)(2,1)}, u32[]{:S(2)}, u32[]{:S(2)}) async-start(bf16[128,32,1536]{0,2,1:T(8,128)(2,1)} %bitcast_select_fusion), calls=%async_computation.3 | async-start | bytes 25165824 | tf_op jit(solution)/shard_map/all_to_all | solution.py:107
  536.1 356.9 %reduce-scatter.7.cloned.1.call-start = ((), (), s32[]{:S(2)}) async-start(), calls=%async_computation.7 | async-start | bytes 6488064 | tf_op jit(solution)/shard_map/reduce_scatter | solution.py:95
  539.9 0.7 copy-start.15
  539.9 0.9 copy-start.11
  539.9 10.1 copy-start.14
  709.2 28.9 %all-to-all-start = ((s32[128,32,8]{0,2,1:T(8,128)}), s32[128,32,8]{0,2,1:T(8,128)S(1)}, u32[]{:S(2)}, u32[]{:S(2)}) async-start(s32[128,32,8]{0,2,1:T(8,128)} %bitcast_select_fusion.1), calls=%async_computation.2 | async-start | bytes 262144 | tf_op jit(solution)/shard_map/all_to_all | solution.py:108
  713.1 458.9 %all-reduce.9.cloned.1.call-start = ((), (), s32[]{:S(2)}) async-start(), calls=%async_computation.8 | async-start | bytes 131072
  721.6 529.4 %all-reduce.11.cloned.1.call-start = ((), (), s32[]{:S(2)}) async-start(), calls=%async_computation.9 | async-start | bytes 4718592 | tf_op jit(solution)/shard_map/psum | solution.py:98
  818.3 74.8 %copy-start.21 = (u32[128]{0:T(128)S(1)}, u32[128]{0:T(128)}, u32[]{:S(2)}) copy-start(u32[128]{0:T(128)} %constant.96) | copy-start | bytes 1540
  818.3 79.5 %copy-start.4 = (f32[128,16,192]{2,1,0:T(8,128)S(1)}, f32[128,16,192]{2,1,0:T(8,128)}, u32[]{:S(2)}) copy-start(f32[128,16,192]{2,1,0:T(8,128)} %fusion.40) | copy-start | bytes 4718596
  897.8 355.2 %copy-start.16 = (f32[2048]{0:T(1024)S(1)}, f32[2048]{0:T(1024)}, u32[]{:S(2)}) copy-start(f32[2048]{0:T(1024)} %param.25) | copy-start | bytes 24580
  1253.6 4.3 copy-start.12
  1253.6 4.9 copy-start.9
Sparse Core Ops, SparseCore 0:
  9.6 132.7 all-gather.3
  144.1 158.0 all-gather.5
  420.8 296.1 reduce-scatter.4
  719.4 173.5 reduce-scatter.6
  896.1 275.7 all-reduce.8
  1174.5 76.4 all-reduce.10
where the time goes:
time: 1280 us; the launch traced here: 1270 us
  waiting for transfers between devices  414 us (32%)
  blocking collectives  358 us (28%)
  local copies, waits for them, and re-layouts  204 us (16%)
  matrix products  163 us (13%)
  other arithmetic  80.7 us (6%)
  loops' own time  20.8 us (2%)
  between operations  16.4 us (1%)
    all_to_all x1, waiting for transfers between devices, body(): lax.all_to_all(dx_owner, 'wide', split_axis=1, concat_axis=0, tiled=True)  158 us
    unnamed x7, waiting for transfers between devices  137 us
    unnamed x1, blocking collectives  130 us
    reduce_scatter x1, waiting for transfers between devices, body(): lax.psum_scatter(grads[3], 'wide', scatter_dimension=0, tiled=True)  71.3 us
    all_gather x1, blocking collectives, body(): lax.all_gather(gain_flat, 'wide', axis=0, tiled=True)  69.3 us
    all_gather x1, blocking collectives, body(): lax.all_gather(w_lcb, 'wide', axis=0, tiled=True)  65.8 us
    all_gather x1, blocking collectives, body(): lax.all_gather(proj, 'wide', axis=0, tiled=True)  63 us
    psum x1, waiting for transfers between devices, body(): lax.psum((shards[0], shards[1], shards[2], shards[3], shards[4]), 'rep')  47.2 us
  transfers between devices with their start and end apart: 8, of which 4 were waited for; matrix products, arithmetic and copies ran while one was open for 27% of the time, Pallas kernels for 0%

commit v1 on v0

v1 whole, which is shorter than its diff:
```python
import functools

import jax
import jax.numpy as jnp
from jax import lax
from jax.experimental import pallas as pl
from jax.experimental.pallas import tpu as pltpu
from jax.sharding import Mesh, PartitionSpec as P

LEARN = 0.1
EPS = 1e-05
F32 = jnp.float32
BF16 = jnp.bfloat16
D = 192
DP = 256
K = 16
NN = (((1,), (0,)), ((), ()))
NT = (((1,), (1,)), ((), ()))
TN = (((0,), (0,)), ((), ()))


def dot(a, b, dims=NN):
    return lax.dot_general(a, b, dims, preferred_element_type=F32)


def params(mib=56):
    return pltpu.CompilerParams(vmem_limit_bytes=mib * 1024 * 1024)


def cost(flops, nbytes):
    return pl.CostEstimate(flops=int(flops), bytes_accessed=int(nbytes), transcendentals=0)


def split(v):
    hi = v.astype(BF16)
    return hi, (v - hi.astype(F32)).astype(BF16)


def unfold_kernel(x_ref, o_ref, lo, hi):
    rows, tables = o_ref.shape[0], o_ref.shape[1]

    def pair(j, _):
        v = x_ref[:, pl.ds(pl.multiple_of(j * 384, 128), 384)].astype(F32)
        w = pltpu.roll(v, 192, 1)
        lo[pl.ds(2 * j, rows, stride=tables), :] = v[:, :128]
        hi[pl.ds(2 * j, rows, stride=tables), :] = v[:, 128:256]
        lo[pl.ds(2 * j + 1, rows, stride=tables), :] = w[:, :128]
        hi[pl.ds(2 * j + 1, rows, stride=tables), :] = w[:, 128:256]
        return 0

    lax.fori_loop(0, tables // 2, pair, 0, unroll=4)
    keep = lax.broadcasted_iota(jnp.int32, (tables, 128), 1) < 64
    for b in range(rows):
        o_ref[b, :, :128] = lo[b * tables : (b + 1) * tables, :].astype(BF16)
        o_ref[b, :, 128:] = jnp.where(keep, hi[b * tables : (b + 1) * tables, :], 0.0).astype(BF16)


def unfold(x, tables, first, rows=16):
    count = x.shape[0]
    return pl.pallas_call(
        unfold_kernel,
        grid=(count // rows,),
        in_specs=[pl.BlockSpec((rows, tables * D), lambda i: (i, first))],
        out_specs=pl.BlockSpec((rows, tables, DP), lambda i: (i, 0, 0)),
        out_shape=jax.ShapeDtypeStruct((count, tables, DP), BF16),
        scratch_shapes=[pltpu.VMEM((rows * tables, 128), F32)] * 2,
        compiler_params=params(),
        cost_estimate=cost(1e9, count * tables * 900),
        name="unfold",
    )(x)


def first_kernel(x_ref, g_ref, w_ref, s_ref, dl_ref, xh_ref, inv_ref, lo, hi):
    rows = x_ref.shape[0]
    n = x_ref.shape[1]
    w = w_ref[...]
    keep = lax.broadcasted_iota(jnp.int32, (1, DP), 1) < D
    for b in range(rows):
        xb = x_ref[b]
        r = dot(w, xb)
        shi, slo = split(r[:K])
        s_ref[b, :K, :] = shi
        s_ref[b, K:, :] = slo
        f2 = dot(jnp.concatenate([shi, slo], axis=0), xb, NT)
        fm = f2[:K] + f2[K:]
        mean = jnp.sum(fm) * (1.0 / (K * n))
        c = fm - mean
        inv = 1.0 / jnp.sqrt(jnp.full((1, 128), jnp.sum(c * c), F32) * (1.0 / (K * n)) + EPS)
        inv_ref[b : b + 1, :] = inv
        xh = c * inv[:, :1]
        lo[pl.ds(b, K, stride=rows), :] = xh[:, :128]
        hi[pl.ds(b, K, stride=rows), :] = xh[:, 128:]
        lout = r[K:]
        grad = g_ref[b].astype(F32)
        mid = jnp.where(keep, lout - jnp.sum(lout, axis=1, keepdims=True) * (1.0 / D), 0.0)
        oinv = 1.0 / jnp.sqrt(jnp.sum(mid * mid, axis=1, keepdims=True) * (1.0 / D) + EPS)
        chat = mid * oinv
        gm = jnp.sum(grad, axis=1, keepdims=True) * (1.0 / D)
        gc = jnp.sum(grad * chat, axis=1, keepdims=True) * (1.0 / D)
        dl_ref[b] = jnp.where(keep, oinv * (grad - gm - chat * gc), 0.0).astype(BF16)
    xh_ref[:, :, :128] = lo[...].reshape(K, rows, 128)
    xh_ref[:, :, 128:] = hi[...].reshape(K, rows, 128)


def first(x3, g2, wt, rows=8):
    count, n, _ = x3.shape
    nl = g2.shape[1]
    return pl.pallas_call(
        first_kernel,
        grid=(count // rows,),
        in_specs=[
            pl.BlockSpec((rows, n, DP), lambda i: (i, 0, 0)),
            pl.BlockSpec((rows, nl, DP), lambda i: (i, 0, 0)),
            pl.BlockSpec(wt.shape, lambda i: (0, 0)),
        ],
        out_specs=[
            pl.BlockSpec((rows, 2 * K, DP), lambda i: (i, 0, 0)),
            pl.BlockSpec((rows, nl, DP), lambda i: (i, 0, 0)),
            pl.BlockSpec((K, rows, n), lambda i: (0, i, 0)),
            pl.BlockSpec((rows, 128), lambda i: (i, 0)),
        ],
        out_shape=[
            jax.ShapeDtypeStruct((count, 2 * K, DP), BF16),
            jax.ShapeDtypeStruct((count, nl, DP), BF16),
            jax.ShapeDtypeStruct((K, count, n), F32),
            jax.ShapeDtypeStruct((count, 128), F32),
        ],
        scratch_shapes=[pltpu.VMEM((K * rows, 128), F32)] * 2,
        compiler_params=params(),
        cost_estimate=cost(2e10, count * n * DP * 2),
        name="first",
    )(x3, g2, wt)


def batch_kernel(
    xh_ref, inv_ref, gain_ref, win_ref, wout_ref, g_ref,
    gout_ref, gin_ref, ggain_ref, dfm_ref, pre_s, hid_s, dhid_s, norm_s, e_s,
):
    step = pl.program_id(0)
    count, n = xh_ref.shape[1], xh_ref.shape[2]

    @pl.when(step == 0)
    def _():
        pre = jnp.zeros((count, 128), F32)
        for k in range(K):
            normed = (xh_ref[k] * gain_ref[k : k + 1, :]).astype(BF16)
            norm_s[k] = normed
            pre = pre + dot(normed, win_ref[k])
        pre_s[...] = pre
        hid_s[...] = (pre / (1.0 + jnp.exp(-pre))).astype(BF16)
        dhid_s[...] = jnp.zeros_like(dhid_s)

    hid = hid_s[...]
    w = wout_ref[...]
    rows = w.shape[0]
    fout = dot(w, hid, NT).reshape(rows // D, D, count)
    grad = g_ref[...].astype(F32).T.reshape(rows // D, D, count)
    mid = fout - jnp.sum(fout, axis=1, keepdims=True) * (1.0 / D)
    oinv = 1.0 / jnp.sqrt(jnp.sum(mid * mid, axis=1, keepdims=True) * (1.0 / D) + EPS)
    chat = mid * oinv
    gm = jnp.sum(grad, axis=1, keepdims=True) * (1.0 / D)
    gc = jnp.sum(grad * chat, axis=1, keepdims=True) * (1.0 / D)
    df = (oinv * (grad - gm - chat * gc)).reshape(rows, count).astype(BF16)
    gout_ref[...] = dot(df, hid).astype(BF16)
    dhid_s[...] += dot(w, df, TN)

    @pl.when(step == pl.num_programs(0) - 1)
    def _():
        pre = pre_s[...]
        sig = 1.0 / (1.0 + jnp.exp(-pre))
        dpre = (dhid_s[...].T * sig * (1.0 + pre * (1.0 - sig))).astype(BF16)
        m1 = jnp.zeros((count, n), F32)
        m2 = jnp.zeros((count, n), F32)
        for k in range(K):
            gin_ref[k] = dot(norm_s[k], dpre, TN)
            dn = dot(dpre, win_ref[k], NT)
            xh = xh_ref[k]
            ggain_ref[k : k + 1, :] = jnp.sum(dn * xh, axis=0, keepdims=True)
            e = dn * gain_ref[k : k + 1, :]
            e_s[k] = e
            m1 = m1 + e
            m2 = m2 + e * xh
        a1 = jnp.sum(m1, axis=1, keepdims=True) * (1.0 / (K * n))
        a2 = jnp.sum(m2, axis=1, keepdims=True) * (1.0 / (K * n))
        inv = inv_ref[:, :1]
        for k in range(K):
            dfm_ref[k] = inv * (e_s[k] - a1 - xh_ref[k] * a2)


def batch(xh, inv, gain, win, wout, out_grad, feats=4):
    k, count, n = xh.shape
    total = wout.shape[0]
    rows = feats * D
    whole = lambda shape: pl.BlockSpec(shape, lambda i: (0,) * len(shape))
    return pl.pallas_call(
        batch_kernel,
        grid=(total // rows,),
        in_specs=[
            whole((k, count, n)),
            whole((count, 128)),
            whole((k, n)),
            whole((k, n, 128)),
            pl.BlockSpec((rows, 128), lambda i: (i, 0)),
            pl.BlockSpec((count, rows), lambda i: (0, i)),
        ],
        out_specs=[
            pl.BlockSpec((rows, 128), lambda i: (i, 0)),
            whole((k, n, 128)),
            whole((k, n)),
            whole((k, count, n)),
        ],
        out_shape=[
            jax.ShapeDtypeStruct((total, 128), BF16),
            jax.ShapeDtypeStruct((k, n, 128), F32),
            jax.ShapeDtypeStruct((k, n), F32),
            jax.ShapeDtypeStruct((k, count, n), F32),
        ],
        scratch_shapes=[
            pltpu.VMEM((count, 128), F32),
            pltpu.VMEM((count, 128), BF16),
            pltpu.VMEM((128, count), F32),
            pltpu.VMEM((k, count, n), BF16),
            pltpu.VMEM((k, count, n), F32),
        ],
        compiler_params=params(),
        cost_estimate=cost(2e10, 2e7),
        name="batch",
    )(xh, inv, gain, win, wout, out_grad)


def last_kernel(order_ref, x_ref, s_ref, dl_ref, dfm_ref, wt_ref, out_ref, acc_ref, flo, fhi, lo, hi):
    rows, n = x_ref.shape[0], x_ref.shape[1]
    owners = out_ref.shape[0]

    @pl.when(pl.program_id(0) == 0)
    def _():
        acc_ref[...] = jnp.zeros_like(acc_ref)

    flo[...] = dfm_ref[:, :, :128].reshape(K * rows, 128)
    fhi[...] = dfm_ref[:, :, 128:].reshape(K * rows, 128)
    proj = wt_ref[:K, :]
    shared = wt_ref[...]

    def sample(b, _):
        dfm = jnp.concatenate(
            [flo[pl.ds(b, K, stride=rows), :], fhi[pl.ds(b, K, stride=rows), :]], axis=1
        ).astype(BF16)
        xb = x_ref[b]
        dhi, dlo = split(dot(dfm, xb))
        dl = dl_ref[b]
        low = jnp.concatenate([dhi, dlo, dl], axis=0)
        acc_ref[...] += dot(low, xb, NT)
        left = jnp.concatenate([dfm, dfm, proj, shared], axis=0)
        right = jnp.concatenate([s_ref[b], dlo, dhi, dl], axis=0)
        dx = dot(left, right, TN)
        lo[pl.ds(b, n, stride=rows), :] = dx[:, :128]
        hi[pl.ds(b, n, stride=rows), :] = dx[:, 128:]
        return 0

    lax.fori_loop(0, rows, sample, 0, unroll=2)
    keep = lax.broadcasted_iota(jnp.int32, (rows, 128), 1) < 64

    def owner(o, _):
        for q in range(n // owners // 2):
            t0 = order_ref[o * (n // owners) + 2 * q]
            t1 = order_ref[o * (n // owners) + 2 * q + 1]
            p0 = pl.ds(pl.multiple_of(t0 * rows, rows), rows)
            p1 = pl.ds(pl.multiple_of(t1 * rows, rows), rows)
            a1 = pltpu.roll(lo[p1, :], 64, 1)
            b1 = pltpu.roll(hi[p1, :], 64, 1)
            v = jnp.concatenate(
                [lo[p0, :], jnp.where(keep, hi[p0, :], a1), jnp.where(keep, a1, b1)], axis=1
            )
            out_ref[o, :, 384 * q : 384 * (q + 1)] = v.astype(BF16)
        return 0

    lax.fori_loop(0, owners, owner, 0, unroll=2)


def last(order, x3, s, dl, dfm, wt, owners, rows=16):
    count, n, _ = x3.shape
    nl = dl.shape[1]
    per = n // owners * D
    grid = pltpu.PrefetchScalarGridSpec(
        num_scalar_prefetch=1,
        grid=(count // rows,),
        in_specs=[
            pl.BlockSpec((rows, n, DP), lambda i, o: (i, 0, 0)),
            pl.BlockSpec((rows, 2 * K, DP), lambda i, o: (i, 0, 0)),
            pl.BlockSpec((rows, nl, DP), lambda i, o: (i, 0, 0)),
            pl.BlockSpec((K, rows, n), lambda i, o: (0, i, 0)),
            pl.BlockSpec(wt.shape, lambda i, o: (0, 0)),
        ],
        out_specs=[
            pl.BlockSpec((owners, rows, per), lambda i, o: (0, i, 0)),
            pl.BlockSpec((2 * K + nl, n), lambda i, o: (0, 0)),
        ],
        scratch_shapes=[pltpu.VMEM((K * rows, 128), F32)] * 2
        + [pltpu.VMEM((n * rows, 128), F32)] * 2,
    )
    return pl.pallas_call(
        last_kernel,
        grid_spec=grid,
        out_shape=[
            jax.ShapeDtypeStruct((owners, count, per), BF16),
            jax.ShapeDtypeStruct((2 * K + nl, n), F32),
        ],
        compiler_params=params(),
        cost_estimate=cost(2e10, count * n * DP * 4),
        name="last",
    )(order, x3, s, dl, dfm, wt)


def rows_kernel(slot_ref, dx_ref, ids_ref, out_ref, acc, turn):
    step = pl.program_id(0)
    srcs, tables, count = ids_ref.shape
    state = out_ref.shape[0]
    rows = state // tables

    @pl.when(step == 0)
    def _():
        acc[...] = jnp.zeros_like(acc)

    iota = lax.broadcasted_iota(jnp.int32, (rows, count), 0)
    for j in range(tables):
        start = 384 * (j // 2) + 128 * (j % 2)
        total = jnp.zeros((rows, DP), F32)
        for s in range(0, srcs, 2):
            hot = [
                jnp.where(iota == ids_ref[s + i, j : j + 1, :], 1.0, 0.0).astype(BF16)
                for i in range(2)
            ]
            block = dx_ref[s : s + 2, :, start : start + DP].reshape(2 * count, DP)
            total = total + dot(jnp.concatenate(hot, axis=1), block)
        acc[j * rows : (j + 1) * rows, :] += total

    @pl.when(step == pl.num_programs(0) - 1)
    def _():
        for j in range(1, tables, 2):
            part = slice(j * rows, (j + 1) * rows)
            acc[part, :] = pltpu.roll(acc[part, :], DP - 64, 1)

        def place(i, _):
            turn[pl.ds(slot_ref[i], 1), :] = acc[pl.ds(i, 1), :]
            return 0

        lax.fori_loop(0, state, place, 0, unroll=8)
        out_ref[...] = turn[:, :D].astype(BF16)


def row_sums(slots, dx, ids, state, srcs=8):
    total, count, per = dx.shape
    tables = ids.shape[1]
    grid = pltpu.PrefetchScalarGridSpec(
        num_scalar_prefetch=1,
        grid=(total // srcs,),
        in_specs=[
            pl.BlockSpec((srcs, count, per), lambda i, s: (i, 0, 0)),
            pl.BlockSpec((srcs, tables, count), lambda i, s: (i, 0, 0)),
        ],
        out_specs=pl.BlockSpec((state, D), lambda i, s: (0, 0)),
        scratch_shapes=[pltpu.VMEM((state, DP), F32)] * 2,
    )
    return pl.pallas_call(
        rows_kernel,
        grid_spec=grid,
        out_shape=jax.ShapeDtypeStruct((state, D), BF16),
        compiler_params=params(),
        cost_estimate=cost(1e10, dx.size * 2),
        name="row_sums",
    )(slots, dx, ids)


def layer(samples, out_grad, order, proj, gain, w_in, w_out, w_lcb, owners):
    n = proj.shape[0]
    nl = w_lcb.shape[1]
    x3 = unfold(samples, n, 0)
    g2 = unfold(out_grad, nl, out_grad.shape[1] // D // nl - 1)
    wt = jnp.concatenate([proj.T, w_lcb.T], axis=0)
    gain_t = gain.reshape(n, K).T.astype(F32)
    win_t = w_in.reshape(n, K, 128).transpose(1, 0, 2)
    s, dl, xh, inv = first(x3, g2, wt)
    g_out, g_in, g_gain, dfm = batch(xh, inv, gain_t, win_t, w_out, out_grad)
    dx, acc = last(order, x3, s, dl, dfm, wt, owners)
    g_proj = acc[:K] + acc[K : 2 * K]
    return g_proj, g_gain, g_in, g_out, acc[2 * K :], dx


WIDE = ("z", "x", "yl")


def gather(a):
    n = 32
    return lax.all_to_all(jnp.broadcast_to(a[None], (n,) + a.shape), WIDE, 0, 0, tiled=True)


def rep_sum(v):
    swap = [(0, 1), (1, 0)]
    for axis in ("c", "yh"):
        v = v.astype(BF16)
        v = v.astype(F32) + lax.ppermute(v, axis, swap).astype(F32)
    return v


def body(
    samples, out_grad, row_ids, table_owner, slot_map, proj, gain_flat, w_in, w_out, w_lcb,
    table_rows, row_accum,
):
    owners = 32
    count = samples.shape[0]
    per = proj.shape[0]
    n = per * owners
    nl = w_lcb.shape[1]
    small = jnp.concatenate([proj, gain_flat.reshape(per, K), w_lcb], axis=1)
    small = jnp.pad(small, ((0, 8), (0, 128 - small.shape[1])))
    packed = gather(jnp.concatenate([w_in, small], axis=0))
    w_in_f = packed[:, : w_in.shape[0]].reshape(-1, 128)
    small_f = packed[:, w_in.shape[0] : w_in.shape[0] + per].reshape(n, 128)
    proj_f = small_f[:, :K]
    gain_f = small_f[:, K : 2 * K].reshape(-1)
    w_lcb_f = small_f[:, 2 * K : 2 * K + nl]
    w_out_f = gather(w_out).reshape(-1, 128)

    order = jnp.zeros((n,), jnp.int32).at[table_owner].set(jnp.arange(n, dtype=jnp.int32))
    ids = jnp.take(row_ids.T, order, axis=0).reshape(owners, per, count)
    ids = lax.all_to_all(ids, WIDE, 0, 0, tiled=True)

    g_proj, g_gain, g_in, g_out, g_lcb, dx = layer(
        samples, out_grad, order, proj_f, gain_f, w_in_f, w_out_f, w_lcb_f, owners
    )
    big = jnp.concatenate(
        [
            g_out.reshape(owners, -1, 128),
            g_in.astype(BF16).transpose(1, 0, 2).reshape(owners, -1, 128),
        ],
        axis=1,
    )
    big = lax.all_to_all(big, WIDE, 0, 0, tiled=True)
    little = jnp.concatenate([g_proj, g_gain, g_lcb], axis=0).T.reshape(owners, per, -1)
    little = lax.all_to_all(little, WIDE, 0, 0, tiled=True)
    recv = lax.all_to_all(dx, WIDE, 0, 0, tiled=True)
    part = row_sums(slot_map.reshape(-1), recv, ids, table_rows.shape[0])
    total = rep_sum(part)
    big = rep_sum(jnp.sum(big.astype(F32), axis=0))
    little = rep_sum(jnp.sum(little, axis=0))
    split_at = w_out.shape[0]
    new_accum = row_accum + jnp.mean(total * total, axis=1)
    new_rows = table_rows - LEARN * total / jnp.sqrt(new_accum)[:, None]
    return (
        little[:, :K],
        little[:, K : 2 * K].reshape(-1),
        big[split_at:],
        big[:split_at],
        little[:, 2 * K :],
        new_rows,
        new_accum,
    )


def solution(mesh):
    cube = Mesh(mesh.devices.reshape(4, 4, 2, 2, 2), ("z", "x", "yl", "yh", "c"))
    batch_spec = P(("z", "x", "yl", "yh", "c"), None)
    two, one = P(WIDE, None), P(WIDE)
    in_specs = (batch_spec,) * 3 + (P(), two, two, one, two, two, two, two, one)
    out_specs = (two, one, two, two, two, two, one)
    return jax.shard_map(body, mesh=cube, in_specs=in_specs, out_specs=out_specs, check_vma=False)
```

time: 1280 us -> 518 us (0.40)
  blocking collectives: 358 us -> 15.1 us
  waiting for transfers between devices: 414 us -> 220 us
  Pallas kernels: 0 us -> 184 us
  local copies, waits for them, and re-layouts: 204 us -> 24 us
  matrix products: 163 us -> 0 us
  other arithmetic: 80.7 us -> 12.8 us
  starting transfers between devices: 9.16 us -> 60.3 us
  loops' own time: 20.8 us -> 0 us
  between operations: 16.4 us -> 0.99 us
    all_gather x3 -> x0, blocking collectives: 198 us -> none  [the longest x1 69.3 us: body(): lax.all_gather(gain_flat, 'wide', axis=0, tiled=True)]
    pallas_call x0 -> x6, Pallas kernels: none -> 184 us  [the longest x2 60.6 us: unfold(): pl.pallas_call(unfold_kernel, grid=(count // rows,), in_specs=[pl.BlockSp...]
    dot_general x23 -> x0, matrix products: 163 us -> none  [the longest x8 44.1 us: table_rows_grad(): return jnp.einsum('mr,md->rd', onehot, block, preferred_element_type=f32)]
    unnamed x7 -> x0, waiting for transfers between devices: 137 us -> none
    unnamed x1 -> x0, blocking collectives: 130 us -> none
    reduce_scatter x2 -> x0, waiting for transfers between devices: 71.3 us -> none  [the longest x1 71.3 us: body(): lax.psum_scatter(grads[3], 'wide', scatter_dimension=0, tiled=True)]
    psum x1 -> x0, waiting for transfers between devices: 47.2 us -> none  [body(): lax.psum((shards[0], shards[1], shards[2], shards[3], shards[4]), 'rep')]
    gather x4 -> x1, local copies, waits for them, and re-layouts: 43.9 us -> 0.73 us  [body(): ids = jnp.take(row_ids.T, order, axis=0).reshape(owners, per, count)]
  transfers between devices with their start and end apart: 8 -> 11, of which waited for: 4 -> 4; matrix products, arithmetic and copies ran while one was open for 27% -> 4% of each run, Pallas kernels for 0% -> 36%
where the time goes in v1:
time: 518 us; the launch traced here: 516 us
  waiting for transfers between devices  220 us (42%)
  Pallas kernels  184 us (36%)
  starting transfers between devices  60.3 us (12%)
  local copies, waits for them, and re-layouts  24 us (5%)
  blocking collectives  15.1 us (3%)
  other arithmetic  12.8 us (2%)
    all_to_all x1, waiting for transfers between devices, body(): recv = lax.all_to_all(dx, WIDE, 0, 0, tiled=True)  163 us
    pallas_call x2, Pallas kernels, unfold(): pl.pallas_call(unfold_kernel, grid=(count // rows,), in_specs=[pl.BlockSp...  60.6 us
    pallas_call x1, Pallas kernels, last(): pl.pallas_call(last_kernel, grid_spec=grid, out_shape=[jax.ShapeDtypeStru...  53.3 us
    pallas_call x1, Pallas kernels, first(): pl.pallas_call(first_kernel, grid=(count // rows,), in_specs=[pl.BlockSpe...  32.9 us
    all_to_all x1, waiting for transfers between devices, body(): big = lax.all_to_all(big, WIDE, 0, 0, tiled=True)  22.6 us
    pallas_call x1, Pallas kernels, batch(): pl.pallas_call(batch_kernel, grid=(total // rows,), in_specs=[whole((k, c...  19.4 us
    ppermute x6, waiting for transfers between devices, rep_sum(): v = v.astype(F32) + lax.ppermute(v, axis, swap).astype(F32)  18.5 us
    pallas_call x1, Pallas kernels, row_sums(): pl.pallas_call(rows_kernel, grid_spec=grid, out_shape=jax.ShapeDtypeStruc...  17.3 us
  transfers between devices with their start and end apart: 11, of which 4 were waited for; matrix products, arithmetic and copies ran while one was open for 4% of the time, Pallas kernels for 36%

profile of v1, /device:TPU:1, one launch (start us, length us, event | category | flops | bytes accessed | tf_op | source)
XLA Modules:
  0.0 516.4 jit_solution(9847896481266827577)
XLA Ops:
  0.7 0.8 reshape.53
  1.4 0.8 fusion.8
  2.2 0.8 pad_maximum_fusion.2
  3.0 1.2 broadcast_in_dim.31
  4.1 9.9 %all-to-all-start = ((bf16[32,144,128]{2,1,0:T(8,128)(2,1)}), bf16[32,144,128]{2,1,0:T(8,128)(2,1)S(1)}, u32[]{:S(2)}, u32[]{:S(2)}) async-start(bf16[32,144,128]{2,1,0:T(8,128)(2,1)} %broadcast_in_dim.31), calls=%async_computation | async-start | bytes 2359296 | tf_op jit(solution)/shard_map/all_to_all | solution.py:394
  14.1 1.4 scatter_custom_fusion.order_ref
  15.7 0.7 gather_fusion
  16.4 15.6 %all-to-all-done = bf16[32,144,128]{2,1,0:T(8,128)(2,1)S(1)} async-done(((bf16[32,144,128]{2,1,0:T(8,128)(2,1)}), bf16[32,144,128]{2,1,0:T(8,128)(2,1)S(1)}, u32[]{:S(2)}, u32[]{:S(2)}) %all-to-all-start) | async-done | bytes 1179680 | tf_op jit(solution)/shard_map/all_to_all | solution.py:394
  32.0 2.5 broadcast_in_dim.32
  34.5 4.8 all-to-all-start.1
  39.4 47.5 %unfold.2.x_ref = bf16[128,256,256]{2,1,0:T(8,128)(2,1)} custom-call(bf16[128,49152]{1,0:T(8,128)(2,1)} %x_ref.2), custom_call_target="tpu_custom_call" | custom-call | flops 1000000000 | bytes 29491200 | tf_op jit(solution)/shard_map/unfold/pallas_call | solution.py:60
  86.8 13.1 %unfold.3.g_ref = bf16[128,64,256]{2,1,0:T(8,128)(2,1)} custom-call(bf16[128,24576]{1,0:T(8,128)(2,1)} %g_ref.1), custom_call_target="tpu_custom_call" | custom-call | flops 1000000000 | bytes 7372800 | tf_op jit(solution)/shard_map/unfold/pallas_call | solution.py:60
  99.9 0.8 bitcast_select_fusion
  101.3 1.2 copy.50
  102.5 0.6 pad_maximum_fusion.1.w_ref.wt_ref
  103.1 0.6 convert_bitcast_fusion.1.gain_ref
  103.7 32.9 %first.1 = (bf16[128,32,256]{2,1,0:T(8,128)(2,1)}, bf16[128,64,256]{2,1,0:T(8,128)(2,1)}, f32[16,128,256]{2,1,0:T(8,128)}, f32[128,128]{1,0:T(8,128)}) custom-call(bf16[128,256,256]{2,1,0:T(8,128)(2,1)} %unfold.2.x_ref, bf16[128,64,256]{2,1,0:T(8,128)(2,1)} %unfold.3.g_ref, bf16[80,256]{1,0:T(8,128)(2,1)} %pad_maximum_fusion.1.w_ref.wt_ref), custom_call_target="tpu_custom_call" | custom-call | flops 20000000000 | bytes 16777216 | tf_op jit(solution)/shard_map/first/pallas_call | solution.py:108
  136.7 7.7 %all-to-all-start.5 = ((s32[32,8,128]{2,1,0:T(8,128)}), s32[32,8,128]{2,1,0:T(8,128)S(1)}, u32[]{:S(2)}, u32[]{:S(2)}) async-start(s32[32,8,128]{2,1,0:T(8,128)} %bitcast_select_fusion), calls=%async_computation.5 | async-start | bytes 262144 | tf_op jit(solution)/shard_map/all_to_all | solution.py:426
  144.4 19.4 %batch.1 = (bf16[12288,128]{1,0:T(8,128)(2,1)}, f32[16,256,128]{2,1,0:T(8,128)}, f32[16,256]{1,0:T(8,128)}, f32[16,128,256]{2,1,0:T(8,128)}) custom-call(f32[16,128,256]{2,1,0:T(8,128)} %get-tuple-element.19.xh_ref, f32[128,128]{1,0:T(8,128)} %get-tuple-element.20.inv_ref, f32[16,256]{1,0:T(8,128)} %convert_bitcast_fusion.1.gain_ref, ...), custom_call_target="tpu_custom_call" | custom-call | flops 20000000000 | bytes 20000000 | tf_op jit(solution)/shard_map/batch/pallas_call | solution.py:195
  163.8 53.3 %last.1 = (bf16[32,128,1536]{2,1,0:T(8,128)(2,1)}, f32[96,256]{1,0:T(8,128)}) custom-call(s32[256]{0:T(256)} %copy-done.12, bf16[128,256,256]{2,1,0:T(8,128)(2,1)} %unfold.2.x_ref, bf16[128,32,256]{2,1,0:T(8,128)(2,1)} %get-tuple-element.17.s_ref, bf16[128,64,256]{2,1,0:T(8,128)(2,1)} %get-tuple-element.18.dl_ref, ...), custom_call_target="tpu_custom_call" | custom-call | flops 20000000000 | bytes 33554432 | tf_op jit(solution)/shard_map/last/pallas_call | solution.py:301
  217.1 0.7 slice_add_fusion
  217.8 0.8 slice.46
  218.8 15.1 %all_to_all.30 = f32[32,8,96]{2,1,0:T(8,128)S(1)} all-to-all(f32[32,8,96]{2,1,0:T(8,128)S(1)} %bitcast.28), channel_id=1, replica_groups=mesh['z'=4,'x'=4,'yl'=2,'yh'=2,'c'=2] {'z','x','yl'}, dimensions={0} | all-to-all | bytes 196608 | tf_op jit(solution)/shard_map/all_to_all | solution.py:440
  233.9 5.2 %all-to-all-start.4 = ((bf16[32,128,1536]{2,1,0:T(8,128)(2,1)}), bf16[32,128,1536]{2,1,0:T(8,128)(2,1)}, u32[]{:S(2)}, u32[]{:S(2)}) async-start(bf16[32,128,1536]{2,1,0:T(8,128)(2,1)} %get-tuple-element.26), calls=%async_computation.4 | async-start | bytes 25165824 | tf_op jit(solution)/shard_map/all_to_all | solution.py:441
  239.3 0.7 copy.37
  240.0 1.0 copy-done.2
  241.0 2.2 pad_maximum_fusion
  243.2 162.9 %all-to-all-done.4.dx_ref = bf16[32,128,1536]{2,1,0:T(8,128)(2,1)} async-done(((bf16[32,128,1536]{2,1,0:T(8,128)(2,1)}), bf16[32,128,1536]{2,1,0:T(8,128)(2,1)}, u32[]{:S(2)}, u32[]{:S(2)}) %all-to-all-start.4) | async-done | bytes 12582944 | tf_op jit(solution)/shard_map/all_to_all | solution.py:441
  406.1 17.0 %all-to-all-start.3 = ((bf16[32,512,128]{2,1,0:T(8,128)(2,1)}), bf16[32,512,128]{2,1,0:T(8,128)(2,1)}, u32[]{:S(2)}, u32[]{:S(2)}) async-start(bf16[32,512,128]{2,1,0:T(8,128)(2,1)} %pad_maximum_fusion), calls=%async_computation.3 | async-start | bytes 8388608 | tf_op jit(solution)/shard_map/all_to_all | solution.py:438
  423.2 0.6 copy.48
  423.8 17.3 %row_sums.1 = bf16[2048,192]{1,0:T(8,128)(2,1)} custom-call(s32[2048]{0:T(1024)} %bitcast.32, bf16[32,128,1536]{2,1,0:T(8,128)(2,1)} %all-to-all-done.4.dx_ref, s32[32,8,128]{2,1,0:T(8,128)} %copy-done.6), custom_call_target="tpu_custom_call" | custom-call | flops 10000000000 | bytes 12582912 | tf_op jit(solution)/shard_map/row_sums/pallas_call | solution.py:364
  441.1 1.6 copy.39
  442.7 4.7 collective-permute-start.4
  447.5 1.8 copy.43
  449.3 2.7 collective-permute-start.1
  452.0 22.6 %all-to-all-done.3 = bf16[32,512,128]{2,1,0:T(8,128)(2,1)} async-done(((bf16[32,512,128]{2,1,0:T(8,128)(2,1)}), bf16[32,512,128]{2,1,0:T(8,128)(2,1)}, u32[]{:S(2)}, u32[]{:S(2)}) %all-to-all-start.3) | async-done | bytes 4194336 | tf_op jit(solution)/shard_map/all_to_all | solution.py:438
  474.5 2.8 reduce_sum.31
  477.3 5.2 %collective-permute-start.2 = (bf16[512,128]{1,0:T(8,128)(2,1)S(1)}, bf16[512,128]{1,0:T(8,128)(2,1)S(1)}, u32[]{:S(2)}, u32[]{:S(2)}) collective-permute-start(bf16[512,128]{1,0:T(8,128)(2,1)S(1)} %reduce_sum.31), channel_id=1, source_target_pairs={{0,1},{1,0},{2,3},{3,2},{4,5},{5,4},{6,7},{7,6},{8,9},{9,8},{10,11... | collective-permute-start | bytes 393224 | tf_op jit(solution)/shard_map/ppermute | solution.py:401
  482.5 1.4 copy.40
  484.7 2.6 collective-permute-start.5
  487.4 0.7 slice.51
  488.6 0.6 fusion.13
  489.8 18.5 %collective-permute-done.3 = bf16[512,128]{1,0:T(8,128)(2,1)S(1)} collective-permute-done((bf16[512,128]{1,0:T(8,128)(2,1)S(1)}, bf16[512,128]{1,0:T(8,128)(2,1)S(1)}, u32[]{:S(2)}, u32[]{:S(2)}) %collective-permute-start.3) | collective-permute-done | bytes 131104 | tf_op jit(solution)/shard_map/ppermute | solution.py:401
  508.3 0.7 slice.60
  509.0 0.6 slice.59
  510.6 0.6 fusion.11
  511.8 1.9 divide_subtract_fusion
  513.6 2.8 copy.44
  (61 shorter events, 4.6 us)
Async XLA Ops:
  0.6 13.4 %copy-start.5 = (s32[128,256]{1,0:T(8,128)S(1)}, s32[128,256]{1,0:T(8,128)}, u32[]{:S(2)}) copy-start(s32[128,256]{1,0:T(8,128)} %param.14) | copy-start | bytes 393220
  0.6 13.5 %copy-start.11 = (s32[256]{0:T(256)S(1)}, s32[256]{0:T(256)}, u32[]{:S(2)}) copy-start(s32[256]{0:T(256)} %param.15) | copy-start | bytes 3076
  4.1 27.9 %copy-start.7 = (bf16[384,128]{1,0:T(8,128)(2,1)S(1)}, bf16[384,128]{1,0:T(8,128)(2,1)}, u32[]{:S(2)}) copy-start(bf16[384,128]{1,0:T(8,128)(2,1)} %param.20) | copy-start | bytes 294916
  4.1 27.9 %all-to-all-start = ((bf16[32,144,128]{2,1,0:T(8,128)(2,1)}), bf16[32,144,128]{2,1,0:T(8,128)(2,1)S(1)}, u32[]{:S(2)}, u32[]{:S(2)}) async-start(bf16[32,144,128]{2,1,0:T(8,128)(2,1)} %broadcast_in_dim.31), calls=%async_computation | async-start | bytes 2359296 | tf_op jit(solution)/shard_map/all_to_all | solution.py:394
  15.5 19.0 %copy-start.12 = (s32[256]{0:T(256)}, s32[256]{0:T(256)S(1)}, u32[]{:S(2)}) copy-start(s32[256]{0:T(256)S(1)} %scatter_custom_fusion.order_ref) | copy-start | bytes 3076
  34.5 102.2 %all-to-all-start.1 = ((bf16[32,384,128]{2,1,0:T(8,128)(2,1)}), bf16[32,384,128]{2,1,0:T(8,128)(2,1)}, u32[]{:S(2)}, u32[]{:S(2)}) async-start(bf16[32,384,128]{2,1,0:T(8,128)(2,1)} %broadcast_in_dim.32), calls=%async_computation.1 | async-start | bytes 6291456 | tf_op jit(solution)/shard_map/all_to_all | solution.py:394
  136.7 82.1 %all-to-all-start.5 = ((s32[32,8,128]{2,1,0:T(8,128)}), s32[32,8,128]{2,1,0:T(8,128)S(1)}, u32[]{:S(2)}, u32[]{:S(2)}) async-start(s32[32,8,128]{2,1,0:T(8,128)} %bitcast_select_fusion), calls=%async_computation.5 | async-start | bytes 262144 | tf_op jit(solution)/shard_map/all_to_all | solution.py:426
  163.8 54.9 %copy-start.8 = (f32[16,256]{1,0:T(8,128)S(1)}, f32[16,256]{1,0:T(8,128)}, u32[]{:S(2)}) copy-start(f32[16,256]{1,0:T(8,128)} %get-tuple-element.23) | copy-start | bytes 49156
  218.8 15.1 %copy-start.6 = (s32[32,8,128]{2,1,0:T(8,128)}, s32[32,8,128]{2,1,0:T(8,128)S(1)}, u32[]{:S(2)}) copy-start(s32[32,8,128]{2,1,0:T(8,128)S(1)} %all-to-all-done.5.ids_ref) | copy-start | bytes 393220
  233.9 5.2 %copy-start.3 = (f32[16,256,128]{2,1,0:T(8,128)S(1)}, f32[16,256,128]{2,1,0:T(8,128)}, u32[]{:S(2)}) copy-start(f32[16,256,128]{2,1,0:T(8,128)} %get-tuple-element.25) | copy-start | bytes 6291460
  233.9 172.2 %all-to-all-start.4 = ((bf16[32,128,1536]{2,1,0:T(8,128)(2,1)}), bf16[32,128,1536]{2,1,0:T(8,128)(2,1)}, u32[]{:S(2)}, u32[]{:S(2)}) async-start(bf16[32,128,1536]{2,1,0:T(8,128)(2,1)} %get-tuple-element.26), calls=%async_computation.4 | async-start | bytes 25165824 | tf_op jit(solution)/shard_map/all_to_all | solution.py:441
  239.1 1.9 copy-start.2
  243.2 180.0 %copy-start.9 = (s32[8,256]{1,0:T(8,128)S(1)}, s32[8,256]{1,0:T(8,128)}, u32[]{:S(2)}) copy-start(s32[8,256]{1,0:T(8,128)} %param.16) | copy-start | bytes 24580
  406.1 68.4 %all-to-all-start.3 = ((bf16[32,512,128]{2,1,0:T(8,128)(2,1)}), bf16[32,512,128]{2,1,0:T(8,128)(2,1)}, u32[]{:S(2)}, u32[]{:S(2)}) async-start(bf16[32,512,128]{2,1,0:T(8,128)(2,1)} %pad_maximum_fusion), calls=%async_computation.3 | async-start | bytes 8388608 | tf_op jit(solution)/shard_map/all_to_all | solution.py:438
  441.1 6.4 %copy-start.4 = (f32[2048,192]{0,1:T(8,128)S(1)}, f32[2048,192]{0,1:T(8,128)}, u32[]{:S(2)}) copy-start(f32[2048,192]{0,1:T(8,128)} %param.22) | copy-start | bytes 4718596
  442.7 39.8 %collective-permute-start.4 = (bf16[2048,192]{0,1:T(8,128)(2,1)S(1)}, bf16[2048,192]{0,1:T(8,128)(2,1)}, u32[]{:S(2)}, u32[]{:S(2)}) collective-permute-start(bf16[2048,192]{0,1:T(8,128)(2,1)S(1)} %copy.39), channel_id=1, source_target_pairs={{0,1},{1,0},{2,3},{3,2},{4,5},{5,4},{6,7},{7,6},{8,9},{9,8},{10,11... | collective-permute-start | bytes 2359304 | tf_op jit(solution)/shard_map/ppermute | solution.py:401
  447.4 1.9 collective-permute-start
  449.3 34.6 %copy-start.1 = (bf16[2048,192]{1,0:T(8,128)(2,1)S(1)}, bf16[2048,192]{1,0:T(8,128)(2,1)}, u32[]{:S(2)}) copy-start(bf16[2048,192]{1,0:T(8,128)(2,1)} %row_sums.1) | copy-start | bytes 2359300
  449.3 38.1 %collective-permute-start.1 = (bf16[8,96]{1,0:T(8,128)(2,1)S(1)}, bf16[8,96]{1,0:T(8,128)(2,1)S(1)}, u32[]{:S(2)}, u32[]{:S(2)}) collective-permute-start(bf16[8,96]{1,0:T(8,128)(2,1)S(1)} %add_convert_fusion.2), channel_id=1, source_target_pairs={{0,2},{2,0},{1,3},{3,1},{4,6},{6,4},{5,7},{7,5},{8,10},{10,8},{9,1... | collective-permute-start | bytes 4616 | tf_op jit(solution)/shard_map/ppermute | solution.py:401
  477.3 10.7 %collective-permute-start.2 = (bf16[512,128]{1,0:T(8,128)(2,1)S(1)}, bf16[512,128]{1,0:T(8,128)(2,1)S(1)}, u32[]{:S(2)}, u32[]{:S(2)}) collective-permute-start(bf16[512,128]{1,0:T(8,128)(2,1)S(1)} %reduce_sum.31), channel_id=1, source_target_pairs={{0,1},{1,0},{2,3},{3,2},{4,5},{5,4},{6,7},{7,6},{8,9},{9,8},{10,11... | collective-permute-start | bytes 393224 | tf_op jit(solution)/shard_map/ppermute | solution.py:401
  484.7 24.9 %collective-permute-start.5 = (bf16[2048,192]{0,1:T(8,128)(2,1)S(1)}, bf16[2048,192]{0,1:T(8,128)(2,1)S(1)}, u32[]{:S(2)}, u32[]{:S(2)}) collective-permute-start(bf16[2048,192]{0,1:T(8,128)(2,1)S(1)} %copy.41), channel_id=1, source_target_pairs={{0,2},{2,0},{1,3},{3,1},{4,6},{6,4},{5,7},{7,5},{8,10},{10,8},{9,1... | collective-permute-start | bytes 2359304 | tf_op jit(solution)/shard_map/ppermute | solution.py:401
  488.1 20.2 %collective-permute-start.3 = (bf16[512,128]{1,0:T(8,128)(2,1)S(1)}, bf16[512,128]{1,0:T(8,128)(2,1)S(1)}, u32[]{:S(2)}, u32[]{:S(2)}) collective-permute-start(bf16[512,128]{1,0:T(8,128)(2,1)S(1)} %add_convert_fusion.1), channel_id=1, source_target_pairs={{0,2},{2,0},{1,3},{3,1},{4,6},{6,4},{5,7},{7,5},{8,10},{10,8},{9,1... | collective-permute-start | bytes 393224 | tf_op jit(solution)/shard_map/ppermute | solution.py:401
  509.0 1.6 copy-start.10
  510.2 1.6 copy-start

commit v2 on v1

--- a/solution.py
+++ b/solution.py
@@ -36,23 +36,23 @@
     return hi, (v - hi.astype(F32)).astype(BF16)
 
 
-def unfold_kernel(x_ref, o_ref, lo, hi):
-    rows, tables = o_ref.shape[0], o_ref.shape[1]
-
-    def pair(j, _):
-        v = x_ref[:, pl.ds(pl.multiple_of(j * 384, 128), 384)].astype(F32)
-        w = pltpu.roll(v, 192, 1)
-        lo[pl.ds(2 * j, rows, stride=tables), :] = v[:, :128]
-        hi[pl.ds(2 * j, rows, stride=tables), :] = v[:, 128:256]
-        lo[pl.ds(2 * j + 1, rows, stride=tables), :] = w[:, :128]
-        hi[pl.ds(2 * j + 1, rows, stride=tables), :] = w[:, 128:256]
+def unfold_kernel(x_ref, o_ref):
+    tables = o_ref.shape[1]
+    keep = lax.broadcasted_iota(jnp.int32, (1, 1, 128), 2) < 64
+
+    def group(j, _):
+        lo, hi = [], []
+        for p in range(8):
+            v = x_ref[:, pl.ds(pl.multiple_of(j * 3072 + 384 * p, 128), 384)].astype(F32)
+            w = pltpu.roll(v, 192, 1)
+            lo += [v[:, :128], w[:, :128]]
+            hi += [v[:, 128:256], w[:, 128:256]]
+        at = pl.ds(pl.multiple_of(j * 16, 16), 16)
+        o_ref[:, at, :128] = jnp.swapaxes(jnp.stack(lo), 0, 1).astype(BF16)
+        o_ref[:, at, 128:] = jnp.where(keep, jnp.swapaxes(jnp.stack(hi), 0, 1), 0.0).astype(BF16)
         return 0
 
-    lax.fori_loop(0, tables // 2, pair, 0, unroll=4)
-    keep = lax.broadcasted_iota(jnp.int32, (tables, 128), 1) < 64
-    for b in range(rows):
-        o_ref[b, :, :128] = lo[b * tables : (b + 1) * tables, :].astype(BF16)
-        o_ref[b, :, 128:] = jnp.where(keep, hi[b * tables : (b + 1) * tables, :], 0.0).astype(BF16)
+    lax.fori_loop(0, tables // 16, group, 0)
 
 
 def unfold(x, tables, first, rows=16):
@@ -63,7 +63,6 @@
         in_specs=[pl.BlockSpec((rows, tables * D), lambda i: (i, first))],
         out_specs=pl.BlockSpec((rows, tables, DP), lambda i: (i, 0, 0)),
         out_shape=jax.ShapeDtypeStruct((count, tables, DP), BF16),
-        scratch_shapes=[pltpu.VMEM((rows * tables, 128), F32)] * 2,
         compiler_params=params(),
         cost_estimate=cost(1e9, count * tables * 900),
         name="unfold",
@@ -228,9 +227,11 @@
     )(xh, inv, gain, win, wout, out_grad)
 
 
-def last_kernel(order_ref, x_ref, s_ref, dl_ref, dfm_ref, wt_ref, out_ref, acc_ref, flo, fhi, lo, hi):
+def last_kernel(
+    order_ref, x_ref, s_ref, dl_ref, dfm_ref, wt_ref, keep_ref, send_ref, acc_ref, flo, fhi, lo, hi
+):
     rows, n = x_ref.shape[0], x_ref.shape[1]
-    owners = out_ref.shape[0]
+    pairs = keep_ref.shape[0]
 
     @pl.when(pl.program_id(0) == 0)
     def _():
@@ -260,10 +261,10 @@
     lax.fori_loop(0, rows, sample, 0, unroll=2)
     keep = lax.broadcasted_iota(jnp.int32, (rows, 128), 1) < 64
 
-    def owner(o, _):
-        for q in range(n // owners // 2):
-            t0 = order_ref[o * (n // owners) + 2 * q]
-            t1 = order_ref[o * (n // owners) + 2 * q + 1]
+    def pair(i, _):
+        for part, ref in enumerate((keep_ref, send_ref)):
+            t0 = order_ref[part * 2 * pairs + 2 * i]
+            t1 = order_ref[part * 2 * pairs + 2 * i + 1]
             p0 = pl.ds(pl.multiple_of(t0 * rows, rows), rows)
             p1 = pl.ds(pl.multiple_of(t1 * rows, rows), rows)
             a1 = pltpu.roll(lo[p1, :], 64, 1)
@@ -271,16 +272,16 @@
             v = jnp.concatenate(
                 [lo[p0, :], jnp.where(keep, hi[p0, :], a1), jnp.where(keep, a1, b1)], axis=1
             )
-            out_ref[o, :, 384 * q : 384 * (q + 1)] = v.astype(BF16)
+            ref[i] = v.astype(BF16)
         return 0
 
-    lax.fori_loop(0, owners, owner, 0, unroll=2)
-
-
-def last(order, x3, s, dl, dfm, wt, owners, rows=16):
+    lax.fori_loop(0, pairs, pair, 0, unroll=4)
+
+
+def last(order, x3, s, dl, dfm, wt, rows=16):
     count, n, _ = x3.shape
     nl = dl.shape[1]
-    per = n // owners * D
+    pairs = n // 4
     grid = pltpu.PrefetchScalarGridSpec(
         num_scalar_prefetch=1,
         grid=(count // rows,),
@@ -292,7 +293,8 @@
             pl.BlockSpec(wt.shape, lambda i, o: (0, 0)),
         ],
         out_specs=[
-            pl.BlockSpec((owners, rows, per), lambda i, o: (0, i, 0)),
+            pl.BlockSpec((pairs, rows, 2 * D), lambda i, o: (0, i, 0)),
+            pl.BlockSpec((pairs, rows, 2 * D), lambda i, o: (0, i, 0)),
             pl.BlockSpec((2 * K + nl, n), lambda i, o: (0, 0)),
         ],
         scratch_shapes=[pltpu.VMEM((K * rows, 128), F32)] * 2
@@ -302,7 +304,8 @@
         last_kernel,
         grid_spec=grid,
         out_shape=[
-            jax.ShapeDtypeStruct((owners, count, per), BF16),
+            jax.ShapeDtypeStruct((pairs, count, 2 * D), BF16),
+            jax.ShapeDtypeStruct((pairs, count, 2 * D), BF16),
             jax.ShapeDtypeStruct((2 * K + nl, n), F32),
         ],
         compiler_params=params(),
@@ -311,67 +314,122 @@
     )(order, x3, s, dl, dfm, wt)
 
 
-def rows_kernel(slot_ref, dx_ref, ids_ref, out_ref, acc, turn):
-    step = pl.program_id(0)
-    srcs, tables, count = ids_ref.shape
+def fold(v, even):
+    half = v.shape[0] // 2
+    main, tail = (v[:, :128], v[:, 128:]) if even else (v[:, 128:], v[:, :128])
+    keep = lax.broadcasted_iota(jnp.int32, (half, 128), 1) < 64
+    if even:
+        tail = jnp.where(keep, tail[:half], pltpu.roll(tail[half:], 64, 1))
+    else:
+        tail = jnp.where(keep, pltpu.roll(tail[:half], 64, 1), tail[half:])
+    return main.astype(BF16), tail.astype(BF16)
+
+
+def sums_kernel(at_ref, mine_ref, other_ref, ids_ref, oid_ref, even_ref, odd_ref):
+    pairs, count, _ = mine_ref.shape
+    rows = 2 * count
+    iota = lax.broadcasted_iota(jnp.int32, (rows, count), 0)
+    for i in range(pairs):
+        for t, ref in enumerate((even_ref, odd_ref)):
+            hot = jnp.concatenate(
+                [
+                    jnp.where(iota == r[i, t : t + 1, :], 1.0, 0.0).astype(BF16)
+                    for r in (ids_ref, oid_ref)
+                ],
+                axis=1,
+            )
+            cols = slice(128 * t, 128 * t + DP)
+            block = jnp.concatenate([mine_ref[i, :, cols], other_ref[i, :, cols]], axis=0)
+            main, tail = fold(dot(hot, block), t == 0)
+            ref[0, 0, i, :rows, :] = main
+            ref[0, 0, i, rows:, :] = tail
+
+
+def sums(at, mine, other, ids, oids, nz, nx):
+    total, count, wide = mine.shape
+    ny = total // (nz * nx)
+    grid = pltpu.PrefetchScalarGridSpec(
+        num_scalar_prefetch=1,
+        grid=(nz, nx),
+        in_specs=[
+            pl.BlockSpec((ny, count, wide), lambda z, x, at: (z * nx + x, 0, 0)),
+            pl.BlockSpec((ny, count, wide), lambda z, x, at: (z * nx + x, 0, 0)),
+            pl.BlockSpec((ny, 2, count), lambda z, x, at: (z * nx + x, 0, 0)),
+            pl.BlockSpec((ny, 2, count), lambda z, x, at: (z * nx + x, 0, 0)),
+        ],
+        out_specs=[
+            pl.BlockSpec(
+                (1, 1, ny, 384, 128),
+                lambda z, x, at: ((z + nz - at[0]) % nz, (x + nx - at[1]) % nx, 0, 0, 0),
+            ),
+            pl.BlockSpec(
+                (1, 1, ny, 384, 128),
+                lambda z, x, at: ((x + nx - at[1]) % nx, (z + nz - at[0]) % nz, 0, 0, 0),
+            ),
+        ],
+    )
+    return pl.pallas_call(
+        sums_kernel,
+        grid_spec=grid,
+        out_shape=[
+            jax.ShapeDtypeStruct((nz, nx, ny, 384, 128), BF16),
+            jax.ShapeDtypeStruct((nx, nz, ny, 384, 128), BF16),
+        ],
+        compiler_params=params(),
+        cost_estimate=cost(1e10, mine.size * 8),
+        name="sums",
+    )(at, mine, other, ids, oids)
+
+
+def place_kernel(slot_ref, sum_ref, out_ref, acc, turn):
+    tables = sum_ref.shape[0]
     state = out_ref.shape[0]
     rows = state // tables
-
-    @pl.when(step == 0)
-    def _():
-        acc[...] = jnp.zeros_like(acc)
-
-    iota = lax.broadcasted_iota(jnp.int32, (rows, count), 0)
-    for j in range(tables):
-        start = 384 * (j // 2) + 128 * (j % 2)
-        total = jnp.zeros((rows, DP), F32)
-        for s in range(0, srcs, 2):
-            hot = [
-                jnp.where(iota == ids_ref[s + i, j : j + 1, :], 1.0, 0.0).astype(BF16)
-                for i in range(2)
-            ]
-            block = dx_ref[s : s + 2, :, start : start + DP].reshape(2 * count, DP)
-            total = total + dot(jnp.concatenate(hot, axis=1), block)
-        acc[j * rows : (j + 1) * rows, :] += total
-
-    @pl.when(step == pl.num_programs(0) - 1)
-    def _():
-        for j in range(1, tables, 2):
-            part = slice(j * rows, (j + 1) * rows)
-            acc[part, :] = pltpu.roll(acc[part, :], DP - 64, 1)
-
-        def place(i, _):
-            turn[pl.ds(slot_ref[i], 1), :] = acc[pl.ds(i, 1), :]
-            return 0
-
-        lax.fori_loop(0, state, place, 0, unroll=8)
-        out_ref[...] = turn[:, :D].astype(BF16)
-
-
-def row_sums(slots, dx, ids, state, srcs=8):
-    total, count, per = dx.shape
-    tables = ids.shape[1]
+    half = rows // 2
+    keep = lax.broadcasted_iota(jnp.int32, (half, 128), 1) < 64
+    for t in range(tables):
+        main = sum_ref[t, :rows, :].astype(F32)
+        tail = sum_ref[t, rows:, :].astype(F32)
+        first, second = slice(t * rows, t * rows + half), slice(t * rows + half, (t + 1) * rows)
+        flip = pltpu.roll(tail, 64, 1)
+        if t % 2 == 0:
+            acc[t * rows : (t + 1) * rows, :128] = main
+            acc[first, 128:] = tail
+            acc[second, 128:] = flip
+        else:
+            turned = pltpu.roll(main, 64, 1)
+            acc[first, :128] = jnp.where(keep, tail, turned[:half])
+            acc[second, :128] = jnp.where(keep, flip, turned[half:])
+            acc[t * rows : (t + 1) * rows, 128:] = turned
+
+    def place(i, _):
+        turn[pl.ds(slot_ref[i], 1), :] = acc[pl.ds(i, 1), :]
+        return 0
+
+    lax.fori_loop(0, state, place, 0, unroll=8)
+    out_ref[...] = turn[:, :D]
+
+
+def place(slots, sums):
+    state = slots.shape[0]
     grid = pltpu.PrefetchScalarGridSpec(
         num_scalar_prefetch=1,
-        grid=(total // srcs,),
-        in_specs=[
-            pl.BlockSpec((srcs, count, per), lambda i, s: (i, 0, 0)),
-            pl.BlockSpec((srcs, tables, count), lambda i, s: (i, 0, 0)),
-        ],
+        grid=(1,),
+        in_specs=[pl.BlockSpec(sums.shape, lambda i, s: (0, 0, 0))],
         out_specs=pl.BlockSpec((state, D), lambda i, s: (0, 0)),
         scratch_shapes=[pltpu.VMEM((state, DP), F32)] * 2,
     )
     return pl.pallas_call(
-        rows_kernel,
+        place_kernel,
         grid_spec=grid,
-        out_shape=jax.ShapeDtypeStruct((state, D), BF16),
+        out_shape=jax.ShapeDtypeStruct((state, D), F32),
         compiler_params=params(),
-        cost_estimate=cost(1e10, dx.size * 2),
-        name="row_sums",
-    )(slots, dx, ids)
-
-
-def layer(samples, out_grad, order, proj, gain, w_in, w_out, w_lcb, owners):
+        cost_estimate=cost(1e8, state * D * 8),
+        name="place",
+    )(slots, sums)
+
+
+def layer(samples, out_grad, order, proj, gain, w_in, w_out, w_lcb):
     n = proj.shape[0]
     nl = w_lcb.shape[1]
     x3 = unfold(samples, n, 0)
@@ -381,9 +439,9 @@
     win_t = w_in.reshape(n, K, 128).transpose(1, 0, 2)
     s, dl, xh, inv = first(x3, g2, wt)
     g_out, g_in, g_gain, dfm = batch(xh, inv, gain_t, win_t, w_out, out_grad)
-    dx, acc = last(order, x3, s, dl, dfm, wt, owners)
+    keep, send, acc = last(order, x3, s, dl, dfm, wt)
     g_proj = acc[:K] + acc[K : 2 * K]
-    return g_proj, g_gain, g_in, g_out, acc[2 * K :], dx
+    return g_proj, g_gain, g_in, g_out, acc[2 * K :], keep, send
 
 
 WIDE = ("z", "x", "yl")
@@ -394,8 +452,37 @@
     return lax.all_to_all(jnp.broadcast_to(a[None], (n,) + a.shape), WIDE, 0, 0, tiled=True)
 
 
+def ring_step(axis, by, v):
+    n = 4
+    return lax.ppermute(v, axis, [(i, (i + by) % n) for i in range(n)])
+
+
+def add(*terms):
+    total = terms[0].astype(F32)
+    for term in terms[1:]:
+        total = total + term.astype(F32)
+    return total.astype(BF16)
+
+
+def ring_sums(parts):
+    fore = [ring_step(axis, 1, v[2, :2]) for axis, v in parts]
+    back = [ring_step(axis, -1, v[2, 2:]) for axis, v in parts]
+    fore = [
+        ring_step(axis, 1, jnp.concatenate([add(v[1, :2], f), v[1, 2:]], axis=0))
+        for (axis, v), f in zip(parts, fore)
+    ]
+    back = [
+        ring_step(axis, -1, jnp.concatenate([v[3, :2], add(v[3, 2:], b)], axis=0))
+        for (axis, v), b in zip(parts, back)
+    ]
+    return [add(v[0], f, b) for (_, v), f, b in zip(parts, fore, back)]
+
+
+SWAP = [(0, 1), (1, 0)]
+
+
 def rep_sum(v):
-    swap = [(0, 1), (1, 0)]
+    swap = SWAP
     for axis in ("c", "yh"):
         v = v.astype(BF16)
         v = v.astype(F32) + lax.ppermute(v, axis, swap).astype(F32)
@@ -421,12 +508,15 @@
     w_lcb_f = small_f[:, 2 * K : 2 * K + nl]
     w_out_f = gather(w_out).reshape(-1, 128)
 
+    core = lax.axis_index("c")
     order = jnp.zeros((n,), jnp.int32).at[table_owner].set(jnp.arange(n, dtype=jnp.int32))
-    ids = jnp.take(row_ids.T, order, axis=0).reshape(owners, per, count)
-    ids = lax.all_to_all(ids, WIDE, 0, 0, tiled=True)
-
-    g_proj, g_gain, g_in, g_out, g_lcb, dx = layer(
-        samples, out_grad, order, proj_f, gain_f, w_in_f, w_out_f, w_lcb_f, owners
+    order = order.reshape(owners, 2, per // 2).transpose(1, 0, 2)
+    order = jnp.where(core == 0, order, order[::-1]).reshape(-1)
+    ids = jnp.take(row_ids.T, order, axis=0).reshape(2, n // 4, 2, count)
+    other_ids = lax.ppermute(ids[1], "c", SWAP)
+
+    g_proj, g_gain, g_in, g_out, g_lcb, keep, send = layer(
+        samples, out_grad, order, proj_f, gain_f, w_in_f, w_out_f, w_lcb_f
     )
     big = jnp.concatenate(
         [
@@ -436,13 +526,25 @@
         axis=1,
     )
     big = lax.all_to_all(big, WIDE, 0, 0, tiled=True)
+    big = rep_sum(jnp.sum(big.astype(F32), axis=0))
     little = jnp.concatenate([g_proj, g_gain, g_lcb], axis=0).T.reshape(owners, per, -1)
     little = lax.all_to_all(little, WIDE, 0, 0, tiled=True)
-    recv = lax.all_to_all(dx, WIDE, 0, 0, tiled=True)
-    part = row_sums(slot_map.reshape(-1), recv, ids, table_rows.shape[0])
-    total = rep_sum(part)
-    big = rep_sum(jnp.sum(big.astype(F32), axis=0))
     little = rep_sum(jnp.sum(little, axis=0))
+
+    other = lax.ppermute(send, "c", SWAP)
+    at = jnp.stack([lax.axis_index("z"), lax.axis_index("x")]).astype(jnp.int32)
+    even, odd = sums(at, keep, other, ids[0], other_ids, 4, 4)
+    even, odd = ring_sums([("z", even), ("x", odd)])
+    even, odd = ring_sums([("x", even), ("z", odd)])
+    both = jnp.stack([even, odd], axis=1).reshape(2, 1, 2, 2, 384, 128)
+    both = jnp.broadcast_to(both, (2, 2, 2, 2, 384, 128)).reshape(4, 4, 384, 128)
+    both = lax.all_to_all(both, ("yl", "yh"), 0, 0, tiled=True)
+    mine = jnp.sum(both.astype(F32), axis=0).astype(BF16)
+    others = lax.ppermute(mine, "c", SWAP)
+    owned = jnp.where(
+        core == 0, jnp.concatenate([mine, others], axis=0), jnp.concatenate([others, mine], axis=0)
+    )
+    total = place(slot_map.reshape(-1), owned)
     split_at = w_out.shape[0]
     new_accum = row_accum + jnp.mean(total * total, axis=1)
     new_rows = table_rows - LEARN * total / jnp.sqrt(new_accum)[:, None]

time: 518 us -> 416 us (0.80)
  waiting for transfers between devices: 220 us -> 101 us
  starting transfers between devices: 60.3 us -> 87.6 us
  Pallas kernels: 184 us -> 165 us
  other arithmetic: 12.8 us -> 30.9 us
  blocking collectives: 15.1 us -> 0 us
    all_to_all x2, waiting for transfers between devices: 163 us -> 0.01 us  [the longest x1 0.01 us: body(): little = lax.all_to_all(little, WIDE, 0, 0, tiled=True)]
    ppermute x0 -> x19, waiting for transfers between devices: none -> 83.2 us  [the longest x16 75.4 us: ring_step(): return lax.ppermute(v, axis, [(i, (i + by) % n) for i in range(n)])]
    ppermute x0 -> x19, starting transfers between devices: none -> 41.2 us  [the longest x16 35.6 us: ring_step(): return lax.ppermute(v, axis, [(i, (i + by) % n) for i in range(n)])]
    pallas_call x2, Pallas kernels: 60.6 us -> 30.4 us  [unfold(): pl.pallas_call(unfold_kernel, grid=(count // rows,), in_specs=[pl.BlockSp...]
    all_to_all x1, waiting for transfers between devices: 22.6 us -> 0.01 us  [body(): big = lax.all_to_all(big, WIDE, 0, 0, tiled=True)]
    ppermute x6 -> x4, waiting for transfers between devices: 18.5 us -> 1.14 us  [rep_sum(): v = v.astype(F32) + lax.ppermute(v, axis, swap).astype(F32)]
    all_to_all x1 -> x0, blocking collectives: 15.1 us -> none  [body(): little = lax.all_to_all(little, WIDE, 0, 0, tiled=True)]
    pallas_call x1 -> x2, Pallas kernels: 17.3 us -> 28.7 us  [the longest x1 17.7 us: sums(): pl.pallas_call(sums_kernel, grid_spec=grid, out_shape=[jax.ShapeDtypeStru...]
  transfers between devices with their start and end apart: 11 -> 28, of which waited for: 4 -> 13; matrix products, arithmetic and copies ran while one was open for 4% -> 9% of each run, Pallas kernels for 36% -> 15%
where the time goes in v2:
time: 416 us; the launch traced here: 412 us
  Pallas kernels  165 us (40%)
  waiting for transfers between devices  101 us (24%)
  starting transfers between devices  87.6 us (21%)
  other arithmetic  30.9 us (7%)
  local copies, waits for them, and re-layouts  26.9 us (6%)
    ppermute x16, waiting for transfers between devices, ring_step(): return lax.ppermute(v, axis, [(i, (i + by) % n) for i in range(n)])  75.4 us
    pallas_call x1, Pallas kernels, last(): pl.pallas_call(last_kernel, grid_spec=grid, out_shape=[jax.ShapeDtypeStru...  53.4 us
    ppermute x16, starting transfers between devices, ring_step(): return lax.ppermute(v, axis, [(i, (i + by) % n) for i in range(n)])  35.6 us
    pallas_call x1, Pallas kernels, first(): pl.pallas_call(first_kernel, grid=(count // rows,), in_specs=[pl.BlockSpe...  32.9 us
    pallas_call x2, Pallas kernels, unfold(): pl.pallas_call(unfold_kernel, grid=(count // rows,), in_specs=[pl.BlockSp...  30.4 us
    pallas_call x1, Pallas kernels, batch(): pl.pallas_call(batch_kernel, grid=(total // rows,), in_specs=[whole((k, c...  19.4 us
    pallas_call x1, Pallas kernels, sums(): pl.pallas_call(sums_kernel, grid_spec=grid, out_shape=[jax.ShapeDtypeStru...  17.7 us
    all_to_all x2, waiting for transfers between devices, gather(): lax.all_to_all(jnp.broadcast_to(a[None], (n,) + a.shape), WIDE, 0, 0, til...  16.4 us
  transfers between devices with their start and end apart: 28, of which 13 were waited for; matrix products, arithmetic and copies ran while one was open for 9% of the time, Pallas kernels for 15%

profile of v2, /device:TPU:1, one launch (start us, length us, event | category | flops | bytes accessed | tf_op | source)
XLA Modules:
  0.0 412.0 jit_solution(17406268122063944544)
XLA Ops:
  4.1 9.7 %all-to-all-start = ((bf16[32,144,128]{2,1,0:T(8,128)(2,1)}), bf16[32,144,128]{2,1,0:T(8,128)(2,1)S(1)}, u32[]{:S(2)}, u32[]{:S(2)}) async-start(bf16[32,144,128]{2,1,0:T(8,128)(2,1)} %broadcast_in_dim.34), calls=%async_computation | async-start | bytes 2359296 | tf_op jit(solution)/shard_map/all_to_all | solution.py:452
  15.5 16.4 %all-to-all-done = bf16[32,144,128]{2,1,0:T(8,128)(2,1)S(1)} async-done(((bf16[32,144,128]{2,1,0:T(8,128)(2,1)}), bf16[32,144,128]{2,1,0:T(8,128)(2,1)S(1)}, u32[]{:S(2)}, u32[]{:S(2)}) %all-to-all-start) | async-done | bytes 1179680 | tf_op jit(solution)/shard_map/all_to_all | solution.py:452
  31.9 2.5 broadcast_in_dim.35
  34.4 4.8 %all-to-all-start.1 = ((bf16[32,384,128]{2,1,0:T(8,128)(2,1)}), bf16[32,384,128]{2,1,0:T(8,128)(2,1)}, u32[]{:S(2)}, u32[]{:S(2)}) async-start(bf16[32,384,128]{2,1,0:T(8,128)(2,1)} %broadcast_in_dim.35), calls=%async_computation.1 | async-start | bytes 6291456 | tf_op jit(solution)/shard_map/all_to_all | solution.py:452
  39.9 21.9 %unfold.2.x_ref = bf16[128,256,256]{2,1,0:T(8,128)(2,1)} custom-call(bf16[128,49152]{1,0:T(8,128)(2,1)} %x_ref.2), custom_call_target="tpu_custom_call" | custom-call | flops 1000000000 | bytes 29491200 | tf_op jit(solution)/shard_map/unfold/pallas_call | solution.py:60
  61.8 8.5 %unfold.3.g_ref = bf16[128,64,256]{2,1,0:T(8,128)(2,1)} custom-call(bf16[128,24576]{1,0:T(8,128)(2,1)} %g_ref.1), custom_call_target="tpu_custom_call" | custom-call | flops 1000000000 | bytes 7372800 | tf_op jit(solution)/shard_map/unfold/pallas_call | solution.py:60
  73.4 32.9 %first.1 = (bf16[128,32,256]{2,1,0:T(8,128)(2,1)}, bf16[128,64,256]{2,1,0:T(8,128)(2,1)}, f32[16,128,256]{2,1,0:T(8,128)}, f32[128,128]{1,0:T(8,128)}) custom-call(bf16[128,256,256]{2,1,0:T(8,128)(2,1)} %unfold.2.x_ref, bf16[128,64,256]{2,1,0:T(8,128)(2,1)} %unfold.3.g_ref, bf16[80,256]{1,0:T(8,128)(2,1)} %pad_maximum_fusion.9.w_ref.wt_ref), custom_call_target="tpu_custom_call" | custom-call | flops 20000000000 | bytes 16777216 | tf_op jit(solution)/shard_map/first/pallas_call | solution.py:107
  106.3 19.4 %batch.1 = (bf16[12288,128]{1,0:T(8,128)(2,1)}, f32[16,256,128]{2,1,0:T(8,128)}, f32[16,256]{1,0:T(8,128)}, f32[16,128,256]{2,1,0:T(8,128)}) custom-call(f32[16,128,256]{2,1,0:T(8,128)} %get-tuple-element.22.xh_ref, f32[128,128]{1,0:T(8,128)} %get-tuple-element.23.inv_ref, f32[16,256]{1,0:T(8,128)} %convert_bitcast_fusion.1.gain_ref, ...), custom_call_target="tpu_custom_call" | custom-call | flops 20000000000 | bytes 20000000 | tf_op jit(solution)/shard_map/batch/pallas_call | solution.py:194
  125.7 53.4 %last.1 = (bf16[64,128,384]{2,1,0:T(8,128)(2,1)}, bf16[64,128,384]{2,1,0:T(8,128)(2,1)}, f32[96,256]{1,0:T(8,128)}) custom-call(s32[256]{0:T(256)} %reshape.121.order_ref, bf16[128,256,256]{2,1,0:T(8,128)(2,1)} %unfold.2.x_ref, bf16[128,32,256]{2,1,0:T(8,128)(2,1)} %get-tuple-element.20.s_ref, bf16[128,64,256]{2,1,0:T(8,128)(2,1)} %get-tuple-element.21.dl_ref, ...), custom_call_target="tpu_custom_call" | custom-call | flops 20000000000 | bytes 33554432 | tf_op jit(solution)/shard_map/last/pallas_call | solution.py:303
  179.1 2.2 collective-permute-start.4
  183.6 7.6 %collective-permute-done.5.oid_ref = s32[64,2,128]{2,1,0:T(2,128)S(1)} collective-permute-done((s32[64,2,128]{2,1,0:T(2,128)S(1)}, s32[64,2,128]{2,1,0:T(2,128)S(1)}, u32[]{:S(2)}, u32[]{:S(2)}) %collective-permute-start.5) | collective-permute-done | bytes 65568 | tf_op jit(solution)/shard_map/ppermute | solution.py:516
  191.8 17.7 %sums.1 = (bf16[4,4,4,384,128]{4,3,2,1,0:T(8,128)(2,1)}, bf16[4,4,4,384,128]{4,3,2,1,0:T(8,128)(2,1)}) custom-call(s32[2]{0:T(128)} %pad_add_fusion.at_ref, bf16[64,128,384]{2,1,0:T(8,128)(2,1)} %get-tuple-element.29.mine_ref, bf16[64,128,384]{2,1,0:T(8,128)(2,1)} %collective-permute-done.4.other_ref, s32[64,2,128]{2,1,0:T(2,128)} %bitcast.122, ...), custom_call_target="tpu_custom_call" | custom-call | flops 10000000000 | bytes 25165824 | tf_op jit(solution)/shard_map/sums/pallas_call | solution.py:371
  209.5 3.0 slice_bitcast_fusion.7
  216.1 6.7 %all-to-all-start.2 = ((f32[32,8,96]{2,1,0:T(8,128)}), f32[32,8,96]{2,1,0:T(8,128)S(1)}, u32[]{:S(2)}, u32[]{:S(2)}) async-start(f32[32,8,96]{2,1,0:T(8,128)} %bitcast.9), calls=%async_computation.2 | async-start | bytes 262144 | tf_op jit(solution)/shard_map/all_to_all | solution.py:531
  222.8 1.8 convert_bitcast_fusion
  225.2 2.1 slice_bitcast_fusion.3
  227.3 1.5 collective-permute-start.14
  230.2 4.0 collective-permute-done.6
  234.2 2.3 fusion.7
  238.6 2.1 collective-permute-start.9
  240.7 2.2 pad_maximum_fusion
  242.9 3.8 collective-permute-done.14
  246.7 1.8 fusion.5
  250.4 7.7 %all-to-all-start.3 = ((bf16[32,512,128]{2,1,0:T(8,128)(2,1)}), bf16[32,512,128]{2,1,0:T(8,128)(2,1)}, u32[]{:S(2)}, u32[]{:S(2)}) async-start(bf16[32,512,128]{2,1,0:T(8,128)(2,1)} %pad_maximum_fusion), calls=%async_computation.3 | async-start | bytes 8388608 | tf_op jit(solution)/shard_map/all_to_all | solution.py:528
  258.2 2.4 collective-permute-start.17
  260.7 24.6 %collective-permute-done.7 = bf16[4,4,384,128]{3,2,1,0:T(8,128)(2,1)} collective-permute-done((bf16[4,4,384,128]{3,2,1,0:T(8,128)(2,1)}, bf16[4,4,384,128]{3,2,1,0:T(8,128)(2,1)}, u32[]{:S(2)}, u32[]{:S(2)}) %collective-permute-start.7) | collective-permute-done | bytes 1572896 | tf_op jit(solution)/shard_map/ppermute | solution.py:457
  285.3 3.1 fusion.3
  288.4 12.6 %collective-permute-start.10 = (bf16[2,384,128]{2,1,0:T(8,128)(2,1)S(1)}, bf16[2,384,128]{2,1,0:T(8,128)(2,1)S(1)}, u32[]{:S(2)}, u32[]{:S(2)}) collective-permute-start(bf16[2,384,128]{2,1,0:T(8,128)(2,1)S(1)} %get-tuple-element.70), channel_id=1, source_target_pairs={{0,8},{8,16},{16,24},{24,0},{1,9},{9,17},{17,25},{25,1},{2,10},{10... | collective-permute-start | bytes 589832 | tf_op jit(solution)/shard_map/ppermute | solution.py:457
  301.0 3.1 collective-permute-start.12
  304.1 35.5 %collective-permute-done.17 = bf16[4,4,384,128]{3,2,1,0:T(8,128)(2,1)S(1)} collective-permute-done((bf16[4,4,384,128]{3,2,1,0:T(8,128)(2,1)S(1)}, bf16[4,4,384,128]{3,2,1,0:T(8,128)(2,1)S(1)}, u32[]{:S(2)}, u32[]{:S(2)}) %collective-permute-start.17) | collective-permute-done | bytes 1572896 | tf_op jit(solution)/shard_map/ppermute | solution.py:457
  339.7 2.5 fusion.1
  343.0 2.1 collective-permute-start.20
  346.5 1.6 collective-permute-start.13
  349.6 1.5 collective-permute-start.21
  351.1 2.3 collective-permute-done.11
  354.3 4.2 %collective-permute-done.19 = bf16[4,384,128]{2,1,0:T(8,128)(2,1)S(1)} collective-permute-done((bf16[4,384,128]{2,1,0:T(8,128)(2,1)S(1)}, bf16[4,384,128]{2,1,0:T(8,128)(2,1)S(1)}, u32[]{:S(2)}, u32[]{:S(2)}) %collective-permute-start.19) | collective-permute-done | bytes 393248 | tf_op jit(solution)/shard_map/ppermute | solution.py:457
  359.1 1.4 broadcast_in_dim.39
  360.5 4.8 %all-to-all-start.4 = ((bf16[4,4,384,128]{3,2,1,0:T(8,128)(2,1)}), bf16[4,4,384,128]{3,2,1,0:T(8,128)(2,1)}, u32[]{:S(2)}, u32[]{:S(2)}) async-start(bf16[4,4,384,128]{3,2,1,0:T(8,128)(2,1)} %bitcast.50), calls=%async_computation.4 | async-start | bytes 3145728 | tf_op jit(solution)/shard_map/all_to_all | solution.py:541
  365.4 8.5 %collective-permute-start = (bf16[8,96]{1,0:T(8,128)(2,1)S(1)}, bf16[8,96]{1,0:T(8,128)(2,1)S(1)}, u32[]{:S(2)}, u32[]{:S(2)}) collective-permute-start(bf16[8,96]{1,0:T(8,128)(2,1)S(1)} %reduce_sum.42), channel_id=1, source_target_pairs={{0,1},{1,0},{2,3},{3,2},{4,5},{5,4},{6,7},{7,6},{8,9},{9,8},{10,11... | collective-permute-start | bytes 4616 | tf_op jit(solution)/shard_map/ppermute | solution.py:488
  374.7 3.2 collective-permute-start.1
  378.6 1.8 copy.46
  380.4 2.8 reduce_sum.43
  385.0 1.7 reduce_sum.44
  386.8 3.4 collective-permute-start.22
  393.7 11.0 %place.1 = f32[2048,192]{1,0:T(8,128)} custom-call(s32[2048]{0:T(1024)} %bitcast.124, bf16[8,384,128]{2,1,0:T(8,128)(2,1)} %maximum_select_fusion.sum_ref), custom_call_target="tpu_custom_call" | custom-call | flops 100000000 | bytes 3145728 | tf_op jit(solution)/shard_map/place/pallas_call | solution.py:422
  404.8 2.1 multiply_reduce_fusion
  407.5 1.8 divide_subtract_fusion
  409.3 2.8 copy.47
  (118 shorter events, 34.1 us)
Async XLA Ops:
  0.6 13.2 %copy-start.9 = (s32[256]{0:T(256)S(1)}, s32[256]{0:T(256)}, u32[]{:S(2)}) copy-start(s32[256]{0:T(256)} %param.15) | copy-start | bytes 3076
  0.6 31.3 %copy-start.3 = (bf16[384,128]{1,0:T(8,128)(2,1)S(1)}, bf16[384,128]{1,0:T(8,128)(2,1)}, u32[]{:S(2)}) copy-start(bf16[384,128]{1,0:T(8,128)(2,1)} %param.20) | copy-start | bytes 294916
  4.1 27.8 %all-to-all-start = ((bf16[32,144,128]{2,1,0:T(8,128)(2,1)}), bf16[32,144,128]{2,1,0:T(8,128)(2,1)S(1)}, u32[]{:S(2)}, u32[]{:S(2)}) async-start(bf16[32,144,128]{2,1,0:T(8,128)(2,1)} %broadcast_in_dim.34), calls=%async_computation | async-start | bytes 2359296 | tf_op jit(solution)/shard_map/all_to_all | solution.py:452
  34.4 71.9 %all-to-all-start.1 = ((bf16[32,384,128]{2,1,0:T(8,128)(2,1)}), bf16[32,384,128]{2,1,0:T(8,128)(2,1)}, u32[]{:S(2)}, u32[]{:S(2)}) async-start(bf16[32,384,128]{2,1,0:T(8,128)(2,1)} %broadcast_in_dim.35), calls=%async_computation.1 | async-start | bytes 6291456 | tf_op jit(solution)/shard_map/all_to_all | solution.py:452
  125.7 55.7 %copy-start.2 = (s32[128,256]{1,0:T(8,128)S(1)}, s32[128,256]{1,0:T(8,128)}, u32[]{:S(2)}) copy-start(s32[128,256]{1,0:T(8,128)} %param.14) | copy-start | bytes 393220
  125.7 56.6 %copy-start.8 = (s32[256]{0:T(256)S(1)}, s32[256]{0:T(256)}, u32[]{:S(2)}) copy-start(s32[256]{0:T(256)} %reshape.121.order_ref) | copy-start | bytes 3076
  179.1 12.3 %collective-permute-start.4 = (bf16[64,128,384]{2,1,0:T(8,128)(2,1)}, bf16[64,128,384]{2,1,0:T(8,128)(2,1)}, u32[]{:S(2)}, u32[]{:S(2)}) collective-permute-start(bf16[64,128,384]{2,1,0:T(8,128)(2,1)} %get-tuple-element.30), channel_id=1, source_target_pairs={{0,1},{1,0},{2,3},{3,2},{4,5},{5,4},{6,7},{7,6},{8,9},{9,8},{10,11... | collective-permute-start | bytes 18874376 | tf_op jit(solution)/shard_map/ppermute | solution.py:534
  183.0 8.1 %collective-permute-start.5 = (s32[64,2,128]{2,1,0:T(2,128)S(1)}, s32[64,2,128]{2,1,0:T(2,128)S(1)}, u32[]{:S(2)}, u32[]{:S(2)}) collective-permute-start(s32[64,2,128]{2,1,0:T(2,128)S(1)} %bitcast.123), channel_id=1, source_target_pairs={{0,1},{1,0},{2,3},{3,2},{4,5},{5,4},{6,7},{7,6},{8,9},{9,8},{10,11... | collective-permute-start | bytes 196616 | tf_op jit(solution)/shard_map/ppermute | solution.py:516
  191.2 0.6 copy-start.10
  209.5 5.8 %copy-start.4 = (f32[96,256]{1,0:T(8,128)S(1)}, f32[96,256]{1,0:T(8,128)}, u32[]{:S(2)}) copy-start(f32[96,256]{1,0:T(8,128)} %get-tuple-element.25) | copy-start | bytes 294916
  209.5 5.8 %copy-start.5 = (f32[16,256]{1,0:T(8,128)S(1)}, f32[16,256]{1,0:T(8,128)}, u32[]{:S(2)}) copy-start(f32[16,256]{1,0:T(8,128)} %get-tuple-element.26) | copy-start | bytes 49156
  212.5 21.7 %collective-permute-start.6 = (bf16[2,4,384,128]{3,2,1,0:T(8,128)(2,1)}, bf16[2,4,384,128]{3,2,1,0:T(8,128)(2,1)}, u32[]{:S(2)}, u32[]{:S(2)}) collective-permute-start(bf16[2,4,384,128]{3,2,1,0:T(8,128)(2,1)} %get-tuple-element.58), channel_id=1, source_target_pairs={{0,32},{32,64},{64,96},{96,0},{1,33},{33,65},{65,97},{97,1},{2,34}... | collective-permute-start | bytes 2359304 | tf_op jit(solution)/shard_map/ppermute | solution.py:457
  213.8 20.4 %collective-permute-start.8 = (bf16[2,4,384,128]{3,2,1,0:T(8,128)(2,1)S(1)}, bf16[2,4,384,128]{3,2,1,0:T(8,128)(2,1)}, u32[]{:S(2)}, u32[]{:S(2)}) collective-permute-start(bf16[2,4,384,128]{3,2,1,0:T(8,128)(2,1)S(1)} %get-tuple-element.59), channel_id=1, source_target_pairs={{0,96},{32,0},{64,32},{96,64},{1,97},{33,1},{65,33},{97,65},{2,98}... | collective-permute-start | bytes 2359304 | tf_op jit(solution)/shard_map/ppermute | solution.py:457
  216.1 34.3 %all-to-all-start.2 = ((f32[32,8,96]{2,1,0:T(8,128)}), f32[32,8,96]{2,1,0:T(8,128)S(1)}, u32[]{:S(2)}, u32[]{:S(2)}) async-start(f32[32,8,96]{2,1,0:T(8,128)} %bitcast.9), calls=%async_computation.2 | async-start | bytes 262144 | tf_op jit(solution)/shard_map/all_to_all | solution.py:531
  227.3 19.4 %collective-permute-start.14 = (bf16[2,4,384,128]{3,2,1,0:T(8,128)(2,1)S(1)}, bf16[2,4,384,128]{3,2,1,0:T(8,128)(2,1)S(1)}, u32[]{:S(2)}, u32[]{:S(2)}) collective-permute-start(bf16[2,4,384,128]{3,2,1,0:T(8,128)(2,1)S(1)} %get-tuple-element.64), channel_id=1, source_target_pairs={{0,8},{8,16},{16,24},{24,0},{1,9},{9,17},{17,25},{25,1},{2,10},{10... | collective-permute-start | bytes 2359304 | tf_op jit(solution)/shard_map/ppermute | solution.py:457
  228.8 17.9 %collective-permute-start.16 = (bf16[2,4,384,128]{3,2,1,0:T(8,128)(2,1)S(1)}, bf16[2,4,384,128]{3,2,1,0:T(8,128)(2,1)S(1)}, u32[]{:S(2)}, u32[]{:S(2)}) collective-permute-start(bf16[2,4,384,128]{3,2,1,0:T(8,128)(2,1)S(1)} %get-tuple-element.65), channel_id=1, source_target_pairs={{0,24},{8,0},{16,8},{24,16},{1,25},{9,1},{17,9},{25,17},{2,26},{10... | collective-permute-start | bytes 2359304 | tf_op jit(solution)/shard_map/ppermute | solution.py:457
  237.8 2.9 copy-start.1
  237.8 47.5 %collective-permute-start.7 = (bf16[4,4,384,128]{3,2,1,0:T(8,128)(2,1)}, bf16[4,4,384,128]{3,2,1,0:T(8,128)(2,1)}, u32[]{:S(2)}, u32[]{:S(2)}) collective-permute-start(bf16[4,4,384,128]{3,2,1,0:T(8,128)(2,1)} %pad_maximum_fusion.1), channel_id=1, source_target_pairs={{0,32},{32,64},{64,96},{96,0},{1,33},{33,65},{65,97},{97,1},{2,34}... | collective-permute-start | bytes 4718600 | tf_op jit(solution)/shard_map/ppermute | solution.py:457
  238.6 46.7 %collective-permute-start.9 = (bf16[4,4,384,128]{3,2,1,0:T(8,128)(2,1)S(1)}, bf16[4,4,384,128]{3,2,1,0:T(8,128)(2,1)}, u32[]{:S(2)}, u32[]{:S(2)}) collective-permute-start(bf16[4,4,384,128]{3,2,1,0:T(8,128)(2,1)S(1)} %pad_maximum_fusion.2), channel_id=1, source_target_pairs={{0,96},{32,0},{64,32},{96,64},{1,97},{33,1},{65,33},{97,65},{2,98}... | collective-permute-start | bytes 4718600 | tf_op jit(solution)/shard_map/ppermute | solution.py:457
  249.7 54.4 %collective-permute-start.15 = (bf16[4,4,384,128]{3,2,1,0:T(8,128)(2,1)}, bf16[4,4,384,128]{3,2,1,0:T(8,128)(2,1)}, u32[]{:S(2)}, u32[]{:S(2)}) collective-permute-start(bf16[4,4,384,128]{3,2,1,0:T(8,128)(2,1)} %pad_maximum_fusion.3), channel_id=1, source_target_pairs={{0,8},{8,16},{16,24},{24,0},{1,9},{9,17},{17,25},{25,1},{2,10},{10... | collective-permute-start | bytes 4718600 | tf_op jit(solution)/shard_map/ppermute | solution.py:457
  250.4 108.7 %all-to-all-start.3 = ((bf16[32,512,128]{2,1,0:T(8,128)(2,1)}), bf16[32,512,128]{2,1,0:T(8,128)(2,1)}, u32[]{:S(2)}, u32[]{:S(2)}) async-start(bf16[32,512,128]{2,1,0:T(8,128)(2,1)} %pad_maximum_fusion), calls=%async_computation.3 | async-start | bytes 8388608 | tf_op jit(solution)/shard_map/all_to_all | solution.py:528
  258.2 81.4 %collective-permute-start.17 = (bf16[4,4,384,128]{3,2,1,0:T(8,128)(2,1)S(1)}, bf16[4,4,384,128]{3,2,1,0:T(8,128)(2,1)S(1)}, u32[]{:S(2)}, u32[]{:S(2)}) collective-permute-start(bf16[4,4,384,128]{3,2,1,0:T(8,128)(2,1)S(1)} %pad_maximum_fusion.4), channel_id=1, source_target_pairs={{0,24},{8,0},{16,8},{24,16},{1,25},{9,1},{17,9},{25,17},{2,26},{10... | collective-permute-start | bytes 4718600 | tf_op jit(solution)/shard_map/ppermute | solution.py:457
  288.4 56.6 %collective-permute-start.10 = (bf16[2,384,128]{2,1,0:T(8,128)(2,1)S(1)}, bf16[2,384,128]{2,1,0:T(8,128)(2,1)S(1)}, u32[]{:S(2)}, u32[]{:S(2)}) collective-permute-start(bf16[2,384,128]{2,1,0:T(8,128)(2,1)S(1)} %get-tuple-element.70), channel_id=1, source_target_pairs={{0,8},{8,16},{16,24},{24,0},{1,9},{9,17},{17,25},{25,1},{2,10},{10... | collective-permute-start | bytes 589832 | tf_op jit(solution)/shard_map/ppermute | solution.py:457
  301.0 44.0 %collective-permute-start.12 = (bf16[2,384,128]{2,1,0:T(8,128)(2,1)S(1)}, bf16[2,384,128]{2,1,0:T(8,128)(2,1)S(1)}, u32[]{:S(2)}, u32[]{:S(2)}) collective-permute-start(bf16[2,384,128]{2,1,0:T(8,128)(2,1)S(1)} %get-tuple-element.71), channel_id=1, source_target_pairs={{0,24},{8,0},{16,8},{24,16},{1,25},{9,1},{17,9},{25,17},{2,26},{10... | collective-permute-start | bytes 589832 | tf_op jit(solution)/shard_map/ppermute | solution.py:457
  342.3 5.8 %collective-permute-start.18 = (bf16[2,384,128]{2,1,0:T(8,128)(2,1)S(1)}, bf16[2,384,128]{2,1,0:T(8,128)(2,1)S(1)}, u32[]{:S(2)}, u32[]{:S(2)}) collective-permute-start(bf16[2,384,128]{2,1,0:T(8,128)(2,1)S(1)} %get-tuple-element.76), channel_id=1, source_target_pairs={{0,32},{32,64},{64,96},{96,0},{1,33},{33,65},{65,97},{97,1},{2,34}... | collective-permute-start | bytes 589832 | tf_op jit(solution)/shard_map/ppermute | solution.py:457
  343.0 5.1 %collective-permute-start.20 = (bf16[2,384,128]{2,1,0:T(8,128)(2,1)S(1)}, bf16[2,384,128]{2,1,0:T(8,128)(2,1)S(1)}, u32[]{:S(2)}, u32[]{:S(2)}) collective-permute-start(bf16[2,384,128]{2,1,0:T(8,128)(2,1)S(1)} %get-tuple-element.77), channel_id=1, source_target_pairs={{0,96},{32,0},{64,32},{96,64},{1,97},{33,1},{65,33},{97,65},{2,98}... | collective-permute-start | bytes 589832 | tf_op jit(solution)/shard_map/ppermute | solution.py:457
  345.2 8.2 %collective-permute-start.11 = (bf16[4,384,128]{2,1,0:T(8,128)(2,1)S(1)}, bf16[4,384,128]{2,1,0:T(8,128)(2,1)S(1)}, u32[]{:S(2)}, u32[]{:S(2)}) collective-permute-start(bf16[4,384,128]{2,1,0:T(8,128)(2,1)S(1)} %pad_maximum_fusion.5), channel_id=1, source_target_pairs={{0,8},{8,16},{16,24},{24,0},{1,9},{9,17},{17,25},{25,1},{2,10},{10... | collective-permute-start | bytes 1179656 | tf_op jit(solution)/shard_map/ppermute | solution.py:457
  346.5 7.7 %collective-permute-start.13 = (bf16[4,384,128]{2,1,0:T(8,128)(2,1)S(1)}, bf16[4,384,128]{2,1,0:T(8,128)(2,1)S(1)}, u32[]{:S(2)}, u32[]{:S(2)}) collective-permute-start(bf16[4,384,128]{2,1,0:T(8,128)(2,1)S(1)} %pad_maximum_fusion.6), channel_id=1, source_target_pairs={{0,24},{8,0},{16,8},{24,16},{1,25},{9,1},{17,9},{25,17},{2,26},{10... | collective-permute-start | bytes 1179656 | tf_op jit(solution)/shard_map/ppermute | solution.py:457
  348.3 10.3 %collective-permute-start.19 = (bf16[4,384,128]{2,1,0:T(8,128)(2,1)S(1)}, bf16[4,384,128]{2,1,0:T(8,128)(2,1)S(1)}, u32[]{:S(2)}, u32[]{:S(2)}) collective-permute-start(bf16[4,384,128]{2,1,0:T(8,128)(2,1)S(1)} %pad_maximum_fusion.7), channel_id=1, source_target_pairs={{0,32},{32,64},{64,96},{96,0},{1,33},{33,65},{65,97},{97,1},{2,34}... | collective-permute-start | bytes 1179656 | tf_op jit(solution)/shard_map/ppermute | solution.py:457
  349.6 9.1 %collective-permute-start.21 = (bf16[4,384,128]{2,1,0:T(8,128)(2,1)S(1)}, bf16[4,384,128]{2,1,0:T(8,128)(2,1)S(1)}, u32[]{:S(2)}, u32[]{:S(2)}) collective-permute-start(bf16[4,384,128]{2,1,0:T(8,128)(2,1)S(1)} %pad_maximum_fusion.8), channel_id=1, source_target_pairs={{0,96},{32,0},{64,32},{96,64},{1,97},{33,1},{65,33},{97,65},{2,98}... | collective-permute-start | bytes 1179656 | tf_op jit(solution)/shard_map/ppermute | solution.py:457
  360.5 17.5 %copy-start.6 = (s32[8,256]{1,0:T(8,128)S(1)}, s32[8,256]{1,0:T(8,128)}, u32[]{:S(2)}) copy-start(s32[8,256]{1,0:T(8,128)} %param.16) | copy-start | bytes 24580
  360.5 24.5 %all-to-all-start.4 = ((bf16[4,4,384,128]{3,2,1,0:T(8,128)(2,1)}), bf16[4,4,384,128]{3,2,1,0:T(8,128)(2,1)}, u32[]{:S(2)}, u32[]{:S(2)}) async-start(bf16[4,4,384,128]{3,2,1,0:T(8,128)(2,1)} %bitcast.50), calls=%async_computation.4 | async-start | bytes 3145728 | tf_op jit(solution)/shard_map/all_to_all | solution.py:541
  365.4 9.4 %collective-permute-start = (bf16[8,96]{1,0:T(8,128)(2,1)S(1)}, bf16[8,96]{1,0:T(8,128)(2,1)S(1)}, u32[]{:S(2)}, u32[]{:S(2)}) collective-permute-start(bf16[8,96]{1,0:T(8,128)(2,1)S(1)} %reduce_sum.42), channel_id=1, source_target_pairs={{0,1},{1,0},{2,3},{3,2},{4,5},{5,4},{6,7},{7,6},{8,9},{9,8},{10,11... | collective-permute-start | bytes 4616 | tf_op jit(solution)/shard_map/ppermute | solution.py:488
  374.7 9.2 %collective-permute-start.1 = (bf16[8,96]{1,0:T(8,128)(2,1)S(1)}, bf16[8,96]{1,0:T(8,128)(2,1)S(1)}, u32[]{:S(2)}, u32[]{:S(2)}) collective-permute-start(bf16[8,96]{1,0:T(8,128)(2,1)S(1)} %add_convert_fusion.1), channel_id=1, source_target_pairs={{0,2},{2,0},{1,3},{3,1},{4,6},{6,4},{5,7},{7,5},{8,10},{10,8},{9,1... | collective-permute-start | bytes 4616 | tf_op jit(solution)/shard_map/ppermute | solution.py:488
  383.2 1.7 collective-permute-start.2
  384.9 6.4 %collective-permute-start.3 = (bf16[512,128]{1,0:T(8,128)(2,1)S(1)}, bf16[512,128]{1,0:T(8,128)(2,1)S(1)}, u32[]{:S(2)}, u32[]{:S(2)}) collective-permute-start(bf16[512,128]{1,0:T(8,128)(2,1)S(1)} %add_convert_fusion), channel_id=1, source_target_pairs={{0,2},{2,0},{1,3},{3,1},{4,6},{6,4},{5,7},{7,5},{8,10},{10,8},{9,1... | collective-permute-start | bytes 393224 | tf_op jit(solution)/shard_map/ppermute | solution.py:488
  386.8 6.0 %collective-permute-start.22 = (bf16[4,384,128]{2,1,0:T(8,128)(2,1)S(1)}, bf16[4,384,128]{2,1,0:T(8,128)(2,1)S(1)}, u32[]{:S(2)}, u32[]{:S(2)}) collective-permute-start(bf16[4,384,128]{2,1,0:T(8,128)(2,1)S(1)} %reduce_sum.44), channel_id=1, source_target_pairs={{0,1},{1,0},{2,3},{3,2},{4,5},{5,4},{6,7},{7,6},{8,9},{9,8},{10,11... | collective-permute-start | bytes 1179656 | tf_op jit(solution)/shard_map/ppermute | solution.py:543
  393.7 13.1 %copy-start.7 = (f32[2048]{0:T(1024)S(1)}, f32[2048]{0:T(1024)}, u32[]{:S(2)}) copy-start(f32[2048]{0:T(1024)} %param.23) | copy-start | bytes 24580
  404.8 2.7 copy-start

commit v3 on v2

--- a/solution.py
+++ b/solution.py
@@ -38,24 +38,31 @@
 
 def unfold_kernel(x_ref, o_ref):
     tables = o_ref.shape[1]
-    keep = lax.broadcasted_iota(jnp.int32, (1, 1, 128), 2) < 64
+    low = lax.broadcasted_iota(jnp.int32, (1, 1, 128), 2) < 64
 
     def group(j, _):
-        lo, hi = [], []
-        for p in range(8):
-            v = x_ref[:, pl.ds(pl.multiple_of(j * 3072 + 384 * p, 128), 384)].astype(F32)
-            w = pltpu.roll(v, 192, 1)
-            lo += [v[:, :128], w[:, :128]]
-            hi += [v[:, 128:256], w[:, 128:256]]
         at = pl.ds(pl.multiple_of(j * 16, 16), 16)
-        o_ref[:, at, :128] = jnp.swapaxes(jnp.stack(lo), 0, 1).astype(BF16)
-        o_ref[:, at, 128:] = jnp.where(keep, jnp.swapaxes(jnp.stack(hi), 0, 1), 0.0).astype(BF16)
+        for h in range(2):
+            lo, hi = [], []
+            part = slice(16 * h, 16 * h + 16)
+            for p in range(8):
+                v = x_ref[part, pl.ds(pl.multiple_of(j * 3072 + 384 * p, 128), 384)].astype(F32)
+                w = pltpu.roll(v, 192, 1)
+                lo += [v[:, :128], w[:, :128]]
+                if h == 0:
+                    hi += [v[:, 128:256], w[:, 128:256]]
+                else:
+                    hi += [pltpu.roll(v[:, 128:256], 64, 1), v[:, 256:]]
+            hi = jnp.swapaxes(jnp.stack(hi), 0, 1)
+            hi = jnp.where(low, hi, 0.0) if h == 0 else jnp.where(low, 0.0, hi)
+            o_ref[part, at, :128] = jnp.swapaxes(jnp.stack(lo), 0, 1).astype(BF16)
+            o_ref[part, at, 128:] = hi.astype(BF16)
         return 0
 
     lax.fori_loop(0, tables // 16, group, 0)
 
 
-def unfold(x, tables, first, rows=16):
+def unfold(x, tables, first, rows=32):
     count = x.shape[0]
     return pl.pallas_call(
         unfold_kernel,
@@ -73,7 +80,10 @@
     rows = x_ref.shape[0]
     n = x_ref.shape[1]
     w = w_ref[...]
-    keep = lax.broadcasted_iota(jnp.int32, (1, DP), 1) < D
+    lane = lax.broadcasted_iota(jnp.int32, (1, DP), 1)
+    half = (pl.program_id(0) * rows // 16) % 2
+    keep = (lane < 128) | ((lane >= 128 + 64 * half) & (lane < 192 + 64 * half))
+    total = lambda v: jnp.sum(jnp.sum(v, axis=0, keepdims=True), axis=1, keepdims=True)
     for b in range(rows):
         xb = x_ref[b]
         r = dot(w, xb)
@@ -82,11 +92,10 @@
         s_ref[b, K:, :] = slo
         f2 = dot(jnp.concatenate([shi, slo], axis=0), xb, NT)
         fm = f2[:K] + f2[K:]
-        mean = jnp.sum(fm) * (1.0 / (K * n))
-        c = fm - mean
-        inv = 1.0 / jnp.sqrt(jnp.full((1, 128), jnp.sum(c * c), F32) * (1.0 / (K * n)) + EPS)
-        inv_ref[b : b + 1, :] = inv
-        xh = c * inv[:, :1]
+        c = fm - total(fm) * (1.0 / (K * n))
+        inv = 1.0 / jnp.sqrt(total(c * c) * (1.0 / (K * n)) + EPS)
+        inv_ref[b : b + 1, :] = jnp.broadcast_to(inv, (1, 128))
+        xh = c * inv
         lo[pl.ds(b, K, stride=rows), :] = xh[:, :128]
         hi[pl.ds(b, K, stride=rows), :] = xh[:, 128:]
         lout = r[K:]
@@ -228,10 +237,9 @@
 
 
 def last_kernel(
-    order_ref, x_ref, s_ref, dl_ref, dfm_ref, wt_ref, keep_ref, send_ref, acc_ref, flo, fhi, lo, hi
+    at_ref, x_ref, s_ref, dl_ref, dfm_ref, wt_ref, keep_ref, send_ref, acc_ref, flo, fhi, dx, both
 ):
     rows, n = x_ref.shape[0], x_ref.shape[1]
-    pairs = keep_ref.shape[0]
 
     @pl.when(pl.program_id(0) == 0)
     def _():
@@ -253,35 +261,30 @@
         acc_ref[...] += dot(low, xb, NT)
         left = jnp.concatenate([dfm, dfm, proj, shared], axis=0)
         right = jnp.concatenate([s_ref[b], dlo, dhi, dl], axis=0)
-        dx = dot(left, right, TN)
-        lo[pl.ds(b, n, stride=rows), :] = dx[:, :128]
-        hi[pl.ds(b, n, stride=rows), :] = dx[:, 128:]
+        dx[b] = dot(left, right, TN)
         return 0
 
-    lax.fori_loop(0, rows, sample, 0, unroll=2)
-    keep = lax.broadcasted_iota(jnp.int32, (rows, 128), 1) < 64
-
-    def pair(i, _):
-        for part, ref in enumerate((keep_ref, send_ref)):
-            t0 = order_ref[part * 2 * pairs + 2 * i]
-            t1 = order_ref[part * 2 * pairs + 2 * i + 1]
-            p0 = pl.ds(pl.multiple_of(t0 * rows, rows), rows)
-            p1 = pl.ds(pl.multiple_of(t1 * rows, rows), rows)
-            a1 = pltpu.roll(lo[p1, :], 64, 1)
-            b1 = pltpu.roll(hi[p1, :], 64, 1)
-            v = jnp.concatenate(
-                [lo[p0, :], jnp.where(keep, hi[p0, :], a1), jnp.where(keep, a1, b1)], axis=1
-            )
-            ref[i] = v.astype(BF16)
+    lax.fori_loop(0, rows, sample, 0, unroll=8)
+
+    def turn(j, _):
+        at = pl.ds(pl.multiple_of(j * 16, 16), 16)
+        lo = jnp.swapaxes(dx[:, at, :128], 0, 1).astype(BF16)
+        hi = jnp.swapaxes(dx[:16, at, 128:] + dx[16:, at, 128:], 0, 1).astype(BF16)
+        for i in range(16):
+            p = at_ref[j * 16 + i]
+            both[p, :rows, :] = lo[i]
+            both[p, rows:, :] = hi[i]
         return 0
 
-    lax.fori_loop(0, pairs, pair, 0, unroll=4)
-
-
-def last(order, x3, s, dl, dfm, wt, rows=16):
+    lax.fori_loop(0, n // 16, turn, 0)
+    keep_ref[:, 0] = both[: n // 2]
+    send_ref[:, 0] = both[n // 2 :]
+
+
+def last(at, x3, s, dl, dfm, wt, rows=32):
     count, n, _ = x3.shape
     nl = dl.shape[1]
-    pairs = n // 4
+    out = pl.BlockSpec((n // 2, 1, rows + rows // 2, 128), lambda i, o: (0, i, 0, 0))
     grid = pltpu.PrefetchScalarGridSpec(
         num_scalar_prefetch=1,
         grid=(count // rows,),
@@ -292,44 +295,30 @@
             pl.BlockSpec((K, rows, n), lambda i, o: (0, i, 0)),
             pl.BlockSpec(wt.shape, lambda i, o: (0, 0)),
         ],
-        out_specs=[
-            pl.BlockSpec((pairs, rows, 2 * D), lambda i, o: (0, i, 0)),
-            pl.BlockSpec((pairs, rows, 2 * D), lambda i, o: (0, i, 0)),
-            pl.BlockSpec((2 * K + nl, n), lambda i, o: (0, 0)),
-        ],
+        out_specs=[out, out, pl.BlockSpec((2 * K + nl, n), lambda i, o: (0, 0))],
         scratch_shapes=[pltpu.VMEM((K * rows, 128), F32)] * 2
-        + [pltpu.VMEM((n * rows, 128), F32)] * 2,
+        + [pltpu.VMEM((rows, n, DP), F32), pltpu.VMEM((n, rows + rows // 2, 128), BF16)],
     )
+    half = jax.ShapeDtypeStruct((n // 2, count // rows, rows + rows // 2, 128), BF16)
     return pl.pallas_call(
         last_kernel,
         grid_spec=grid,
-        out_shape=[
-            jax.ShapeDtypeStruct((pairs, count, 2 * D), BF16),
-            jax.ShapeDtypeStruct((pairs, count, 2 * D), BF16),
-            jax.ShapeDtypeStruct((2 * K + nl, n), F32),
-        ],
+        out_shape=[half, half, jax.ShapeDtypeStruct((2 * K + nl, n), F32)],
         compiler_params=params(),
         cost_estimate=cost(2e10, count * n * DP * 4),
         name="last",
-    )(order, x3, s, dl, dfm, wt)
-
-
-def fold(v, even):
-    half = v.shape[0] // 2
-    main, tail = (v[:, :128], v[:, 128:]) if even else (v[:, 128:], v[:, :128])
-    keep = lax.broadcasted_iota(jnp.int32, (half, 128), 1) < 64
-    if even:
-        tail = jnp.where(keep, tail[:half], pltpu.roll(tail[half:], 64, 1))
-    else:
-        tail = jnp.where(keep, pltpu.roll(tail[:half], 64, 1), tail[half:])
-    return main.astype(BF16), tail.astype(BF16)
+    )(at, x3, s, dl, dfm, wt)
 
 
 def sums_kernel(at_ref, mine_ref, other_ref, ids_ref, oid_ref, even_ref, odd_ref):
-    pairs, count, _ = mine_ref.shape
+    tables, steps, height, _ = mine_ref.shape
+    part = height // 3
+    count = ids_ref.shape[2]
     rows = 2 * count
     iota = lax.broadcasted_iota(jnp.int32, (rows, count), 0)
-    for i in range(pairs):
+    low = lax.broadcasted_iota(jnp.int32, (1, 128), 1) < 64
+    zero = jnp.zeros((part, 128), BF16)
+    for i in range(tables // 2):
         for t, ref in enumerate((even_ref, odd_ref)):
             hot = jnp.concatenate(
                 [
@@ -338,25 +327,31 @@
                 ],
                 axis=1,
             )
-            cols = slice(128 * t, 128 * t + DP)
-            block = jnp.concatenate([mine_ref[i, :, cols], other_ref[i, :, cols]], axis=0)
-            main, tail = fold(dot(hot, block), t == 0)
-            ref[0, 0, i, :rows, :] = main
-            ref[0, 0, i, rows:, :] = tail
+            main, rest = [], []
+            for r in (mine_ref, other_ref):
+                for s in range(steps):
+                    tail = r[2 * i + t, s, 2 * part :, :]
+                    main.append(r[2 * i + t, s, : 2 * part, :])
+                    rest += [jnp.where(low, tail, zero), jnp.where(low, zero, tail)]
+            block = jnp.concatenate(
+                [jnp.concatenate(main, axis=0), jnp.concatenate(rest, axis=0)], axis=1
+            )
+            out = dot(hot, block)
+            tail = out[:, 128:] + pltpu.roll(out[:, 128:], 64, 1)
+            ref[0, 0, i, :rows, :] = out[:, :128].astype(BF16)
+            ref[0, 0, i, rows:, :] = jnp.where(low, tail[:count], tail[count:]).astype(BF16)
 
 
 def sums(at, mine, other, ids, oids, nz, nx):
-    total, count, wide = mine.shape
-    ny = total // (nz * nx)
+    tables, steps, height, _ = mine.shape
+    count = ids.shape[2]
+    ny = tables // (2 * nz * nx)
+    data = pl.BlockSpec((2 * ny, steps, height, 128), lambda z, x, at: (z * nx + x, 0, 0, 0))
+    index = pl.BlockSpec((ny, 2, count), lambda z, x, at: (z * nx + x, 0, 0))
     grid = pltpu.PrefetchScalarGridSpec(
         num_scalar_prefetch=1,
         grid=(nz, nx),
-        in_specs=[
-            pl.BlockSpec((ny, count, wide), lambda z, x, at: (z * nx + x, 0, 0)),
-            pl.BlockSpec((ny, count, wide), lambda z, x, at: (z * nx + x, 0, 0)),
-            pl.BlockSpec((ny, 2, count), lambda z, x, at: (z * nx + x, 0, 0)),
-            pl.BlockSpec((ny, 2, count), lambda z, x, at: (z * nx + x, 0, 0)),
-        ],
+        in_specs=[data, data, index, index],
         out_specs=[
             pl.BlockSpec(
                 (1, 1, ny, 384, 128),
@@ -381,69 +376,65 @@
     )(at, mine, other, ids, oids)
 
 
-def place_kernel(slot_ref, sum_ref, out_ref, acc, turn):
+def update_kernel(slot_ref, sum_ref, rows_ref, accum_ref, new_rows_ref, new_accum_ref, acc):
     tables = sum_ref.shape[0]
-    state = out_ref.shape[0]
+    state = rows_ref.shape[1]
     rows = state // tables
     half = rows // 2
-    keep = lax.broadcasted_iota(jnp.int32, (half, 128), 1) < 64
     for t in range(tables):
-        main = sum_ref[t, :rows, :].astype(F32)
-        tail = sum_ref[t, rows:, :].astype(F32)
-        first, second = slice(t * rows, t * rows + half), slice(t * rows + half, (t + 1) * rows)
-        flip = pltpu.roll(tail, 64, 1)
-        if t % 2 == 0:
-            acc[t * rows : (t + 1) * rows, :128] = main
-            acc[first, 128:] = tail
-            acc[second, 128:] = flip
-        else:
-            turned = pltpu.roll(main, 64, 1)
-            acc[first, :128] = jnp.where(keep, tail, turned[:half])
-            acc[second, :128] = jnp.where(keep, flip, turned[half:])
-            acc[t * rows : (t + 1) * rows, 128:] = turned
-
-    def place(i, _):
-        turn[pl.ds(slot_ref[i], 1), :] = acc[pl.ds(i, 1), :]
-        return 0
-
-    lax.fori_loop(0, state, place, 0, unroll=8)
-    out_ref[...] = turn[:, :D]
-
-
-def place(slots, sums):
-    state = slots.shape[0]
-    grid = pltpu.PrefetchScalarGridSpec(
-        num_scalar_prefetch=1,
-        grid=(1,),
-        in_specs=[pl.BlockSpec(sums.shape, lambda i, s: (0, 0, 0))],
-        out_specs=pl.BlockSpec((state, D), lambda i, s: (0, 0)),
-        scratch_shapes=[pltpu.VMEM((state, DP), F32)] * 2,
-    )
+        first = slice(t * rows, t * rows + half)
+        second = slice(t * rows + half, (t + 1) * rows)
+        main = sum_ref[t, :rows, :].astype(F32).T.astype(BF16)
+        tail = sum_ref[t, rows:, :].astype(F32).T.astype(BF16)
+        acc[:128, t * rows : (t + 1) * rows] = main
+        acc[128:, first] = tail[:64]
+        acc[128:, second] = tail[64:]
+    size = 256
+    iota = lax.broadcasted_iota(jnp.int32, (size, state), 0)
+    slots = slot_ref[...]
+    for i in range(state // size):
+        at = slice(i * size, (i + 1) * size)
+        hot = jnp.where(iota == slots - i * size, 1.0, 0.0).astype(BF16)
+        total = dot(acc[...], hot, NT)
+        accum = accum_ref[:, at] + jnp.sum(total * total, axis=0, keepdims=True) * (1.0 / D)
+        new_accum_ref[:, at] = accum
+        new_rows_ref[:, at] = rows_ref[:, at] - LEARN * total / jnp.sqrt(accum)
+
+
+def update(slots, sums, table_rows, row_accum):
+    state = slots.shape[1]
     return pl.pallas_call(
-        place_kernel,
-        grid_spec=grid,
-        out_shape=jax.ShapeDtypeStruct((state, D), F32),
+        update_kernel,
+        out_shape=[
+            jax.ShapeDtypeStruct((D, state), F32),
+            jax.ShapeDtypeStruct((1, state), F32),
+        ],
+        scratch_shapes=[pltpu.VMEM((D, state), BF16)],
         compiler_params=params(),
-        cost_estimate=cost(1e8, state * D * 8),
-        name="place",
-    )(slots, sums)
-
-
-def layer(samples, out_grad, order, proj, gain, w_in, w_out, w_lcb):
+        cost_estimate=cost(4e9, state * D * 12),
+        name="update",
+    )(slots, sums, table_rows, row_accum)
+
+
+def forward(x3, g2, proj, w_lcb):
+    wt = jnp.concatenate([proj.T, w_lcb.T], axis=0)
+    return (wt,) + tuple(first(x3, g2, wt))
+
+
+def layer(samples, out_grad, spot, proj, gain, w_in, w_out, w_lcb):
     n = proj.shape[0]
     nl = w_lcb.shape[1]
     x3 = unfold(samples, n, 0)
     g2 = unfold(out_grad, nl, out_grad.shape[1] // D // nl - 1)
-    wt = jnp.concatenate([proj.T, w_lcb.T], axis=0)
+    wt, s, dl, xh, inv = forward(x3, g2, proj, w_lcb)
     gain_t = gain.reshape(n, K).T.astype(F32)
     win_t = w_in.reshape(n, K, 128).transpose(1, 0, 2)
-    s, dl, xh, inv = first(x3, g2, wt)
     g_out, g_in, g_gain, dfm = batch(xh, inv, gain_t, win_t, w_out, out_grad)
-    keep, send, acc = last(order, x3, s, dl, dfm, wt)
-    g_proj = acc[:K] + acc[K : 2 * K]
-    return g_proj, g_gain, g_in, g_out, acc[2 * K :], keep, send
-
-
+    keep, send, acc = last(spot, x3, s, dl, dfm, wt)
+    return acc[:K] + acc[K : 2 * K], g_gain, g_in, g_out, acc[2 * K :], keep, send
+
+
+SWAP = [(0, 1), (1, 0)]
 WIDE = ("z", "x", "yl")
 
 
@@ -478,9 +469,6 @@
     return [add(v[0], f, b) for (_, v), f, b in zip(parts, fore, back)]
 
 
-SWAP = [(0, 1), (1, 0)]
-
-
 def rep_sum(v):
     swap = SWAP
     for axis in ("c", "yh"):
@@ -498,26 +486,33 @@
     per = proj.shape[0]
     n = per * owners
     nl = w_lcb.shape[1]
+    core = lax.axis_index("c")
     small = jnp.concatenate([proj, gain_flat.reshape(per, K), w_lcb], axis=1)
-    small = jnp.pad(small, ((0, 8), (0, 128 - small.shape[1])))
-    packed = gather(jnp.concatenate([w_in, small], axis=0))
-    w_in_f = packed[:, : w_in.shape[0]].reshape(-1, 128)
-    small_f = packed[:, w_in.shape[0] : w_in.shape[0] + per].reshape(n, 128)
-    proj_f = small_f[:, :K]
-    gain_f = small_f[:, K : 2 * K].reshape(-1)
-    w_lcb_f = small_f[:, 2 * K : 2 * K + nl]
-    w_out_f = gather(w_out).reshape(-1, 128)
-
-    core = lax.axis_index("c")
-    order = jnp.zeros((n,), jnp.int32).at[table_owner].set(jnp.arange(n, dtype=jnp.int32))
-    order = order.reshape(owners, 2, per // 2).transpose(1, 0, 2)
-    order = jnp.where(core == 0, order, order[::-1]).reshape(-1)
+    small = gather(jnp.pad(small, ((0, 8), (0, 128 - small.shape[1]))))[:, :per].reshape(n, 128)
+    proj_f = small[:, :K]
+    gain_t = small[:, K : 2 * K].T.astype(F32)
+    w_lcb_f = small[:, 2 * K : 2 * K + nl]
+    shard = jnp.concatenate([w_in, w_out], axis=0)
+    rows = shard.shape[0] // 2
+    near = gather(lax.dynamic_slice_in_dim(shard, core * rows, rows, 0))
+    far = lax.ppermute(near, "c", SWAP)
+    lower, upper = jnp.where(core == 0, near, far), jnp.where(core == 0, far, near)
+    w_in_t = lower[:, : w_in.shape[0]].reshape(n, K, 128).transpose(1, 0, 2)
+    w_out_f = jnp.concatenate([lower[:, w_in.shape[0] :], upper], axis=1).reshape(-1, 128)
+
+    quad = per // 2
+    spot = table_owner // per * quad + table_owner % quad
+    spot = jnp.where((table_owner % per) // quad == core, spot, spot + n // 2)
+    order = jnp.zeros((n,), jnp.int32).at[spot].set(jnp.arange(n, dtype=jnp.int32))
     ids = jnp.take(row_ids.T, order, axis=0).reshape(2, n // 4, 2, count)
     other_ids = lax.ppermute(ids[1], "c", SWAP)
 
-    g_proj, g_gain, g_in, g_out, g_lcb, keep, send = layer(
-        samples, out_grad, order, proj_f, gain_f, w_in_f, w_out_f, w_lcb_f
-    )
+    x3 = unfold(samples, n, 0)
+    g2 = unfold(out_grad, nl, out_grad.shape[1] // D // nl - 1)
+    wt, score, dl, xh, inv = forward(x3, g2, proj_f, w_lcb_f)
+    g_out, g_in, g_gain, dfm = batch(xh, inv, gain_t, w_in_t, w_out_f, out_grad)
+    keep, send, acc = last(spot, x3, score, dl, dfm, wt)
+    g_proj, g_lcb = acc[:K] + acc[K : 2 * K], acc[2 * K :]
     big = jnp.concatenate(
         [
             g_out.reshape(owners, -1, 128),
@@ -526,6 +521,7 @@
         axis=1,
     )
     big = lax.all_to_all(big, WIDE, 0, 0, tiled=True)
+    big, send = lax.optimization_barrier((big, send))
     big = rep_sum(jnp.sum(big.astype(F32), axis=0))
     little = jnp.concatenate([g_proj, g_gain, g_lcb], axis=0).T.reshape(owners, per, -1)
     little = lax.all_to_all(little, WIDE, 0, 0, tiled=True)
@@ -544,18 +540,18 @@
     owned = jnp.where(
         core == 0, jnp.concatenate([mine, others], axis=0), jnp.concatenate([others, mine], axis=0)
     )
-    total = place(slot_map.reshape(-1), owned)
+    new_rows, new_accum = update(
+        slot_map.reshape(1, -1), owned, table_rows.T, row_accum.reshape(1, -1)
+    )
     split_at = w_out.shape[0]
-    new_accum = row_accum + jnp.mean(total * total, axis=1)
-    new_rows = table_rows - LEARN * total / jnp.sqrt(new_accum)[:, None]
     return (
         little[:, :K],
         little[:, K : 2 * K].reshape(-1),
         big[split_at:],
         big[:split_at],
         little[:, 2 * K :],
-        new_rows,
-        new_accum,
+        new_rows.T,
+        new_accum.reshape(-1),
     )
 
 

time: 416 us -> 338 us (0.81)
  Pallas kernels: 165 us -> 127 us
  starting transfers between devices: 87.6 us -> 69 us
  local copies, waits for them, and re-layouts: 26.9 us -> 17.8 us
  waiting for transfers between devices: 101 us -> 93.5 us
  other arithmetic: 30.9 us -> 23.6 us
    ppermute x16, waiting for transfers between devices: 75.4 us -> 50 us  [ring_step(): return lax.ppermute(v, axis, [(i, (i + by) % n) for i in range(n)])]
    pallas_call x2, Pallas kernels: 64.5 us -> 44.6 us  [the longest x1 38.6 us: last(): pl.pallas_call(last_kernel, grid_spec=grid, out_shape=[half, half, jax.Sh...]
    all_to_all x1, waiting for transfers between devices: 0.01 us -> 19.5 us  [body(): big = lax.all_to_all(big, WIDE, 0, 0, tiled=True)]
    ppermute x16, starting transfers between devices: 35.6 us -> 21.9 us  [ring_step(): return lax.ppermute(v, axis, [(i, (i + by) % n) for i in range(n)])]
    pallas_call x1, Pallas kernels: 32.9 us -> 21.6 us  [first(): pl.pallas_call(first_kernel, grid=(count // rows,), in_specs=[pl.BlockSpe...]
    all_to_all x2, waiting for transfers between devices: 16.4 us -> 9.34 us  [gather(): lax.all_to_all(jnp.broadcast_to(a[None], (n,) + a.shape), WIDE, 0, 0, til...]
    pallas_call x2, Pallas kernels: 30.4 us -> 24 us  [unfold(): pl.pallas_call(unfold_kernel, grid=(count // rows,), in_specs=[pl.BlockSp...]
    convert_element_type x8, other arithmetic: 10.2 us -> 4.84 us  [add(): return total.astype(BF16)]
  transfers between devices with their start and end apart: 28 -> 29, of which waited for: 13 -> 15; matrix products, arithmetic and copies ran while one was open for 9% -> 7% of each run, Pallas kernels for 15% -> 25%
where the time goes in v3:
time: 338 us; the launch traced here: 332 us
  Pallas kernels  127 us (38%)
  waiting for transfers between devices  93.5 us (28%)
  starting transfers between devices  69 us (20%)
  other arithmetic  23.6 us (7%)
  local copies, waits for them, and re-layouts  17.8 us (5%)
    ppermute x16, waiting for transfers between devices, ring_step(): return lax.ppermute(v, axis, [(i, (i + by) % n) for i in range(n)])  50 us
    pallas_call x1, Pallas kernels, last(): pl.pallas_call(last_kernel, grid_spec=grid, out_shape=[half, half, jax.Sh...  38.6 us
    pallas_call x2, Pallas kernels, unfold(): pl.pallas_call(unfold_kernel, grid=(count // rows,), in_specs=[pl.BlockSp...  24 us
    ppermute x16, starting transfers between devices, ring_step(): return lax.ppermute(v, axis, [(i, (i + by) % n) for i in range(n)])  21.9 us
    pallas_call x1, Pallas kernels, first(): pl.pallas_call(first_kernel, grid=(count // rows,), in_specs=[pl.BlockSpe...  21.6 us
    all_to_all x1, waiting for transfers between devices, body(): big = lax.all_to_all(big, WIDE, 0, 0, tiled=True)  19.5 us
    pallas_call x1, Pallas kernels, batch(): pl.pallas_call(batch_kernel, grid=(total // rows,), in_specs=[whole((k, c...  19.4 us
    pallas_call x1, Pallas kernels, sums(): pl.pallas_call(sums_kernel, grid_spec=grid, out_shape=[jax.ShapeDtypeStru...  17.8 us
  transfers between devices with their start and end apart: 29, of which 15 were waited for; matrix products, arithmetic and copies ran while one was open for 7% of the time, Pallas kernels for 25%

profile of v3, /device:TPU:1, one launch (start us, length us, event | category | flops | bytes accessed | tf_op | source)
XLA Modules:
  0.0 332.4 jit_solution(12246084944489838140)
XLA Ops:
  2.8 9.7 %all-to-all-start = ((bf16[32,16,128]{2,1,0:T(8,128)(2,1)}), bf16[32,16,128]{2,1,0:T(8,128)(2,1)S(1)}, u32[]{:S(2)}, u32[]{:S(2)}) async-start(bf16[32,16,128]{2,1,0:T(8,128)(2,1)} %broadcast_in_dim.34), calls=%async_computation | async-start | bytes 262144 | tf_op jit(solution)/shard_map/all_to_all | solution.py:443
  13.4 6.7 %all-to-all-done = bf16[32,16,128]{2,1,0:T(8,128)(2,1)S(1)} async-done(((bf16[32,16,128]{2,1,0:T(8,128)(2,1)}), bf16[32,16,128]{2,1,0:T(8,128)(2,1)S(1)}, u32[]{:S(2)}, u32[]{:S(2)}) %all-to-all-start) | async-done | bytes 131104 | tf_op jit(solution)/shard_map/all_to_all | solution.py:443
  20.2 1.8 broadcast_in_dim.35
  22.0 4.0 %all-to-all-start.1 = ((bf16[32,256,128]{2,1,0:T(8,128)(2,1)}), bf16[32,256,128]{2,1,0:T(8,128)(2,1)S(1)}, u32[]{:S(2)}, u32[]{:S(2)}) async-start(bf16[32,256,128]{2,1,0:T(8,128)(2,1)} %broadcast_in_dim.35), calls=%async_computation.1 | async-start | bytes 4194304 | tf_op jit(solution)/shard_map/all_to_all | solution.py:443
  26.0 17.7 %unfold.2.x_ref = bf16[128,256,256]{2,1,0:T(8,128)(2,1)} custom-call(bf16[128,49152]{1,0:T(8,128)(2,1)} %x_ref.2), custom_call_target="tpu_custom_call" | custom-call | flops 1000000000 | bytes 29491200 | tf_op jit(solution)/shard_map/unfold/pallas_call | solution.py:67
  43.7 6.3 %unfold.3.g_ref = bf16[128,64,256]{2,1,0:T(8,128)(2,1)} custom-call(bf16[128,24576]{1,0:T(8,128)(2,1)} %g_ref.1), custom_call_target="tpu_custom_call" | custom-call | flops 1000000000 | bytes 7372800 | tf_op jit(solution)/shard_map/unfold/pallas_call | solution.py:67
  51.1 2.6 all-to-all-done.1
  53.7 3.3 %collective-permute-start = (bf16[32,256,128]{2,1,0:T(8,128)(2,1)S(1)}, bf16[32,256,128]{2,1,0:T(8,128)(2,1)S(1)}, u32[]{:S(2)}, u32[]{:S(2)}) collective-permute-start(bf16[32,256,128]{2,1,0:T(8,128)(2,1)S(1)} %all-to-all-done.1), channel_id=1, source_target_pairs={{0,1},{1,0},{2,3},{3,2},{4,5},{5,4},{6,7},{7,6},{8,9},{9,8},{10,11... | collective-permute-start | bytes 6291464 | tf_op jit(solution)/shard_map/ppermute | solution.py:498
  57.6 21.6 %first.1 = (bf16[128,32,256]{2,1,0:T(8,128)(2,1)}, bf16[128,64,256]{2,1,0:T(8,128)(2,1)}, f32[16,128,256]{2,1,0:T(8,128)}, f32[128,128]{1,0:T(8,128)}) custom-call(bf16[128,256,256]{2,1,0:T(8,128)(2,1)} %unfold.2.x_ref, bf16[128,64,256]{2,1,0:T(8,128)(2,1)} %unfold.3.g_ref, bf16[80,256]{1,0:T(8,128)(2,1)} %pad_maximum_fusion.10.w_ref.wt_ref), custom_call_target="tpu_custom_call" | custom-call | flops 20000000000 | bytes 16777216 | tf_op jit(solution)/shard_map/first/pallas_call | solution.py:116
  79.7 1.2 copy.43
  81.0 2.0 pad_maximum_fusion.1
  83.0 19.4 %batch.1 = (bf16[12288,128]{1,0:T(8,128)(2,1)}, f32[16,256,128]{2,1,0:T(8,128)}, f32[16,256]{1,0:T(8,128)}, f32[16,128,256]{2,1,0:T(8,128)}) custom-call(f32[16,128,256]{2,1,0:T(8,128)} %get-tuple-element.26.xh_ref, f32[128,128]{1,0:T(8,128)} %get-tuple-element.27.inv_ref, f32[16,256]{1,0:T(8,128)} %convert_bitcast_fusion.1.gain_ref, ...), custom_call_target="tpu_custom_call" | custom-call | flops 20000000000 | bytes 20000000 | tf_op jit(solution)/shard_map/batch/pallas_call | solution.py:203
  102.4 1.9 convert_bitcast_fusion
  105.0 2.3 pad_maximum_fusion
  107.3 5.0 %all-to-all-start.3 = ((bf16[32,512,128]{2,1,0:T(8,128)(2,1)}), bf16[32,512,128]{2,1,0:T(8,128)(2,1)}, u32[]{:S(2)}, u32[]{:S(2)}) async-start(bf16[32,512,128]{2,1,0:T(8,128)(2,1)} %pad_maximum_fusion), calls=%async_computation.3 | async-start | bytes 8388608 | tf_op jit(solution)/shard_map/all_to_all | solution.py:523
  112.9 38.6 %last.1 = (bf16[128,4,48,128]{3,2,1,0:T(8,128)(2,1)}, bf16[128,4,48,128]{3,2,1,0:T(8,128)(2,1)}, f32[96,256]{1,0:T(8,128)}) custom-call(s32[256]{0:T(256)} %get-tuple-element.42.at_ref, bf16[128,256,256]{2,1,0:T(8,128)(2,1)} %unfold.2.x_ref, bf16[128,32,256]{2,1,0:T(8,128)(2,1)} %get-tuple-element.24.s_ref, bf16[128,64,256]{2,1,0:T(8,128)(2,1)} %get-tuple-element.25.dl_ref, ...), custom_call_target="tpu_custom_call" | custom-call | flops 20000000000 | bytes 33554432 | tf_op jit(solution)/shard_map/last/pallas_call | solution.py:303
  151.5 19.5 %all-to-all-done.3 = bf16[32,512,128]{2,1,0:T(8,128)(2,1)} async-done(((bf16[32,512,128]{2,1,0:T(8,128)(2,1)}), bf16[32,512,128]{2,1,0:T(8,128)(2,1)}, u32[]{:S(2)}, u32[]{:S(2)}) %all-to-all-start.3) | async-done | bytes 4194336 | tf_op jit(solution)/shard_map/all_to_all | solution.py:523
  171.7 1.4 scatter_custom_fusion
  175.2 6.3 %collective-permute-done.6.oid_ref = s32[64,2,128]{2,1,0:T(2,128)S(1)} collective-permute-done((s32[64,2,128]{2,1,0:T(2,128)S(1)}, s32[64,2,128]{2,1,0:T(2,128)S(1)}, u32[]{:S(2)}, u32[]{:S(2)}) %collective-permute-start.6) | collective-permute-done | bytes 65568 | tf_op jit(solution)/shard_map/ppermute | solution.py:508
  182.1 17.8 %sums.1 = (bf16[4,4,4,384,128]{4,3,2,1,0:T(8,128)(2,1)}, bf16[4,4,4,384,128]{4,3,2,1,0:T(8,128)(2,1)}) custom-call(s32[2]{0:T(128)} %pad_add_fusion.at_ref, bf16[128,4,48,128]{3,2,1,0:T(8,128)(2,1)} %get-tuple-element.35.mine_ref, bf16[128,4,48,128]{3,2,1,0:T(8,128)(2,1)} %collective-permute-done.5.other_ref, s32[64,2,128]{2,1,0:T(2,128)} %bitcast.124, ...), custom_call_target="tpu_custom_call" | custom-call | flops 10000000000 | bytes 25165824 | tf_op jit(solution)/shard_map/sums/pallas_call | solution.py:366
  199.9 2.3 slice_bitcast_fusion.7
  202.3 2.7 collective-permute-start.9
  205.3 1.5 collective-permute-start.15
  206.8 1.2 collective-permute-start.17
  208.0 14.3 %collective-permute-done.7 = bf16[2,4,384,128]{3,2,1,0:T(8,128)(2,1)S(1)} collective-permute-done((bf16[2,4,384,128]{3,2,1,0:T(8,128)(2,1)S(1)}, bf16[2,4,384,128]{3,2,1,0:T(8,128)(2,1)S(1)}, u32[]{:S(2)}, u32[]{:S(2)}) %collective-permute-start.7) | collective-permute-done | bytes 786464 | tf_op jit(solution)/shard_map/ppermute | solution.py:448
  223.1 2.7 collective-permute-start.10
  225.8 4.2 %collective-permute-done.17 = bf16[2,4,384,128]{3,2,1,0:T(8,128)(2,1)S(1)} collective-permute-done((bf16[2,4,384,128]{3,2,1,0:T(8,128)(2,1)S(1)}, bf16[2,4,384,128]{3,2,1,0:T(8,128)(2,1)S(1)}, u32[]{:S(2)}, u32[]{:S(2)}) %collective-permute-start.17) | collective-permute-done | bytes 786464 | tf_op jit(solution)/shard_map/ppermute | solution.py:448
  230.5 1.2 collective-permute-start.16
  231.9 1.6 collective-permute-start.18
  233.5 25.3 %collective-permute-done.8 = bf16[4,4,384,128]{3,2,1,0:T(8,128)(2,1)S(1)} collective-permute-done((bf16[4,4,384,128]{3,2,1,0:T(8,128)(2,1)S(1)}, bf16[4,4,384,128]{3,2,1,0:T(8,128)(2,1)S(1)}, u32[]{:S(2)}, u32[]{:S(2)}) %collective-permute-start.8) | collective-permute-done | bytes 1572896 | tf_op jit(solution)/shard_map/ppermute | solution.py:448
  259.5 1.5 collective-permute-start.11
  262.2 3.6 %collective-permute-done.16 = bf16[4,4,384,128]{3,2,1,0:T(8,128)(2,1)S(1)} collective-permute-done((bf16[4,4,384,128]{3,2,1,0:T(8,128)(2,1)S(1)}, bf16[4,4,384,128]{3,2,1,0:T(8,128)(2,1)S(1)}, u32[]{:S(2)}, u32[]{:S(2)}) %collective-permute-start.16) | collective-permute-done | bytes 1572896 | tf_op jit(solution)/shard_map/ppermute | solution.py:448
  265.8 1.4 collective-permute-done.18
  268.1 2.7 collective-permute-start.21
  274.6 1.8 collective-permute-start.14
  278.0 2.7 collective-permute-start.22
  281.5 3.9 %all-to-all-start.2 = ((f32[32,8,96]{2,1,0:T(8,128)}), f32[32,8,96]{2,1,0:T(8,128)S(1)}, u32[]{:S(2)}, u32[]{:S(2)}) async-start(f32[32,8,96]{2,1,0:T(8,128)} %bitcast.8), calls=%async_computation.2 | async-start | bytes 262144 | tf_op jit(solution)/shard_map/all_to_all | solution.py:527
  285.4 1.3 fusion.11
  286.7 1.3 fusion.9
  288.1 4.8 %all-to-all-done.2 = f32[32,8,96]{2,1,0:T(8,128)S(1)} async-done(((f32[32,8,96]{2,1,0:T(8,128)}), f32[32,8,96]{2,1,0:T(8,128)S(1)}, u32[]{:S(2)}, u32[]{:S(2)}) %all-to-all-start.2) | async-done | bytes 98336 | tf_op jit(solution)/shard_map/all_to_all | solution.py:527
  292.9 1.4 broadcast_in_dim.41
  294.4 4.0 %all-to-all-start.4 = ((bf16[4,4,384,128]{3,2,1,0:T(8,128)(2,1)}), bf16[4,4,384,128]{3,2,1,0:T(8,128)(2,1)S(1)}, u32[]{:S(2)}, u32[]{:S(2)}) async-start(bf16[4,4,384,128]{3,2,1,0:T(8,128)(2,1)} %bitcast.48), calls=%async_computation.4 | async-start | bytes 3145728 | tf_op jit(solution)/shard_map/all_to_all | solution.py:537
  298.5 6.7 %collective-permute-start.1 = (bf16[8,96]{1,0:T(8,128)(2,1)S(1)}, bf16[8,96]{1,0:T(8,128)(2,1)S(1)}, u32[]{:S(2)}, u32[]{:S(2)}) collective-permute-start(bf16[8,96]{1,0:T(8,128)(2,1)S(1)} %reduce_sum.33), channel_id=1, source_target_pairs={{0,1},{1,0},{2,3},{3,2},{4,5},{5,4},{6,7},{7,6},{8,9},{9,8},{10,11... | collective-permute-start | bytes 4616 | tf_op jit(solution)/shard_map/ppermute | solution.py:476
  306.0 3.2 collective-permute-start.2
  309.9 2.8 reduce_sum.34
  314.5 2.2 all-to-all-done.4
  317.1 5.8 %collective-permute-start.23 = (bf16[4,384,128]{2,1,0:T(8,128)(2,1)S(1)}, bf16[4,384,128]{2,1,0:T(8,128)(2,1)S(1)}, u32[]{:S(2)}, u32[]{:S(2)}) collective-permute-start(bf16[4,384,128]{2,1,0:T(8,128)(2,1)S(1)} %reduce_sum.35), channel_id=1, source_target_pairs={{0,1},{1,0},{2,3},{3,2},{4,5},{5,4},{6,7},{7,6},{8,9},{9,8},{10,11... | collective-permute-start | bytes 1179656 | tf_op jit(solution)/shard_map/ppermute | solution.py:539
  326.4 6.0 %update.1 = (f32[192,2048]{1,0:T(8,128)}, f32[1,2048]{1,0:T(1,128)}) custom-call(s32[1,2048]{1,0:T(1,128)} %bitcast.128, bf16[8,384,128]{2,1,0:T(8,128)(2,1)} %maximum_select_fusion.sum_ref, f32[192,2048]{1,0:T(8,128)} %bitcast.129, f32[1,2048]{1,0:T(1,128)} %bitcast.130), custom_call_target="tpu_custom_call" | custom-call | flops 4000000000 | bytes 4718592 | tf_op jit(solution)/shard_map/update/pallas_call | solution.py:406
  (107 shorter events, 27.9 us)
Async XLA Ops:
  2.8 17.3 %all-to-all-start = ((bf16[32,16,128]{2,1,0:T(8,128)(2,1)}), bf16[32,16,128]{2,1,0:T(8,128)(2,1)S(1)}, u32[]{:S(2)}, u32[]{:S(2)}) async-start(bf16[32,16,128]{2,1,0:T(8,128)(2,1)} %broadcast_in_dim.34), calls=%async_computation | async-start | bytes 262144 | tf_op jit(solution)/shard_map/all_to_all | solution.py:443
  22.0 31.7 %all-to-all-start.1 = ((bf16[32,256,128]{2,1,0:T(8,128)(2,1)}), bf16[32,256,128]{2,1,0:T(8,128)(2,1)S(1)}, u32[]{:S(2)}, u32[]{:S(2)}) async-start(bf16[32,256,128]{2,1,0:T(8,128)(2,1)} %broadcast_in_dim.35), calls=%async_computation.1 | async-start | bytes 4194304 | tf_op jit(solution)/shard_map/all_to_all | solution.py:443
  53.7 25.6 %collective-permute-start = (bf16[32,256,128]{2,1,0:T(8,128)(2,1)S(1)}, bf16[32,256,128]{2,1,0:T(8,128)(2,1)S(1)}, u32[]{:S(2)}, u32[]{:S(2)}) collective-permute-start(bf16[32,256,128]{2,1,0:T(8,128)(2,1)S(1)} %all-to-all-done.1), channel_id=1, source_target_pairs={{0,1},{1,0},{2,3},{3,2},{4,5},{5,4},{6,7},{7,6},{8,9},{9,8},{10,11... | collective-permute-start | bytes 6291464 | tf_op jit(solution)/shard_map/ppermute | solution.py:498
  102.4 2.6 copy-start.2
  107.3 5.0 %copy-start.7 = (s32[256]{0:T(256)S(1)}, s32[256]{0:T(256)}, u32[]{:S(2)}) copy-start(s32[256]{0:T(256)} %param.15) | copy-start | bytes 3076
  107.3 63.7 %all-to-all-start.3 = ((bf16[32,512,128]{2,1,0:T(8,128)(2,1)}), bf16[32,512,128]{2,1,0:T(8,128)(2,1)}, u32[]{:S(2)}, u32[]{:S(2)}) async-start(bf16[32,512,128]{2,1,0:T(8,128)(2,1)} %pad_maximum_fusion), calls=%async_computation.3 | async-start | bytes 8388608 | tf_op jit(solution)/shard_map/all_to_all | solution.py:523
  112.9 58.7 %copy-start.3 = (s32[128,256]{1,0:T(8,128)S(1)}, s32[128,256]{1,0:T(8,128)}, u32[]{:S(2)}) copy-start(s32[128,256]{1,0:T(8,128)} %param.14) | copy-start | bytes 393220
  171.0 10.7 %collective-permute-start.5 = (bf16[128,4,48,128]{3,2,1,0:T(8,128)(2,1)}, bf16[128,4,48,128]{3,2,1,0:T(8,128)(2,1)}, u32[]{:S(2)}, u32[]{:S(2)}) collective-permute-start(bf16[128,4,48,128]{3,2,1,0:T(8,128)(2,1)} %get-tuple-element.36), channel_id=1, source_target_pairs={{0,1},{1,0},{2,3},{3,2},{4,5},{5,4},{6,7},{7,6},{8,9},{9,8},{10,11... | collective-permute-start | bytes 18874376 | tf_op jit(solution)/shard_map/ppermute | solution.py:530
  174.6 6.9 %collective-permute-start.6 = (s32[64,2,128]{2,1,0:T(2,128)S(1)}, s32[64,2,128]{2,1,0:T(2,128)S(1)}, u32[]{:S(2)}, u32[]{:S(2)}) collective-permute-start(s32[64,2,128]{2,1,0:T(2,128)S(1)} %bitcast.125), channel_id=1, source_target_pairs={{0,1},{1,0},{2,3},{3,2},{4,5},{5,4},{6,7},{7,6},{8,9},{9,8},{10,11... | collective-permute-start | bytes 196616 | tf_op jit(solution)/shard_map/ppermute | solution.py:508
  181.4 0.6 copy-start.8
  199.9 5.1 %copy-start = (bf16[4,4,4,384,128]{4,3,2,1,0:T(8,128)(2,1)S(1)}, bf16[4,4,4,384,128]{4,3,2,1,0:T(8,128)(2,1)}, u32[]{:S(2)}) copy-start(bf16[4,4,4,384,128]{4,3,2,1,0:T(8,128)(2,1)} %get-tuple-element.38) | copy-start | bytes 18874372
  202.2 20.0 %collective-permute-start.7 = (bf16[2,4,384,128]{3,2,1,0:T(8,128)(2,1)S(1)}, bf16[2,4,384,128]{3,2,1,0:T(8,128)(2,1)S(1)}, u32[]{:S(2)}, u32[]{:S(2)}) collective-permute-start(bf16[2,4,384,128]{3,2,1,0:T(8,128)(2,1)S(1)} %get-tuple-element.45), channel_id=1, source_target_pairs={{0,32},{32,64},{64,96},{96,0},{1,33},{33,65},{65,97},{97,1},{2,34}... | collective-permute-start | bytes 2359304 | tf_op jit(solution)/shard_map/ppermute | solution.py:448
  202.3 19.9 %collective-permute-start.9 = (bf16[2,4,384,128]{3,2,1,0:T(8,128)(2,1)S(1)}, bf16[2,4,384,128]{3,2,1,0:T(8,128)(2,1)S(1)}, u32[]{:S(2)}, u32[]{:S(2)}) collective-permute-start(bf16[2,4,384,128]{3,2,1,0:T(8,128)(2,1)S(1)} %get-tuple-element.46), channel_id=1, source_target_pairs={{0,96},{32,0},{64,32},{96,64},{1,97},{33,1},{65,33},{97,65},{2,98}... | collective-permute-start | bytes 2359304 | tf_op jit(solution)/shard_map/ppermute | solution.py:448
  205.0 17.3 %copy-start.1 = (bf16[4,4,4,384,128]{4,3,2,1,0:T(8,128)(2,1)S(1)}, bf16[4,4,4,384,128]{4,3,2,1,0:T(8,128)(2,1)}, u32[]{:S(2)}) copy-start(bf16[4,4,4,384,128]{4,3,2,1,0:T(8,128)(2,1)} %get-tuple-element.37) | copy-start | bytes 18874372
  205.3 20.5 %collective-permute-start.15 = (bf16[2,4,384,128]{3,2,1,0:T(8,128)(2,1)S(1)}, bf16[2,4,384,128]{3,2,1,0:T(8,128)(2,1)S(1)}, u32[]{:S(2)}, u32[]{:S(2)}) collective-permute-start(bf16[2,4,384,128]{3,2,1,0:T(8,128)(2,1)S(1)} %get-tuple-element.51), channel_id=1, source_target_pairs={{0,8},{8,16},{16,24},{24,0},{1,9},{9,17},{17,25},{25,1},{2,10},{10... | collective-permute-start | bytes 2359304 | tf_op jit(solution)/shard_map/ppermute | solution.py:448
  206.8 23.2 %collective-permute-start.17 = (bf16[2,4,384,128]{3,2,1,0:T(8,128)(2,1)S(1)}, bf16[2,4,384,128]{3,2,1,0:T(8,128)(2,1)S(1)}, u32[]{:S(2)}, u32[]{:S(2)}) collective-permute-start(bf16[2,4,384,128]{3,2,1,0:T(8,128)(2,1)S(1)} %get-tuple-element.52), channel_id=1, source_target_pairs={{0,24},{8,0},{16,8},{24,16},{1,25},{9,1},{17,9},{25,17},{2,26},{10... | collective-permute-start | bytes 2359304 | tf_op jit(solution)/shard_map/ppermute | solution.py:448
  222.8 36.0 %collective-permute-start.8 = (bf16[4,4,384,128]{3,2,1,0:T(8,128)(2,1)S(1)}, bf16[4,4,384,128]{3,2,1,0:T(8,128)(2,1)S(1)}, u32[]{:S(2)}, u32[]{:S(2)}) collective-permute-start(bf16[4,4,384,128]{3,2,1,0:T(8,128)(2,1)S(1)} %pad_maximum_fusion.2), channel_id=1, source_target_pairs={{0,32},{32,64},{64,96},{96,0},{1,33},{33,65},{65,97},{97,1},{2,34}... | collective-permute-start | bytes 4718600 | tf_op jit(solution)/shard_map/ppermute | solution.py:448
  223.1 35.7 %collective-permute-start.10 = (bf16[4,4,384,128]{3,2,1,0:T(8,128)(2,1)S(1)}, bf16[4,4,384,128]{3,2,1,0:T(8,128)(2,1)S(1)}, u32[]{:S(2)}, u32[]{:S(2)}) collective-permute-start(bf16[4,4,384,128]{3,2,1,0:T(8,128)(2,1)S(1)} %pad_maximum_fusion.3), channel_id=1, source_target_pairs={{0,96},{32,0},{64,32},{96,64},{1,97},{33,1},{65,33},{97,65},{2,98}... | collective-permute-start | bytes 4718600 | tf_op jit(solution)/shard_map/ppermute | solution.py:448
  230.5 35.3 %collective-permute-start.16 = (bf16[4,4,384,128]{3,2,1,0:T(8,128)(2,1)S(1)}, bf16[4,4,384,128]{3,2,1,0:T(8,128)(2,1)S(1)}, u32[]{:S(2)}, u32[]{:S(2)}) collective-permute-start(bf16[4,4,384,128]{3,2,1,0:T(8,128)(2,1)S(1)} %pad_maximum_fusion.4), channel_id=1, source_target_pairs={{0,8},{8,16},{16,24},{24,0},{1,9},{9,17},{17,25},{25,1},{2,10},{10... | collective-permute-start | bytes 4718600 | tf_op jit(solution)/shard_map/ppermute | solution.py:448
  231.9 35.4 %collective-permute-start.18 = (bf16[4,4,384,128]{3,2,1,0:T(8,128)(2,1)S(1)}, bf16[4,4,384,128]{3,2,1,0:T(8,128)(2,1)S(1)}, u32[]{:S(2)}, u32[]{:S(2)}) collective-permute-start(bf16[4,4,384,128]{3,2,1,0:T(8,128)(2,1)S(1)} %pad_maximum_fusion.5), channel_id=1, source_target_pairs={{0,24},{8,0},{16,8},{24,16},{1,25},{9,1},{17,9},{25,17},{2,26},{10... | collective-permute-start | bytes 4718600 | tf_op jit(solution)/shard_map/ppermute | solution.py:448
  259.5 11.2 %collective-permute-start.11 = (bf16[2,384,128]{2,1,0:T(8,128)(2,1)S(1)}, bf16[2,384,128]{2,1,0:T(8,128)(2,1)S(1)}, u32[]{:S(2)}, u32[]{:S(2)}) collective-permute-start(bf16[2,384,128]{2,1,0:T(8,128)(2,1)S(1)} %get-tuple-element.61), channel_id=1, source_target_pairs={{0,8},{8,16},{16,24},{24,0},{1,9},{9,17},{17,25},{25,1},{2,10},{10... | collective-permute-start | bytes 589832 | tf_op jit(solution)/shard_map/ppermute | solution.py:448
  261.0 10.9 %collective-permute-start.13 = (bf16[2,384,128]{2,1,0:T(8,128)(2,1)S(1)}, bf16[2,384,128]{2,1,0:T(8,128)(2,1)S(1)}, u32[]{:S(2)}, u32[]{:S(2)}) collective-permute-start(bf16[2,384,128]{2,1,0:T(8,128)(2,1)S(1)} %get-tuple-element.62), channel_id=1, source_target_pairs={{0,24},{8,0},{16,8},{24,16},{1,25},{9,1},{17,9},{25,17},{2,26},{10... | collective-permute-start | bytes 589832 | tf_op jit(solution)/shard_map/ppermute | solution.py:448
  268.0 8.4 %collective-permute-start.19 = (bf16[2,384,128]{2,1,0:T(8,128)(2,1)S(1)}, bf16[2,384,128]{2,1,0:T(8,128)(2,1)S(1)}, u32[]{:S(2)}, u32[]{:S(2)}) collective-permute-start(bf16[2,384,128]{2,1,0:T(8,128)(2,1)S(1)} %get-tuple-element.67), channel_id=1, source_target_pairs={{0,32},{32,64},{64,96},{96,0},{1,33},{33,65},{65,97},{97,1},{2,34}... | collective-permute-start | bytes 589832 | tf_op jit(solution)/shard_map/ppermute | solution.py:448
  268.1 8.3 %collective-permute-start.21 = (bf16[2,384,128]{2,1,0:T(8,128)(2,1)S(1)}, bf16[2,384,128]{2,1,0:T(8,128)(2,1)S(1)}, u32[]{:S(2)}, u32[]{:S(2)}) collective-permute-start(bf16[2,384,128]{2,1,0:T(8,128)(2,1)S(1)} %get-tuple-element.68), channel_id=1, source_target_pairs={{0,96},{32,0},{64,32},{96,64},{1,97},{33,1},{65,33},{97,65},{2,98}... | collective-permute-start | bytes 589832 | tf_op jit(solution)/shard_map/ppermute | solution.py:448
  272.0 8.7 %copy-start.4 = (f32[96,256]{1,0:T(8,128)S(1)}, f32[96,256]{1,0:T(8,128)}, u32[]{:S(2)}) copy-start(f32[96,256]{1,0:T(8,128)} %get-tuple-element.29) | copy-start | bytes 294916
  272.1 8.7 %copy-start.5 = (f32[16,256]{1,0:T(8,128)S(1)}, f32[16,256]{1,0:T(8,128)}, u32[]{:S(2)}) copy-start(f32[16,256]{1,0:T(8,128)} %get-tuple-element.30) | copy-start | bytes 49156
  272.9 12.5 %collective-permute-start.12 = (bf16[4,384,128]{2,1,0:T(8,128)(2,1)}, bf16[4,384,128]{2,1,0:T(8,128)(2,1)}, u32[]{:S(2)}, u32[]{:S(2)}) collective-permute-start(bf16[4,384,128]{2,1,0:T(8,128)(2,1)} %pad_maximum_fusion.6), channel_id=1, source_target_pairs={{0,8},{8,16},{16,24},{24,0},{1,9},{9,17},{17,25},{25,1},{2,10},{10... | collective-permute-start | bytes 1179656 | tf_op jit(solution)/shard_map/ppermute | solution.py:448
  274.6 10.8 %collective-permute-start.14 = (bf16[4,384,128]{2,1,0:T(8,128)(2,1)}, bf16[4,384,128]{2,1,0:T(8,128)(2,1)}, u32[]{:S(2)}, u32[]{:S(2)}) collective-permute-start(bf16[4,384,128]{2,1,0:T(8,128)(2,1)} %pad_maximum_fusion.7), channel_id=1, source_target_pairs={{0,24},{8,0},{16,8},{24,16},{1,25},{9,1},{17,9},{25,17},{2,26},{10... | collective-permute-start | bytes 1179656 | tf_op jit(solution)/shard_map/ppermute | solution.py:448
  277.2 9.4 %collective-permute-start.20 = (bf16[4,384,128]{2,1,0:T(8,128)(2,1)}, bf16[4,384,128]{2,1,0:T(8,128)(2,1)}, u32[]{:S(2)}, u32[]{:S(2)}) collective-permute-start(bf16[4,384,128]{2,1,0:T(8,128)(2,1)} %pad_maximum_fusion.8), channel_id=1, source_target_pairs={{0,32},{32,64},{64,96},{96,0},{1,33},{33,65},{65,97},{97,1},{2,34}... | collective-permute-start | bytes 1179656 | tf_op jit(solution)/shard_map/ppermute | solution.py:448
  278.0 8.6 %collective-permute-start.22 = (bf16[4,384,128]{2,1,0:T(8,128)(2,1)}, bf16[4,384,128]{2,1,0:T(8,128)(2,1)}, u32[]{:S(2)}, u32[]{:S(2)}) collective-permute-start(bf16[4,384,128]{2,1,0:T(8,128)(2,1)} %pad_maximum_fusion.9), channel_id=1, source_target_pairs={{0,96},{32,0},{64,32},{96,64},{1,97},{33,1},{65,33},{97,65},{2,98}... | collective-permute-start | bytes 1179656 | tf_op jit(solution)/shard_map/ppermute | solution.py:448
  281.5 11.4 %all-to-all-start.2 = ((f32[32,8,96]{2,1,0:T(8,128)}), f32[32,8,96]{2,1,0:T(8,128)S(1)}, u32[]{:S(2)}, u32[]{:S(2)}) async-start(f32[32,8,96]{2,1,0:T(8,128)} %bitcast.8), calls=%async_computation.2 | async-start | bytes 262144 | tf_op jit(solution)/shard_map/all_to_all | solution.py:527
  294.4 14.9 %copy-start.6 = (s32[8,256]{1,0:T(8,128)S(1)}, s32[8,256]{1,0:T(8,128)}, u32[]{:S(2)}) copy-start(s32[8,256]{1,0:T(8,128)} %param.16) | copy-start | bytes 24580
  294.4 22.3 %all-to-all-start.4 = ((bf16[4,4,384,128]{3,2,1,0:T(8,128)(2,1)}), bf16[4,4,384,128]{3,2,1,0:T(8,128)(2,1)S(1)}, u32[]{:S(2)}, u32[]{:S(2)}) async-start(bf16[4,4,384,128]{3,2,1,0:T(8,128)(2,1)} %bitcast.48), calls=%async_computation.4 | async-start | bytes 3145728 | tf_op jit(solution)/shard_map/all_to_all | solution.py:537
  298.5 7.6 %collective-permute-start.1 = (bf16[8,96]{1,0:T(8,128)(2,1)S(1)}, bf16[8,96]{1,0:T(8,128)(2,1)S(1)}, u32[]{:S(2)}, u32[]{:S(2)}) collective-permute-start(bf16[8,96]{1,0:T(8,128)(2,1)S(1)} %reduce_sum.33), channel_id=1, source_target_pairs={{0,1},{1,0},{2,3},{3,2},{4,5},{5,4},{6,7},{7,6},{8,9},{9,8},{10,11... | collective-permute-start | bytes 4616 | tf_op jit(solution)/shard_map/ppermute | solution.py:476
  306.0 7.4 %collective-permute-start.2 = (bf16[8,96]{1,0:T(8,128)(2,1)S(1)}, bf16[8,96]{1,0:T(8,128)(2,1)S(1)}, u32[]{:S(2)}, u32[]{:S(2)}) collective-permute-start(bf16[8,96]{1,0:T(8,128)(2,1)S(1)} %add_convert_fusion.1), channel_id=1, source_target_pairs={{0,2},{2,0},{1,3},{3,1},{4,6},{6,4},{5,7},{7,5},{8,10},{10,8},{9,1... | collective-permute-start | bytes 4616 | tf_op jit(solution)/shard_map/ppermute | solution.py:476
  312.7 1.7 collective-permute-start.3
  314.4 9.6 %collective-permute-start.4 = (bf16[512,128]{1,0:T(8,128)(2,1)S(1)}, bf16[512,128]{1,0:T(8,128)(2,1)S(1)}, u32[]{:S(2)}, u32[]{:S(2)}) collective-permute-start(bf16[512,128]{1,0:T(8,128)(2,1)S(1)} %add_convert_fusion), channel_id=1, source_target_pairs={{0,2},{2,0},{1,3},{3,1},{4,6},{6,4},{5,7},{7,5},{8,10},{10,8},{9,1... | collective-permute-start | bytes 393224 | tf_op jit(solution)/shard_map/ppermute | solution.py:476
  317.1 8.3 %collective-permute-start.23 = (bf16[4,384,128]{2,1,0:T(8,128)(2,1)S(1)}, bf16[4,384,128]{2,1,0:T(8,128)(2,1)S(1)}, u32[]{:S(2)}, u32[]{:S(2)}) collective-permute-start(bf16[4,384,128]{2,1,0:T(8,128)(2,1)S(1)} %reduce_sum.35), channel_id=1, source_target_pairs={{0,1},{1,0},{2,3},{3,2},{4,5},{5,4},{6,7},{7,6},{8,9},{9,8},{10,11... | collective-permute-start | bytes 1179656 | tf_op jit(solution)/shard_map/ppermute | solution.py:539

commit v4 on v3

--- a/solution.py
+++ b/solution.py
@@ -310,19 +310,21 @@
     )(at, x3, s, dl, dfm, wt)
 
 
-def sums_kernel(at_ref, mine_ref, other_ref, ids_ref, oid_ref, even_ref, odd_ref):
+def sums_kernel(at_ref, mine_ref, other_ref, ids_ref, oid_ref, small_ref, a_ref, b_ref, c_ref):
     tables, steps, height, _ = mine_ref.shape
     part = height // 3
     count = ids_ref.shape[2]
     rows = 2 * count
-    iota = lax.broadcasted_iota(jnp.int32, (rows, count), 0)
+    iota = lax.broadcasted_iota(jnp.int32, (rows, count), 0).astype(F32).astype(BF16)
+    one, none = jnp.ones((rows, count), BF16), jnp.zeros((rows, count), BF16)
     low = lax.broadcasted_iota(jnp.int32, (1, 128), 1) < 64
     zero = jnp.zeros((part, 128), BF16)
+    b_ref[0, 0, :, 96:112, :] = small_ref[0, 0]
     for i in range(tables // 2):
-        for t, ref in enumerate((even_ref, odd_ref)):
+        for t in range(2):
             hot = jnp.concatenate(
                 [
-                    jnp.where(iota == r[i, t : t + 1, :], 1.0, 0.0).astype(BF16)
+                    jnp.where(iota == r[i, t : t + 1, :].astype(F32).astype(BF16), one, none)
                     for r in (ids_ref, oid_ref)
                 ],
                 axis=1,
@@ -338,54 +340,71 @@
             )
             out = dot(hot, block)
             tail = out[:, 128:] + pltpu.roll(out[:, 128:], 64, 1)
-            ref[0, 0, i, :rows, :] = out[:, :128].astype(BF16)
-            ref[0, 0, i, rows:, :] = jnp.where(low, tail[:count], tail[count:]).astype(BF16)
-
-
-def sums(at, mine, other, ids, oids, nz, nx):
+            main = out[:, :128].astype(BF16)
+            tail = jnp.where(low, tail[:count], tail[count:]).astype(BF16)
+            if t == 0:
+                a_ref[0, 0, i, :256, :] = main
+                a_ref[0, 0, i, 256:, :] = tail[:32]
+                b_ref[0, 0, i, :96, :] = tail[32:]
+            else:
+                b_ref[0, 0, i, 112:, :] = main[:160]
+                c_ref[i, 0, 0, :96, :] = main[160:]
+                c_ref[i, 0, 0, 96:, :] = tail
+
+
+def sums(at, mine, other, ids, oids, small):
     tables, steps, height, _ = mine.shape
     count = ids.shape[2]
-    ny = tables // (2 * nz * nx)
+    nz, nx, ny = small.shape[:3]
+    extra = small.shape[3]
     data = pl.BlockSpec((2 * ny, steps, height, 128), lambda z, x, at: (z * nx + x, 0, 0, 0))
     index = pl.BlockSpec((ny, 2, count), lambda z, x, at: (z * nx + x, 0, 0))
     grid = pltpu.PrefetchScalarGridSpec(
         num_scalar_prefetch=1,
         grid=(nz, nx),
-        in_specs=[data, data, index, index],
+        in_specs=[
+            data, data, index, index,
+            pl.BlockSpec((1, 1, ny, extra, 128), lambda z, x, at: (z, x, 0, 0, 0)),
+        ],
         out_specs=[
             pl.BlockSpec(
-                (1, 1, ny, 384, 128),
+                (1, 1, ny, 288, 128),
                 lambda z, x, at: ((z + nz - at[0]) % nz, (x + nx - at[1]) % nx, 0, 0, 0),
             ),
             pl.BlockSpec(
-                (1, 1, ny, 384, 128),
+                (1, 1, ny, 272, 128),
                 lambda z, x, at: ((x + nx - at[1]) % nx, (z + nz - at[0]) % nz, 0, 0, 0),
             ),
+            pl.BlockSpec((ny, 1, 1, 224, 128), lambda z, x, at: (0, z, x, 0, 0)),
         ],
     )
     return pl.pallas_call(
         sums_kernel,
         grid_spec=grid,
         out_shape=[
-            jax.ShapeDtypeStruct((nz, nx, ny, 384, 128), BF16),
-            jax.ShapeDtypeStruct((nx, nz, ny, 384, 128), BF16),
+            jax.ShapeDtypeStruct((nz, nx, ny, 288, 128), BF16),
+            jax.ShapeDtypeStruct((nx, nz, ny, 272, 128), BF16),
+            jax.ShapeDtypeStruct((ny, nz, nx, 224, 128), BF16),
         ],
         compiler_params=params(),
         cost_estimate=cost(1e10, mine.size * 8),
         name="sums",
-    )(at, mine, other, ids, oids)
+    )(at, mine, other, ids, oids, small)
 
 
 def update_kernel(slot_ref, sum_ref, rows_ref, accum_ref, new_rows_ref, new_accum_ref, acc):
-    tables = sum_ref.shape[0]
+    cores, runs, height, _ = sum_ref.shape
+    tables = 2 * cores * runs
     state = rows_ref.shape[1]
     rows = state // tables
     half = rows // 2
     for t in range(tables):
+        where = t // 2 // runs, t // 2 % runs
+        base = (t % 2) * (height - 384)
         first = slice(t * rows, t * rows + half)
         second = slice(t * rows + half, (t + 1) * rows)
-        main = sum_ref[t, :rows, :].astype(F32).T.astype(BF16)
-        tail = sum_ref[t, rows:, :].astype(F32).T.astype(BF16)
+        main = sum_ref[where + (slice(base, base + rows),)].astype(F32).T.astype(BF16)
+        tail = sum_ref[where + (slice(base + rows, base + 384),)].astype(F32).T.astype(BF16)
         acc[:128, t * rows : (t + 1) * rows] = main
         acc[128:, first] = tail[:64]
         acc[128:, second] = tail[64:]
@@ -469,14 +488,6 @@
     return [add(v[0], f, b) for (_, v), f, b in zip(parts, fore, back)]
 
 
-def rep_sum(v):
-    swap = SWAP
-    for axis in ("c", "yh"):
-        v = v.astype(BF16)
-        v = v.astype(F32) + lax.ppermute(v, axis, swap).astype(F32)
-    return v
-
-
 def body(
     samples, out_grad, row_ids, table_owner, slot_map, proj, gain_flat, w_in, w_out, w_lcb,
     table_rows, row_accum,
@@ -488,13 +499,18 @@
     nl = w_lcb.shape[1]
     core = lax.axis_index("c")
     small = jnp.concatenate([proj, gain_flat.reshape(per, K), w_lcb], axis=1)
-    small = gather(jnp.pad(small, ((0, 8), (0, 128 - small.shape[1]))))[:, :per].reshape(n, 128)
+    small = jnp.pad(small, ((0, 8), (0, 128 - small.shape[1])))
+    shard = jnp.concatenate([w_in, w_out], axis=0)
+    rows = shard.shape[0] // 2
+    near = jnp.concatenate([lax.dynamic_slice_in_dim(shard, core * rows, rows, 0), small], axis=0)
+    x3 = unfold(samples, n, 0)
+    g2 = unfold(out_grad, nl, out_grad.shape[1] // D // nl - 1)
+    near, x3, g2 = lax.optimization_barrier((gather(near), x3, g2))
+    small = near[:, rows : rows + per].reshape(n, 128)
     proj_f = small[:, :K]
     gain_t = small[:, K : 2 * K].T.astype(F32)
     w_lcb_f = small[:, 2 * K : 2 * K + nl]
-    shard = jnp.concatenate([w_in, w_out], axis=0)
-    rows = shard.shape[0] // 2
-    near = gather(lax.dynamic_slice_in_dim(shard, core * rows, rows, 0))
+    near = near[:, :rows]
     far = lax.ppermute(near, "c", SWAP)
     lower, upper = jnp.where(core == 0, near, far), jnp.where(core == 0, far, near)
     w_in_t = lower[:, : w_in.shape[0]].reshape(n, K, 128).transpose(1, 0, 2)
@@ -507,39 +523,58 @@
     ids = jnp.take(row_ids.T, order, axis=0).reshape(2, n // 4, 2, count)
     other_ids = lax.ppermute(ids[1], "c", SWAP)
 
-    x3 = unfold(samples, n, 0)
-    g2 = unfold(out_grad, nl, out_grad.shape[1] // D // nl - 1)
     wt, score, dl, xh, inv = forward(x3, g2, proj_f, w_lcb_f)
     g_out, g_in, g_gain, dfm = batch(xh, inv, gain_t, w_in_t, w_out_f, out_grad)
-    keep, send, acc = last(spot, x3, score, dl, dfm, wt)
-    g_proj, g_lcb = acc[:K] + acc[K : 2 * K], acc[2 * K :]
-    big = jnp.concatenate(
+    w_grads = jnp.concatenate(
         [
             g_out.reshape(owners, -1, 128),
             g_in.astype(BF16).transpose(1, 0, 2).reshape(owners, -1, 128),
         ],
         axis=1,
     )
-    big = lax.all_to_all(big, WIDE, 0, 0, tiled=True)
-    big, send = lax.optimization_barrier((big, send))
-    big = rep_sum(jnp.sum(big.astype(F32), axis=0))
-    little = jnp.concatenate([g_proj, g_gain, g_lcb], axis=0).T.reshape(owners, per, -1)
-    little = lax.all_to_all(little, WIDE, 0, 0, tiled=True)
-    little = rep_sum(jnp.sum(little, axis=0))
+    top, bottom = w_grads[:, :rows], w_grads[:, rows:]
+    theirs = lax.ppermute(jnp.where(core == 0, bottom, top), "c", SWAP)
+    w_grads = add(jnp.where(core == 0, top, bottom), theirs)
+    w_grads, dfm = lax.optimization_barrier((w_grads, dfm))
+    w_grads = lax.all_to_all(w_grads, WIDE, 0, 0, tiled=True)
+    keep, send, acc = last(spot, x3, score, dl, dfm, wt)
+    w_grads, send = lax.optimization_barrier((w_grads, send))
+    g_proj, g_lcb = acc[:K] + acc[K : 2 * K], acc[2 * K :]
+    little = jnp.concatenate([g_proj, g_gain, g_lcb], axis=0).T.reshape(4, 4, 2, 1, per, -1)
+    pad = ((0, 0),) * 3 + ((0, 1), (0, 8), (0, 128 - little.shape[-1]))
+    little = jnp.pad(little.astype(BF16), pad).reshape(4, 4, 4, 16, 128)
 
     other = lax.ppermute(send, "c", SWAP)
     at = jnp.stack([lax.axis_index("z"), lax.axis_index("x")]).astype(jnp.int32)
-    even, odd = sums(at, keep, other, ids[0], other_ids, 4, 4)
-    even, odd = ring_sums([("z", even), ("x", odd)])
-    even, odd = ring_sums([("x", even), ("z", odd)])
-    both = jnp.stack([even, odd], axis=1).reshape(2, 1, 2, 2, 384, 128)
-    both = jnp.broadcast_to(both, (2, 2, 2, 2, 384, 128)).reshape(4, 4, 384, 128)
+    a, b, c = sums(at, keep, other, ids[0], other_ids, little)
+    c = lax.all_to_all(c, ("yl", "yh"), 0, 0, tiled=True)
+    a, b = ring_sums([("z", a), ("x", b)])
+    c = jnp.sum(c.astype(F32), axis=0).astype(BF16)
+    a, b, c = lax.optimization_barrier((a, b, c))
+    c = lax.all_to_all(c.reshape((16,) + c.shape[2:]), ("z", "x"), 0, 0, tiled=True)
+    a, b = ring_sums([("x", a), ("z", b)])
+    c = jnp.sum(c.astype(F32), axis=0).astype(BF16)
+    w_grads = jnp.sum(w_grads.astype(F32), axis=0).astype(BF16)
+    w_grads = w_grads.astype(F32) + lax.ppermute(w_grads, "yh", SWAP).astype(F32)
+    w_theirs = lax.ppermute(w_grads, "c", SWAP)
+    low, high = jnp.where(core == 0, w_grads, w_theirs), jnp.where(core == 0, w_theirs, w_grads)
+    big = jnp.concatenate([low, high], axis=0)
+    a, b, c, big = lax.optimization_barrier((a, b, c, big))
+    ab = jnp.concatenate([a, b], axis=1)
+    ab = ab.reshape((2, 1, 2) + ab.shape[1:])
+    here = (jnp.arange(2)[:, None] == lax.axis_index("yl")) & (
+        jnp.arange(2)[None, :] == lax.axis_index("yh")
+    )
+    c = jnp.where(here.reshape(2, 1, 2, 1, 1), c, jnp.zeros_like(c))
+    both = jnp.concatenate(
+        [jnp.broadcast_to(v, (2, 2, 2) + v.shape[3:]) for v in (ab, c)], axis=3
+    )
+    both = both.reshape((4, 2) + both.shape[3:])
     both = lax.all_to_all(both, ("yl", "yh"), 0, 0, tiled=True)
     mine = jnp.sum(both.astype(F32), axis=0).astype(BF16)
     others = lax.ppermute(mine, "c", SWAP)
-    owned = jnp.where(
-        core == 0, jnp.concatenate([mine, others], axis=0), jnp.concatenate([others, mine], axis=0)
-    )
+    owned = jnp.where(core == 0, jnp.stack([mine, others]), jnp.stack([others, mine]))
+    little = (mine[0, 384:392].astype(F32) + others[0, 384:392].astype(F32))[:, : 2 * K + nl]
     new_rows, new_accum = update(
         slot_map.reshape(1, -1), owned, table_rows.T, row_accum.reshape(1, -1)
     )

time: 338 us -> 315 us (0.932); the launches traced: 332 us -> 313 us
  waiting for transfers between devices: 93.5 us -> 48.6 us
  blocking collectives: 0 us -> 22 us
  starting transfers between devices: 69 us -> 54.4 us
  other arithmetic: 23.6 us -> 37.3 us
  local copies, waits for them, and re-layouts: 17.8 us -> 21.9 us
    ppermute x16, waiting for transfers between devices: 50 us -> 15.3 us  [ring_step(): return lax.ppermute(v, axis, [(i, (i + by) % n) for i in range(n)])]
    all_to_all x3, waiting for transfers between devices: 26.5 us -> 0.01 us  [the longest x1 0.01 us: body(): lax.all_to_all(c.reshape((16,) + c.shape[2:]), ('z', 'x'), 0, 0, tiled=True)]
    all_to_all x0 -> x1, blocking collectives: none -> 22 us  [body(): both = lax.all_to_all(both, ('yl', 'yh'), 0, 0, tiled=True)]
    ppermute x4 -> x3, waiting for transfers between devices: 1.14 us -> 23 us  [the longest x1 17.9 us: body(): lax.ppermute(w_grads, 'yh', SWAP).astype(F32)]
    convert_element_type x8 -> x9, other arithmetic: 4.84 us -> 12.9 us  [add(): return total.astype(BF16)]
    ppermute x4 -> x3, starting transfers between devices: 10.8 us -> 4.52 us  [the longest x1 2.57 us: body(): lax.ppermute(w_grads, 'yh', SWAP).astype(F32)]
    all_to_all x2 -> x1, starting transfers between devices: 13.7 us -> 9.73 us  [gather(): lax.all_to_all(jnp.broadcast_to(a[None], (n,) + a.shape), WIDE, 0, 0, til...]
    squeeze x4, local copies, waits for them, and re-layouts: 2.71 us -> 6.14 us  [ring_sums(): fore = [ring_step(axis, 1, v[2, :2]) for axis, v in parts]]
  transfers between devices with their start and end apart: 29 -> 27, of which waited for: 15 -> 10; matrix products, arithmetic and copies ran while one was open for 7% -> 10% of each run, Pallas kernels for 25% -> 27%
where the time goes in v4:
time: 315 us; the launch traced here: 313 us
  Pallas kernels  127 us (40%)
  starting transfers between devices  54.4 us (17%)
  waiting for transfers between devices  48.6 us (15%)
  other arithmetic  37.3 us (12%)
  blocking collectives  22 us (7%)
  local copies, waits for them, and re-layouts  21.9 us (7%)
    pallas_call x1, Pallas kernels, last(): pl.pallas_call(last_kernel, grid_spec=grid, out_shape=[half, half, jax.Sh...  38.7 us
    pallas_call x2, Pallas kernels, unfold(): pl.pallas_call(unfold_kernel, grid=(count // rows,), in_specs=[pl.BlockSp...  24 us
    all_to_all x1, blocking collectives, body(): both = lax.all_to_all(both, ('yl', 'yh'), 0, 0, tiled=True)  22 us
    ppermute x16, starting transfers between devices, ring_step(): return lax.ppermute(v, axis, [(i, (i + by) % n) for i in range(n)])  21.8 us
    pallas_call x1, Pallas kernels, first(): pl.pallas_call(first_kernel, grid=(count // rows,), in_specs=[pl.BlockSpe...  21.6 us
    pallas_call x1, Pallas kernels, batch(): pl.pallas_call(batch_kernel, grid=(total // rows,), in_specs=[whole((k, c...  19.5 us
    ppermute x1, waiting for transfers between devices, body(): lax.ppermute(w_grads, 'yh', SWAP).astype(F32)  17.9 us
    pallas_call x1, Pallas kernels, sums(): pl.pallas_call(sums_kernel, grid_spec=grid, out_shape=[jax.ShapeDtypeStru...  17.6 us
  transfers between devices with their start and end apart: 27, of which 10 were waited for; matrix products, arithmetic and copies ran while one was open for 10% of the time, Pallas kernels for 27%

profile of v4, /device:TPU:1, one launch (start us, length us, event | category | flops | bytes accessed | tf_op | source)
XLA Modules:
  0.0 312.8 jit_solution(3492381441231093407)
XLA Ops:
  3.0 1.7 broadcast_in_dim.52
  4.7 9.7 %all-to-all-start = ((bf16[32,272,128]{2,1,0:T(8,128)(2,1)}), bf16[32,272,128]{2,1,0:T(8,128)(2,1)S(1)}, u32[]{:S(2)}, u32[]{:S(2)}) async-start(bf16[32,272,128]{2,1,0:T(8,128)(2,1)} %broadcast_in_dim.52), calls=%async_computation | async-start | bytes 4456448 | tf_op jit(solution)/shard_map/all_to_all | solution.py:462
  14.5 17.7 %unfold.2.x_ref = bf16[128,256,256]{2,1,0:T(8,128)(2,1)} custom-call(bf16[128,49152]{1,0:T(8,128)(2,1)} %x_ref.2), custom_call_target="tpu_custom_call" | custom-call | flops 1000000000 | bytes 29491200 | tf_op jit(solution)/shard_map/unfold/pallas_call | solution.py:67
  32.2 6.3 %unfold.3.g_ref = bf16[128,64,256]{2,1,0:T(8,128)(2,1)} custom-call(bf16[128,24576]{1,0:T(8,128)(2,1)} %g_ref.1), custom_call_target="tpu_custom_call" | custom-call | flops 1000000000 | bytes 7372800 | tf_op jit(solution)/shard_map/unfold/pallas_call | solution.py:67
  38.5 6.7 %all-to-all-done = bf16[32,272,128]{2,1,0:T(8,128)(2,1)S(1)} async-done(((bf16[32,272,128]{2,1,0:T(8,128)(2,1)}), bf16[32,272,128]{2,1,0:T(8,128)(2,1)S(1)}, u32[]{:S(2)}, u32[]{:S(2)}) %all-to-all-start) | async-done | bytes 2228256 | tf_op jit(solution)/shard_map/all_to_all | solution.py:462
  45.1 1.6 slice.158
  46.9 2.1 collective-permute-start
  50.5 21.6 %first.1 = (bf16[128,32,256]{2,1,0:T(8,128)(2,1)}, bf16[128,64,256]{2,1,0:T(8,128)(2,1)}, f32[16,128,256]{2,1,0:T(8,128)}, f32[128,128]{1,0:T(8,128)}) custom-call(bf16[128,256,256]{2,1,0:T(8,128)(2,1)} %unfold.2.x_ref, bf16[128,64,256]{2,1,0:T(8,128)(2,1)} %unfold.3.g_ref, bf16[80,256]{1,0:T(8,128)(2,1)} %pad_maximum_fusion.14.w_ref.wt_ref), custom_call_target="tpu_custom_call" | custom-call | flops 20000000000 | bytes 16777216 | tf_op jit(solution)/shard_map/first/pallas_call | solution.py:116
  72.2 1.9 broadcast_select_fusion.1
  75.5 2.0 pad_maximum_fusion
  77.5 19.5 %batch.1 = (bf16[12288,128]{1,0:T(8,128)(2,1)}, f32[16,256,128]{2,1,0:T(8,128)}, f32[16,256]{1,0:T(8,128)}, f32[16,128,256]{2,1,0:T(8,128)}) custom-call(f32[16,128,256]{2,1,0:T(8,128)} %get-tuple-element.42.xh_ref, f32[128,128]{1,0:T(8,128)} %get-tuple-element.43.inv_ref, f32[16,256]{1,0:T(8,128)} %convert_bitcast_fusion.1.gain_ref, ...), custom_call_target="tpu_custom_call" | custom-call | flops 20000000000 | bytes 20000000 | tf_op jit(solution)/shard_map/batch/pallas_call | solution.py:203
  97.0 1.9 convert_bitcast_fusion
  100.6 4.1 %collective-permute-done.1 = bf16[32,256,128]{2,1,0:T(8,128)(2,1)S(1)} collective-permute-done((bf16[32,256,128]{2,1,0:T(8,128)(2,1)S(1)}, bf16[32,256,128]{2,1,0:T(8,128)(2,1)S(1)}, u32[]{:S(2)}, u32[]{:S(2)}) %collective-permute-start.1) | collective-permute-done | bytes 2097184 | tf_op jit(solution)/shard_map/ppermute | solution.py:536
  104.8 2.3 add_convert_fusion
  107.0 4.1 %all-to-all-start.1 = ((bf16[32,256,128]{2,1,0:T(8,128)(2,1)}), bf16[32,256,128]{2,1,0:T(8,128)(2,1)S(1)}, u32[]{:S(2)}, u32[]{:S(2)}) async-start(bf16[32,256,128]{2,1,0:T(8,128)(2,1)} %add_convert_fusion), calls=%async_computation.1 | async-start | bytes 4194304 | tf_op jit(solution)/shard_map/all_to_all | solution.py:539
  111.8 38.7 %last.1 = (bf16[128,4,48,128]{3,2,1,0:T(8,128)(2,1)}, bf16[128,4,48,128]{3,2,1,0:T(8,128)(2,1)}, f32[96,256]{1,0:T(8,128)}) custom-call(s32[256]{0:T(256)} %get-tuple-element.68.at_ref, bf16[128,256,256]{2,1,0:T(8,128)(2,1)} %unfold.2.x_ref, bf16[128,32,256]{2,1,0:T(8,128)(2,1)} %get-tuple-element.40.s_ref, bf16[128,64,256]{2,1,0:T(8,128)(2,1)} %get-tuple-element.41.dl_ref, ...), custom_call_target="tpu_custom_call" | custom-call | flops 20000000000 | bytes 33554432 | tf_op jit(solution)/shard_map/last/pallas_call | solution.py:303
  150.8 1.6 scatter_custom_fusion
  157.3 3.5 %collective-permute-done.3.oid_ref = s32[64,2,128]{2,1,0:T(2,128)S(1)} collective-permute-done((s32[64,2,128]{2,1,0:T(2,128)S(1)}, s32[64,2,128]{2,1,0:T(2,128)S(1)}, u32[]{:S(2)}, u32[]{:S(2)}) %collective-permute-start.3) | collective-permute-done | bytes 65568 | tf_op jit(solution)/shard_map/ppermute | solution.py:524
  161.4 17.6 %sums.1 = (bf16[4,4,4,288,128]{4,3,2,1,0:T(8,128)(2,1)}, bf16[4,4,4,272,128]{4,3,2,1,0:T(8,128)(2,1)}, bf16[4,4,4,224,128]{4,3,2,1,0:T(8,128)(2,1)}) custom-call(s32[2]{0:T(128)} %pad_add_fusion.at_ref, bf16[128,4,48,128]{3,2,1,0:T(8,128)(2,1)} %get-tuple-element.48.mine_ref, bf16[128,4,48,128]{3,2,1,0:T(8,128)(2,1)} %collective-permute-done.2.other_ref, ...), custom_call_target="tpu_custom_call" | custom-call | flops 10000000000 | bytes 25165824 | tf_op jit(solution)/shard_map/sums/pallas_call | solution.py:381
  179.1 2.7 slice_bitcast_fusion.7
  181.8 2.4 collective-permute-start.10
  184.2 4.8 %all-to-all-start.2 = ((bf16[4,4,4,224,128]{4,3,2,1,0:T(8,128)(2,1)}), bf16[4,4,4,224,128]{4,3,2,1,0:T(8,128)(2,1)}, u32[]{:S(2)}, u32[]{:S(2)}) async-start(bf16[4,4,4,224,128]{4,3,2,1,0:T(8,128)(2,1)} %get-tuple-element.56), calls=%async_computation.2 | async-start | bytes 7340032 | tf_op jit(solution)/shard_map/all_to_all | solution.py:550
  189.0 1.8 slice_bitcast_fusion.3
  190.8 1.3 collective-permute-start.4
  192.1 1.4 collective-permute-start.6
  193.5 2.7 collective-permute-done.10
  196.2 3.1 collective-permute-done.8
  199.2 1.8 fusion.7
  203.3 2.7 collective-permute-start.11
  206.4 1.6 fusion.5
  210.3 1.7 collective-permute-start.7
  212.2 2.6 collective-permute-start.20
  214.8 17.9 %collective-permute-done.20 = bf16[256,128]{1,0:T(8,128)(2,1)S(1)} collective-permute-done((bf16[256,128]{1,0:T(8,128)(2,1)S(1)}, bf16[256,128]{1,0:T(8,128)(2,1)S(1)}, u32[]{:S(2)}, u32[]{:S(2)}) %collective-permute-start.20) | collective-permute-done | bytes 65568 | tf_op jit(solution)/shard_map/ppermute | solution.py:558
  232.7 1.9 collective-permute-start.21
  236.3 2.4 fusion.3
  238.7 2.4 fusion.1
  241.2 3.8 %reduce_sum.48 = bf16[4,4,224,128]{3,2,1,0:T(8,128)(2,1)} reduce(bf16[4,4,4,224,128]{4,3,2,1,0:T(8,128)(2,1)} %all-to-all-done.2, bf16[]{:T(256)} %constant.93.clone.1), dimensions={0}, to_apply=%region_1.2 | reduce | flops 1376256 | bytes 4587522 | tf_op jit(solution)/shard_map/reduce_sum | solution.py:552
  247.1 1.4 collective-permute-start.18
  249.5 2.4 collective-permute-start.14
  251.9 4.2 %all-to-all-start.3 = ((bf16[16,224,128]{2,1,0:T(8,128)(2,1)}), bf16[16,224,128]{2,1,0:T(8,128)(2,1)S(1)}, u32[]{:S(2)}, u32[]{:S(2)}) async-start(bf16[16,224,128]{2,1,0:T(8,128)(2,1)} %bitcast.46), calls=%async_computation.3 | async-start | bytes 1835008 | tf_op jit(solution)/shard_map/all_to_all | solution.py:554
  258.2 1.4 collective-permute-start.17
  260.6 1.4 collective-permute-start.19
  263.1 1.6 collective-permute-start.13
  264.8 1.4 collective-permute-start.15
  266.9 9.1 %collective-permute-done.17 = bf16[4,272,128]{2,1,0:T(8,128)(2,1)S(1)} collective-permute-done((bf16[4,272,128]{2,1,0:T(8,128)(2,1)S(1)}, bf16[4,272,128]{2,1,0:T(8,128)(2,1)S(1)}, u32[]{:S(2)}, u32[]{:S(2)}) %collective-permute-start.17) | collective-permute-done | bytes 278560 | tf_op jit(solution)/shard_map/ppermute | solution.py:467
  277.0 22.0 %all_to_all.25 = bf16[4,2,784,128]{3,2,1,0:T(8,128)(2,1)S(1)} all-to-all(bf16[4,2,784,128]{3,2,1,0:T(8,128)(2,1)S(1)} %bitcast.113), channel_id=1, replica_groups=mesh['z'=4,'x'=4,'yl'=2,'yh'=2,'c'=2] {'yl','yh'}, dimensions={0} | all-to-all | bytes 3211264 | tf_op jit(solution)/shard_map/all_to_all | solution.py:573
  299.4 2.5 collective-permute-start.22
  306.8 6.0 %update.1 = (f32[192,2048]{1,0:T(8,128)}, f32[1,2048]{1,0:T(1,128)}) custom-call(s32[1,2048]{1,0:T(1,128)} %bitcast.127, bf16[2,2,784,128]{3,2,1,0:T(8,128)(2,1)} %maximum_select_fusion.sum_ref, f32[192,2048]{1,0:T(8,128)} %bitcast.128, f32[1,2048]{1,0:T(1,128)} %bitcast.129), custom_call_target="tpu_custom_call" | custom-call | flops 4000000000 | bytes 4718592 | tf_op jit(solution)/shard_map/update/pallas_call | solution.py:425
  (113 shorter events, 34.7 us)
Async XLA Ops:
  4.7 40.4 %all-to-all-start = ((bf16[32,272,128]{2,1,0:T(8,128)(2,1)}), bf16[32,272,128]{2,1,0:T(8,128)(2,1)S(1)}, u32[]{:S(2)}, u32[]{:S(2)}) async-start(bf16[32,272,128]{2,1,0:T(8,128)(2,1)} %broadcast_in_dim.52), calls=%async_computation | async-start | bytes 4456448 | tf_op jit(solution)/shard_map/all_to_all | solution.py:462
  46.9 25.2 %collective-permute-start = (bf16[32,256,128]{2,1,0:T(8,128)(2,1)}, bf16[32,256,128]{2,1,0:T(8,128)(2,1)}, u32[]{:S(2)}, u32[]{:S(2)}) collective-permute-start(bf16[32,256,128]{2,1,0:T(8,128)(2,1)} %slice.158), channel_id=1, source_target_pairs={{0,1},{1,0},{2,3},{3,2},{4,5},{5,4},{6,7},{7,6},{8,9},{9,8},{10,11... | collective-permute-start | bytes 6291464 | tf_op jit(solution)/shard_map/ppermute | solution.py:514
  97.0 2.6 copy-start
  100.5 4.2 %collective-permute-start.1 = (bf16[32,256,128]{2,1,0:T(8,128)(2,1)S(1)}, bf16[32,256,128]{2,1,0:T(8,128)(2,1)S(1)}, u32[]{:S(2)}, u32[]{:S(2)}) collective-permute-start(bf16[32,256,128]{2,1,0:T(8,128)(2,1)S(1)} %broadcast_select_fusion), channel_id=1, source_target_pairs={{0,1},{1,0},{2,3},{3,2},{4,5},{5,4},{6,7},{7,6},{8,9},{9,8},{10,11... | collective-permute-start | bytes 6291464 | tf_op jit(solution)/shard_map/ppermute | solution.py:536
  107.0 4.2 %copy-start.7 = (s32[256]{0:T(256)S(1)}, s32[256]{0:T(256)}, u32[]{:S(2)}) copy-start(s32[256]{0:T(256)} %param.15) | copy-start | bytes 3076
  107.0 43.4 %all-to-all-start.1 = ((bf16[32,256,128]{2,1,0:T(8,128)(2,1)}), bf16[32,256,128]{2,1,0:T(8,128)(2,1)S(1)}, u32[]{:S(2)}, u32[]{:S(2)}) async-start(bf16[32,256,128]{2,1,0:T(8,128)(2,1)} %add_convert_fusion), calls=%async_computation.1 | async-start | bytes 4194304 | tf_op jit(solution)/shard_map/all_to_all | solution.py:539
  111.8 38.9 %copy-start.4 = (s32[128,256]{1,0:T(8,128)S(1)}, s32[128,256]{1,0:T(8,128)}, u32[]{:S(2)}) copy-start(s32[128,256]{1,0:T(8,128)} %param.14) | copy-start | bytes 393220
  111.8 43.1 %copy-start.5 = (f32[16,256]{1,0:T(8,128)S(1)}, f32[16,256]{1,0:T(8,128)}, u32[]{:S(2)}) copy-start(f32[16,256]{1,0:T(8,128)} %get-tuple-element.53) | copy-start | bytes 49156
  150.5 10.6 %collective-permute-start.2 = (bf16[128,4,48,128]{3,2,1,0:T(8,128)(2,1)}, bf16[128,4,48,128]{3,2,1,0:T(8,128)(2,1)}, u32[]{:S(2)}, u32[]{:S(2)}) collective-permute-start(bf16[128,4,48,128]{3,2,1,0:T(8,128)(2,1)} %get-tuple-element.51), channel_id=1, source_target_pairs={{0,1},{1,0},{2,3},{3,2},{4,5},{5,4},{6,7},{7,6},{8,9},{9,8},{10,11... | collective-permute-start | bytes 18874376 | tf_op jit(solution)/shard_map/ppermute | solution.py:547
  153.9 6.9 %collective-permute-start.3 = (s32[64,2,128]{2,1,0:T(2,128)S(1)}, s32[64,2,128]{2,1,0:T(2,128)S(1)}, u32[]{:S(2)}, u32[]{:S(2)}) collective-permute-start(s32[64,2,128]{2,1,0:T(2,128)S(1)} %bitcast.124), channel_id=1, source_target_pairs={{0,1},{1,0},{2,3},{3,2},{4,5},{5,4},{6,7},{7,6},{8,9},{9,8},{10,11... | collective-permute-start | bytes 196616 | tf_op jit(solution)/shard_map/ppermute | solution.py:524
  160.8 0.6 copy-start.8
  181.8 14.4 %collective-permute-start.10 = (bf16[2,4,272,128]{3,2,1,0:T(8,128)(2,1)}, bf16[2,4,272,128]{3,2,1,0:T(8,128)(2,1)}, u32[]{:S(2)}, u32[]{:S(2)}) collective-permute-start(bf16[2,4,272,128]{3,2,1,0:T(8,128)(2,1)} %get-tuple-element.78), channel_id=1, source_target_pairs={{0,24},{8,0},{16,8},{24,16},{1,25},{9,1},{17,9},{25,17},{2,26},{10... | collective-permute-start | bytes 1671176 | tf_op jit(solution)/shard_map/ppermute | solution.py:467
  184.2 15.0 %collective-permute-start.8 = (bf16[2,4,272,128]{3,2,1,0:T(8,128)(2,1)}, bf16[2,4,272,128]{3,2,1,0:T(8,128)(2,1)}, u32[]{:S(2)}, u32[]{:S(2)}) collective-permute-start(bf16[2,4,272,128]{3,2,1,0:T(8,128)(2,1)} %get-tuple-element.77), channel_id=1, source_target_pairs={{0,8},{8,16},{16,24},{24,0},{1,9},{9,17},{17,25},{25,1},{2,10},{10... | collective-permute-start | bytes 1671176 | tf_op jit(solution)/shard_map/ppermute | solution.py:467
  184.2 57.0 %all-to-all-start.2 = ((bf16[4,4,4,224,128]{4,3,2,1,0:T(8,128)(2,1)}), bf16[4,4,4,224,128]{4,3,2,1,0:T(8,128)(2,1)}, u32[]{:S(2)}, u32[]{:S(2)}) async-start(bf16[4,4,4,224,128]{4,3,2,1,0:T(8,128)(2,1)} %get-tuple-element.56), calls=%async_computation.2 | async-start | bytes 7340032 | tf_op jit(solution)/shard_map/all_to_all | solution.py:550
  190.8 15.6 %collective-permute-start.4 = (bf16[2,4,288,128]{3,2,1,0:T(8,128)(2,1)S(1)}, bf16[2,4,288,128]{3,2,1,0:T(8,128)(2,1)S(1)}, u32[]{:S(2)}, u32[]{:S(2)}) collective-permute-start(bf16[2,4,288,128]{3,2,1,0:T(8,128)(2,1)S(1)} %get-tuple-element.71), channel_id=1, source_target_pairs={{0,32},{32,64},{64,96},{96,0},{1,33},{33,65},{65,97},{97,1},{2,34}... | collective-permute-start | bytes 1769480 | tf_op jit(solution)/shard_map/ppermute | solution.py:467
  192.1 14.3 %collective-permute-start.6 = (bf16[2,4,288,128]{3,2,1,0:T(8,128)(2,1)S(1)}, bf16[2,4,288,128]{3,2,1,0:T(8,128)(2,1)S(1)}, u32[]{:S(2)}, u32[]{:S(2)}) collective-permute-start(bf16[2,4,288,128]{3,2,1,0:T(8,128)(2,1)S(1)} %get-tuple-element.72), channel_id=1, source_target_pairs={{0,96},{32,0},{64,32},{96,64},{1,97},{33,1},{65,33},{97,65},{2,98}... | collective-permute-start | bytes 1769480 | tf_op jit(solution)/shard_map/ppermute | solution.py:467
  202.2 34.2 %collective-permute-start.9 = (bf16[4,4,272,128]{3,2,1,0:T(8,128)(2,1)}, bf16[4,4,272,128]{3,2,1,0:T(8,128)(2,1)}, u32[]{:S(2)}, u32[]{:S(2)}) collective-permute-start(bf16[4,4,272,128]{3,2,1,0:T(8,128)(2,1)} %pad_maximum_fusion.5), channel_id=1, source_target_pairs={{0,8},{8,16},{16,24},{24,0},{1,9},{9,17},{17,25},{25,1},{2,10},{10... | collective-permute-start | bytes 3342344 | tf_op jit(solution)/shard_map/ppermute | solution.py:467
  203.3 33.0 %collective-permute-start.11 = (bf16[4,4,272,128]{3,2,1,0:T(8,128)(2,1)}, bf16[4,4,272,128]{3,2,1,0:T(8,128)(2,1)}, u32[]{:S(2)}, u32[]{:S(2)}) collective-permute-start(bf16[4,4,272,128]{3,2,1,0:T(8,128)(2,1)} %pad_maximum_fusion.6), channel_id=1, source_target_pairs={{0,24},{8,0},{16,8},{24,16},{1,25},{9,1},{17,9},{25,17},{2,26},{10... | collective-permute-start | bytes 3342344 | tf_op jit(solution)/shard_map/ppermute | solution.py:467
  208.1 30.6 %collective-permute-start.5 = (bf16[4,4,288,128]{3,2,1,0:T(8,128)(2,1)S(1)}, bf16[4,4,288,128]{3,2,1,0:T(8,128)(2,1)}, u32[]{:S(2)}, u32[]{:S(2)}) collective-permute-start(bf16[4,4,288,128]{3,2,1,0:T(8,128)(2,1)S(1)} %pad_maximum_fusion.3), channel_id=1, source_target_pairs={{0,32},{32,64},{64,96},{96,0},{1,33},{33,65},{65,97},{97,1},{2,34}... | collective-permute-start | bytes 3538952 | tf_op jit(solution)/shard_map/ppermute | solution.py:467
  210.3 28.5 %collective-permute-start.7 = (bf16[4,4,288,128]{3,2,1,0:T(8,128)(2,1)}, bf16[4,4,288,128]{3,2,1,0:T(8,128)(2,1)}, u32[]{:S(2)}, u32[]{:S(2)}) collective-permute-start(bf16[4,4,288,128]{3,2,1,0:T(8,128)(2,1)} %pad_maximum_fusion.4), channel_id=1, source_target_pairs={{0,96},{32,0},{64,32},{96,64},{1,97},{33,1},{65,33},{97,65},{2,98}... | collective-permute-start | bytes 3538952 | tf_op jit(solution)/shard_map/ppermute | solution.py:467
  212.2 20.5 %collective-permute-start.20 = (bf16[256,128]{1,0:T(8,128)(2,1)S(1)}, bf16[256,128]{1,0:T(8,128)(2,1)S(1)}, u32[]{:S(2)}, u32[]{:S(2)}) collective-permute-start(bf16[256,128]{1,0:T(8,128)(2,1)S(1)} %reduce_sum.50), channel_id=1, source_target_pairs={{0,2},{2,0},{1,3},{3,1},{4,6},{6,4},{5,7},{7,5},{8,10},{10,8},{9,1... | collective-permute-start | bytes 196616 | tf_op jit(solution)/shard_map/ppermute | solution.py:558
  232.7 2.8 collective-permute-start.21
  245.8 10.3 %collective-permute-start.16 = (bf16[2,272,128]{2,1,0:T(8,128)(2,1)}, bf16[2,272,128]{2,1,0:T(8,128)(2,1)}, u32[]{:S(2)}, u32[]{:S(2)}) collective-permute-start(bf16[2,272,128]{2,1,0:T(8,128)(2,1)} %get-tuple-element.93), channel_id=1, source_target_pairs={{0,32},{32,64},{64,96},{96,0},{1,33},{33,65},{65,97},{97,1},{2,34}... | collective-permute-start | bytes 417800 | tf_op jit(solution)/shard_map/ppermute | solution.py:467
  247.1 9.1 %collective-permute-start.18 = (bf16[2,272,128]{2,1,0:T(8,128)(2,1)}, bf16[2,272,128]{2,1,0:T(8,128)(2,1)}, u32[]{:S(2)}, u32[]{:S(2)}) collective-permute-start(bf16[2,272,128]{2,1,0:T(8,128)(2,1)} %get-tuple-element.94), channel_id=1, source_target_pairs={{0,96},{32,0},{64,32},{96,64},{1,97},{33,1},{65,33},{97,65},{2,98}... | collective-permute-start | bytes 417800 | tf_op jit(solution)/shard_map/ppermute | solution.py:467
  249.2 12.7 %collective-permute-start.12 = (bf16[2,288,128]{2,1,0:T(8,128)(2,1)}, bf16[2,288,128]{2,1,0:T(8,128)(2,1)}, u32[]{:S(2)}, u32[]{:S(2)}) collective-permute-start(bf16[2,288,128]{2,1,0:T(8,128)(2,1)} %get-tuple-element.87), channel_id=1, source_target_pairs={{0,8},{8,16},{16,24},{24,0},{1,9},{9,17},{17,25},{25,1},{2,10},{10... | collective-permute-start | bytes 442376 | tf_op jit(solution)/shard_map/ppermute | solution.py:467
  249.5 12.5 %collective-permute-start.14 = (bf16[2,288,128]{2,1,0:T(8,128)(2,1)}, bf16[2,288,128]{2,1,0:T(8,128)(2,1)}, u32[]{:S(2)}, u32[]{:S(2)}) collective-permute-start(bf16[2,288,128]{2,1,0:T(8,128)(2,1)} %get-tuple-element.88), channel_id=1, source_target_pairs={{0,24},{8,0},{16,8},{24,16},{1,25},{9,1},{17,9},{25,17},{2,26},{10... | collective-permute-start | bytes 442376 | tf_op jit(solution)/shard_map/ppermute | solution.py:467
  251.9 24.4 %all-to-all-start.3 = ((bf16[16,224,128]{2,1,0:T(8,128)(2,1)}), bf16[16,224,128]{2,1,0:T(8,128)(2,1)S(1)}, u32[]{:S(2)}, u32[]{:S(2)}) async-start(bf16[16,224,128]{2,1,0:T(8,128)(2,1)} %bitcast.46), calls=%async_computation.3 | async-start | bytes 1835008 | tf_op jit(solution)/shard_map/all_to_all | solution.py:554
  256.1 10.0 %copy-start.2 = (f32[256,128]{1,0:T(8,128)S(1)}, f32[256,128]{1,0:T(8,128)}, u32[]{:S(2)}) copy-start(f32[256,128]{1,0:T(8,128)} %get-tuple-element.97) | copy-start | bytes 393220
  256.1 10.0 %copy-start.3 = (f32[256,128]{1,0:T(8,128)S(1)}, f32[256,128]{1,0:T(8,128)}, u32[]{:S(2)}) copy-start(f32[256,128]{1,0:T(8,128)} %get-tuple-element.98) | copy-start | bytes 393220
  258.2 17.8 %collective-permute-start.17 = (bf16[4,272,128]{2,1,0:T(8,128)(2,1)S(1)}, bf16[4,272,128]{2,1,0:T(8,128)(2,1)S(1)}, u32[]{:S(2)}, u32[]{:S(2)}) collective-permute-start(bf16[4,272,128]{2,1,0:T(8,128)(2,1)S(1)} %pad_maximum_fusion.10), channel_id=1, source_target_pairs={{0,32},{32,64},{64,96},{96,0},{1,33},{33,65},{65,97},{97,1},{2,34}... | collective-permute-start | bytes 835592 | tf_op jit(solution)/shard_map/ppermute | solution.py:467
  260.6 15.4 %collective-permute-start.19 = (bf16[4,272,128]{2,1,0:T(8,128)(2,1)S(1)}, bf16[4,272,128]{2,1,0:T(8,128)(2,1)S(1)}, u32[]{:S(2)}, u32[]{:S(2)}) collective-permute-start(bf16[4,272,128]{2,1,0:T(8,128)(2,1)S(1)} %pad_maximum_fusion.11), channel_id=1, source_target_pairs={{0,96},{32,0},{64,32},{96,64},{1,97},{33,1},{65,33},{97,65},{2,98}... | collective-permute-start | bytes 835592 | tf_op jit(solution)/shard_map/ppermute | solution.py:467
  263.1 13.1 %collective-permute-start.13 = (bf16[4,288,128]{2,1,0:T(8,128)(2,1)S(1)}, bf16[4,288,128]{2,1,0:T(8,128)(2,1)S(1)}, u32[]{:S(2)}, u32[]{:S(2)}) collective-permute-start(bf16[4,288,128]{2,1,0:T(8,128)(2,1)S(1)} %pad_maximum_fusion.8), channel_id=1, source_target_pairs={{0,8},{8,16},{16,24},{24,0},{1,9},{9,17},{17,25},{25,1},{2,10},{10... | collective-permute-start | bytes 884744 | tf_op jit(solution)/shard_map/ppermute | solution.py:467
  264.8 11.4 %collective-permute-start.15 = (bf16[4,288,128]{2,1,0:T(8,128)(2,1)S(1)}, bf16[4,288,128]{2,1,0:T(8,128)(2,1)S(1)}, u32[]{:S(2)}, u32[]{:S(2)}) collective-permute-start(bf16[4,288,128]{2,1,0:T(8,128)(2,1)S(1)} %pad_maximum_fusion.9), channel_id=1, source_target_pairs={{0,24},{8,0},{16,8},{24,16},{1,25},{9,1},{17,9},{25,17},{2,26},{10... | collective-permute-start | bytes 884744 | tf_op jit(solution)/shard_map/ppermute | solution.py:467
  276.9 25.0 %copy-start.6 = (s32[8,256]{1,0:T(8,128)S(1)}, s32[8,256]{1,0:T(8,128)}, u32[]{:S(2)}) copy-start(s32[8,256]{1,0:T(8,128)} %param.16) | copy-start | bytes 24580
  276.9 25.6 %copy-start.1 = (f32[512,128]{1,0:T(8,128)S(1)}, f32[512,128]{1,0:T(8,128)}, u32[]{:S(2)}) copy-start(f32[512,128]{1,0:T(8,128)} %pad_maximum_fusion.12) | copy-start | bytes 786436
  299.4 4.5 %collective-permute-start.22 = (bf16[2,784,128]{2,1,0:T(8,128)(2,1)S(1)}, bf16[2,784,128]{2,1,0:T(8,128)(2,1)S(1)}, u32[]{:S(2)}, u32[]{:S(2)}) collective-permute-start(bf16[2,784,128]{2,1,0:T(8,128)(2,1)S(1)} %reduce_sum.51), channel_id=1, source_target_pairs={{0,1},{1,0},{2,3},{3,2},{4,5},{5,4},{6,7},{7,6},{8,9},{9,8},{10,11... | collective-permute-start | bytes 1204232 | tf_op jit(solution)/shard_map/ppermute | solution.py:575

commit v5 on v4

--- a/solution.py
+++ b/solution.py
@@ -110,7 +110,7 @@
     xh_ref[:, :, 128:] = hi[...].reshape(K, rows, 128)
 
 
-def first(x3, g2, wt, rows=8):
+def first(x3, g2, wt, rows=16):
     count, n, _ = x3.shape
     nl = g2.shape[1]
     return pl.pallas_call(
@@ -141,25 +141,34 @@
 
 
 def batch_kernel(
-    xh_ref, inv_ref, gain_ref, win_ref, wout_ref, g_ref,
-    gout_ref, gin_ref, ggain_ref, dfm_ref, pre_s, hid_s, dhid_s, norm_s, e_s,
+    core_ref, xh_ref, inv_ref, gain_ref, nraw_ref, fraw_ref, near_ref, far_ref, g_ref,
+    gout_ref, gin_ref, ggain_ref, dfm_ref, pre_s, hid_s, dhid_s, norm_s, e_s, win_ref, gin_s,
 ):
     step = pl.program_id(0)
     count, n = xh_ref.shape[1], xh_ref.shape[2]
+    owners = nraw_ref.shape[0]
+    per = n // owners
+    first_core = core_ref[0] == 0
 
     @pl.when(step == 0)
     def _():
+        for o in range(owners):
+            v = jnp.where(first_core, nraw_ref[o], fraw_ref[o]).astype(F32)
+            v = jnp.swapaxes(v.reshape(per, K, 128), 0, 1)
+            win_ref[:, o * per : (o + 1) * per, :] = v
         pre = jnp.zeros((count, 128), F32)
         for k in range(K):
             normed = (xh_ref[k] * gain_ref[k : k + 1, :]).astype(BF16)
             norm_s[k] = normed
-            pre = pre + dot(normed, win_ref[k])
+            pre = pre + dot(normed, win_ref[k].astype(BF16))
         pre_s[...] = pre
         hid_s[...] = (pre / (1.0 + jnp.exp(-pre))).astype(BF16)
         dhid_s[...] = jnp.zeros_like(dhid_s)
 
     hid = hid_s[...]
-    w = wout_ref[...]
+    near, far = near_ref[...], far_ref[...]
+    lower = jnp.where(first_core, near[:, per * K :], far[:, per * K :])
+    w = jnp.concatenate([lower, jnp.where(first_core, far, near)], axis=1).reshape(-1, 128)
     rows = w.shape[0]
     fout = dot(w, hid, NT).reshape(rows // D, D, count)
     grad = g_ref[...].astype(F32).T.reshape(rows // D, D, count)
@@ -180,8 +189,8 @@
         m1 = jnp.zeros((count, n), F32)
         m2 = jnp.zeros((count, n), F32)
         for k in range(K):
-            gin_ref[k] = dot(norm_s[k], dpre, TN)
-            dn = dot(dpre, win_ref[k], NT)
+            gin_s[k] = dot(norm_s[k], dpre, TN)
+            dn = dot(dpre, win_ref[k].astype(BF16), NT)
             xh = xh_ref[k]
             ggain_ref[k : k + 1, :] = jnp.sum(dn * xh, axis=0, keepdims=True)
             e = dn * gain_ref[k : k + 1, :]
@@ -193,33 +202,42 @@
         inv = inv_ref[:, :1]
         for k in range(K):
             dfm_ref[k] = inv * (e_s[k] - a1 - xh_ref[k] * a2)
-
-
-def batch(xh, inv, gain, win, wout, out_grad, feats=4):
+        for o in range(owners):
+            v = jnp.swapaxes(gin_s[:, o * per : (o + 1) * per, :], 0, 1)
+            gin_ref[o] = v.reshape(per * K, 128).astype(BF16)
+
+
+def batch(core, xh, inv, gain, near, far, half, out_grad, feats=16):
     k, count, n = xh.shape
-    total = wout.shape[0]
+    owners = near.shape[0]
+    per = n // owners * k
+    total = owners * (2 * half - per)
     rows = feats * D
+    some = rows * owners // total
     whole = lambda shape: pl.BlockSpec(shape, lambda i: (0,) * len(shape))
     return pl.pallas_call(
         batch_kernel,
         grid=(total // rows,),
         in_specs=[
+            pl.BlockSpec(memory_space=pltpu.SMEM),
             whole((k, count, n)),
             whole((count, 128)),
             whole((k, n)),
-            whole((k, n, 128)),
-            pl.BlockSpec((rows, 128), lambda i: (i, 0)),
+            pl.BlockSpec((owners, per, 128), lambda i: (0, 0, 0)),
+            pl.BlockSpec((owners, per, 128), lambda i: (0, 0, 0)),
+            pl.BlockSpec((some, half, 128), lambda i: (i, 0, 0)),
+            pl.BlockSpec((some, half, 128), lambda i: (i, 0, 0)),
             pl.BlockSpec((count, rows), lambda i: (0, i)),
         ],
         out_specs=[
             pl.BlockSpec((rows, 128), lambda i: (i, 0)),
-            whole((k, n, 128)),
+            whole((owners, per, 128)),
             whole((k, n)),
             whole((k, count, n)),
         ],
         out_shape=[
             jax.ShapeDtypeStruct((total, 128), BF16),
-            jax.ShapeDtypeStruct((k, n, 128), F32),
+            jax.ShapeDtypeStruct((owners, per, 128), BF16),
             jax.ShapeDtypeStruct((k, n), F32),
             jax.ShapeDtypeStruct((k, count, n), F32),
         ],
@@ -229,11 +247,13 @@
             pltpu.VMEM((128, count), F32),
             pltpu.VMEM((k, count, n), BF16),
             pltpu.VMEM((k, count, n), F32),
+            pltpu.VMEM((k, n, 128), F32),
+            pltpu.VMEM((k, n, 128), F32),
         ],
         compiler_params=params(),
         cost_estimate=cost(2e10, 2e7),
         name="batch",
-    )(xh, inv, gain, win, wout, out_grad)
+    )(core, xh, inv, gain, near, far, near, far, out_grad)
 
 
 def last_kernel(
@@ -310,8 +330,10 @@
     )(at, x3, s, dl, dfm, wt)
 
 
-def sums_kernel(at_ref, mine_ref, other_ref, ids_ref, oid_ref, small_ref, a_ref, b_ref, c_ref):
-    tables, steps, height, _ = mine_ref.shape
+def sums_kernel(at_ref, mine_ref, other_ref, ids_ref, oid_ref, a_ref, b_ref, c_ref):
+    nx = b_ref.shape[0]
+    ny = c_ref.shape[0]
+    _, steps, height, _ = mine_ref.shape
     part = height // 3
     count = ids_ref.shape[2]
     rows = 2 * count
@@ -319,63 +341,60 @@
     one, none = jnp.ones((rows, count), BF16), jnp.zeros((rows, count), BF16)
     low = lax.broadcasted_iota(jnp.int32, (1, 128), 1) < 64
     zero = jnp.zeros((part, 128), BF16)
-    b_ref[0, 0, :, 96:112, :] = small_ref[0, 0]
-    for i in range(tables // 2):
-        for t in range(2):
-            hot = jnp.concatenate(
-                [
-                    jnp.where(iota == r[i, t : t + 1, :].astype(F32).astype(BF16), one, none)
+
+    def column(x, _):
+        ahead = lax.rem(x + nx - at_ref[1], nx)
+        for y in range(ny):
+            pair = x * ny + y
+            for t in range(2):
+                hot = [
+                    jnp.where(iota == r[pair, t : t + 1, :].astype(F32).astype(BF16), one, none)
                     for r in (ids_ref, oid_ref)
-                ],
-                axis=1,
-            )
-            main, rest = [], []
-            for r in (mine_ref, other_ref):
-                for s in range(steps):
-                    tail = r[2 * i + t, s, 2 * part :, :]
-                    main.append(r[2 * i + t, s, : 2 * part, :])
-                    rest += [jnp.where(low, tail, zero), jnp.where(low, zero, tail)]
-            block = jnp.concatenate(
-                [jnp.concatenate(main, axis=0), jnp.concatenate(rest, axis=0)], axis=1
-            )
-            out = dot(hot, block)
-            tail = out[:, 128:] + pltpu.roll(out[:, 128:], 64, 1)
-            main = out[:, :128].astype(BF16)
-            tail = jnp.where(low, tail[:count], tail[count:]).astype(BF16)
-            if t == 0:
-                a_ref[0, 0, i, :256, :] = main
-                a_ref[0, 0, i, 256:, :] = tail[:32]
-                b_ref[0, 0, i, :96, :] = tail[32:]
-            else:
-                b_ref[0, 0, i, 112:, :] = main[:160]
-                c_ref[i, 0, 0, :96, :] = main[160:]
-                c_ref[i, 0, 0, 96:, :] = tail
-
-
-def sums(at, mine, other, ids, oids, small):
+                ]
+                main, rest = [], []
+                for r in (mine_ref, other_ref):
+                    for s in range(steps):
+                        tail = r[2 * pair + t, s, 2 * part :, :]
+                        main.append(r[2 * pair + t, s, : 2 * part, :])
+                        rest += [jnp.where(low, tail, zero), jnp.where(low, zero, tail)]
+                block = jnp.concatenate(
+                    [jnp.concatenate(main, axis=0), jnp.concatenate(rest, axis=0)], axis=1
+                )
+                out = dot(jnp.concatenate(hot, axis=1), block)
+                tail = out[:, 128:] + pltpu.roll(out[:, 128:], 64, 1)
+                main = out[:, :128].astype(BF16)
+                tail = jnp.where(low, tail[:count], tail[count:]).astype(BF16)
+                if t == 0:
+                    a_ref[0, ahead, y, :256, :] = main
+                    a_ref[0, ahead, y, 256:, :] = tail[:32]
+                    b_ref[ahead, 0, y, :96, :] = tail[32:]
+                else:
+                    b_ref[ahead, 0, y, 96:, :] = main[:160]
+                    c_ref[y, 0, x, :96, :] = main[160:]
+                    c_ref[y, 0, x, 96:, :] = tail
+        return 0
+
+    lax.fori_loop(0, nx, column, 0)
+
+
+def sums(at, mine, other, ids, oids, nz=4, nx=4):
     tables, steps, height, _ = mine.shape
     count = ids.shape[2]
-    nz, nx, ny = small.shape[:3]
-    extra = small.shape[3]
-    data = pl.BlockSpec((2 * ny, steps, height, 128), lambda z, x, at: (z * nx + x, 0, 0, 0))
-    index = pl.BlockSpec((ny, 2, count), lambda z, x, at: (z * nx + x, 0, 0))
+    ny = tables // (2 * nz * nx)
+    data = pl.BlockSpec((2 * nx * ny, steps, height, 128), lambda z, at: (z, 0, 0, 0))
+    index = pl.BlockSpec((nx * ny, 2, count), lambda z, at: (z, 0, 0))
     grid = pltpu.PrefetchScalarGridSpec(
         num_scalar_prefetch=1,
-        grid=(nz, nx),
-        in_specs=[
-            data, data, index, index,
-            pl.BlockSpec((1, 1, ny, extra, 128), lambda z, x, at: (z, x, 0, 0, 0)),
-        ],
+        grid=(nz,),
+        in_specs=[data, data, index, index],
         out_specs=[
             pl.BlockSpec(
-                (1, 1, ny, 288, 128),
-                lambda z, x, at: ((z + nz - at[0]) % nz, (x + nx - at[1]) % nx, 0, 0, 0),
+                (1, nx, ny, 288, 128), lambda z, at: (lax.rem(z + nz - at[0], nz), 0, 0, 0, 0)
             ),
             pl.BlockSpec(
-                (1, 1, ny, 272, 128),
-                lambda z, x, at: ((x + nx - at[1]) % nx, (z + nz - at[0]) % nz, 0, 0, 0),
+                (nx, 1, ny, 256, 128), lambda z, at: (0, lax.rem(z + nz - at[0], nz), 0, 0, 0)
             ),
-            pl.BlockSpec((ny, 1, 1, 224, 128), lambda z, x, at: (0, z, x, 0, 0)),
+            pl.BlockSpec((ny, 1, nx, 224, 128), lambda z, at: (0, z, 0, 0, 0)),
         ],
     )
     return pl.pallas_call(
@@ -383,13 +402,13 @@
         grid_spec=grid,
         out_shape=[
             jax.ShapeDtypeStruct((nz, nx, ny, 288, 128), BF16),
-            jax.ShapeDtypeStruct((nx, nz, ny, 272, 128), BF16),
+            jax.ShapeDtypeStruct((nx, nz, ny, 256, 128), BF16),
             jax.ShapeDtypeStruct((ny, nz, nx, 224, 128), BF16),
         ],
         compiler_params=params(),
         cost_estimate=cost(1e10, mine.size * 8),
         name="sums",
-    )(at, mine, other, ids, oids, small)
+    )(at, mine, other, ids, oids)
 
 
 def update_kernel(slot_ref, sum_ref, rows_ref, accum_ref, new_rows_ref, new_accum_ref, acc):
@@ -440,19 +459,6 @@
     return (wt,) + tuple(first(x3, g2, wt))
 
 
-def layer(samples, out_grad, spot, proj, gain, w_in, w_out, w_lcb):
-    n = proj.shape[0]
-    nl = w_lcb.shape[1]
-    x3 = unfold(samples, n, 0)
-    g2 = unfold(out_grad, nl, out_grad.shape[1] // D // nl - 1)
-    wt, s, dl, xh, inv = forward(x3, g2, proj, w_lcb)
-    gain_t = gain.reshape(n, K).T.astype(F32)
-    win_t = w_in.reshape(n, K, 128).transpose(1, 0, 2)
-    g_out, g_in, g_gain, dfm = batch(xh, inv, gain_t, win_t, w_out, out_grad)
-    keep, send, acc = last(spot, x3, s, dl, dfm, wt)
-    return acc[:K] + acc[K : 2 * K], g_gain, g_in, g_out, acc[2 * K :], keep, send
-
-
 SWAP = [(0, 1), (1, 0)]
 WIDE = ("z", "x", "yl")
 
@@ -478,11 +484,11 @@
     fore = [ring_step(axis, 1, v[2, :2]) for axis, v in parts]
     back = [ring_step(axis, -1, v[2, 2:]) for axis, v in parts]
     fore = [
-        ring_step(axis, 1, jnp.concatenate([add(v[1, :2], f), v[1, 2:]], axis=0))
+        ring_step(axis, 1, add(v[1], jnp.pad(f, ((0, 2),) + ((0, 0),) * (f.ndim - 1))))
         for (axis, v), f in zip(parts, fore)
     ]
     back = [
-        ring_step(axis, -1, jnp.concatenate([v[3, :2], add(v[3, 2:], b)], axis=0))
+        ring_step(axis, -1, add(v[3], jnp.pad(b, ((2, 0),) + ((0, 0),) * (b.ndim - 1))))
         for (axis, v), b in zip(parts, back)
     ]
     return [add(v[0], f, b) for (_, v), f, b in zip(parts, fore, back)]
@@ -510,11 +516,7 @@
     proj_f = small[:, :K]
     gain_t = small[:, K : 2 * K].T.astype(F32)
     w_lcb_f = small[:, 2 * K : 2 * K + nl]
-    near = near[:, :rows]
     far = lax.ppermute(near, "c", SWAP)
-    lower, upper = jnp.where(core == 0, near, far), jnp.where(core == 0, far, near)
-    w_in_t = lower[:, : w_in.shape[0]].reshape(n, K, 128).transpose(1, 0, 2)
-    w_out_f = jnp.concatenate([lower[:, w_in.shape[0] :], upper], axis=1).reshape(-1, 128)
 
     quad = per // 2
     spot = table_owner // per * quad + table_owner % quad
@@ -524,11 +526,13 @@
     other_ids = lax.ppermute(ids[1], "c", SWAP)
 
     wt, score, dl, xh, inv = forward(x3, g2, proj_f, w_lcb_f)
-    g_out, g_in, g_gain, dfm = batch(xh, inv, gain_t, w_in_t, w_out_f, out_grad)
+    g_out, g_in, g_gain, dfm = batch(
+        core.reshape(1), xh, inv, gain_t, near, far, rows, out_grad
+    )
     w_grads = jnp.concatenate(
         [
             g_out.reshape(owners, -1, 128),
-            g_in.astype(BF16).transpose(1, 0, 2).reshape(owners, -1, 128),
+            g_in,
         ],
         axis=1,
     )
@@ -540,26 +544,28 @@
     keep, send, acc = last(spot, x3, score, dl, dfm, wt)
     w_grads, send = lax.optimization_barrier((w_grads, send))
     g_proj, g_lcb = acc[:K] + acc[K : 2 * K], acc[2 * K :]
-    little = jnp.concatenate([g_proj, g_gain, g_lcb], axis=0).T.reshape(4, 4, 2, 1, per, -1)
-    pad = ((0, 0),) * 3 + ((0, 1), (0, 8), (0, 128 - little.shape[-1]))
-    little = jnp.pad(little.astype(BF16), pad).reshape(4, 4, 4, 16, 128)
+    little = jnp.concatenate([g_proj, g_gain, g_lcb], axis=0).T.reshape(owners, per, -1)
+    little = jnp.pad(little, ((0, 0), (0, 0), (0, 128 - little.shape[2])))
+    little = lax.all_to_all(little, WIDE, 0, 0, tiled=True)
 
     other = lax.ppermute(send, "c", SWAP)
     at = jnp.stack([lax.axis_index("z"), lax.axis_index("x")]).astype(jnp.int32)
-    a, b, c = sums(at, keep, other, ids[0], other_ids, little)
+    a, b, c = sums(at, keep, other, ids[0], other_ids)
+    a, b, c, little = lax.optimization_barrier((a, b, c, little))
     c = lax.all_to_all(c, ("yl", "yh"), 0, 0, tiled=True)
     a, b = ring_sums([("z", a), ("x", b)])
     c = jnp.sum(c.astype(F32), axis=0).astype(BF16)
-    a, b, c = lax.optimization_barrier((a, b, c))
+    mixed = jnp.concatenate([jnp.sum(w_grads.astype(F32), axis=0), jnp.sum(little, axis=0)], axis=0)
+    a, b, c, mixed = lax.optimization_barrier((a, b, c, mixed))
     c = lax.all_to_all(c.reshape((16,) + c.shape[2:]), ("z", "x"), 0, 0, tiled=True)
     a, b = ring_sums([("x", a), ("z", b)])
     c = jnp.sum(c.astype(F32), axis=0).astype(BF16)
-    w_grads = jnp.sum(w_grads.astype(F32), axis=0).astype(BF16)
-    w_grads = w_grads.astype(F32) + lax.ppermute(w_grads, "yh", SWAP).astype(F32)
-    w_theirs = lax.ppermute(w_grads, "c", SWAP)
-    low, high = jnp.where(core == 0, w_grads, w_theirs), jnp.where(core == 0, w_theirs, w_grads)
-    big = jnp.concatenate([low, high], axis=0)
-    a, b, c, big = lax.optimization_barrier((a, b, c, big))
+    mixed = mixed + lax.ppermute(mixed, "yh", SWAP)
+    swapped = lax.ppermute(mixed, "c", SWAP)
+    little = (mixed[rows:] + swapped[rows:])[:, : 2 * K + nl]
+    low, high = jnp.where(core == 0, mixed, swapped), jnp.where(core == 0, swapped, mixed)
+    big = jnp.concatenate([low[:rows], high[:rows]], axis=0)
+    a, b, c, big, little = lax.optimization_barrier((a, b, c, big, little))
     ab = jnp.concatenate([a, b], axis=1)
     ab = ab.reshape((2, 1, 2) + ab.shape[1:])
     here = (jnp.arange(2)[:, None] == lax.axis_index("yl")) & (
@@ -574,7 +580,6 @@
     mine = jnp.sum(both.astype(F32), axis=0).astype(BF16)
     others = lax.ppermute(mine, "c", SWAP)
     owned = jnp.where(core == 0, jnp.stack([mine, others]), jnp.stack([others, mine]))
-    little = (mine[0, 384:392].astype(F32) + others[0, 384:392].astype(F32))[:, : 2 * K + nl]
     new_rows, new_accum = update(
         slot_map.reshape(1, -1), owned, table_rows.T, row_accum.reshape(1, -1)
     )

time: 315 us -> 294 us (0.933)
  Pallas kernels: 127 us -> 114 us
  starting transfers between devices: 54.4 us -> 64 us
  other arithmetic: 37.3 us -> 28 us
  local copies, waits for them, and re-layouts: 21.9 us -> 16.1 us
    ppermute x16, waiting for transfers between devices: 15.3 us -> 36.5 us  [ring_step(): return lax.ppermute(v, axis, [(i, (i + by) % n) for i in range(n)])]
    ppermute x2, waiting for transfers between devices: 18.9 us -> 0.01 us  [the longest x1 0.01 us: body(): mixed = mixed + lax.ppermute(mixed, 'yh', SWAP)]
    concatenate x10 -> x2, other arithmetic: 8.08 us -> 0.03 us  [the longest x1 0.02 us: body(): big = jnp.concatenate([low[:rows], high[:rows]], axis=0)]
    all_to_all x0 -> x1, starting transfers between devices: none -> 7.78 us  [body(): little = lax.all_to_all(little, WIDE, 0, 0, tiled=True)]
    pallas_call x1, Pallas kernels: 19.5 us -> 14 us  [batch(): pl.pallas_call(batch_kernel, grid=(total // rows,), in_specs=[pl.BlockSpe...]
    pallas_call x1, Pallas kernels: 21.6 us -> 17.5 us  [first(): pl.pallas_call(first_kernel, grid=(count // rows,), in_specs=[pl.BlockSpe...]
    ppermute x2, starting transfers between devices: 4.43 us -> 8.41 us  [the longest x1 6.27 us: body(): swapped = lax.ppermute(mixed, 'c', SWAP)]
    pallas_call x1, Pallas kernels: 17.6 us -> 13.8 us  [sums(): pl.pallas_call(sums_kernel, grid_spec=grid, out_shape=[jax.ShapeDtypeStru...]
  transfers between devices with their start and end apart: 27 -> 28, of which waited for: 10 -> 10; matrix products, arithmetic and copies ran while one was open for 10% -> 10% of each run, Pallas kernels for 27% -> 32%
where the time goes in v5:
time: 294 us; the launch traced here: 292 us
  Pallas kernels  114 us (39%)
  starting transfers between devices  64 us (22%)
  waiting for transfers between devices  47.1 us (16%)
  other arithmetic  28 us (10%)
  blocking collectives  21.9 us (7%)
  local copies, waits for them, and re-layouts  16.1 us (5%)
    pallas_call x1, Pallas kernels, last(): pl.pallas_call(last_kernel, grid_spec=grid, out_shape=[half, half, jax.Sh...  38.8 us
    ppermute x16, waiting for transfers between devices, ring_step(): return lax.ppermute(v, axis, [(i, (i + by) % n) for i in range(n)])  36.5 us
    pallas_call x2, Pallas kernels, unfold(): pl.pallas_call(unfold_kernel, grid=(count // rows,), in_specs=[pl.BlockSp...  24 us
    all_to_all x1, blocking collectives, body(): both = lax.all_to_all(both, ('yl', 'yh'), 0, 0, tiled=True)  21.9 us
    ppermute x16, starting transfers between devices, ring_step(): return lax.ppermute(v, axis, [(i, (i + by) % n) for i in range(n)])  20.4 us
    pallas_call x1, Pallas kernels, first(): pl.pallas_call(first_kernel, grid=(count // rows,), in_specs=[pl.BlockSpe...  17.5 us
    pallas_call x1, Pallas kernels, batch(): pl.pallas_call(batch_kernel, grid=(total // rows,), in_specs=[pl.BlockSpe...  14 us
    pallas_call x1, Pallas kernels, sums(): pl.pallas_call(sums_kernel, grid_spec=grid, out_shape=[jax.ShapeDtypeStru...  13.8 us
  transfers between devices with their start and end apart: 28, of which 10 were waited for; matrix products, arithmetic and copies ran while one was open for 10% of the time, Pallas kernels for 32%

profile of v5, /device:TPU:1, one launch (start us, length us, event | category | flops | bytes accessed | tf_op | source)
XLA Modules:
  0.0 292.3 jit_solution(1645143412845264070)
XLA Ops:
  3.0 1.7 broadcast_in_dim.52
  4.7 9.7 %all-to-all-start = ((bf16[32,272,128]{2,1,0:T(8,128)(2,1)}), bf16[32,272,128]{2,1,0:T(8,128)(2,1)S(1)}, u32[]{:S(2)}, u32[]{:S(2)}) async-start(bf16[32,272,128]{2,1,0:T(8,128)(2,1)} %broadcast_in_dim.52), calls=%async_computation | async-start | bytes 4456448 | tf_op jit(solution)/shard_map/all_to_all | solution.py:468
  14.5 17.7 %unfold.2.x_ref = bf16[128,256,256]{2,1,0:T(8,128)(2,1)} custom-call(bf16[128,49152]{1,0:T(8,128)(2,1)} %x_ref.2), custom_call_target="tpu_custom_call" | custom-call | flops 1000000000 | bytes 29491200 | tf_op jit(solution)/shard_map/unfold/pallas_call | solution.py:67
  32.1 6.3 %unfold.3.g_ref = bf16[128,64,256]{2,1,0:T(8,128)(2,1)} custom-call(bf16[128,24576]{1,0:T(8,128)(2,1)} %g_ref.1), custom_call_target="tpu_custom_call" | custom-call | flops 1000000000 | bytes 7372800 | tf_op jit(solution)/shard_map/unfold/pallas_call | solution.py:67
  38.5 6.7 %all-to-all-done.nraw_ref.near_ref = bf16[32,272,128]{2,1,0:T(8,128)(2,1)S(1)} async-done(((bf16[32,272,128]{2,1,0:T(8,128)(2,1)}), bf16[32,272,128]{2,1,0:T(8,128)(2,1)S(1)}, u32[]{:S(2)}, u32[]{:S(2)}) %all-to-all-start) | async-done | bytes 2228256 | tf_op jit(solution)/shard_map/all_to_all | solution.py:468
  45.1 2.1 collective-permute-start
  48.9 17.5 %first.1 = (bf16[128,32,256]{2,1,0:T(8,128)(2,1)}, bf16[128,64,256]{2,1,0:T(8,128)(2,1)}, f32[16,128,256]{2,1,0:T(8,128)}, f32[128,128]{1,0:T(8,128)}) custom-call(bf16[128,256,256]{2,1,0:T(8,128)(2,1)} %unfold.2.x_ref, bf16[128,64,256]{2,1,0:T(8,128)(2,1)} %unfold.3.g_ref, bf16[80,256]{1,0:T(8,128)(2,1)} %pad_maximum_fusion.6.w_ref.wt_ref), custom_call_target="tpu_custom_call" | custom-call | flops 20000000000 | bytes 16777216 | tf_op jit(solution)/shard_map/first/pallas_call | solution.py:116
  66.4 14.0 %batch.1 = (bf16[12288,128]{1,0:T(8,128)(2,1)}, bf16[32,128,128]{2,1,0:T(8,128)(2,1)}, f32[16,256]{1,0:T(8,128)}, f32[16,128,256]{2,1,0:T(8,128)}) custom-call(s32[1]{0:T(128)} %bitcast.5.core_ref, f32[16,128,256]{2,1,0:T(8,128)} %get-tuple-element.48.xh_ref, f32[128,128]{1,0:T(8,128)} %get-tuple-element.49.inv_ref, f32[16,256]{1,0:T(8,128)} %convert_bitcast_fusion.gain_ref, ...), custom_call_target="tpu_custom_call" | custom-call | flops 20000000000 | bytes 20000000 | tf_op jit(solution)/shard_map/batch/pallas_call | solution.py:218
  80.5 3.1 %broadcast_select_fusion = bf16[32,256,128]{2,1,0:T(8,128)(2,1)S(1)} fusion(pred[]{:T(512)S(6)} %eq.40, bf16[32,384,128]{2,1,0:T(8,128)(2,1)} %bitcast.81, bf16[32,128,128]{2,1,0:T(8,128)(2,1)} %get-tuple-element.51), kind=kLoop, calls=%fused_computation.19 | loop fusion | flops 5242880 | bytes 8388609 | tf_op jit(solution)/shard_map/jit(_where)/select_n | solution.py:540
  83.9 3.9 %collective-permute-done.1 = bf16[32,256,128]{2,1,0:T(8,128)(2,1)S(1)} collective-permute-done((bf16[32,256,128]{2,1,0:T(8,128)(2,1)S(1)}, bf16[32,256,128]{2,1,0:T(8,128)(2,1)S(1)}, u32[]{:S(2)}, u32[]{:S(2)}) %collective-permute-start.1) | collective-permute-done | bytes 2097184 | tf_op jit(solution)/shard_map/ppermute | solution.py:540
  87.8 2.3 add_convert_fusion
  90.1 4.1 %all-to-all-start.1 = ((bf16[32,256,128]{2,1,0:T(8,128)(2,1)}), bf16[32,256,128]{2,1,0:T(8,128)(2,1)S(1)}, u32[]{:S(2)}, u32[]{:S(2)}) async-start(bf16[32,256,128]{2,1,0:T(8,128)(2,1)} %add_convert_fusion), calls=%async_computation.1 | async-start | bytes 4194304 | tf_op jit(solution)/shard_map/all_to_all | solution.py:543
  94.8 38.8 %last.1 = (bf16[128,4,48,128]{3,2,1,0:T(8,128)(2,1)}, bf16[128,4,48,128]{3,2,1,0:T(8,128)(2,1)}, f32[96,256]{1,0:T(8,128)}) custom-call(s32[256]{0:T(256)} %get-tuple-element.80.at_ref, bf16[128,256,256]{2,1,0:T(8,128)(2,1)} %unfold.2.x_ref, bf16[128,32,256]{2,1,0:T(8,128)(2,1)} %get-tuple-element.46.s_ref, bf16[128,64,256]{2,1,0:T(8,128)(2,1)} %get-tuple-element.47.dl_ref, ...), custom_call_target="tpu_custom_call" | custom-call | flops 20000000000 | bytes 33554432 | tf_op jit(solution)/shard_map/last/pallas_call | solution.py:323
  134.3 1.4 scatter_custom_fusion
  140.4 7.8 %all-to-all-start.2 = ((f32[32,8,128]{2,1,0:T(8,128)}), f32[32,8,128]{2,1,0:T(8,128)S(1)}, u32[]{:S(2)}, u32[]{:S(2)}) async-start(f32[32,8,128]{2,1,0:T(8,128)} %pad.41), calls=%async_computation.2 | async-start | bytes 262144 | tf_op jit(solution)/shard_map/all_to_all | solution.py:549
  148.8 13.8 %sums.1 = (bf16[4,4,4,288,128]{4,3,2,1,0:T(8,128)(2,1)}, bf16[4,4,4,256,128]{4,3,2,1,0:T(8,128)(2,1)}, bf16[4,4,4,224,128]{4,3,2,1,0:T(8,128)(2,1)}) custom-call(s32[2]{0:T(128)} %pad_add_fusion.at_ref, bf16[128,4,48,128]{3,2,1,0:T(8,128)(2,1)} %get-tuple-element.54.mine_ref, bf16[128,4,48,128]{3,2,1,0:T(8,128)(2,1)} %collective-permute-done.2.other_ref, ...), custom_call_target="tpu_custom_call" | custom-call | flops 10000000000 | bytes 25165824 | tf_op jit(solution)/shard_map/sums/pallas_call | solution.py:400
  162.6 4.7 %all-to-all-start.3 = ((bf16[4,4,4,224,128]{4,3,2,1,0:T(8,128)(2,1)}), bf16[4,4,4,224,128]{4,3,2,1,0:T(8,128)(2,1)}, u32[]{:S(2)}, u32[]{:S(2)}) async-start(bf16[4,4,4,224,128]{4,3,2,1,0:T(8,128)(2,1)} %get-tuple-element.65), calls=%async_computation.3 | async-start | bytes 7340032 | tf_op jit(solution)/shard_map/all_to_all | solution.py:555
  167.4 1.4 slice_bitcast_fusion.3
  168.8 2.5 collective-permute-start.10
  171.3 1.3 slice_bitcast_fusion.1
  172.7 1.3 collective-permute-start.4
  173.9 1.5 collective-permute-start.6
  175.4 6.3 %collective-permute-done.10 = bf16[2,4,256,128]{3,2,1,0:T(8,128)(2,1)S(1)} collective-permute-done((bf16[2,4,256,128]{3,2,1,0:T(8,128)(2,1)S(1)}, bf16[2,4,256,128]{3,2,1,0:T(8,128)(2,1)S(1)}, u32[]{:S(2)}, u32[]{:S(2)}) %collective-permute-start.10) | collective-permute-done | bytes 524320 | tf_op jit(solution)/shard_map/ppermute | solution.py:473
  181.7 3.1 %collective-permute-done.8 = bf16[2,4,256,128]{3,2,1,0:T(8,128)(2,1)S(1)} collective-permute-done((bf16[2,4,256,128]{3,2,1,0:T(8,128)(2,1)S(1)}, bf16[2,4,256,128]{3,2,1,0:T(8,128)(2,1)S(1)}, u32[]{:S(2)}, u32[]{:S(2)}) %collective-permute-start.8) | collective-permute-done | bytes 524320 | tf_op jit(solution)/shard_map/ppermute | solution.py:473
  184.7 1.7 fusion.5
  187.9 1.4 fusion.1
  189.2 1.2 collective-permute-start.5
  190.5 1.5 collective-permute-start.7
  192.3 16.9 %collective-permute-done.11 = bf16[4,4,256,128]{3,2,1,0:T(8,128)(2,1)} collective-permute-done((bf16[4,4,256,128]{3,2,1,0:T(8,128)(2,1)}, bf16[4,4,256,128]{3,2,1,0:T(8,128)(2,1)}, u32[]{:S(2)}, u32[]{:S(2)}) %collective-permute-start.11) | collective-permute-done | bytes 1048608 | tf_op jit(solution)/shard_map/ppermute | solution.py:473
  209.2 1.5 collective-permute-done.9
  210.7 2.3 fusion.7
  213.0 2.5 collective-permute-done.5
  215.5 2.4 fusion.3
  218.0 3.8 %reduce_sum.54 = bf16[4,4,224,128]{3,2,1,0:T(8,128)(2,1)} reduce(bf16[4,4,4,224,128]{4,3,2,1,0:T(8,128)(2,1)} %all-to-all-done.3, bf16[]{:T(256)} %constant.93.clone.1), dimensions={0}, to_apply=%region_1.2 | reduce | flops 1376256 | bytes 4587522 | tf_op jit(solution)/shard_map/reduce_sum | solution.py:557
  221.7 2.1 collective-permute-start.20
  225.3 1.9 collective-permute-start.18
  228.3 2.4 collective-permute-start.14
  230.7 3.6 %all-to-all-start.4 = ((bf16[16,224,128]{2,1,0:T(8,128)(2,1)}), bf16[16,224,128]{2,1,0:T(8,128)(2,1)S(1)}, u32[]{:S(2)}, u32[]{:S(2)}) async-start(bf16[16,224,128]{2,1,0:T(8,128)(2,1)} %bitcast.33), calls=%async_computation.4 | async-start | bytes 1835008 | tf_op jit(solution)/shard_map/all_to_all | solution.py:560
  235.4 1.3 collective-permute-start.17
  236.7 1.4 collective-permute-start.19
  239.1 6.3 %collective-permute-start.21 = (f32[264,128]{1,0:T(8,128)S(1)}, f32[264,128]{1,0:T(8,128)S(1)}, u32[]{:S(2)}, u32[]{:S(2)}) collective-permute-start(f32[264,128]{1,0:T(8,128)S(1)} %add.143), channel_id=1, source_target_pairs={{0,1},{1,0},{2,3},{3,2},{4,5},{5,4},{6,7},{7,6},{8,9},{9,8},{10,11... | collective-permute-start | bytes 405512 | tf_op jit(solution)/shard_map/ppermute | solution.py:564
  246.3 1.6 collective-permute-start.13
  247.9 1.3 collective-permute-start.15
  249.3 2.7 collective-permute-done.17
  253.1 3.3 %collective-permute-done.13 = bf16[4,288,128]{2,1,0:T(8,128)(2,1)S(1)} collective-permute-done((bf16[4,288,128]{2,1,0:T(8,128)(2,1)S(1)}, bf16[4,288,128]{2,1,0:T(8,128)(2,1)S(1)}, u32[]{:S(2)}, u32[]{:S(2)}) %collective-permute-start.13) | collective-permute-done | bytes 294944 | tf_op jit(solution)/shard_map/ppermute | solution.py:473
  257.1 21.9 %all_to_all.30 = bf16[4,2,768,128]{3,2,1,0:T(8,128)(2,1)S(1)} all-to-all(bf16[4,2,768,128]{3,2,1,0:T(8,128)(2,1)S(1)} %bitcast.84), channel_id=1, replica_groups=mesh['z'=4,'x'=4,'yl'=2,'yh'=2,'c'=2] {'yl','yh'}, dimensions={0} | all-to-all | bytes 3145728 | tf_op jit(solution)/shard_map/all_to_all | solution.py:579
  279.5 2.0 collective-permute-start.22
  286.3 6.0 %update.1 = (f32[192,2048]{1,0:T(8,128)}, f32[1,2048]{1,0:T(1,128)}) custom-call(s32[1,2048]{1,0:T(1,128)} %bitcast.96, bf16[2,2,768,128]{3,2,1,0:T(8,128)(2,1)} %maximum_select_fusion.sum_ref, f32[192,2048]{1,0:T(8,128)} %bitcast.97, f32[1,2048]{1,0:T(1,128)} %bitcast.98), custom_call_target="tpu_custom_call" | custom-call | flops 4000000000 | bytes 4718592 | tf_op jit(solution)/shard_map/update/pallas_call | solution.py:444
  (105 shorter events, 25.3 us)
Async XLA Ops:
  4.7 40.4 %all-to-all-start = ((bf16[32,272,128]{2,1,0:T(8,128)(2,1)}), bf16[32,272,128]{2,1,0:T(8,128)(2,1)S(1)}, u32[]{:S(2)}, u32[]{:S(2)}) async-start(bf16[32,272,128]{2,1,0:T(8,128)(2,1)} %broadcast_in_dim.52), calls=%async_computation | async-start | bytes 4456448 | tf_op jit(solution)/shard_map/all_to_all | solution.py:468
  45.1 21.3 %copy-start.4 = (bf16[32,272,128]{2,1,0:T(8,128)(2,1)}, bf16[32,272,128]{2,1,0:T(8,128)(2,1)S(1)}, u32[]{:S(2)}) copy-start(bf16[32,272,128]{2,1,0:T(8,128)(2,1)S(1)} %all-to-all-done.nraw_ref.near_ref) | copy-start | bytes 6684676
  45.1 21.3 %collective-permute-start = (bf16[32,272,128]{2,1,0:T(8,128)(2,1)S(1)}, bf16[32,272,128]{2,1,0:T(8,128)(2,1)}, u32[]{:S(2)}, u32[]{:S(2)}) collective-permute-start(bf16[32,272,128]{2,1,0:T(8,128)(2,1)S(1)} %all-to-all-done.nraw_ref.near_ref), channel_id=1, source_target_pairs={{0,1},{1,0},{2,3},{3,2},{4,5},{5,4},{6,7},{7,6},{8,9},{9,8},{10,11... | collective-permute-start | bytes 6684680 | tf_op jit(solution)/shard_map/ppermute | solution.py:519
  80.4 7.4 %copy-start = (bf16[12288,128]{1,0:T(8,128)(2,1)S(1)}, bf16[12288,128]{1,0:T(8,128)(2,1)}, u32[]{:S(2)}) copy-start(bf16[12288,128]{1,0:T(8,128)(2,1)} %get-tuple-element.50) | copy-start | bytes 9437188
  80.4 7.4 %copy-start.3 = (bf16[32,128,128]{2,1,0:T(8,128)(2,1)S(1)}, bf16[32,128,128]{2,1,0:T(8,128)(2,1)}, u32[]{:S(2)}) copy-start(bf16[32,128,128]{2,1,0:T(8,128)(2,1)} %get-tuple-element.51) | copy-start | bytes 3145732
  83.6 4.2 %collective-permute-start.1 = (bf16[32,256,128]{2,1,0:T(8,128)(2,1)S(1)}, bf16[32,256,128]{2,1,0:T(8,128)(2,1)S(1)}, u32[]{:S(2)}, u32[]{:S(2)}) collective-permute-start(bf16[32,256,128]{2,1,0:T(8,128)(2,1)S(1)} %broadcast_select_fusion), channel_id=1, source_target_pairs={{0,1},{1,0},{2,3},{3,2},{4,5},{5,4},{6,7},{7,6},{8,9},{9,8},{10,11... | collective-permute-start | bytes 6291464 | tf_op jit(solution)/shard_map/ppermute | solution.py:540
  90.1 4.2 %copy-start.9 = (s32[256]{0:T(256)S(1)}, s32[256]{0:T(256)}, u32[]{:S(2)}) copy-start(s32[256]{0:T(256)} %param.15) | copy-start | bytes 3076
  90.1 43.6 %all-to-all-start.1 = ((bf16[32,256,128]{2,1,0:T(8,128)(2,1)}), bf16[32,256,128]{2,1,0:T(8,128)(2,1)S(1)}, u32[]{:S(2)}, u32[]{:S(2)}) async-start(bf16[32,256,128]{2,1,0:T(8,128)(2,1)} %add_convert_fusion), calls=%async_computation.1 | async-start | bytes 4194304 | tf_op jit(solution)/shard_map/all_to_all | solution.py:543
  94.8 39.4 %copy-start.6 = (s32[128,256]{1,0:T(8,128)S(1)}, s32[128,256]{1,0:T(8,128)}, u32[]{:S(2)}) copy-start(s32[128,256]{1,0:T(8,128)} %param.14) | copy-start | bytes 393220
  133.7 6.0 %copy-start.7 = (f32[16,256]{1,0:T(8,128)S(1)}, f32[16,256]{1,0:T(8,128)}, u32[]{:S(2)}) copy-start(f32[16,256]{1,0:T(8,128)} %get-tuple-element.62) | copy-start | bytes 49156
  133.7 14.6 %collective-permute-start.2 = (bf16[128,4,48,128]{3,2,1,0:T(8,128)(2,1)}, bf16[128,4,48,128]{3,2,1,0:T(8,128)(2,1)}, u32[]{:S(2)}, u32[]{:S(2)}) collective-permute-start(bf16[128,4,48,128]{3,2,1,0:T(8,128)(2,1)} %get-tuple-element.57), channel_id=1, source_target_pairs={{0,1},{1,0},{2,3},{3,2},{4,5},{5,4},{6,7},{7,6},{8,9},{9,8},{10,11... | collective-permute-start | bytes 18874376 | tf_op jit(solution)/shard_map/ppermute | solution.py:551
  137.2 11.0 %collective-permute-start.3 = (s32[64,2,128]{2,1,0:T(2,128)S(1)}, s32[64,2,128]{2,1,0:T(2,128)S(1)}, u32[]{:S(2)}, u32[]{:S(2)}) collective-permute-start(s32[64,2,128]{2,1,0:T(2,128)S(1)} %bitcast.93), channel_id=1, source_target_pairs={{0,1},{1,0},{2,3},{3,2},{4,5},{5,4},{6,7},{7,6},{8,9},{9,8},{10,11... | collective-permute-start | bytes 196616 | tf_op jit(solution)/shard_map/ppermute | solution.py:526
  140.4 22.2 %all-to-all-start.2 = ((f32[32,8,128]{2,1,0:T(8,128)}), f32[32,8,128]{2,1,0:T(8,128)S(1)}, u32[]{:S(2)}, u32[]{:S(2)}) async-start(f32[32,8,128]{2,1,0:T(8,128)} %pad.41), calls=%async_computation.2 | async-start | bytes 262144 | tf_op jit(solution)/shard_map/all_to_all | solution.py:549
  148.2 0.6 copy-start.10
  162.6 55.4 %all-to-all-start.3 = ((bf16[4,4,4,224,128]{4,3,2,1,0:T(8,128)(2,1)}), bf16[4,4,4,224,128]{4,3,2,1,0:T(8,128)(2,1)}, u32[]{:S(2)}, u32[]{:S(2)}) async-start(bf16[4,4,4,224,128]{4,3,2,1,0:T(8,128)(2,1)} %get-tuple-element.65), calls=%async_computation.3 | async-start | bytes 7340032 | tf_op jit(solution)/shard_map/all_to_all | solution.py:555
  167.4 17.4 %copy-start.2 = (bf16[4,4,4,256,128]{4,3,2,1,0:T(8,128)(2,1)S(1)}, bf16[4,4,4,256,128]{4,3,2,1,0:T(8,128)(2,1)}, u32[]{:S(2)}) copy-start(bf16[4,4,4,256,128]{4,3,2,1,0:T(8,128)(2,1)} %get-tuple-element.64) | copy-start | bytes 12582916
  168.8 12.9 %collective-permute-start.10 = (bf16[2,4,256,128]{3,2,1,0:T(8,128)(2,1)S(1)}, bf16[2,4,256,128]{3,2,1,0:T(8,128)(2,1)S(1)}, u32[]{:S(2)}, u32[]{:S(2)}) collective-permute-start(bf16[2,4,256,128]{3,2,1,0:T(8,128)(2,1)S(1)} %get-tuple-element.88), channel_id=1, source_target_pairs={{0,24},{8,0},{16,8},{24,16},{1,25},{9,1},{17,9},{25,17},{2,26},{10... | collective-permute-start | bytes 1572872 | tf_op jit(solution)/shard_map/ppermute | solution.py:473
  171.3 13.4 %collective-permute-start.8 = (bf16[2,4,256,128]{3,2,1,0:T(8,128)(2,1)S(1)}, bf16[2,4,256,128]{3,2,1,0:T(8,128)(2,1)S(1)}, u32[]{:S(2)}, u32[]{:S(2)}) collective-permute-start(bf16[2,4,256,128]{3,2,1,0:T(8,128)(2,1)S(1)} %get-tuple-element.87), channel_id=1, source_target_pairs={{0,8},{8,16},{16,24},{24,0},{1,9},{9,17},{17,25},{25,1},{2,10},{10... | collective-permute-start | bytes 1572872 | tf_op jit(solution)/shard_map/ppermute | solution.py:473
  172.7 15.2 %collective-permute-start.4 = (bf16[2,4,288,128]{3,2,1,0:T(8,128)(2,1)S(1)}, bf16[2,4,288,128]{3,2,1,0:T(8,128)(2,1)S(1)}, u32[]{:S(2)}, u32[]{:S(2)}) collective-permute-start(bf16[2,4,288,128]{3,2,1,0:T(8,128)(2,1)S(1)} %get-tuple-element.83), channel_id=1, source_target_pairs={{0,32},{32,64},{64,96},{96,0},{1,33},{33,65},{65,97},{97,1},{2,34}... | collective-permute-start | bytes 1769480 | tf_op jit(solution)/shard_map/ppermute | solution.py:473
  173.9 13.9 %copy-start.1 = (bf16[4,4,4,288,128]{4,3,2,1,0:T(8,128)(2,1)S(1)}, bf16[4,4,4,288,128]{4,3,2,1,0:T(8,128)(2,1)}, u32[]{:S(2)}) copy-start(bf16[4,4,4,288,128]{4,3,2,1,0:T(8,128)(2,1)} %get-tuple-element.63) | copy-start | bytes 14155780
  173.9 13.9 %collective-permute-start.6 = (bf16[2,4,288,128]{3,2,1,0:T(8,128)(2,1)S(1)}, bf16[2,4,288,128]{3,2,1,0:T(8,128)(2,1)S(1)}, u32[]{:S(2)}, u32[]{:S(2)}) collective-permute-start(bf16[2,4,288,128]{3,2,1,0:T(8,128)(2,1)S(1)} %get-tuple-element.84), channel_id=1, source_target_pairs={{0,96},{32,0},{64,32},{96,64},{1,97},{33,1},{65,33},{97,65},{2,98}... | collective-permute-start | bytes 1769480 | tf_op jit(solution)/shard_map/ppermute | solution.py:473
  186.4 22.8 %collective-permute-start.11 = (bf16[4,4,256,128]{3,2,1,0:T(8,128)(2,1)}, bf16[4,4,256,128]{3,2,1,0:T(8,128)(2,1)}, u32[]{:S(2)}, u32[]{:S(2)}) collective-permute-start(bf16[4,4,256,128]{3,2,1,0:T(8,128)(2,1)} %get-tuple-element.86), channel_id=1, source_target_pairs={{0,24},{8,0},{16,8},{24,16},{1,25},{9,1},{17,9},{25,17},{2,26},{10... | collective-permute-start | bytes 3145736 | tf_op jit(solution)/shard_map/ppermute | solution.py:473
  186.7 24.0 %collective-permute-start.9 = (bf16[4,4,256,128]{3,2,1,0:T(8,128)(2,1)}, bf16[4,4,256,128]{3,2,1,0:T(8,128)(2,1)}, u32[]{:S(2)}, u32[]{:S(2)}) collective-permute-start(bf16[4,4,256,128]{3,2,1,0:T(8,128)(2,1)} %get-tuple-element.85), channel_id=1, source_target_pairs={{0,8},{8,16},{16,24},{24,0},{1,9},{9,17},{17,25},{25,1},{2,10},{10... | collective-permute-start | bytes 3145736 | tf_op jit(solution)/shard_map/ppermute | solution.py:473
  189.2 26.3 %collective-permute-start.5 = (bf16[4,4,288,128]{3,2,1,0:T(8,128)(2,1)}, bf16[4,4,288,128]{3,2,1,0:T(8,128)(2,1)}, u32[]{:S(2)}, u32[]{:S(2)}) collective-permute-start(bf16[4,4,288,128]{3,2,1,0:T(8,128)(2,1)} %get-tuple-element.81), channel_id=1, source_target_pairs={{0,32},{32,64},{64,96},{96,0},{1,33},{33,65},{65,97},{97,1},{2,34}... | collective-permute-start | bytes 3538952 | tf_op jit(solution)/shard_map/ppermute | solution.py:473
  190.5 25.1 %collective-permute-start.7 = (bf16[4,4,288,128]{3,2,1,0:T(8,128)(2,1)S(1)}, bf16[4,4,288,128]{3,2,1,0:T(8,128)(2,1)}, u32[]{:S(2)}, u32[]{:S(2)}) collective-permute-start(bf16[4,4,288,128]{3,2,1,0:T(8,128)(2,1)S(1)} %get-tuple-element.82), channel_id=1, source_target_pairs={{0,96},{32,0},{64,32},{96,64},{1,97},{33,1},{65,33},{97,65},{2,98}... | collective-permute-start | bytes 3538952 | tf_op jit(solution)/shard_map/ppermute | solution.py:473
  221.7 16.4 %collective-permute-start.20 = (f32[264,128]{1,0:T(8,128)S(1)}, f32[264,128]{1,0:T(8,128)}, u32[]{:S(2)}, u32[]{:S(2)}) collective-permute-start(f32[264,128]{1,0:T(8,128)S(1)} %pad_maximum_fusion.4), channel_id=1, source_target_pairs={{0,2},{2,0},{1,3},{3,1},{4,6},{6,4},{5,7},{7,5},{8,10},{10,8},{9,1... | collective-permute-start | bytes 405512 | tf_op jit(solution)/shard_map/ppermute | solution.py:563
  224.6 9.7 %collective-permute-start.16 = (bf16[2,256,128]{2,1,0:T(8,128)(2,1)}, bf16[2,256,128]{2,1,0:T(8,128)(2,1)}, u32[]{:S(2)}, u32[]{:S(2)}) collective-permute-start(bf16[2,256,128]{2,1,0:T(8,128)(2,1)} %get-tuple-element.95), channel_id=1, source_target_pairs={{0,32},{32,64},{64,96},{96,0},{1,33},{33,65},{65,97},{97,1},{2,34}... | collective-permute-start | bytes 393224 | tf_op jit(solution)/shard_map/ppermute | solution.py:473
  225.3 9.0 %collective-permute-start.18 = (bf16[2,256,128]{2,1,0:T(8,128)(2,1)}, bf16[2,256,128]{2,1,0:T(8,128)(2,1)}, u32[]{:S(2)}, u32[]{:S(2)}) collective-permute-start(bf16[2,256,128]{2,1,0:T(8,128)(2,1)} %get-tuple-element.96), channel_id=1, source_target_pairs={{0,96},{32,0},{64,32},{96,64},{1,97},{33,1},{65,33},{97,65},{2,98}... | collective-permute-start | bytes 393224 | tf_op jit(solution)/shard_map/ppermute | solution.py:473
  228.0 17.3 %collective-permute-start.12 = (bf16[2,288,128]{2,1,0:T(8,128)(2,1)}, bf16[2,288,128]{2,1,0:T(8,128)(2,1)S(1)}, u32[]{:S(2)}, u32[]{:S(2)}) collective-permute-start(bf16[2,288,128]{2,1,0:T(8,128)(2,1)} %get-tuple-element.91), channel_id=1, source_target_pairs={{0,8},{8,16},{16,24},{24,0},{1,9},{9,17},{17,25},{25,1},{2,10},{10... | collective-permute-start | bytes 442376 | tf_op jit(solution)/shard_map/ppermute | solution.py:473
  228.3 17.0 %collective-permute-start.14 = (bf16[2,288,128]{2,1,0:T(8,128)(2,1)}, bf16[2,288,128]{2,1,0:T(8,128)(2,1)}, u32[]{:S(2)}, u32[]{:S(2)}) collective-permute-start(bf16[2,288,128]{2,1,0:T(8,128)(2,1)} %get-tuple-element.92), channel_id=1, source_target_pairs={{0,24},{8,0},{16,8},{24,16},{1,25},{9,1},{17,9},{25,17},{2,26},{10... | collective-permute-start | bytes 442376 | tf_op jit(solution)/shard_map/ppermute | solution.py:473
  230.7 25.8 %all-to-all-start.4 = ((bf16[16,224,128]{2,1,0:T(8,128)(2,1)}), bf16[16,224,128]{2,1,0:T(8,128)(2,1)S(1)}, u32[]{:S(2)}, u32[]{:S(2)}) async-start(bf16[16,224,128]{2,1,0:T(8,128)(2,1)} %bitcast.33), calls=%async_computation.4 | async-start | bytes 1835008 | tf_op jit(solution)/shard_map/all_to_all | solution.py:560
  235.4 16.6 %collective-permute-start.17 = (bf16[4,256,128]{2,1,0:T(8,128)(2,1)S(1)}, bf16[4,256,128]{2,1,0:T(8,128)(2,1)S(1)}, u32[]{:S(2)}, u32[]{:S(2)}) collective-permute-start(bf16[4,256,128]{2,1,0:T(8,128)(2,1)S(1)} %get-tuple-element.93), channel_id=1, source_target_pairs={{0,32},{32,64},{64,96},{96,0},{1,33},{33,65},{65,97},{97,1},{2,34}... | collective-permute-start | bytes 786440 | tf_op jit(solution)/shard_map/ppermute | solution.py:473
  236.7 15.5 %collective-permute-start.19 = (bf16[4,256,128]{2,1,0:T(8,128)(2,1)S(1)}, bf16[4,256,128]{2,1,0:T(8,128)(2,1)S(1)}, u32[]{:S(2)}, u32[]{:S(2)}) collective-permute-start(bf16[4,256,128]{2,1,0:T(8,128)(2,1)S(1)} %get-tuple-element.94), channel_id=1, source_target_pairs={{0,96},{32,0},{64,32},{96,64},{1,97},{33,1},{65,33},{97,65},{2,98}... | collective-permute-start | bytes 786440 | tf_op jit(solution)/shard_map/ppermute | solution.py:473
  239.1 10.2 %collective-permute-start.21 = (f32[264,128]{1,0:T(8,128)S(1)}, f32[264,128]{1,0:T(8,128)S(1)}, u32[]{:S(2)}, u32[]{:S(2)}) collective-permute-start(f32[264,128]{1,0:T(8,128)S(1)} %add.143), channel_id=1, source_target_pairs={{0,1},{1,0},{2,3},{3,2},{4,5},{5,4},{6,7},{7,6},{8,9},{9,8},{10,11... | collective-permute-start | bytes 405512 | tf_op jit(solution)/shard_map/ppermute | solution.py:564
  246.3 10.0 %collective-permute-start.13 = (bf16[4,288,128]{2,1,0:T(8,128)(2,1)S(1)}, bf16[4,288,128]{2,1,0:T(8,128)(2,1)S(1)}, u32[]{:S(2)}, u32[]{:S(2)}) collective-permute-start(bf16[4,288,128]{2,1,0:T(8,128)(2,1)S(1)} %get-tuple-element.89), channel_id=1, source_target_pairs={{0,8},{8,16},{16,24},{24,0},{1,9},{9,17},{17,25},{25,1},{2,10},{10... | collective-permute-start | bytes 884744 | tf_op jit(solution)/shard_map/ppermute | solution.py:473
  247.9 8.5 %collective-permute-start.15 = (bf16[4,288,128]{2,1,0:T(8,128)(2,1)S(1)}, bf16[4,288,128]{2,1,0:T(8,128)(2,1)S(1)}, u32[]{:S(2)}, u32[]{:S(2)}) collective-permute-start(bf16[4,288,128]{2,1,0:T(8,128)(2,1)S(1)} %get-tuple-element.90), channel_id=1, source_target_pairs={{0,24},{8,0},{16,8},{24,16},{1,25},{9,1},{17,9},{25,17},{2,26},{10... | collective-permute-start | bytes 884744 | tf_op jit(solution)/shard_map/ppermute | solution.py:473
  253.1 3.6 %copy-start.5 = (bf16[4,256,128]{2,1,0:T(8,128)(2,1)S(1)}, bf16[4,256,128]{2,1,0:T(8,128)(2,1)}, u32[]{:S(2)}) copy-start(bf16[4,256,128]{2,1,0:T(8,128)(2,1)} %fusion.15) | copy-start | bytes 786436
  257.1 24.4 %copy-start.8 = (s32[8,256]{1,0:T(8,128)S(1)}, s32[8,256]{1,0:T(8,128)}, u32[]{:S(2)}) copy-start(s32[8,256]{1,0:T(8,128)} %param.16) | copy-start | bytes 24580
  279.5 5.7 %collective-permute-start.22 = (bf16[2,768,128]{2,1,0:T(8,128)(2,1)S(1)}, bf16[2,768,128]{2,1,0:T(8,128)(2,1)S(1)}, u32[]{:S(2)}, u32[]{:S(2)}) collective-permute-start(bf16[2,768,128]{2,1,0:T(8,128)(2,1)S(1)} %reduce_sum.58), channel_id=1, source_target_pairs={{0,1},{1,0},{2,3},{3,2},{4,5},{5,4},{6,7},{7,6},{8,9},{9,8},{10,11... | collective-permute-start | bytes 1179656 | tf_op jit(solution)/shard_map/ppermute | solution.py:581

commit v6 on v5

--- a/solution.py
+++ b/solution.py
@@ -330,7 +330,7 @@
     )(at, x3, s, dl, dfm, wt)
 
 
-def sums_kernel(at_ref, mine_ref, other_ref, ids_ref, oid_ref, a_ref, b_ref, c_ref):
+def sums_kernel(at_ref, mine_ref, other_ref, ids_ref, oid_ref, a_ref, b_ref, c_ref, af_ref, ab_ref, bf_ref, bb_ref):
     nx = b_ref.shape[0]
     ny = c_ref.shape[0]
     _, steps, height, _ = mine_ref.shape
@@ -366,15 +366,30 @@
                 tail = jnp.where(low, tail[:count], tail[count:]).astype(BF16)
                 if t == 0:
                     a_ref[0, ahead, y, :256, :] = main
-                    a_ref[0, ahead, y, 256:, :] = tail[:32]
-                    b_ref[ahead, 0, y, :96, :] = tail[32:]
+                    a_ref[0, ahead, y, 256:, :] = tail[:48]
+                    b_ref[ahead, 0, y, :80, :] = tail[48:]
                 else:
-                    b_ref[ahead, 0, y, 96:, :] = main[:160]
-                    c_ref[y, 0, x, :96, :] = main[160:]
-                    c_ref[y, 0, x, 96:, :] = tail
+                    b_ref[ahead, 0, y, 80:, :] = main[:192]
+                    c_ref[y, 0, x, :64, :] = main[192:]
+                    c_ref[y, 0, x, 64:, :] = tail
         return 0
 
     lax.fori_loop(0, nx, column, 0)
+    nz = pl.num_programs(0)
+    ahead = lax.rem(pl.program_id(0) + nz - at_ref[0], nz)
+
+    @pl.when(ahead == 2)
+    def _():
+        af_ref[...] = a_ref[0, :2]
+        ab_ref[...] = a_ref[0, 2:]
+
+    @pl.when(ahead < 2)
+    def _():
+        bf_ref[ahead] = b_ref[2, 0]
+
+    @pl.when(ahead >= 2)
+    def _():
+        bb_ref[ahead - 2] = b_ref[2, 0]
 
 
 def sums(at, mine, other, ids, oids, nz=4, nx=4):
@@ -389,22 +404,24 @@
         in_specs=[data, data, index, index],
         out_specs=[
             pl.BlockSpec(
-                (1, nx, ny, 288, 128), lambda z, at: (lax.rem(z + nz - at[0], nz), 0, 0, 0, 0)
+                (1, nx, ny, 304, 128), lambda z, at: (lax.rem(z + nz - at[0], nz), 0, 0, 0, 0)
             ),
             pl.BlockSpec(
-                (nx, 1, ny, 256, 128), lambda z, at: (0, lax.rem(z + nz - at[0], nz), 0, 0, 0)
+                (nx, 1, ny, 272, 128), lambda z, at: (0, lax.rem(z + nz - at[0], nz), 0, 0, 0)
             ),
-            pl.BlockSpec((ny, 1, nx, 224, 128), lambda z, at: (0, z, 0, 0, 0)),
-        ],
+            pl.BlockSpec((ny, 1, nx, 192, 128), lambda z, at: (0, z, 0, 0, 0)),
+        ]
+        + [pl.BlockSpec((2, ny, h, 128), lambda z, at: (0, 0, 0, 0)) for h in (304, 304, 272, 272)],
     )
     return pl.pallas_call(
         sums_kernel,
         grid_spec=grid,
         out_shape=[
-            jax.ShapeDtypeStruct((nz, nx, ny, 288, 128), BF16),
-            jax.ShapeDtypeStruct((nx, nz, ny, 256, 128), BF16),
-            jax.ShapeDtypeStruct((ny, nz, nx, 224, 128), BF16),
-        ],
+            jax.ShapeDtypeStruct((nz, nx, ny, 304, 128), BF16),
+            jax.ShapeDtypeStruct((nx, nz, ny, 272, 128), BF16),
+            jax.ShapeDtypeStruct((ny, nz, nx, 192, 128), BF16),
+        ]
+        + [jax.ShapeDtypeStruct((2, ny, h, 128), BF16) for h in (304, 304, 272, 272)],
         compiler_params=params(),
         cost_estimate=cost(1e10, mine.size * 8),
         name="sums",
@@ -480,9 +497,11 @@
     return total.astype(BF16)
 
 
-def ring_sums(parts):
-    fore = [ring_step(axis, 1, v[2, :2]) for axis, v in parts]
-    back = [ring_step(axis, -1, v[2, 2:]) for axis, v in parts]
+def ring_sums(parts, sends=None):
+    if sends is None:
+        sends = [(v[2, :2], v[2, 2:]) for _, v in parts]
+    fore = [ring_step(axis, 1, f) for (axis, _), (f, _) in zip(parts, sends)]
+    back = [ring_step(axis, -1, b) for (axis, _), (_, b) in zip(parts, sends)]
     fore = [
         ring_step(axis, 1, add(v[1], jnp.pad(f, ((0, 2),) + ((0, 0),) * (f.ndim - 1))))
         for (axis, v), f in zip(parts, fore)
@@ -529,42 +548,34 @@
     g_out, g_in, g_gain, dfm = batch(
         core.reshape(1), xh, inv, gain_t, near, far, rows, out_grad
     )
-    w_grads = jnp.concatenate(
-        [
-            g_out.reshape(owners, -1, 128),
-            g_in,
-        ],
-        axis=1,
-    )
-    top, bottom = w_grads[:, :rows], w_grads[:, rows:]
-    theirs = lax.ppermute(jnp.where(core == 0, bottom, top), "c", SWAP)
-    w_grads = add(jnp.where(core == 0, top, bottom), theirs)
-    w_grads, dfm = lax.optimization_barrier((w_grads, dfm))
-    w_grads = lax.all_to_all(w_grads, WIDE, 0, 0, tiled=True)
+    g_out = g_out.reshape(owners, -1, 128)
+    w_first, dfm = lax.optimization_barrier((g_out, dfm))
+    w_first = lax.all_to_all(w_first, WIDE, 0, 0, tiled=True)
     keep, send, acc = last(spot, x3, score, dl, dfm, wt)
-    w_grads, send = lax.optimization_barrier((w_grads, send))
-    g_proj, g_lcb = acc[:K] + acc[K : 2 * K], acc[2 * K :]
-    little = jnp.concatenate([g_proj, g_gain, g_lcb], axis=0).T.reshape(owners, per, -1)
-    little = jnp.pad(little, ((0, 0), (0, 0), (0, 128 - little.shape[2])))
-    little = lax.all_to_all(little, WIDE, 0, 0, tiled=True)
+    w_first, send = lax.optimization_barrier((w_first, send))
+    little = jnp.concatenate([acc[:K] + acc[K : 2 * K], g_gain, acc[2 * K :]], axis=0)
+    little = jnp.pad(little.T, ((0, 0), (0, 128 - little.shape[0]))).reshape(owners, per, 128)
+    w_second = jnp.concatenate([g_in, *split(little)], axis=1)
+    w_second = lax.all_to_all(w_second, WIDE, 0, 0, tiled=True)
 
     other = lax.ppermute(send, "c", SWAP)
     at = jnp.stack([lax.axis_index("z"), lax.axis_index("x")]).astype(jnp.int32)
-    a, b, c = sums(at, keep, other, ids[0], other_ids)
-    a, b, c, little = lax.optimization_barrier((a, b, c, little))
+    a, b, c, af, ab, bf, bb = sums(at, keep, other, ids[0], other_ids)
+    c, w_second = lax.optimization_barrier((c, w_second))
+    a, b = ring_sums([("z", a), ("x", b)], [(af, ab), (bf, bb)])
     c = lax.all_to_all(c, ("yl", "yh"), 0, 0, tiled=True)
-    a, b = ring_sums([("z", a), ("x", b)])
     c = jnp.sum(c.astype(F32), axis=0).astype(BF16)
-    mixed = jnp.concatenate([jnp.sum(w_grads.astype(F32), axis=0), jnp.sum(little, axis=0)], axis=0)
+    mixed = jnp.concatenate(
+        [jnp.sum(v.astype(F32), axis=0) for v in (w_first, w_second)], axis=0
+    )
+    mixed = jnp.concatenate([mixed[: 2 * rows], mixed[2 * rows : -per] + mixed[-per:]], axis=0)
     a, b, c, mixed = lax.optimization_barrier((a, b, c, mixed))
     c = lax.all_to_all(c.reshape((16,) + c.shape[2:]), ("z", "x"), 0, 0, tiled=True)
     a, b = ring_sums([("x", a), ("z", b)])
     c = jnp.sum(c.astype(F32), axis=0).astype(BF16)
     mixed = mixed + lax.ppermute(mixed, "yh", SWAP)
-    swapped = lax.ppermute(mixed, "c", SWAP)
-    little = (mixed[rows:] + swapped[rows:])[:, : 2 * K + nl]
-    low, high = jnp.where(core == 0, mixed, swapped), jnp.where(core == 0, swapped, mixed)
-    big = jnp.concatenate([low[:rows], high[:rows]], axis=0)
+    mixed = mixed + lax.ppermute(mixed, "c", SWAP)
+    little, big = mixed[2 * rows :, : 2 * K + nl], mixed[: 2 * rows]
     a, b, c, big, little = lax.optimization_barrier((a, b, c, big, little))
     ab = jnp.concatenate([a, b], axis=1)
     ab = ab.reshape((2, 1, 2) + ab.shape[1:])

time: 294 us -> 285 us (0.969)
  waiting for transfers between devices: 47.1 us -> 39 us
  local copies, waits for them, and re-layouts: 16.1 us -> 12.7 us
    ppermute x16, waiting for transfers between devices: 36.5 us -> 27.8 us  [ring_step(): return lax.ppermute(v, axis, [(i, (i + by) % n) for i in range(n)])]
    all_to_all x2, waiting for transfers between devices: 0.01 us -> 4.47 us  [the longest x1 4.47 us: body(): w_first = lax.all_to_all(w_first, WIDE, 0, 0, tiled=True)]
    ppermute x2 -> x1, waiting for transfers between devices: 3.9 us -> 0.01 us  [body(): mixed = mixed + lax.ppermute(mixed, 'c', SWAP)]
    select_n x2 -> x0, other arithmetic: 3.12 us -> none  [the longest x1 3.09 us: body(): theirs = lax.ppermute(jnp.where(core == 0, bottom, top), 'c', SWAP)]
    convert_element_type x9 -> x8, other arithmetic: 13 us -> 14 us  [add(): return total.astype(BF16)]
    ppermute x2 -> x1, starting transfers between devices: 6.61 us -> 6.69 us  [body(): mixed = mixed + lax.ppermute(mixed, 'c', SWAP)]
  transfers between devices with their start and end apart: 28 -> 27, of which waited for: 10 -> 8; matrix products, arithmetic and copies ran while one was open for 10% -> 11% of each run, Pallas kernels for 32% -> 34%
where the time goes in v6:
time: 285 us; the launch traced here: 283 us
  Pallas kernels  115 us (40%)
  starting transfers between devices  65.5 us (23%)
  waiting for transfers between devices  39 us (14%)
  other arithmetic  30.1 us (11%)
  blocking collectives  19.9 us (7%)
  local copies, waits for them, and re-layouts  12.7 us (4%)
    pallas_call x1, Pallas kernels, last(): pl.pallas_call(last_kernel, grid_spec=grid, out_shape=[half, half, jax.Sh...  38.6 us
    ppermute x16, waiting for transfers between devices, ring_step(): return lax.ppermute(v, axis, [(i, (i + by) % n) for i in range(n)])  27.8 us
    pallas_call x2, Pallas kernels, unfold(): pl.pallas_call(unfold_kernel, grid=(count // rows,), in_specs=[pl.BlockSp...  24 us
    ppermute x16, starting transfers between devices, ring_step(): return lax.ppermute(v, axis, [(i, (i + by) % n) for i in range(n)])  21.3 us
    all_to_all x1, blocking collectives, body(): both = lax.all_to_all(both, ('yl', 'yh'), 0, 0, tiled=True)  19.9 us
    pallas_call x1, Pallas kernels, first(): pl.pallas_call(first_kernel, grid=(count // rows,), in_specs=[pl.BlockSpe...  17.5 us
    pallas_call x1, Pallas kernels, sums(): pl.pallas_call(sums_kernel, grid_spec=grid, out_shape=[jax.ShapeDtypeStru...  14.7 us
    convert_element_type x8, other arithmetic, add(): return total.astype(BF16)  14 us
  transfers between devices with their start and end apart: 27, of which 8 were waited for; matrix products, arithmetic and copies ran while one was open for 11% of the time, Pallas kernels for 34%

profile of v6, /device:TPU:1, one launch (start us, length us, event | category | flops | bytes accessed | tf_op | source)
XLA Modules:
  0.0 283.1 jit_solution(8589153938766167806)
XLA Ops:
  3.0 1.7 broadcast_in_dim.52
  4.7 9.7 %all-to-all-start = ((bf16[32,272,128]{2,1,0:T(8,128)(2,1)}), bf16[32,272,128]{2,1,0:T(8,128)(2,1)S(1)}, u32[]{:S(2)}, u32[]{:S(2)}) async-start(bf16[32,272,128]{2,1,0:T(8,128)(2,1)} %broadcast_in_dim.52), calls=%async_computation | async-start | bytes 4456448 | tf_op jit(solution)/shard_map/all_to_all | solution.py:485
  14.5 17.7 %unfold.2.x_ref = bf16[128,256,256]{2,1,0:T(8,128)(2,1)} custom-call(bf16[128,49152]{1,0:T(8,128)(2,1)} %x_ref.2), custom_call_target="tpu_custom_call" | custom-call | flops 1000000000 | bytes 29491200 | tf_op jit(solution)/shard_map/unfold/pallas_call | solution.py:67
  32.2 6.3 %unfold.3.g_ref = bf16[128,64,256]{2,1,0:T(8,128)(2,1)} custom-call(bf16[128,24576]{1,0:T(8,128)(2,1)} %g_ref.1), custom_call_target="tpu_custom_call" | custom-call | flops 1000000000 | bytes 7372800 | tf_op jit(solution)/shard_map/unfold/pallas_call | solution.py:67
  38.5 6.7 %all-to-all-done.nraw_ref.near_ref = bf16[32,272,128]{2,1,0:T(8,128)(2,1)S(1)} async-done(((bf16[32,272,128]{2,1,0:T(8,128)(2,1)}), bf16[32,272,128]{2,1,0:T(8,128)(2,1)S(1)}, u32[]{:S(2)}, u32[]{:S(2)}) %all-to-all-start) | async-done | bytes 2228256 | tf_op jit(solution)/shard_map/all_to_all | solution.py:485
  45.1 2.1 collective-permute-start
  48.9 17.5 %first.1 = (bf16[128,32,256]{2,1,0:T(8,128)(2,1)}, bf16[128,64,256]{2,1,0:T(8,128)(2,1)}, f32[16,128,256]{2,1,0:T(8,128)}, f32[128,128]{1,0:T(8,128)}) custom-call(bf16[128,256,256]{2,1,0:T(8,128)(2,1)} %unfold.2.x_ref, bf16[128,64,256]{2,1,0:T(8,128)(2,1)} %unfold.3.g_ref, bf16[80,256]{1,0:T(8,128)(2,1)} %pad_maximum_fusion.4.w_ref.wt_ref), custom_call_target="tpu_custom_call" | custom-call | flops 20000000000 | bytes 16777216 | tf_op jit(solution)/shard_map/first/pallas_call | solution.py:116
  66.5 14.0 %batch.1 = (bf16[12288,128]{1,0:T(8,128)(2,1)}, bf16[32,128,128]{2,1,0:T(8,128)(2,1)}, f32[16,256]{1,0:T(8,128)}, f32[16,128,256]{2,1,0:T(8,128)}) custom-call(s32[1]{0:T(128)} %bitcast.5.core_ref, f32[16,128,256]{2,1,0:T(8,128)} %get-tuple-element.50.xh_ref, f32[128,128]{1,0:T(8,128)} %get-tuple-element.51.inv_ref, f32[16,256]{1,0:T(8,128)} %convert_bitcast_fusion.gain_ref, ...), custom_call_target="tpu_custom_call" | custom-call | flops 20000000000 | bytes 20000000 | tf_op jit(solution)/shard_map/batch/pallas_call | solution.py:218
  80.4 4.1 %all-to-all-start.1 = ((bf16[32,384,128]{2,1,0:T(8,128)(2,1)}), bf16[32,384,128]{2,1,0:T(8,128)(2,1)S(1)}, u32[]{:S(2)}, u32[]{:S(2)}) async-start(bf16[32,384,128]{2,1,0:T(8,128)(2,1)} %bitcast.81), calls=%async_computation.1 | async-start | bytes 6291456 | tf_op jit(solution)/shard_map/all_to_all | solution.py:553
  85.1 38.6 %last.1 = (bf16[128,4,48,128]{3,2,1,0:T(8,128)(2,1)}, bf16[128,4,48,128]{3,2,1,0:T(8,128)(2,1)}, f32[96,256]{1,0:T(8,128)}) custom-call(s32[256]{0:T(256)} %get-tuple-element.84.at_ref, bf16[128,256,256]{2,1,0:T(8,128)(2,1)} %unfold.2.x_ref, bf16[128,32,256]{2,1,0:T(8,128)(2,1)} %get-tuple-element.48.s_ref, bf16[128,64,256]{2,1,0:T(8,128)(2,1)} %get-tuple-element.49.dl_ref, ...), custom_call_target="tpu_custom_call" | custom-call | flops 20000000000 | bytes 33554432 | tf_op jit(solution)/shard_map/last/pallas_call | solution.py:323
  123.8 4.5 %all-to-all-done.1 = bf16[32,384,128]{2,1,0:T(8,128)(2,1)S(1)} async-done(((bf16[32,384,128]{2,1,0:T(8,128)(2,1)}), bf16[32,384,128]{2,1,0:T(8,128)(2,1)S(1)}, u32[]{:S(2)}, u32[]{:S(2)}) %all-to-all-start.1) | async-done | bytes 3145760 | tf_op jit(solution)/shard_map/all_to_all | solution.py:553
  129.4 1.4 scatter_custom_fusion
  134.6 2.4 pad_maximum_fusion.1
  137.0 5.7 %all-to-all-start.2 = ((bf16[32,144,128]{2,1,0:T(8,128)(2,1)}), bf16[32,144,128]{2,1,0:T(8,128)(2,1)}, u32[]{:S(2)}, u32[]{:S(2)}) async-start(bf16[32,144,128]{2,1,0:T(8,128)(2,1)} %pad_maximum_fusion.1), calls=%async_computation.2 | async-start | bytes 2359296 | tf_op jit(solution)/shard_map/all_to_all | solution.py:559
  143.3 14.7 %sums.1 = (bf16[4,4,4,304,128]{4,3,2,1,0:T(8,128)(2,1)}, bf16[4,4,4,272,128]{4,3,2,1,0:T(8,128)(2,1)}, bf16[4,4,4,192,128]{4,3,2,1,0:T(8,128)(2,1)}, bf16[2,4,30...) custom-call(s32[2]{0:T(128)} %pad_add_fusion.at_ref, ...), custom_call_target="tpu_custom_call" | custom-call | flops 10000000000 | bytes 25165824 | tf_op jit(solution)/shard_map/sums/pallas_call | solution.py:416
  158.0 1.2 collective-permute-start.7
  159.2 1.5 collective-permute-start.9
  160.7 1.2 collective-permute-start.3
  162.0 1.5 collective-permute-start.5
  163.4 4.6 %all-to-all-start.3 = ((bf16[4,4,4,192,128]{4,3,2,1,0:T(8,128)(2,1)}), bf16[4,4,4,192,128]{4,3,2,1,0:T(8,128)(2,1)}, u32[]{:S(2)}, u32[]{:S(2)}) async-start(bf16[4,4,4,192,128]{4,3,2,1,0:T(8,128)(2,1)} %get-tuple-element.69), calls=%async_computation.3 | async-start | bytes 6291456 | tf_op jit(solution)/shard_map/all_to_all | solution.py:566
  168.1 4.9 %collective-permute-done.7 = bf16[2,4,272,128]{3,2,1,0:T(8,128)(2,1)} collective-permute-done((bf16[2,4,272,128]{3,2,1,0:T(8,128)(2,1)}, bf16[2,4,272,128]{3,2,1,0:T(8,128)(2,1)}, u32[]{:S(2)}, u32[]{:S(2)}) %collective-permute-start.7) | collective-permute-done | bytes 557088 | tf_op jit(solution)/shard_map/ppermute | solution.py:490
  173.0 3.7 %fusion.5 = (bf16[4,4,272,128]{3,2,1,0:T(8,128)(2,1)}, bf16[4,4,272,128]{3,2,1,0:T(8,128)(2,1)}) fusion(bf16[2,4,272,128]{3,2,1,0:T(8,128)(2,1)} %collective-permute-done.7, bf16[4,4,4,272,128]{4,3,2,1,0:T(8,128)(2,1)} %get-tuple-element.62, bf16[2,4,272,128]{3,2,1,0:T(8,128)(2,1)} %collective-permute-done.9), kind=kLoop, calls=%fused_computation.14 | loop fusion | flops 4456448 | bytes 5570560 | tf_op jit(solution)/shard_map/convert_element_type | solution.py:497
  176.6 2.4 collective-permute-start.10
  179.0 3.1 %fusion.1 = (bf16[4,4,304,128]{3,2,1,0:T(8,128)(2,1)}, bf16[4,4,304,128]{3,2,1,0:T(8,128)(2,1)}) fusion(bf16[2,4,304,128]{3,2,1,0:T(8,128)(2,1)} %collective-permute-done.3, bf16[4,4,4,304,128]{4,3,2,1,0:T(8,128)(2,1)S(1)} %copy-done, bf16[2,4,304,128]{3,2,1,0:T(8,128)(2,1)} %collective-permute-done.5), kind=kLoop, calls=%fused_computation.6 | loop fusion | flops 4980736 | bytes 6225920 | tf_op jit(solution)/shard_map/convert_element_type | solution.py:497
  183.0 1.7 collective-permute-start.6
  185.7 1.4 convert_reduce_fusion.1
  187.2 14.2 %collective-permute-done.10 = bf16[4,4,272,128]{3,2,1,0:T(8,128)(2,1)} collective-permute-done((bf16[4,4,272,128]{3,2,1,0:T(8,128)(2,1)}, bf16[4,4,272,128]{3,2,1,0:T(8,128)(2,1)}, u32[]{:S(2)}, u32[]{:S(2)}) %collective-permute-start.10) | collective-permute-done | bytes 1114144 | tf_op jit(solution)/shard_map/ppermute | solution.py:490
  201.3 3.0 %collective-permute-done.8 = bf16[4,4,272,128]{3,2,1,0:T(8,128)(2,1)} collective-permute-done((bf16[4,4,272,128]{3,2,1,0:T(8,128)(2,1)}, bf16[4,4,272,128]{3,2,1,0:T(8,128)(2,1)}, u32[]{:S(2)}, u32[]{:S(2)}) %collective-permute-start.8) | collective-permute-done | bytes 1114144 | tf_op jit(solution)/shard_map/ppermute | solution.py:490
  204.3 2.4 fusion.7
  206.7 3.5 %collective-permute-done.4 = bf16[4,4,304,128]{3,2,1,0:T(8,128)(2,1)} collective-permute-done((bf16[4,4,304,128]{3,2,1,0:T(8,128)(2,1)}, bf16[4,4,304,128]{3,2,1,0:T(8,128)(2,1)}, u32[]{:S(2)}, u32[]{:S(2)}) %collective-permute-start.4) | collective-permute-done | bytes 1245216 | tf_op jit(solution)/shard_map/ppermute | solution.py:490
  210.2 2.5 fusion.3
  212.7 3.6 %reduce_sum.54 = bf16[4,4,192,128]{3,2,1,0:T(8,128)(2,1)} reduce(bf16[4,4,4,192,128]{4,3,2,1,0:T(8,128)(2,1)} %all-to-all-done.3, bf16[]{:T(256)} %constant.93.clone.1), dimensions={0}, to_apply=%region_1.2 | reduce | flops 1179648 | bytes 3932162 | tf_op jit(solution)/shard_map/reduce_sum | solution.py:567
  216.3 2.6 collective-permute-start.19
  220.0 2.3 collective-permute-start.17
  223.0 2.7 collective-permute-start.13
  225.7 3.6 %all-to-all-start.4 = ((bf16[16,192,128]{2,1,0:T(8,128)(2,1)}), bf16[16,192,128]{2,1,0:T(8,128)(2,1)S(1)}, u32[]{:S(2)}, u32[]{:S(2)}) async-start(bf16[16,192,128]{2,1,0:T(8,128)(2,1)} %bitcast.82), calls=%async_computation.4 | async-start | bytes 1572864 | tf_op jit(solution)/shard_map/all_to_all | solution.py:573
  229.3 1.1 fusion.13
  230.4 1.3 collective-permute-start.16
  231.7 1.4 collective-permute-start.18
  233.2 1.1 fusion.9
  234.2 1.3 collective-permute-start.12
  235.5 1.4 collective-permute-start.14
  238.0 6.7 %collective-permute-start.20 = (f32[520,128]{1,0:T(8,128)S(1)}, f32[520,128]{1,0:T(8,128)S(1)}, u32[]{:S(2)}, u32[]{:S(2)}) collective-permute-start(f32[520,128]{1,0:T(8,128)S(1)} %add.143), channel_id=1, source_target_pairs={{0,1},{1,0},{2,3},{3,2},{4,5},{5,4},{6,7},{7,6},{8,9},{9,8},{10,11... | collective-permute-start | bytes 798728 | tf_op jit(solution)/shard_map/ppermute | solution.py:577
  244.7 1.1 collective-permute-done.18
  245.9 1.2 collective-permute-done.12
  247.9 19.9 %all_to_all.30 = bf16[4,2,768,128]{3,2,1,0:T(8,128)(2,1)S(1)} all-to-all(bf16[4,2,768,128]{3,2,1,0:T(8,128)(2,1)S(1)} %bitcast.80), channel_id=1, replica_groups=mesh['z'=4,'x'=4,'yl'=2,'yh'=2,'c'=2] {'yl','yh'}, dimensions={0} | all-to-all | bytes 3145728 | tf_op jit(solution)/shard_map/all_to_all | solution.py:590
  268.3 4.0 %collective-permute-start.21 = (bf16[2,768,128]{2,1,0:T(8,128)(2,1)S(1)}, bf16[2,768,128]{2,1,0:T(8,128)(2,1)S(1)}, u32[]{:S(2)}, u32[]{:S(2)}) collective-permute-start(bf16[2,768,128]{2,1,0:T(8,128)(2,1)S(1)} %reduce_sum.58), channel_id=1, source_target_pairs={{0,1},{1,0},{2,3},{3,2},{4,5},{5,4},{6,7},{7,6},{8,9},{9,8},{10,11... | collective-permute-start | bytes 1179656 | tf_op jit(solution)/shard_map/ppermute | solution.py:592
  277.1 6.0 %update.1 = (f32[192,2048]{1,0:T(8,128)}, f32[1,2048]{1,0:T(1,128)}) custom-call(s32[1,2048]{1,0:T(1,128)} %bitcast.91, bf16[2,2,768,128]{3,2,1,0:T(8,128)(2,1)} %maximum_select_fusion.sum_ref, f32[192,2048]{1,0:T(8,128)} %bitcast.92, f32[1,2048]{1,0:T(1,128)} %bitcast.93), custom_call_target="tpu_custom_call" | custom-call | flops 4000000000 | bytes 4718592 | tf_op jit(solution)/shard_map/update/pallas_call | solution.py:461
  (96 shorter events, 21.1 us)
Async XLA Ops:
  4.7 40.4 %all-to-all-start = ((bf16[32,272,128]{2,1,0:T(8,128)(2,1)}), bf16[32,272,128]{2,1,0:T(8,128)(2,1)S(1)}, u32[]{:S(2)}, u32[]{:S(2)}) async-start(bf16[32,272,128]{2,1,0:T(8,128)(2,1)} %broadcast_in_dim.52), calls=%async_computation | async-start | bytes 4456448 | tf_op jit(solution)/shard_map/all_to_all | solution.py:485
  45.1 21.3 %copy-start.1 = (bf16[32,272,128]{2,1,0:T(8,128)(2,1)}, bf16[32,272,128]{2,1,0:T(8,128)(2,1)S(1)}, u32[]{:S(2)}) copy-start(bf16[32,272,128]{2,1,0:T(8,128)(2,1)S(1)} %all-to-all-done.nraw_ref.near_ref) | copy-start | bytes 6684676
  45.1 21.3 %collective-permute-start = (bf16[32,272,128]{2,1,0:T(8,128)(2,1)S(1)}, bf16[32,272,128]{2,1,0:T(8,128)(2,1)}, u32[]{:S(2)}, u32[]{:S(2)}) collective-permute-start(bf16[32,272,128]{2,1,0:T(8,128)(2,1)S(1)} %all-to-all-done.nraw_ref.near_ref), channel_id=1, source_target_pairs={{0,1},{1,0},{2,3},{3,2},{4,5},{5,4},{6,7},{7,6},{8,9},{9,8},{10,11... | collective-permute-start | bytes 6684680 | tf_op jit(solution)/shard_map/ppermute | solution.py:538
  80.4 4.1 %copy-start.5 = (s32[256]{0:T(256)S(1)}, s32[256]{0:T(256)}, u32[]{:S(2)}) copy-start(s32[256]{0:T(256)} %param.15) | copy-start | bytes 3076
  80.4 47.8 %all-to-all-start.1 = ((bf16[32,384,128]{2,1,0:T(8,128)(2,1)}), bf16[32,384,128]{2,1,0:T(8,128)(2,1)S(1)}, u32[]{:S(2)}, u32[]{:S(2)}) async-start(bf16[32,384,128]{2,1,0:T(8,128)(2,1)} %bitcast.81), calls=%async_computation.1 | async-start | bytes 6291456 | tf_op jit(solution)/shard_map/all_to_all | solution.py:553
  85.1 44.1 %copy-start.2 = (s32[128,256]{1,0:T(8,128)S(1)}, s32[128,256]{1,0:T(8,128)}, u32[]{:S(2)}) copy-start(s32[128,256]{1,0:T(8,128)} %param.14) | copy-start | bytes 393220
  123.8 10.7 %copy-start.3 = (f32[16,256]{1,0:T(8,128)S(1)}, f32[16,256]{1,0:T(8,128)}, u32[]{:S(2)}) copy-start(f32[16,256]{1,0:T(8,128)} %get-tuple-element.68) | copy-start | bytes 49156
  128.2 14.4 %collective-permute-start.1 = (bf16[128,4,48,128]{3,2,1,0:T(8,128)(2,1)}, bf16[128,4,48,128]{3,2,1,0:T(8,128)(2,1)}, u32[]{:S(2)}, u32[]{:S(2)}) collective-permute-start(bf16[128,4,48,128]{3,2,1,0:T(8,128)(2,1)} %get-tuple-element.58), channel_id=1, source_target_pairs={{0,1},{1,0},{2,3},{3,2},{4,5},{5,4},{6,7},{7,6},{8,9},{9,8},{10,11... | collective-permute-start | bytes 18874376 | tf_op jit(solution)/shard_map/ppermute | solution.py:561
  132.3 10.4 %collective-permute-start.2 = (s32[64,2,128]{2,1,0:T(2,128)S(1)}, s32[64,2,128]{2,1,0:T(2,128)S(1)}, u32[]{:S(2)}, u32[]{:S(2)}) collective-permute-start(s32[64,2,128]{2,1,0:T(2,128)S(1)} %bitcast.88), channel_id=1, source_target_pairs={{0,1},{1,0},{2,3},{3,2},{4,5},{5,4},{6,7},{7,6},{8,9},{9,8},{10,11... | collective-permute-start | bytes 196616 | tf_op jit(solution)/shard_map/ppermute | solution.py:545
  137.0 26.5 %all-to-all-start.2 = ((bf16[32,144,128]{2,1,0:T(8,128)(2,1)}), bf16[32,144,128]{2,1,0:T(8,128)(2,1)}, u32[]{:S(2)}, u32[]{:S(2)}) async-start(bf16[32,144,128]{2,1,0:T(8,128)(2,1)} %pad_maximum_fusion.1), calls=%async_computation.2 | async-start | bytes 2359296 | tf_op jit(solution)/shard_map/all_to_all | solution.py:559
  142.7 0.6 copy-start.7
  158.0 15.0 %collective-permute-start.7 = (bf16[2,4,272,128]{3,2,1,0:T(8,128)(2,1)}, bf16[2,4,272,128]{3,2,1,0:T(8,128)(2,1)}, u32[]{:S(2)}, u32[]{:S(2)}) collective-permute-start(bf16[2,4,272,128]{3,2,1,0:T(8,128)(2,1)} %get-tuple-element.63), channel_id=1, source_target_pairs={{0,8},{8,16},{16,24},{24,0},{1,9},{9,17},{17,25},{25,1},{2,10},{10... | collective-permute-start | bytes 1671176 | tf_op jit(solution)/shard_map/ppermute | solution.py:490
  159.2 13.7 %collective-permute-start.9 = (bf16[2,4,272,128]{3,2,1,0:T(8,128)(2,1)}, bf16[2,4,272,128]{3,2,1,0:T(8,128)(2,1)}, u32[]{:S(2)}, u32[]{:S(2)}) collective-permute-start(bf16[2,4,272,128]{3,2,1,0:T(8,128)(2,1)} %get-tuple-element.64), channel_id=1, source_target_pairs={{0,24},{8,0},{16,8},{24,16},{1,25},{9,1},{17,9},{25,17},{2,26},{10... | collective-permute-start | bytes 1671176 | tf_op jit(solution)/shard_map/ppermute | solution.py:490
  160.7 18.3 %collective-permute-start.3 = (bf16[2,4,304,128]{3,2,1,0:T(8,128)(2,1)}, bf16[2,4,304,128]{3,2,1,0:T(8,128)(2,1)}, u32[]{:S(2)}, u32[]{:S(2)}) collective-permute-start(bf16[2,4,304,128]{3,2,1,0:T(8,128)(2,1)} %get-tuple-element.60), channel_id=1, source_target_pairs={{0,32},{32,64},{64,96},{96,0},{1,33},{33,65},{65,97},{97,1},{2,34}... | collective-permute-start | bytes 1867784 | tf_op jit(solution)/shard_map/ppermute | solution.py:490
  162.0 17.1 %collective-permute-start.5 = (bf16[2,4,304,128]{3,2,1,0:T(8,128)(2,1)}, bf16[2,4,304,128]{3,2,1,0:T(8,128)(2,1)}, u32[]{:S(2)}, u32[]{:S(2)}) collective-permute-start(bf16[2,4,304,128]{3,2,1,0:T(8,128)(2,1)} %get-tuple-element.61), channel_id=1, source_target_pairs={{0,96},{32,0},{64,32},{96,64},{1,97},{33,1},{65,33},{97,65},{2,98}... | collective-permute-start | bytes 1867784 | tf_op jit(solution)/shard_map/ppermute | solution.py:490
  163.4 49.3 %all-to-all-start.3 = ((bf16[4,4,4,192,128]{4,3,2,1,0:T(8,128)(2,1)}), bf16[4,4,4,192,128]{4,3,2,1,0:T(8,128)(2,1)}, u32[]{:S(2)}, u32[]{:S(2)}) async-start(bf16[4,4,4,192,128]{4,3,2,1,0:T(8,128)(2,1)} %get-tuple-element.69), calls=%async_computation.3 | async-start | bytes 6291456 | tf_op jit(solution)/shard_map/all_to_all | solution.py:566
  173.0 6.1 %copy-start = (bf16[4,4,4,304,128]{4,3,2,1,0:T(8,128)(2,1)S(1)}, bf16[4,4,4,304,128]{4,3,2,1,0:T(8,128)(2,1)}, u32[]{:S(2)}) copy-start(bf16[4,4,4,304,128]{4,3,2,1,0:T(8,128)(2,1)} %get-tuple-element.59) | copy-start | bytes 14942212
  176.6 24.7 %collective-permute-start.10 = (bf16[4,4,272,128]{3,2,1,0:T(8,128)(2,1)}, bf16[4,4,272,128]{3,2,1,0:T(8,128)(2,1)}, u32[]{:S(2)}, u32[]{:S(2)}) collective-permute-start(bf16[4,4,272,128]{3,2,1,0:T(8,128)(2,1)} %get-tuple-element.88), channel_id=1, source_target_pairs={{0,24},{8,0},{16,8},{24,16},{1,25},{9,1},{17,9},{25,17},{2,26},{10... | collective-permute-start | bytes 3342344 | tf_op jit(solution)/shard_map/ppermute | solution.py:490
  179.0 25.3 %collective-permute-start.8 = (bf16[4,4,272,128]{3,2,1,0:T(8,128)(2,1)}, bf16[4,4,272,128]{3,2,1,0:T(8,128)(2,1)}, u32[]{:S(2)}, u32[]{:S(2)}) collective-permute-start(bf16[4,4,272,128]{3,2,1,0:T(8,128)(2,1)} %get-tuple-element.87), channel_id=1, source_target_pairs={{0,8},{8,16},{16,24},{24,0},{1,9},{9,17},{17,25},{25,1},{2,10},{10... | collective-permute-start | bytes 3342344 | tf_op jit(solution)/shard_map/ppermute | solution.py:490
  182.1 28.1 %collective-permute-start.4 = (bf16[4,4,304,128]{3,2,1,0:T(8,128)(2,1)}, bf16[4,4,304,128]{3,2,1,0:T(8,128)(2,1)}, u32[]{:S(2)}, u32[]{:S(2)}) collective-permute-start(bf16[4,4,304,128]{3,2,1,0:T(8,128)(2,1)} %get-tuple-element.85), channel_id=1, source_target_pairs={{0,32},{32,64},{64,96},{96,0},{1,33},{33,65},{65,97},{97,1},{2,34}... | collective-permute-start | bytes 3735560 | tf_op jit(solution)/shard_map/ppermute | solution.py:490
  183.0 27.2 %collective-permute-start.6 = (bf16[4,4,304,128]{3,2,1,0:T(8,128)(2,1)}, bf16[4,4,304,128]{3,2,1,0:T(8,128)(2,1)}, u32[]{:S(2)}, u32[]{:S(2)}) collective-permute-start(bf16[4,4,304,128]{3,2,1,0:T(8,128)(2,1)} %get-tuple-element.86), channel_id=1, source_target_pairs={{0,96},{32,0},{64,32},{96,64},{1,97},{33,1},{65,33},{97,65},{2,98}... | collective-permute-start | bytes 3735560 | tf_op jit(solution)/shard_map/ppermute | solution.py:490
  216.3 20.8 %collective-permute-start.19 = (f32[520,128]{1,0:T(8,128)S(1)}, f32[520,128]{1,0:T(8,128)}, u32[]{:S(2)}, u32[]{:S(2)}) collective-permute-start(f32[520,128]{1,0:T(8,128)S(1)} %fusion.16), channel_id=1, source_target_pairs={{0,2},{2,0},{1,3},{3,1},{4,6},{6,4},{5,7},{7,5},{8,10},{10,8},{9,1... | collective-permute-start | bytes 798728 | tf_op jit(solution)/shard_map/ppermute | solution.py:576
  219.6 9.7 %collective-permute-start.15 = (bf16[2,272,128]{2,1,0:T(8,128)(2,1)}, bf16[2,272,128]{2,1,0:T(8,128)(2,1)}, u32[]{:S(2)}, u32[]{:S(2)}) collective-permute-start(bf16[2,272,128]{2,1,0:T(8,128)(2,1)} %get-tuple-element.95), channel_id=1, source_target_pairs={{0,32},{32,64},{64,96},{96,0},{1,33},{33,65},{65,97},{97,1},{2,34}... | collective-permute-start | bytes 417800 | tf_op jit(solution)/shard_map/ppermute | solution.py:490
  220.0 9.3 %collective-permute-start.17 = (bf16[2,272,128]{2,1,0:T(8,128)(2,1)S(1)}, bf16[2,272,128]{2,1,0:T(8,128)(2,1)}, u32[]{:S(2)}, u32[]{:S(2)}) collective-permute-start(bf16[2,272,128]{2,1,0:T(8,128)(2,1)S(1)} %get-tuple-element.96), channel_id=1, source_target_pairs={{0,96},{32,0},{64,32},{96,64},{1,97},{33,1},{65,33},{97,65},{2,98}... | collective-permute-start | bytes 417800 | tf_op jit(solution)/shard_map/ppermute | solution.py:490
  223.0 10.1 %collective-permute-start.11 = (bf16[2,304,128]{2,1,0:T(8,128)(2,1)}, bf16[2,304,128]{2,1,0:T(8,128)(2,1)}, u32[]{:S(2)}, u32[]{:S(2)}) collective-permute-start(bf16[2,304,128]{2,1,0:T(8,128)(2,1)} %get-tuple-element.91), channel_id=1, source_target_pairs={{0,8},{8,16},{16,24},{24,0},{1,9},{9,17},{17,25},{25,1},{2,10},{10... | collective-permute-start | bytes 466952 | tf_op jit(solution)/shard_map/ppermute | solution.py:490
  223.0 10.1 %collective-permute-start.13 = (bf16[2,304,128]{2,1,0:T(8,128)(2,1)}, bf16[2,304,128]{2,1,0:T(8,128)(2,1)}, u32[]{:S(2)}, u32[]{:S(2)}) collective-permute-start(bf16[2,304,128]{2,1,0:T(8,128)(2,1)} %get-tuple-element.92), channel_id=1, source_target_pairs={{0,24},{8,0},{16,8},{24,16},{1,25},{9,1},{17,9},{25,17},{2,26},{10... | collective-permute-start | bytes 466952 | tf_op jit(solution)/shard_map/ppermute | solution.py:490
  225.7 21.6 %all-to-all-start.4 = ((bf16[16,192,128]{2,1,0:T(8,128)(2,1)}), bf16[16,192,128]{2,1,0:T(8,128)(2,1)S(1)}, u32[]{:S(2)}, u32[]{:S(2)}) async-start(bf16[16,192,128]{2,1,0:T(8,128)(2,1)} %bitcast.82), calls=%async_computation.4 | async-start | bytes 1572864 | tf_op jit(solution)/shard_map/all_to_all | solution.py:573
  229.3 7.7 %copy-start.6 = (pred[2]{0:T(512)(128)(4,1)S(1)}, pred[2]{0:T(512)(128)(4,1)}, u32[]{:S(2)}) copy-start(pred[2]{0:T(512)(128)(4,1)} %get-tuple-element.104) | copy-start | bytes 10
  230.4 14.3 %collective-permute-start.16 = (bf16[4,272,128]{2,1,0:T(8,128)(2,1)S(1)}, bf16[4,272,128]{2,1,0:T(8,128)(2,1)S(1)}, u32[]{:S(2)}, u32[]{:S(2)}) collective-permute-start(bf16[4,272,128]{2,1,0:T(8,128)(2,1)S(1)} %get-tuple-element.93), channel_id=1, source_target_pairs={{0,32},{32,64},{64,96},{96,0},{1,33},{33,65},{65,97},{97,1},{2,34}... | collective-permute-start | bytes 835592 | tf_op jit(solution)/shard_map/ppermute | solution.py:490
  231.7 14.1 %collective-permute-start.18 = (bf16[4,272,128]{2,1,0:T(8,128)(2,1)S(1)}, bf16[4,272,128]{2,1,0:T(8,128)(2,1)S(1)}, u32[]{:S(2)}, u32[]{:S(2)}) collective-permute-start(bf16[4,272,128]{2,1,0:T(8,128)(2,1)S(1)} %get-tuple-element.94), channel_id=1, source_target_pairs={{0,96},{32,0},{64,32},{96,64},{1,97},{33,1},{65,33},{97,65},{2,98}... | collective-permute-start | bytes 835592 | tf_op jit(solution)/shard_map/ppermute | solution.py:490
  234.2 12.9 %collective-permute-start.12 = (bf16[4,304,128]{2,1,0:T(8,128)(2,1)S(1)}, bf16[4,304,128]{2,1,0:T(8,128)(2,1)S(1)}, u32[]{:S(2)}, u32[]{:S(2)}) collective-permute-start(bf16[4,304,128]{2,1,0:T(8,128)(2,1)S(1)} %get-tuple-element.89), channel_id=1, source_target_pairs={{0,8},{8,16},{16,24},{24,0},{1,9},{9,17},{17,25},{25,1},{2,10},{10... | collective-permute-start | bytes 933896 | tf_op jit(solution)/shard_map/ppermute | solution.py:490
  235.5 11.6 %collective-permute-start.14 = (bf16[4,304,128]{2,1,0:T(8,128)(2,1)S(1)}, bf16[4,304,128]{2,1,0:T(8,128)(2,1)S(1)}, u32[]{:S(2)}, u32[]{:S(2)}) collective-permute-start(bf16[4,304,128]{2,1,0:T(8,128)(2,1)S(1)} %get-tuple-element.90), channel_id=1, source_target_pairs={{0,24},{8,0},{16,8},{24,16},{1,25},{9,1},{17,9},{25,17},{2,26},{10... | collective-permute-start | bytes 933896 | tf_op jit(solution)/shard_map/ppermute | solution.py:490
  238.0 9.2 %collective-permute-start.20 = (f32[520,128]{1,0:T(8,128)S(1)}, f32[520,128]{1,0:T(8,128)S(1)}, u32[]{:S(2)}, u32[]{:S(2)}) collective-permute-start(f32[520,128]{1,0:T(8,128)S(1)} %add.143), channel_id=1, source_target_pairs={{0,1},{1,0},{2,3},{3,2},{4,5},{5,4},{6,7},{7,6},{8,9},{9,8},{10,11... | collective-permute-start | bytes 798728 | tf_op jit(solution)/shard_map/ppermute | solution.py:577
  247.9 24.4 %copy-start.4 = (s32[8,256]{1,0:T(8,128)S(1)}, s32[8,256]{1,0:T(8,128)}, u32[]{:S(2)}) copy-start(s32[8,256]{1,0:T(8,128)} %param.16) | copy-start | bytes 24580
  268.3 7.8 %collective-permute-start.21 = (bf16[2,768,128]{2,1,0:T(8,128)(2,1)S(1)}, bf16[2,768,128]{2,1,0:T(8,128)(2,1)S(1)}, u32[]{:S(2)}, u32[]{:S(2)}) collective-permute-start(bf16[2,768,128]{2,1,0:T(8,128)(2,1)S(1)} %reduce_sum.58), channel_id=1, source_target_pairs={{0,1},{1,0},{2,3},{3,2},{4,5},{5,4},{6,7},{7,6},{8,9},{9,8},{10,11... | collective-permute-start | bytes 1179656 | tf_op jit(solution)/shard_map/ppermute | solution.py:592

commit v7 on v6

--- a/solution.py
+++ b/solution.py
@@ -76,31 +76,37 @@
     )(x)
 
 
-def first_kernel(x_ref, g_ref, w_ref, s_ref, dl_ref, xh_ref, inv_ref, lo, hi):
+def first_kernel(
+    x_ref, g_ref, w_ref, s_ref, dl_ref, xh_ref, inv_ref, lo, hi, lout, fm
+):
     rows = x_ref.shape[0]
     n = x_ref.shape[1]
     w = w_ref[...]
     lane = lax.broadcasted_iota(jnp.int32, (1, DP), 1)
     half = (pl.program_id(0) * rows // 16) % 2
     keep = (lane < 128) | ((lane >= 128 + 64 * half) & (lane < 192 + 64 * half))
-    total = lambda v: jnp.sum(jnp.sum(v, axis=0, keepdims=True), axis=1, keepdims=True)
+    total = lambda v: jnp.sum(jnp.sum(v, axis=1, keepdims=True), axis=2, keepdims=True)
     for b in range(rows):
-        xb = x_ref[b]
-        r = dot(w, xb)
+        r = dot(w, x_ref[b])
         shi, slo = split(r[:K])
         s_ref[b, :K, :] = shi
         s_ref[b, K:, :] = slo
-        f2 = dot(jnp.concatenate([shi, slo], axis=0), xb, NT)
-        fm = f2[:K] + f2[K:]
-        c = fm - total(fm) * (1.0 / (K * n))
-        inv = 1.0 / jnp.sqrt(total(c * c) * (1.0 / (K * n)) + EPS)
-        inv_ref[b : b + 1, :] = jnp.broadcast_to(inv, (1, 128))
-        xh = c * inv
-        lo[pl.ds(b, K, stride=rows), :] = xh[:, :128]
-        hi[pl.ds(b, K, stride=rows), :] = xh[:, 128:]
-        lout = r[K:]
+        lout[b] = r[K:]
+    for b in range(rows):
+        f2 = dot(s_ref[b], x_ref[b], NT)
+        fm[b] = f2[:K] + f2[K:]
+    v = fm[...]
+    c = v - total(v) * (1.0 / (K * n))
+    inv = 1.0 / jnp.sqrt(total(c * c) * (1.0 / (K * n)) + EPS)
+    inv_ref[...] = jnp.broadcast_to(inv.reshape(rows, 1), (rows, 128))
+    xh = c * inv
+    for b in range(rows):
+        lo[pl.ds(b, K, stride=rows), :] = xh[b, :, :128]
+        hi[pl.ds(b, K, stride=rows), :] = xh[b, :, 128:]
+    for b in range(rows):
+        lb = lout[b]
         grad = g_ref[b].astype(F32)
-        mid = jnp.where(keep, lout - jnp.sum(lout, axis=1, keepdims=True) * (1.0 / D), 0.0)
+        mid = jnp.where(keep, lb - jnp.sum(lb, axis=1, keepdims=True) * (1.0 / D), 0.0)
         oinv = 1.0 / jnp.sqrt(jnp.sum(mid * mid, axis=1, keepdims=True) * (1.0 / D) + EPS)
         chat = mid * oinv
         gm = jnp.sum(grad, axis=1, keepdims=True) * (1.0 / D)
@@ -133,7 +139,8 @@
             jax.ShapeDtypeStruct((K, count, n), F32),
             jax.ShapeDtypeStruct((count, 128), F32),
         ],
-        scratch_shapes=[pltpu.VMEM((K * rows, 128), F32)] * 2,
+        scratch_shapes=[pltpu.VMEM((K * rows, 128), F32)] * 2
+        + [pltpu.VMEM((rows, nl, DP), F32), pltpu.VMEM((rows, K, n), F32)],
         compiler_params=params(),
         cost_estimate=cost(2e10, count * n * DP * 2),
         name="first",
@@ -142,7 +149,7 @@
 
 def batch_kernel(
     core_ref, xh_ref, inv_ref, gain_ref, nraw_ref, fraw_ref, near_ref, far_ref, g_ref,
-    gout_ref, gin_ref, ggain_ref, dfm_ref, pre_s, hid_s, dhid_s, norm_s, e_s, win_ref, gin_s,
+    keep_ref, send_ref, ggain_ref, dfm_ref, pre_s, hid_s, dhid_s, norm_s, e_s, win_ref, gin_s,
 ):
     step = pl.program_id(0)
     count, n = xh_ref.shape[1], xh_ref.shape[2]
@@ -178,7 +185,16 @@
     gm = jnp.sum(grad, axis=1, keepdims=True) * (1.0 / D)
     gc = jnp.sum(grad * chat, axis=1, keepdims=True) * (1.0 / D)
     df = (oinv * (grad - gm - chat * gc)).reshape(rows, count).astype(BF16)
-    gout_ref[...] = dot(df, hid).astype(BF16)
+    gout = dot(df, hid).astype(BF16).reshape(near.shape[0], -1, 128)
+    at = pl.ds(pl.multiple_of(step * near.shape[0], near.shape[0]), near.shape[0])
+    cut = near.shape[1]
+
+    def store(top_ref, bottom_ref):
+        top_ref[at] = gout[:, :cut]
+        bottom_ref[at, : gout.shape[1] - cut] = gout[:, cut:]
+
+    pl.when(first_core)(lambda: store(keep_ref, send_ref))
+    pl.when(jnp.logical_not(first_core))(lambda: store(send_ref, keep_ref))
     dhid_s[...] += dot(w, df, TN)
 
     @pl.when(step == pl.num_programs(0) - 1)
@@ -202,9 +218,14 @@
         inv = inv_ref[:, :1]
         for k in range(K):
             dfm_ref[k] = inv * (e_s[k] - a1 - xh_ref[k] * a2)
-        for o in range(owners):
-            v = jnp.swapaxes(gin_s[:, o * per : (o + 1) * per, :], 0, 1)
-            gin_ref[o] = v.reshape(per * K, 128).astype(BF16)
+
+        def store_in(ref):
+            for o in range(owners):
+                v = jnp.swapaxes(gin_s[:, o * per : (o + 1) * per, :], 0, 1)
+                ref[o, -per * K :] = v.reshape(per * K, 128).astype(BF16)
+
+        pl.when(first_core)(lambda: store_in(send_ref))
+        pl.when(jnp.logical_not(first_core))(lambda: store_in(keep_ref))
 
 
 def batch(core, xh, inv, gain, near, far, half, out_grad, feats=16):
@@ -230,14 +251,14 @@
             pl.BlockSpec((count, rows), lambda i: (0, i)),
         ],
         out_specs=[
-            pl.BlockSpec((rows, 128), lambda i: (i, 0)),
-            whole((owners, per, 128)),
+            whole((owners, half, 128)),
+            whole((owners, half, 128)),
             whole((k, n)),
             whole((k, count, n)),
         ],
         out_shape=[
-            jax.ShapeDtypeStruct((total, 128), BF16),
-            jax.ShapeDtypeStruct((owners, per, 128), BF16),
+            jax.ShapeDtypeStruct((owners, half, 128), BF16),
+            jax.ShapeDtypeStruct((owners, half, 128), BF16),
             jax.ShapeDtypeStruct((k, n), F32),
             jax.ShapeDtypeStruct((k, count, n), F32),
         ],
@@ -257,7 +278,7 @@
 
 
 def last_kernel(
-    at_ref, x_ref, s_ref, dl_ref, dfm_ref, wt_ref, keep_ref, send_ref, acc_ref, flo, fhi, dx, both
+    at_ref, x_ref, s_ref, dl_ref, dfm_ref, wt_ref, keep_ref, send_ref, acc_ref, flo, fhi, dx, both, left, low
 ):
     rows, n = x_ref.shape[0], x_ref.shape[1]
 
@@ -270,21 +291,33 @@
     proj = wt_ref[:K, :]
     shared = wt_ref[...]
 
-    def sample(b, _):
+    def score_grad(b, _):
         dfm = jnp.concatenate(
             [flo[pl.ds(b, K, stride=rows), :], fhi[pl.ds(b, K, stride=rows), :]], axis=1
         ).astype(BF16)
-        xb = x_ref[b]
-        dhi, dlo = split(dot(dfm, xb))
-        dl = dl_ref[b]
-        low = jnp.concatenate([dhi, dlo, dl], axis=0)
-        acc_ref[...] += dot(low, xb, NT)
-        left = jnp.concatenate([dfm, dfm, proj, shared], axis=0)
-        right = jnp.concatenate([s_ref[b], dlo, dhi, dl], axis=0)
-        dx[b] = dot(left, right, TN)
+        left[b] = dfm
+        dhi, dlo = split(dot(dfm, x_ref[b]))
+        low[b, :K] = dhi
+        low[b, K:] = dlo
         return 0
 
-    lax.fori_loop(0, rows, sample, 0, unroll=8)
+    lax.fori_loop(0, rows, score_grad, 0, unroll=16)
+
+    def samples(g, _):
+        total = jnp.zeros(acc_ref.shape, F32)
+        for i in range(4):
+            b = g * 4 + i
+            dfm, dl = left[b], dl_ref[b]
+            total = total + dot(jnp.concatenate([low[b], dl], axis=0), x_ref[b], NT)
+            dx[b] = dot(
+                jnp.concatenate([dfm, dfm, proj, shared], axis=0),
+                jnp.concatenate([s_ref[b], low[b, K:], low[b, :K], dl], axis=0),
+                TN,
+            )
+        acc_ref[...] += total
+        return 0
+
+    lax.fori_loop(0, rows // 4, samples, 0, unroll=4)
 
     def turn(j, _):
         at = pl.ds(pl.multiple_of(j * 16, 16), 16)
@@ -317,7 +350,8 @@
         ],
         out_specs=[out, out, pl.BlockSpec((2 * K + nl, n), lambda i, o: (0, 0))],
         scratch_shapes=[pltpu.VMEM((K * rows, 128), F32)] * 2
-        + [pltpu.VMEM((rows, n, DP), F32), pltpu.VMEM((n, rows + rows // 2, 128), BF16)],
+        + [pltpu.VMEM((rows, n, DP), F32), pltpu.VMEM((n, rows + rows // 2, 128), BF16)]
+        + [pltpu.VMEM((rows, K, DP), BF16), pltpu.VMEM((rows, 2 * K, DP), BF16)],
     )
     half = jax.ShapeDtypeStruct((n // 2, count // rows, rows + rows // 2, 128), BF16)
     return pl.pallas_call(
@@ -545,17 +579,20 @@
     other_ids = lax.ppermute(ids[1], "c", SWAP)
 
     wt, score, dl, xh, inv = forward(x3, g2, proj_f, w_lcb_f)
-    g_out, g_in, g_gain, dfm = batch(
+    w_keep, w_send, g_gain, dfm = batch(
         core.reshape(1), xh, inv, gain_t, near, far, rows, out_grad
     )
-    g_out = g_out.reshape(owners, -1, 128)
-    w_first, dfm = lax.optimization_barrier((g_out, dfm))
+    w_other = lax.ppermute(w_send, "c", SWAP)
+    early = 160
+    w_first = add(w_keep[:, :early], w_other[:, :early])
+    w_second = add(w_keep[:, early:], w_other[:, early:])
+    w_first, w_second, dfm = lax.optimization_barrier((w_first, w_second, dfm))
     w_first = lax.all_to_all(w_first, WIDE, 0, 0, tiled=True)
     keep, send, acc = last(spot, x3, score, dl, dfm, wt)
     w_first, send = lax.optimization_barrier((w_first, send))
     little = jnp.concatenate([acc[:K] + acc[K : 2 * K], g_gain, acc[2 * K :]], axis=0)
     little = jnp.pad(little.T, ((0, 0), (0, 128 - little.shape[0]))).reshape(owners, per, 128)
-    w_second = jnp.concatenate([g_in, *split(little)], axis=1)
+    w_second = jnp.concatenate([w_second, *split(little)], axis=1)
     w_second = lax.all_to_all(w_second, WIDE, 0, 0, tiled=True)
 
     other = lax.ppermute(send, "c", SWAP)
@@ -568,14 +605,16 @@
     mixed = jnp.concatenate(
         [jnp.sum(v.astype(F32), axis=0) for v in (w_first, w_second)], axis=0
     )
-    mixed = jnp.concatenate([mixed[: 2 * rows], mixed[2 * rows : -per] + mixed[-per:]], axis=0)
+    mixed = jnp.concatenate([mixed[:rows], mixed[rows:-per] + mixed[-per:]], axis=0)
     a, b, c, mixed = lax.optimization_barrier((a, b, c, mixed))
     c = lax.all_to_all(c.reshape((16,) + c.shape[2:]), ("z", "x"), 0, 0, tiled=True)
     a, b = ring_sums([("x", a), ("z", b)])
     c = jnp.sum(c.astype(F32), axis=0).astype(BF16)
     mixed = mixed + lax.ppermute(mixed, "yh", SWAP)
-    mixed = mixed + lax.ppermute(mixed, "c", SWAP)
-    little, big = mixed[2 * rows :, : 2 * K + nl], mixed[: 2 * rows]
+    swapped = lax.ppermute(mixed, "c", SWAP)
+    little = (mixed[rows:] + swapped[rows:])[:, : 2 * K + nl]
+    big = jnp.stack([mixed[:rows], swapped[:rows]])
+    big = jnp.where(core == 0, big, big[::-1]).reshape(2 * rows, 128)
     a, b, c, big, little = lax.optimization_barrier((a, b, c, big, little))
     ab = jnp.concatenate([a, b], axis=1)
     ab = ab.reshape((2, 1, 2) + ab.shape[1:])

time: 285 us -> 279 us (0.979)
  Pallas kernels: 115 us -> 102 us
  waiting for transfers between devices: 39 us -> 43.1 us
  local copies, waits for them, and re-layouts: 12.7 us -> 15.9 us
  starting transfers between devices: 65.5 us -> 62.4 us
    pallas_call x1, Pallas kernels: 38.6 us -> 26.1 us  [last(): pl.pallas_call(last_kernel, grid_spec=grid, out_shape=[half, half, jax.Sh...]
    ppermute x16, waiting for transfers between devices: 27.8 us -> 32.8 us  [ring_step(): return lax.ppermute(v, axis, [(i, (i + by) % n) for i in range(n)])]
    convert_element_type x8 -> x10, other arithmetic: 14 us -> 18.9 us  [add(): return total.astype(BF16)]
    all_to_all x1, waiting for transfers between devices: 4.47 us -> 0.01 us  [body(): w_first = lax.all_to_all(w_first, WIDE, 0, 0, tiled=True)]
    ppermute x1 -> x2, waiting for transfers between devices: 0.01 us -> 3.58 us  [the longest x1 3.57 us: body(): w_other = lax.ppermute(w_send, 'c', SWAP)]
    ppermute x1 -> x2, starting transfers between devices: 6.69 us -> 5.46 us  [the longest x1 5.25 us: body(): swapped = lax.ppermute(mixed, 'c', SWAP)]
  transfers between devices with their start and end apart: 27 -> 28, of which waited for: 8 -> 9; matrix products, arithmetic and copies ran while one was open for 11% -> 12% of each run, Pallas kernels for 34% -> 29%
where the time goes in v7:
time: 279 us; the launch traced here: 278 us
  Pallas kernels  102 us (37%)
  starting transfers between devices  62.4 us (22%)
  waiting for transfers between devices  43.1 us (15%)
  other arithmetic  31 us (11%)
  blocking collectives  21.8 us (8%)
  local copies, waits for them, and re-layouts  15.9 us (6%)
    ppermute x16, waiting for transfers between devices, ring_step(): return lax.ppermute(v, axis, [(i, (i + by) % n) for i in range(n)])  32.8 us
    pallas_call x1, Pallas kernels, last(): pl.pallas_call(last_kernel, grid_spec=grid, out_shape=[half, half, jax.Sh...  26.1 us
    pallas_call x2, Pallas kernels, unfold(): pl.pallas_call(unfold_kernel, grid=(count // rows,), in_specs=[pl.BlockSp...  24 us
    all_to_all x1, blocking collectives, body(): both = lax.all_to_all(both, ('yl', 'yh'), 0, 0, tiled=True)  21.8 us
    ppermute x16, starting transfers between devices, ring_step(): return lax.ppermute(v, axis, [(i, (i + by) % n) for i in range(n)])  20.6 us
    convert_element_type x10, other arithmetic, add(): return total.astype(BF16)  18.9 us
    pallas_call x1, Pallas kernels, first(): pl.pallas_call(first_kernel, grid=(count // rows,), in_specs=[pl.BlockSpe...  16.1 us
    pallas_call x1, Pallas kernels, batch(): pl.pallas_call(batch_kernel, grid=(total // rows,), in_specs=[pl.BlockSpe...  15.5 us
  transfers between devices with their start and end apart: 28, of which 9 were waited for; matrix products, arithmetic and copies ran while one was open for 12% of the time, Pallas kernels for 29%

profile of v7, /device:TPU:1, one launch (start us, length us, event | category | flops | bytes accessed | tf_op | source)
XLA Modules:
  0.0 277.7 jit_solution(7456150689354115417)
XLA Ops:
  3.0 1.7 broadcast_in_dim.52
  4.7 9.7 %all-to-all-start = ((bf16[32,272,128]{2,1,0:T(8,128)(2,1)}), bf16[32,272,128]{2,1,0:T(8,128)(2,1)S(1)}, u32[]{:S(2)}, u32[]{:S(2)}) async-start(bf16[32,272,128]{2,1,0:T(8,128)(2,1)} %broadcast_in_dim.52), calls=%async_computation | async-start | bytes 4456448 | tf_op jit(solution)/shard_map/all_to_all | solution.py:519
  14.5 17.7 %unfold.2.x_ref = bf16[128,256,256]{2,1,0:T(8,128)(2,1)} custom-call(bf16[128,49152]{1,0:T(8,128)(2,1)} %x_ref.2), custom_call_target="tpu_custom_call" | custom-call | flops 1000000000 | bytes 29491200 | tf_op jit(solution)/shard_map/unfold/pallas_call | solution.py:67
  32.2 6.3 %unfold.3.g_ref = bf16[128,64,256]{2,1,0:T(8,128)(2,1)} custom-call(bf16[128,24576]{1,0:T(8,128)(2,1)} %g_ref.1), custom_call_target="tpu_custom_call" | custom-call | flops 1000000000 | bytes 7372800 | tf_op jit(solution)/shard_map/unfold/pallas_call | solution.py:67
  38.5 6.7 %all-to-all-done.nraw_ref.near_ref = bf16[32,272,128]{2,1,0:T(8,128)(2,1)S(1)} async-done(((bf16[32,272,128]{2,1,0:T(8,128)(2,1)}), bf16[32,272,128]{2,1,0:T(8,128)(2,1)S(1)}, u32[]{:S(2)}, u32[]{:S(2)}) %all-to-all-start) | async-done | bytes 2228256 | tf_op jit(solution)/shard_map/all_to_all | solution.py:519
  45.1 2.1 collective-permute-start
  48.9 16.1 %first.1 = (bf16[128,32,256]{2,1,0:T(8,128)(2,1)}, bf16[128,64,256]{2,1,0:T(8,128)(2,1)}, f32[16,128,256]{2,1,0:T(8,128)}, f32[128,128]{1,0:T(8,128)}) custom-call(bf16[128,256,256]{2,1,0:T(8,128)(2,1)} %unfold.2.x_ref, bf16[128,64,256]{2,1,0:T(8,128)(2,1)} %unfold.3.g_ref, bf16[80,256]{1,0:T(8,128)(2,1)} %pad_maximum_fusion.5.w_ref.wt_ref), custom_call_target="tpu_custom_call" | custom-call | flops 20000000000 | bytes 16777216 | tf_op jit(solution)/shard_map/first/pallas_call | solution.py:122
  65.0 15.5 %batch.1 = (bf16[32,256,128]{2,1,0:T(8,128)(2,1)}, bf16[32,256,128]{2,1,0:T(8,128)(2,1)}, f32[16,256]{1,0:T(8,128)}, f32[16,128,256]{2,1,0:T(8,128)}) custom-call(s32[1]{0:T(128)} %bitcast.5.core_ref, f32[16,128,256]{2,1,0:T(8,128)} %get-tuple-element.51.xh_ref, f32[128,128]{1,0:T(8,128)} %get-tuple-element.52.inv_ref, ...), custom_call_target="tpu_custom_call" | custom-call | flops 20000000000 | bytes 20000000 | tf_op jit(solution)/shard_map/batch/pallas_call | solution.py:239
  81.4 3.6 %collective-permute-done.1 = bf16[32,256,128]{2,1,0:T(8,128)(2,1)S(1)} collective-permute-done((bf16[32,256,128]{2,1,0:T(8,128)(2,1)}, bf16[32,256,128]{2,1,0:T(8,128)(2,1)S(1)}, u32[]{:S(2)}, u32[]{:S(2)}) %collective-permute-start.1) | collective-permute-done | bytes 2097184 | tf_op jit(solution)/shard_map/ppermute | solution.py:585
  84.9 1.4 add_convert_fusion.1
  86.3 1.5 add_convert_fusion
  87.8 4.0 %all-to-all-start.1 = ((bf16[32,160,128]{2,1,0:T(8,128)(2,1)}), bf16[32,160,128]{2,1,0:T(8,128)(2,1)S(1)}, u32[]{:S(2)}, u32[]{:S(2)}) async-start(bf16[32,160,128]{2,1,0:T(8,128)(2,1)} %add_convert_fusion), calls=%async_computation.1 | async-start | bytes 2621440 | tf_op jit(solution)/shard_map/all_to_all | solution.py:590
  91.8 26.1 %last.1 = (bf16[128,4,48,128]{3,2,1,0:T(8,128)(2,1)}, bf16[128,4,48,128]{3,2,1,0:T(8,128)(2,1)}, f32[96,256]{1,0:T(8,128)}) custom-call(s32[256]{0:T(256)} %get-tuple-element.86.at_ref, bf16[128,256,256]{2,1,0:T(8,128)(2,1)} %unfold.2.x_ref, bf16[128,32,256]{2,1,0:T(8,128)(2,1)} %get-tuple-element.49.s_ref, bf16[128,64,256]{2,1,0:T(8,128)(2,1)} %get-tuple-element.50.dl_ref, ...), custom_call_target="tpu_custom_call" | custom-call | flops 20000000000 | bytes 33554432 | tf_op jit(solution)/shard_map/last/pallas_call | solution.py:357
  119.3 1.4 scatter_custom_fusion
  124.3 7.7 %all-to-all-start.2 = ((bf16[32,112,128]{2,1,0:T(8,128)(2,1)}), bf16[32,112,128]{2,1,0:T(8,128)(2,1)S(1)}, u32[]{:S(2)}, u32[]{:S(2)}) async-start(bf16[32,112,128]{2,1,0:T(8,128)(2,1)} %pad_maximum_fusion.1), calls=%async_computation.2 | async-start | bytes 1835008 | tf_op jit(solution)/shard_map/all_to_all | solution.py:596
  132.7 14.6 %sums.1 = (bf16[4,4,4,304,128]{4,3,2,1,0:T(8,128)(2,1)}, bf16[4,4,4,272,128]{4,3,2,1,0:T(8,128)(2,1)}, bf16[4,4,4,192,128]{4,3,2,1,0:T(8,128)(2,1)}, bf16[2,4,30...) custom-call(s32[2]{0:T(128)} %pad_add_fusion.at_ref, ...), custom_call_target="tpu_custom_call" | custom-call | flops 10000000000 | bytes 25165824 | tf_op jit(solution)/shard_map/sums/pallas_call | solution.py:450
  147.3 2.5 collective-permute-start.10
  149.9 1.2 collective-permute-start.4
  151.1 1.4 collective-permute-start.6
  153.5 3.9 %all-to-all-start.3 = ((bf16[4,4,4,192,128]{4,3,2,1,0:T(8,128)(2,1)}), bf16[4,4,4,192,128]{4,3,2,1,0:T(8,128)(2,1)S(1)}, u32[]{:S(2)}, u32[]{:S(2)}) async-start(bf16[4,4,4,192,128]{4,3,2,1,0:T(8,128)(2,1)} %get-tuple-element.71), calls=%async_computation.3 | async-start | bytes 6291456 | tf_op jit(solution)/shard_map/all_to_all | solution.py:603
  157.3 3.8 %collective-permute-done.10 = bf16[2,4,272,128]{3,2,1,0:T(8,128)(2,1)} collective-permute-done((bf16[2,4,272,128]{3,2,1,0:T(8,128)(2,1)}, bf16[2,4,272,128]{3,2,1,0:T(8,128)(2,1)}, u32[]{:S(2)}, u32[]{:S(2)}) %collective-permute-start.10) | collective-permute-done | bytes 557088 | tf_op jit(solution)/shard_map/ppermute | solution.py:524
  161.1 3.1 %collective-permute-done.8 = bf16[2,4,272,128]{3,2,1,0:T(8,128)(2,1)} collective-permute-done((bf16[2,4,272,128]{3,2,1,0:T(8,128)(2,1)}, bf16[2,4,272,128]{3,2,1,0:T(8,128)(2,1)}, u32[]{:S(2)}, u32[]{:S(2)}) %collective-permute-start.8) | collective-permute-done | bytes 557088 | tf_op jit(solution)/shard_map/ppermute | solution.py:524
  164.2 3.7 %fusion.5 = (bf16[4,4,272,128]{3,2,1,0:T(8,128)(2,1)}, bf16[4,4,272,128]{3,2,1,0:T(8,128)(2,1)}) fusion(bf16[2,4,272,128]{3,2,1,0:T(8,128)(2,1)} %collective-permute-done.8, bf16[4,4,4,272,128]{4,3,2,1,0:T(8,128)(2,1)} %get-tuple-element.64, bf16[2,4,272,128]{3,2,1,0:T(8,128)(2,1)} %collective-permute-done.10), kind=kLoop, calls=%fused_computation.14 | loop fusion | flops 4456448 | bytes 5570560 | tf_op jit(solution)/shard_map/convert_element_type | solution.py:531
  169.4 3.0 %fusion.1 = (bf16[4,4,304,128]{3,2,1,0:T(8,128)(2,1)}, bf16[4,4,304,128]{3,2,1,0:T(8,128)(2,1)}) fusion(bf16[2,4,304,128]{3,2,1,0:T(8,128)(2,1)} %collective-permute-done.4, bf16[4,4,4,304,128]{4,3,2,1,0:T(8,128)(2,1)S(1)} %copy-done.5, bf16[2,4,304,128]{3,2,1,0:T(8,128)(2,1)} %collective-permute-done.6), kind=kLoop, calls=%fused_computation.7 | loop fusion | flops 4980736 | bytes 6225920 | tf_op jit(solution)/shard_map/convert_element_type | solution.py:531
  172.4 1.2 collective-permute-start.5
  173.7 1.4 collective-permute-start.7
  175.2 1.6 convert_reduce_fusion
  176.9 15.1 %collective-permute-done.11 = bf16[4,4,272,128]{3,2,1,0:T(8,128)(2,1)} collective-permute-done((bf16[4,4,272,128]{3,2,1,0:T(8,128)(2,1)}, bf16[4,4,272,128]{3,2,1,0:T(8,128)(2,1)}, u32[]{:S(2)}, u32[]{:S(2)}) %collective-permute-start.11) | collective-permute-done | bytes 1114144 | tf_op jit(solution)/shard_map/ppermute | solution.py:524
  192.0 1.5 collective-permute-done.9
  193.5 3.4 %fusion.7 = bf16[4,4,272,128]{3,2,1,0:T(8,128)(2,1)} fusion(bf16[4,4,272,128]{3,2,1,0:T(8,128)(2,1)} %collective-permute-done.11, bf16[4,4,272,128]{3,2,1,0:T(8,128)(2,1)} %collective-permute-done.9, bf16[4,4,4,272,128]{4,3,2,1,0:T(8,128)(2,1)} %get-tuple-element.64), kind=kLoop, calls=%fused_computation.17 | loop fusion | flops 3342336 | bytes 4456448 | tf_op jit(solution)/shard_map/convert_element_type | solution.py:531
  196.9 3.1 %collective-permute-done.5 = bf16[4,4,304,128]{3,2,1,0:T(8,128)(2,1)} collective-permute-done((bf16[4,4,304,128]{3,2,1,0:T(8,128)(2,1)}, bf16[4,4,304,128]{3,2,1,0:T(8,128)(2,1)}, u32[]{:S(2)}, u32[]{:S(2)}) %collective-permute-start.5) | collective-permute-done | bytes 1245216 | tf_op jit(solution)/shard_map/ppermute | solution.py:524
  200.0 3.6 %fusion.3 = bf16[4,4,304,128]{3,2,1,0:T(8,128)(2,1)} fusion(bf16[4,4,304,128]{3,2,1,0:T(8,128)(2,1)} %collective-permute-done.7, bf16[4,4,304,128]{3,2,1,0:T(8,128)(2,1)} %collective-permute-done.5, bf16[4,4,4,304,128]{4,3,2,1,0:T(8,128)(2,1)} %get-tuple-element.61), kind=kLoop, calls=%fused_computation.10 | loop fusion | flops 3735552 | bytes 4980736 | tf_op jit(solution)/shard_map/convert_element_type | solution.py:531
  203.6 1.7 reduce_sum.54
  205.2 2.6 collective-permute-start.20
  207.9 1.7 slice_bitcast_fusion.3
  210.5 1.7 collective-permute-start.18
  212.2 1.7 slice_bitcast_fusion.1
  214.3 2.4 collective-permute-start.14
  216.7 3.6 %all-to-all-start.4 = ((bf16[16,192,128]{2,1,0:T(8,128)(2,1)}), bf16[16,192,128]{2,1,0:T(8,128)(2,1)S(1)}, u32[]{:S(2)}, u32[]{:S(2)}) async-start(bf16[16,192,128]{2,1,0:T(8,128)(2,1)} %bitcast.86), calls=%async_computation.4 | async-start | bytes 1572864 | tf_op jit(solution)/shard_map/all_to_all | solution.py:610
  221.2 5.2 %collective-permute-start.21 = (f32[264,128]{1,0:T(8,128)S(1)}, f32[264,128]{1,0:T(8,128)S(1)}, u32[]{:S(2)}, u32[]{:S(2)}) collective-permute-start(f32[264,128]{1,0:T(8,128)S(1)} %add.151), channel_id=1, source_target_pairs={{0,1},{1,0},{2,3},{3,2},{4,5},{5,4},{6,7},{7,6},{8,9},{9,8},{10,11... | collective-permute-start | bytes 405512 | tf_op jit(solution)/shard_map/ppermute | solution.py:614
  227.6 1.6 collective-permute-start.17
  229.2 1.6 collective-permute-start.19
  231.7 1.3 collective-permute-start.13
  233.0 1.5 collective-permute-start.15
  235.3 5.3 %collective-permute-done.17 = bf16[4,272,128]{2,1,0:T(8,128)(2,1)S(1)} collective-permute-done((bf16[4,272,128]{2,1,0:T(8,128)(2,1)S(1)}, bf16[4,272,128]{2,1,0:T(8,128)(2,1)S(1)}, u32[]{:S(2)}, u32[]{:S(2)}) %collective-permute-start.17) | collective-permute-done | bytes 278560 | tf_op jit(solution)/shard_map/ppermute | solution.py:524
  242.4 21.8 %all_to_all.30 = bf16[4,2,768,128]{3,2,1,0:T(8,128)(2,1)S(1)} all-to-all(bf16[4,2,768,128]{3,2,1,0:T(8,128)(2,1)S(1)} %bitcast.85), channel_id=1, replica_groups=mesh['z'=4,'x'=4,'yl'=2,'yh'=2,'c'=2] {'yl','yh'}, dimensions={0} | all-to-all | bytes 3145728 | tf_op jit(solution)/shard_map/all_to_all | solution.py:629
  264.7 2.2 collective-permute-start.22
  271.7 6.0 %update.1 = (f32[192,2048]{1,0:T(8,128)}, f32[1,2048]{1,0:T(1,128)}) custom-call(s32[1,2048]{1,0:T(1,128)} %bitcast.99, bf16[2,2,768,128]{3,2,1,0:T(8,128)(2,1)} %maximum_select_fusion.sum_ref, f32[192,2048]{1,0:T(8,128)} %bitcast.100, f32[1,2048]{1,0:T(1,128)} %bitcast.101), custom_call_target="tpu_custom_call" | custom-call | flops 4000000000 | bytes 4718592 | tf_op jit(solution)/shard_map/update/pallas_call | solution.py:495
  (116 shorter events, 25.1 us)
Async XLA Ops:
  4.7 40.4 %all-to-all-start = ((bf16[32,272,128]{2,1,0:T(8,128)(2,1)}), bf16[32,272,128]{2,1,0:T(8,128)(2,1)S(1)}, u32[]{:S(2)}, u32[]{:S(2)}) async-start(bf16[32,272,128]{2,1,0:T(8,128)(2,1)} %broadcast_in_dim.52), calls=%async_computation | async-start | bytes 4456448 | tf_op jit(solution)/shard_map/all_to_all | solution.py:519
  45.1 19.9 %copy-start.6 = (bf16[32,272,128]{2,1,0:T(8,128)(2,1)}, bf16[32,272,128]{2,1,0:T(8,128)(2,1)S(1)}, u32[]{:S(2)}) copy-start(bf16[32,272,128]{2,1,0:T(8,128)(2,1)S(1)} %all-to-all-done.nraw_ref.near_ref) | copy-start | bytes 6684676
  45.1 19.9 %collective-permute-start = (bf16[32,272,128]{2,1,0:T(8,128)(2,1)S(1)}, bf16[32,272,128]{2,1,0:T(8,128)(2,1)}, u32[]{:S(2)}, u32[]{:S(2)}) collective-permute-start(bf16[32,272,128]{2,1,0:T(8,128)(2,1)S(1)} %all-to-all-done.nraw_ref.near_ref), channel_id=1, source_target_pairs={{0,1},{1,0},{2,3},{3,2},{4,5},{5,4},{6,7},{7,6},{8,9},{9,8},{10,11... | collective-permute-start | bytes 6684680 | tf_op jit(solution)/shard_map/ppermute | solution.py:572
  65.0 15.8 %copy-start.13 = (s32[256]{0:T(256)S(1)}, s32[256]{0:T(256)}, u32[]{:S(2)}) copy-start(s32[256]{0:T(256)} %param.15) | copy-start | bytes 3076
  80.6 5.8 %copy-start.7 = (bf16[32,256,128]{2,1,0:T(8,128)(2,1)S(1)}, bf16[32,256,128]{2,1,0:T(8,128)(2,1)}, u32[]{:S(2)}) copy-start(bf16[32,256,128]{2,1,0:T(8,128)(2,1)} %get-tuple-element.53) | copy-start | bytes 6291460
  80.6 4.4 %collective-permute-start.1 = (bf16[32,256,128]{2,1,0:T(8,128)(2,1)}, bf16[32,256,128]{2,1,0:T(8,128)(2,1)S(1)}, u32[]{:S(2)}, u32[]{:S(2)}) collective-permute-start(bf16[32,256,128]{2,1,0:T(8,128)(2,1)} %get-tuple-element.54), channel_id=1, source_target_pairs={{0,1},{1,0},{2,3},{3,2},{4,5},{5,4},{6,7},{7,6},{8,9},{9,8},{10,11... | collective-permute-start | bytes 6291464 | tf_op jit(solution)/shard_map/ppermute | solution.py:585
  87.8 30.1 %all-to-all-start.1 = ((bf16[32,160,128]{2,1,0:T(8,128)(2,1)}), bf16[32,160,128]{2,1,0:T(8,128)(2,1)S(1)}, u32[]{:S(2)}, u32[]{:S(2)}) async-start(bf16[32,160,128]{2,1,0:T(8,128)(2,1)} %add_convert_fusion), calls=%async_computation.1 | async-start | bytes 2621440 | tf_op jit(solution)/shard_map/all_to_all | solution.py:590
  91.8 27.4 %copy-start.9 = (s32[128,256]{1,0:T(8,128)S(1)}, s32[128,256]{1,0:T(8,128)}, u32[]{:S(2)}) copy-start(s32[128,256]{1,0:T(8,128)} %param.14) | copy-start | bytes 393220
  117.9 5.2 %copy-start.10 = (f32[96,256]{1,0:T(8,128)S(1)}, f32[96,256]{1,0:T(8,128)}, u32[]{:S(2)}) copy-start(f32[96,256]{1,0:T(8,128)} %get-tuple-element.69) | copy-start | bytes 294916
  117.9 5.2 %copy-start.11 = (f32[16,256]{1,0:T(8,128)S(1)}, f32[16,256]{1,0:T(8,128)}, u32[]{:S(2)}) copy-start(f32[16,256]{1,0:T(8,128)} %get-tuple-element.70) | copy-start | bytes 49156
  117.9 1.1 copy-start
  119.0 13.1 %collective-permute-start.2 = (bf16[128,4,48,128]{3,2,1,0:T(8,128)(2,1)}, bf16[128,4,48,128]{3,2,1,0:T(8,128)(2,1)}, u32[]{:S(2)}, u32[]{:S(2)}) collective-permute-start(bf16[128,4,48,128]{3,2,1,0:T(8,128)(2,1)} %get-tuple-element.60), channel_id=1, source_target_pairs={{0,1},{1,0},{2,3},{3,2},{4,5},{5,4},{6,7},{7,6},{8,9},{9,8},{10,11... | collective-permute-start | bytes 18874376 | tf_op jit(solution)/shard_map/ppermute | solution.py:598
  122.2 9.8 %collective-permute-start.3 = (s32[64,2,128]{2,1,0:T(2,128)S(1)}, s32[64,2,128]{2,1,0:T(2,128)S(1)}, u32[]{:S(2)}, u32[]{:S(2)}) collective-permute-start(s32[64,2,128]{2,1,0:T(2,128)S(1)} %bitcast.96), channel_id=1, source_target_pairs={{0,1},{1,0},{2,3},{3,2},{4,5},{5,4},{6,7},{7,6},{8,9},{9,8},{10,11... | collective-permute-start | bytes 196616 | tf_op jit(solution)/shard_map/ppermute | solution.py:579
  124.3 28.2 %all-to-all-start.2 = ((bf16[32,112,128]{2,1,0:T(8,128)(2,1)}), bf16[32,112,128]{2,1,0:T(8,128)(2,1)S(1)}, u32[]{:S(2)}, u32[]{:S(2)}) async-start(bf16[32,112,128]{2,1,0:T(8,128)(2,1)} %pad_maximum_fusion.1), calls=%async_computation.2 | async-start | bytes 1835008 | tf_op jit(solution)/shard_map/all_to_all | solution.py:596
  132.1 0.6 copy-start.14
  147.3 13.8 %collective-permute-start.10 = (bf16[2,4,272,128]{3,2,1,0:T(8,128)(2,1)}, bf16[2,4,272,128]{3,2,1,0:T(8,128)(2,1)}, u32[]{:S(2)}, u32[]{:S(2)}) collective-permute-start(bf16[2,4,272,128]{3,2,1,0:T(8,128)(2,1)} %get-tuple-element.66), channel_id=1, source_target_pairs={{0,24},{8,0},{16,8},{24,16},{1,25},{9,1},{17,9},{25,17},{2,26},{10... | collective-permute-start | bytes 1671176 | tf_op jit(solution)/shard_map/ppermute | solution.py:524
  149.8 14.3 %collective-permute-start.8 = (bf16[2,4,272,128]{3,2,1,0:T(8,128)(2,1)}, bf16[2,4,272,128]{3,2,1,0:T(8,128)(2,1)}, u32[]{:S(2)}, u32[]{:S(2)}) collective-permute-start(bf16[2,4,272,128]{3,2,1,0:T(8,128)(2,1)} %get-tuple-element.65), channel_id=1, source_target_pairs={{0,8},{8,16},{16,24},{24,0},{1,9},{9,17},{17,25},{25,1},{2,10},{10... | collective-permute-start | bytes 1671176 | tf_op jit(solution)/shard_map/ppermute | solution.py:524
  149.9 19.5 %collective-permute-start.4 = (bf16[2,4,304,128]{3,2,1,0:T(8,128)(2,1)}, bf16[2,4,304,128]{3,2,1,0:T(8,128)(2,1)}, u32[]{:S(2)}, u32[]{:S(2)}) collective-permute-start(bf16[2,4,304,128]{3,2,1,0:T(8,128)(2,1)} %get-tuple-element.62), channel_id=1, source_target_pairs={{0,32},{32,64},{64,96},{96,0},{1,33},{33,65},{65,97},{97,1},{2,34}... | collective-permute-start | bytes 1867784 | tf_op jit(solution)/shard_map/ppermute | solution.py:524
  151.1 18.3 %collective-permute-start.6 = (bf16[2,4,304,128]{3,2,1,0:T(8,128)(2,1)}, bf16[2,4,304,128]{3,2,1,0:T(8,128)(2,1)}, u32[]{:S(2)}, u32[]{:S(2)}) collective-permute-start(bf16[2,4,304,128]{3,2,1,0:T(8,128)(2,1)} %get-tuple-element.63), channel_id=1, source_target_pairs={{0,96},{32,0},{64,32},{96,64},{1,97},{33,1},{65,33},{97,65},{2,98}... | collective-permute-start | bytes 1867784 | tf_op jit(solution)/shard_map/ppermute | solution.py:524
  152.5 0.9 copy-start.3
  153.5 50.1 %all-to-all-start.3 = ((bf16[4,4,4,192,128]{4,3,2,1,0:T(8,128)(2,1)}), bf16[4,4,4,192,128]{4,3,2,1,0:T(8,128)(2,1)S(1)}, u32[]{:S(2)}, u32[]{:S(2)}) async-start(bf16[4,4,4,192,128]{4,3,2,1,0:T(8,128)(2,1)} %get-tuple-element.71), calls=%async_computation.3 | async-start | bytes 6291456 | tf_op jit(solution)/shard_map/all_to_all | solution.py:603
  164.2 5.2 %copy-start.5 = (bf16[4,4,4,304,128]{4,3,2,1,0:T(8,128)(2,1)S(1)}, bf16[4,4,4,304,128]{4,3,2,1,0:T(8,128)(2,1)}, u32[]{:S(2)}) copy-start(bf16[4,4,4,304,128]{4,3,2,1,0:T(8,128)(2,1)} %get-tuple-element.61) | copy-start | bytes 14942212
  167.9 24.1 %collective-permute-start.11 = (bf16[4,4,272,128]{3,2,1,0:T(8,128)(2,1)}, bf16[4,4,272,128]{3,2,1,0:T(8,128)(2,1)}, u32[]{:S(2)}, u32[]{:S(2)}) collective-permute-start(bf16[4,4,272,128]{3,2,1,0:T(8,128)(2,1)} %get-tuple-element.90), channel_id=1, source_target_pairs={{0,24},{8,0},{16,8},{24,16},{1,25},{9,1},{17,9},{25,17},{2,26},{10... | collective-permute-start | bytes 3342344 | tf_op jit(solution)/shard_map/ppermute | solution.py:524
  168.2 25.3 %collective-permute-start.9 = (bf16[4,4,272,128]{3,2,1,0:T(8,128)(2,1)}, bf16[4,4,272,128]{3,2,1,0:T(8,128)(2,1)}, u32[]{:S(2)}, u32[]{:S(2)}) collective-permute-start(bf16[4,4,272,128]{3,2,1,0:T(8,128)(2,1)} %get-tuple-element.89), channel_id=1, source_target_pairs={{0,8},{8,16},{16,24},{24,0},{1,9},{9,17},{17,25},{25,1},{2,10},{10... | collective-permute-start | bytes 3342344 | tf_op jit(solution)/shard_map/ppermute | solution.py:524
  172.4 27.6 %collective-permute-start.5 = (bf16[4,4,304,128]{3,2,1,0:T(8,128)(2,1)}, bf16[4,4,304,128]{3,2,1,0:T(8,128)(2,1)}, u32[]{:S(2)}, u32[]{:S(2)}) collective-permute-start(bf16[4,4,304,128]{3,2,1,0:T(8,128)(2,1)} %get-tuple-element.87), channel_id=1, source_target_pairs={{0,32},{32,64},{64,96},{96,0},{1,33},{33,65},{65,97},{97,1},{2,34}... | collective-permute-start | bytes 3735560 | tf_op jit(solution)/shard_map/ppermute | solution.py:524
  173.7 26.3 %collective-permute-start.7 = (bf16[4,4,304,128]{3,2,1,0:T(8,128)(2,1)}, bf16[4,4,304,128]{3,2,1,0:T(8,128)(2,1)}, u32[]{:S(2)}, u32[]{:S(2)}) collective-permute-start(bf16[4,4,304,128]{3,2,1,0:T(8,128)(2,1)} %get-tuple-element.88), channel_id=1, source_target_pairs={{0,96},{32,0},{64,32},{96,64},{1,97},{33,1},{65,33},{97,65},{2,98}... | collective-permute-start | bytes 3735560 | tf_op jit(solution)/shard_map/ppermute | solution.py:524
  175.1 1.7 copy-start.4
  205.2 21.3 %copy-start.2 = (bf16[4,4,272,128]{3,2,1,0:T(8,128)(2,1)S(1)}, bf16[4,4,272,128]{3,2,1,0:T(8,128)(2,1)}, u32[]{:S(2)}) copy-start(bf16[4,4,272,128]{3,2,1,0:T(8,128)(2,1)} %fusion.7) | copy-start | bytes 3342340
  205.2 15.0 %collective-permute-start.20 = (f32[264,128]{1,0:T(8,128)S(1)}, f32[264,128]{1,0:T(8,128)}, u32[]{:S(2)}, u32[]{:S(2)}) collective-permute-start(f32[264,128]{1,0:T(8,128)S(1)} %fusion.16), channel_id=1, source_target_pairs={{0,2},{2,0},{1,3},{3,1},{4,6},{6,4},{5,7},{7,5},{8,10},{10,8},{9,1... | collective-permute-start | bytes 405512 | tf_op jit(solution)/shard_map/ppermute | solution.py:613
  209.6 16.9 %collective-permute-start.16 = (bf16[2,272,128]{2,1,0:T(8,128)(2,1)}, bf16[2,272,128]{2,1,0:T(8,128)(2,1)}, u32[]{:S(2)}, u32[]{:S(2)}) collective-permute-start(bf16[2,272,128]{2,1,0:T(8,128)(2,1)} %get-tuple-element.97), channel_id=1, source_target_pairs={{0,32},{32,64},{64,96},{96,0},{1,33},{33,65},{65,97},{97,1},{2,34}... | collective-permute-start | bytes 417800 | tf_op jit(solution)/shard_map/ppermute | solution.py:524
  210.5 15.9 %collective-permute-start.18 = (bf16[2,272,128]{2,1,0:T(8,128)(2,1)}, bf16[2,272,128]{2,1,0:T(8,128)(2,1)}, u32[]{:S(2)}, u32[]{:S(2)}) collective-permute-start(bf16[2,272,128]{2,1,0:T(8,128)(2,1)} %get-tuple-element.98), channel_id=1, source_target_pairs={{0,96},{32,0},{64,32},{96,64},{1,97},{33,1},{65,33},{97,65},{2,98}... | collective-permute-start | bytes 417800 | tf_op jit(solution)/shard_map/ppermute | solution.py:524
  214.0 16.8 %copy-start.1 = (bf16[4,4,304,128]{3,2,1,0:T(8,128)(2,1)S(1)}, bf16[4,4,304,128]{3,2,1,0:T(8,128)(2,1)}, u32[]{:S(2)}) copy-start(bf16[4,4,304,128]{3,2,1,0:T(8,128)(2,1)} %fusion.3) | copy-start | bytes 3735556
  214.0 16.8 %collective-permute-start.12 = (bf16[2,304,128]{2,1,0:T(8,128)(2,1)}, bf16[2,304,128]{2,1,0:T(8,128)(2,1)S(1)}, u32[]{:S(2)}, u32[]{:S(2)}) collective-permute-start(bf16[2,304,128]{2,1,0:T(8,128)(2,1)} %get-tuple-element.93), channel_id=1, source_target_pairs={{0,8},{8,16},{16,24},{24,0},{1,9},{9,17},{17,25},{25,1},{2,10},{10... | collective-permute-start | bytes 466952 | tf_op jit(solution)/shard_map/ppermute | solution.py:524
  214.3 16.5 %collective-permute-start.14 = (bf16[2,304,128]{2,1,0:T(8,128)(2,1)}, bf16[2,304,128]{2,1,0:T(8,128)(2,1)}, u32[]{:S(2)}, u32[]{:S(2)}) collective-permute-start(bf16[2,304,128]{2,1,0:T(8,128)(2,1)} %get-tuple-element.94), channel_id=1, source_target_pairs={{0,24},{8,0},{16,8},{24,16},{1,25},{9,1},{17,9},{25,17},{2,26},{10... | collective-permute-start | bytes 466952 | tf_op jit(solution)/shard_map/ppermute | solution.py:524
  216.7 25.2 %all-to-all-start.4 = ((bf16[16,192,128]{2,1,0:T(8,128)(2,1)}), bf16[16,192,128]{2,1,0:T(8,128)(2,1)S(1)}, u32[]{:S(2)}, u32[]{:S(2)}) async-start(bf16[16,192,128]{2,1,0:T(8,128)(2,1)} %bitcast.86), calls=%async_computation.4 | async-start | bytes 1572864 | tf_op jit(solution)/shard_map/all_to_all | solution.py:610
  221.2 13.3 %collective-permute-start.21 = (f32[264,128]{1,0:T(8,128)S(1)}, f32[264,128]{1,0:T(8,128)S(1)}, u32[]{:S(2)}, u32[]{:S(2)}) collective-permute-start(f32[264,128]{1,0:T(8,128)S(1)} %add.151), channel_id=1, source_target_pairs={{0,1},{1,0},{2,3},{3,2},{4,5},{5,4},{6,7},{7,6},{8,9},{9,8},{10,11... | collective-permute-start | bytes 405512 | tf_op jit(solution)/shard_map/ppermute | solution.py:614
  227.6 13.0 %collective-permute-start.17 = (bf16[4,272,128]{2,1,0:T(8,128)(2,1)S(1)}, bf16[4,272,128]{2,1,0:T(8,128)(2,1)S(1)}, u32[]{:S(2)}, u32[]{:S(2)}) collective-permute-start(bf16[4,272,128]{2,1,0:T(8,128)(2,1)S(1)} %get-tuple-element.95), channel_id=1, source_target_pairs={{0,32},{32,64},{64,96},{96,0},{1,33},{33,65},{65,97},{97,1},{2,34}... | collective-permute-start | bytes 835592 | tf_op jit(solution)/shard_map/ppermute | solution.py:524
  229.2 11.4 %collective-permute-start.19 = (bf16[4,272,128]{2,1,0:T(8,128)(2,1)S(1)}, bf16[4,272,128]{2,1,0:T(8,128)(2,1)S(1)}, u32[]{:S(2)}, u32[]{:S(2)}) collective-permute-start(bf16[4,272,128]{2,1,0:T(8,128)(2,1)S(1)} %get-tuple-element.96), channel_id=1, source_target_pairs={{0,96},{32,0},{64,32},{96,64},{1,97},{33,1},{65,33},{97,65},{2,98}... | collective-permute-start | bytes 835592 | tf_op jit(solution)/shard_map/ppermute | solution.py:524
  231.7 9.9 %collective-permute-start.13 = (bf16[4,304,128]{2,1,0:T(8,128)(2,1)S(1)}, bf16[4,304,128]{2,1,0:T(8,128)(2,1)S(1)}, u32[]{:S(2)}, u32[]{:S(2)}) collective-permute-start(bf16[4,304,128]{2,1,0:T(8,128)(2,1)S(1)} %get-tuple-element.91), channel_id=1, source_target_pairs={{0,8},{8,16},{16,24},{24,0},{1,9},{9,17},{17,25},{25,1},{2,10},{10... | collective-permute-start | bytes 933896 | tf_op jit(solution)/shard_map/ppermute | solution.py:524
  233.0 8.7 %collective-permute-start.15 = (bf16[4,304,128]{2,1,0:T(8,128)(2,1)S(1)}, bf16[4,304,128]{2,1,0:T(8,128)(2,1)S(1)}, u32[]{:S(2)}, u32[]{:S(2)}) collective-permute-start(bf16[4,304,128]{2,1,0:T(8,128)(2,1)S(1)} %get-tuple-element.92), channel_id=1, source_target_pairs={{0,24},{8,0},{16,8},{24,16},{1,25},{9,1},{17,9},{25,17},{2,26},{10... | collective-permute-start | bytes 933896 | tf_op jit(solution)/shard_map/ppermute | solution.py:524
  242.4 24.5 %copy-start.12 = (s32[8,256]{1,0:T(8,128)S(1)}, s32[8,256]{1,0:T(8,128)}, u32[]{:S(2)}) copy-start(s32[8,256]{1,0:T(8,128)} %param.16) | copy-start | bytes 24580
  242.4 25.1 %copy-start.8 = (f32[2,256,128]{2,1,0:T(8,128)S(1)}, f32[2,256,128]{2,1,0:T(8,128)}, u32[]{:S(2)}) copy-start(f32[2,256,128]{2,1,0:T(8,128)} %reverse_select_fusion) | copy-start | bytes 786436
  264.7 6.0 %collective-permute-start.22 = (bf16[2,768,128]{2,1,0:T(8,128)(2,1)S(1)}, bf16[2,768,128]{2,1,0:T(8,128)(2,1)S(1)}, u32[]{:S(2)}, u32[]{:S(2)}) collective-permute-start(bf16[2,768,128]{2,1,0:T(8,128)(2,1)S(1)} %reduce_sum.58), channel_id=1, source_target_pairs={{0,1},{1,0},{2,3},{3,2},{4,5},{5,4},{6,7},{7,6},{8,9},{9,8},{10,11... | collective-permute-start | bytes 1179656 | tf_op jit(solution)/shard_map/ppermute | solution.py:631

commit v8 on v7

--- a/solution.py
+++ b/solution.py
@@ -615,19 +615,16 @@
     little = (mixed[rows:] + swapped[rows:])[:, : 2 * K + nl]
     big = jnp.stack([mixed[:rows], swapped[:rows]])
     big = jnp.where(core == 0, big, big[::-1]).reshape(2 * rows, 128)
+    c_far = lax.ppermute(c, "yh", SWAP)
+    near_first = lax.axis_index("yh") == 0
+    c = jnp.stack([jnp.where(near_first, c, c_far), jnp.where(near_first, c_far, c)])
     a, b, c, big, little = lax.optimization_barrier((a, b, c, big, little))
     ab = jnp.concatenate([a, b], axis=1)
-    ab = ab.reshape((2, 1, 2) + ab.shape[1:])
-    here = (jnp.arange(2)[:, None] == lax.axis_index("yl")) & (
-        jnp.arange(2)[None, :] == lax.axis_index("yh")
-    )
-    c = jnp.where(here.reshape(2, 1, 2, 1, 1), c, jnp.zeros_like(c))
-    both = jnp.concatenate(
-        [jnp.broadcast_to(v, (2, 2, 2) + v.shape[3:]) for v in (ab, c)], axis=3
-    )
-    both = both.reshape((4, 2) + both.shape[3:])
-    both = lax.all_to_all(both, ("yl", "yh"), 0, 0, tiled=True)
-    mine = jnp.sum(both.astype(F32), axis=0).astype(BF16)
+    ab = jnp.broadcast_to(ab.reshape((2, 1, 2) + ab.shape[1:]), (2, 2, 2) + ab.shape[1:])
+    ab = ab.reshape((4, 2) + ab.shape[3:])
+    ab = lax.all_to_all(ab, ("yl", "yh"), 0, 0, tiled=True)
+    ab = jnp.sum(ab.astype(F32), axis=0).astype(BF16)
+    mine = jnp.concatenate([ab, c], axis=1)
     others = lax.ppermute(mine, "c", SWAP)
     owned = jnp.where(core == 0, jnp.stack([mine, others]), jnp.stack([others, mine]))
     new_rows, new_accum = update(

time: 279 us -> 273 us (0.978)
  blocking collectives: 21.8 us -> 15.6 us
  starting transfers between devices: 62.4 us -> 66.4 us
    all_to_all x1, blocking collectives: 21.8 us -> 15.6 us  [body(): ab = lax.all_to_all(ab, ('yl', 'yh'), 0, 0, tiled=True)]
  transfers between devices with their start and end apart: 28 -> 29, of which waited for: 9 -> 10; matrix products, arithmetic and copies ran while one was open for 12% -> 11% of each run, Pallas kernels for 29% -> 30%
where the time goes in v8:
time: 273 us; the launch traced here: 272 us
  Pallas kernels  103 us (38%)
  starting transfers between devices  66.4 us (24%)
  waiting for transfers between devices  43.1 us (16%)
  other arithmetic  29.9 us (11%)
  blocking collectives  15.6 us (6%)
  local copies, waits for them, and re-layouts  13.4 us (5%)
    ppermute x16, waiting for transfers between devices, ring_step(): return lax.ppermute(v, axis, [(i, (i + by) % n) for i in range(n)])  32.8 us
    pallas_call x1, Pallas kernels, last(): pl.pallas_call(last_kernel, grid_spec=grid, out_shape=[half, half, jax.Sh...  26.3 us
    pallas_call x2, Pallas kernels, unfold(): pl.pallas_call(unfold_kernel, grid=(count // rows,), in_specs=[pl.BlockSp...  24 us
    ppermute x16, starting transfers between devices, ring_step(): return lax.ppermute(v, axis, [(i, (i + by) % n) for i in range(n)])  20.4 us
    convert_element_type x10, other arithmetic, add(): return total.astype(BF16)  18.9 us
    pallas_call x1, Pallas kernels, first(): pl.pallas_call(first_kernel, grid=(count // rows,), in_specs=[pl.BlockSpe...  16.1 us
    all_to_all x1, blocking collectives, body(): ab = lax.all_to_all(ab, ('yl', 'yh'), 0, 0, tiled=True)  15.6 us
    pallas_call x1, Pallas kernels, batch(): pl.pallas_call(batch_kernel, grid=(total // rows,), in_specs=[pl.BlockSpe...  15.5 us
  transfers between devices with their start and end apart: 29, of which 10 were waited for; matrix products, arithmetic and copies ran while one was open for 11% of the time, Pallas kernels for 30%

profile of v8, /device:TPU:1, one launch (start us, length us, event | category | flops | bytes accessed | tf_op | source)
XLA Modules:
  0.0 272.1 jit_solution(12547200467708090446)
XLA Ops:
  3.0 1.7 broadcast_in_dim.28
  4.7 9.7 %all-to-all-start = ((bf16[32,272,128]{2,1,0:T(8,128)(2,1)}), bf16[32,272,128]{2,1,0:T(8,128)(2,1)S(1)}, u32[]{:S(2)}, u32[]{:S(2)}) async-start(bf16[32,272,128]{2,1,0:T(8,128)(2,1)} %broadcast_in_dim.28), calls=%async_computation | async-start | bytes 4456448 | tf_op jit(solution)/shard_map/all_to_all | solution.py:519
  14.5 17.7 %unfold.2.x_ref = bf16[128,256,256]{2,1,0:T(8,128)(2,1)} custom-call(bf16[128,49152]{1,0:T(8,128)(2,1)} %x_ref.2), custom_call_target="tpu_custom_call" | custom-call | flops 1000000000 | bytes 29491200 | tf_op jit(solution)/shard_map/unfold/pallas_call | solution.py:67
  32.1 6.3 %unfold.3.g_ref = bf16[128,64,256]{2,1,0:T(8,128)(2,1)} custom-call(bf16[128,24576]{1,0:T(8,128)(2,1)} %g_ref.1), custom_call_target="tpu_custom_call" | custom-call | flops 1000000000 | bytes 7372800 | tf_op jit(solution)/shard_map/unfold/pallas_call | solution.py:67
  38.4 6.7 %all-to-all-done.nraw_ref.near_ref = bf16[32,272,128]{2,1,0:T(8,128)(2,1)S(1)} async-done(((bf16[32,272,128]{2,1,0:T(8,128)(2,1)}), bf16[32,272,128]{2,1,0:T(8,128)(2,1)S(1)}, u32[]{:S(2)}, u32[]{:S(2)}) %all-to-all-start) | async-done | bytes 2228256 | tf_op jit(solution)/shard_map/all_to_all | solution.py:519
  45.1 2.1 collective-permute-start
  48.9 16.1 %first.1 = (bf16[128,32,256]{2,1,0:T(8,128)(2,1)}, bf16[128,64,256]{2,1,0:T(8,128)(2,1)}, f32[16,128,256]{2,1,0:T(8,128)}, f32[128,128]{1,0:T(8,128)}) custom-call(bf16[128,256,256]{2,1,0:T(8,128)(2,1)} %unfold.2.x_ref, bf16[128,64,256]{2,1,0:T(8,128)(2,1)} %unfold.3.g_ref, bf16[80,256]{1,0:T(8,128)(2,1)} %pad_maximum_fusion.6.w_ref.wt_ref), custom_call_target="tpu_custom_call" | custom-call | flops 20000000000 | bytes 16777216 | tf_op jit(solution)/shard_map/first/pallas_call | solution.py:122
  65.0 15.5 %batch.1 = (bf16[32,256,128]{2,1,0:T(8,128)(2,1)}, bf16[32,256,128]{2,1,0:T(8,128)(2,1)}, f32[16,256]{1,0:T(8,128)}, f32[16,128,256]{2,1,0:T(8,128)}) custom-call(s32[1]{0:T(128)} %bitcast.5.core_ref, f32[16,128,256]{2,1,0:T(8,128)} %get-tuple-element.51.xh_ref, f32[128,128]{1,0:T(8,128)} %get-tuple-element.52.inv_ref, ...), custom_call_target="tpu_custom_call" | custom-call | flops 20000000000 | bytes 20000000 | tf_op jit(solution)/shard_map/batch/pallas_call | solution.py:239
  81.3 3.6 %collective-permute-done.1 = bf16[32,256,128]{2,1,0:T(8,128)(2,1)S(1)} collective-permute-done((bf16[32,256,128]{2,1,0:T(8,128)(2,1)}, bf16[32,256,128]{2,1,0:T(8,128)(2,1)S(1)}, u32[]{:S(2)}, u32[]{:S(2)}) %collective-permute-start.1) | collective-permute-done | bytes 2097184 | tf_op jit(solution)/shard_map/ppermute | solution.py:585
  84.9 1.4 add_convert_fusion.1
  86.3 1.5 add_convert_fusion
  87.8 4.0 %all-to-all-start.1 = ((bf16[32,160,128]{2,1,0:T(8,128)(2,1)}), bf16[32,160,128]{2,1,0:T(8,128)(2,1)S(1)}, u32[]{:S(2)}, u32[]{:S(2)}) async-start(bf16[32,160,128]{2,1,0:T(8,128)(2,1)} %add_convert_fusion), calls=%async_computation.1 | async-start | bytes 2621440 | tf_op jit(solution)/shard_map/all_to_all | solution.py:590
  91.8 26.3 %last.1 = (bf16[128,4,48,128]{3,2,1,0:T(8,128)(2,1)}, bf16[128,4,48,128]{3,2,1,0:T(8,128)(2,1)}, f32[96,256]{1,0:T(8,128)}) custom-call(s32[256]{0:T(256)} %get-tuple-element.86.at_ref, bf16[128,256,256]{2,1,0:T(8,128)(2,1)} %unfold.2.x_ref, bf16[128,32,256]{2,1,0:T(8,128)(2,1)} %get-tuple-element.49.s_ref, bf16[128,64,256]{2,1,0:T(8,128)(2,1)} %get-tuple-element.50.dl_ref, ...), custom_call_target="tpu_custom_call" | custom-call | flops 20000000000 | bytes 33554432 | tf_op jit(solution)/shard_map/last/pallas_call | solution.py:357
  119.5 1.4 scatter_custom_fusion
  124.5 7.7 %all-to-all-start.2 = ((bf16[32,112,128]{2,1,0:T(8,128)(2,1)}), bf16[32,112,128]{2,1,0:T(8,128)(2,1)S(1)}, u32[]{:S(2)}, u32[]{:S(2)}) async-start(bf16[32,112,128]{2,1,0:T(8,128)(2,1)} %pad_maximum_fusion), calls=%async_computation.2 | async-start | bytes 1835008 | tf_op jit(solution)/shard_map/all_to_all | solution.py:596
  132.9 14.7 %sums.1 = (bf16[4,4,4,304,128]{4,3,2,1,0:T(8,128)(2,1)}, bf16[4,4,4,272,128]{4,3,2,1,0:T(8,128)(2,1)}, bf16[4,4,4,192,128]{4,3,2,1,0:T(8,128)(2,1)}, bf16[2,4,30...) custom-call(s32[2]{0:T(128)} %pad_add_fusion.at_ref, ...), custom_call_target="tpu_custom_call" | custom-call | flops 10000000000 | bytes 25165824 | tf_op jit(solution)/shard_map/sums/pallas_call | solution.py:450
  147.6 2.5 collective-permute-start.10
  150.1 1.2 collective-permute-start.4
  151.3 1.5 collective-permute-start.6
  153.7 3.9 %all-to-all-start.3 = ((bf16[4,4,4,192,128]{4,3,2,1,0:T(8,128)(2,1)}), bf16[4,4,4,192,128]{4,3,2,1,0:T(8,128)(2,1)S(1)}, u32[]{:S(2)}, u32[]{:S(2)}) async-start(bf16[4,4,4,192,128]{4,3,2,1,0:T(8,128)(2,1)} %get-tuple-element.71), calls=%async_computation.3 | async-start | bytes 6291456 | tf_op jit(solution)/shard_map/all_to_all | solution.py:603
  157.6 3.8 %collective-permute-done.10 = bf16[2,4,272,128]{3,2,1,0:T(8,128)(2,1)} collective-permute-done((bf16[2,4,272,128]{3,2,1,0:T(8,128)(2,1)}, bf16[2,4,272,128]{3,2,1,0:T(8,128)(2,1)}, u32[]{:S(2)}, u32[]{:S(2)}) %collective-permute-start.10) | collective-permute-done | bytes 557088 | tf_op jit(solution)/shard_map/ppermute | solution.py:524
  161.4 3.1 %collective-permute-done.8 = bf16[2,4,272,128]{3,2,1,0:T(8,128)(2,1)} collective-permute-done((bf16[2,4,272,128]{3,2,1,0:T(8,128)(2,1)}, bf16[2,4,272,128]{3,2,1,0:T(8,128)(2,1)}, u32[]{:S(2)}, u32[]{:S(2)}) %collective-permute-start.8) | collective-permute-done | bytes 557088 | tf_op jit(solution)/shard_map/ppermute | solution.py:524
  164.4 3.8 %fusion.5 = (bf16[4,4,272,128]{3,2,1,0:T(8,128)(2,1)}, bf16[4,4,272,128]{3,2,1,0:T(8,128)(2,1)}) fusion(bf16[2,4,272,128]{3,2,1,0:T(8,128)(2,1)} %collective-permute-done.8, bf16[4,4,4,272,128]{4,3,2,1,0:T(8,128)(2,1)} %get-tuple-element.64, bf16[2,4,272,128]{3,2,1,0:T(8,128)(2,1)} %collective-permute-done.10), kind=kLoop, calls=%fused_computation.14 | loop fusion | flops 4456448 | bytes 5570560 | tf_op jit(solution)/shard_map/convert_element_type | solution.py:531
  169.6 3.0 %fusion.1 = (bf16[4,4,304,128]{3,2,1,0:T(8,128)(2,1)}, bf16[4,4,304,128]{3,2,1,0:T(8,128)(2,1)}) fusion(bf16[2,4,304,128]{3,2,1,0:T(8,128)(2,1)} %collective-permute-done.4, bf16[4,4,4,304,128]{4,3,2,1,0:T(8,128)(2,1)S(1)} %copy-done.5, bf16[2,4,304,128]{3,2,1,0:T(8,128)(2,1)} %collective-permute-done.6), kind=kLoop, calls=%fused_computation.7 | loop fusion | flops 4980736 | bytes 6225920 | tf_op jit(solution)/shard_map/convert_element_type | solution.py:531
  172.7 1.2 collective-permute-start.5
  173.9 1.5 collective-permute-start.7
  175.4 1.6 convert_reduce_fusion
  177.1 15.2 %collective-permute-done.11 = bf16[4,4,272,128]{3,2,1,0:T(8,128)(2,1)} collective-permute-done((bf16[4,4,272,128]{3,2,1,0:T(8,128)(2,1)}, bf16[4,4,272,128]{3,2,1,0:T(8,128)(2,1)}, u32[]{:S(2)}, u32[]{:S(2)}) %collective-permute-start.11) | collective-permute-done | bytes 1114144 | tf_op jit(solution)/shard_map/ppermute | solution.py:524
  192.3 1.5 collective-permute-done.9
  193.8 3.4 %fusion.7 = bf16[4,4,272,128]{3,2,1,0:T(8,128)(2,1)} fusion(bf16[4,4,272,128]{3,2,1,0:T(8,128)(2,1)} %collective-permute-done.11, bf16[4,4,272,128]{3,2,1,0:T(8,128)(2,1)} %collective-permute-done.9, bf16[4,4,4,272,128]{4,3,2,1,0:T(8,128)(2,1)} %get-tuple-element.64), kind=kLoop, calls=%fused_computation.17 | loop fusion | flops 3342336 | bytes 4456448 | tf_op jit(solution)/shard_map/convert_element_type | solution.py:531
  197.2 3.1 %collective-permute-done.5 = bf16[4,4,304,128]{3,2,1,0:T(8,128)(2,1)} collective-permute-done((bf16[4,4,304,128]{3,2,1,0:T(8,128)(2,1)}, bf16[4,4,304,128]{3,2,1,0:T(8,128)(2,1)}, u32[]{:S(2)}, u32[]{:S(2)}) %collective-permute-start.5) | collective-permute-done | bytes 1245216 | tf_op jit(solution)/shard_map/ppermute | solution.py:524
  200.3 3.6 %fusion.3 = bf16[4,4,304,128]{3,2,1,0:T(8,128)(2,1)} fusion(bf16[4,4,304,128]{3,2,1,0:T(8,128)(2,1)} %collective-permute-done.7, bf16[4,4,304,128]{3,2,1,0:T(8,128)(2,1)} %collective-permute-done.5, bf16[4,4,4,304,128]{4,3,2,1,0:T(8,128)(2,1)} %get-tuple-element.61), kind=kLoop, calls=%fused_computation.10 | loop fusion | flops 3735552 | bytes 4980736 | tf_op jit(solution)/shard_map/convert_element_type | solution.py:531
  203.9 1.7 reduce_sum.54
  205.5 2.6 collective-permute-start.21
  208.1 5.3 %all-to-all-start.4 = ((bf16[16,192,128]{2,1,0:T(8,128)(2,1)}), bf16[16,192,128]{2,1,0:T(8,128)(2,1)S(1)}, u32[]{:S(2)}, u32[]{:S(2)}) async-start(bf16[16,192,128]{2,1,0:T(8,128)(2,1)} %bitcast.91), calls=%async_computation.4 | async-start | bytes 1572864 | tf_op jit(solution)/shard_map/all_to_all | solution.py:610
  214.4 1.4 collective-permute-start.16
  215.8 1.3 collective-permute-start.18
  217.2 1.4 collective-permute-start.12
  218.6 1.3 collective-permute-start.14
  220.0 5.5 %collective-permute-start.22 = (f32[264,128]{1,0:T(8,128)S(1)}, f32[264,128]{1,0:T(8,128)S(1)}, u32[]{:S(2)}, u32[]{:S(2)}) collective-permute-start(f32[264,128]{1,0:T(8,128)S(1)} %add.151), channel_id=1, source_target_pairs={{0,1},{1,0},{2,3},{3,2},{4,5},{5,4},{6,7},{7,6},{8,9},{9,8},{10,11... | collective-permute-start | bytes 405512 | tf_op jit(solution)/shard_map/ppermute | solution.py:614
  225.4 2.2 collective-permute-done.18
  227.8 2.8 %collective-permute-start.19 = (bf16[4,272,128]{2,1,0:T(8,128)(2,1)S(1)}, bf16[4,272,128]{2,1,0:T(8,128)(2,1)S(1)}, u32[]{:S(2)}, u32[]{:S(2)}) collective-permute-start(bf16[4,272,128]{2,1,0:T(8,128)(2,1)S(1)} %get-tuple-element.96), channel_id=1, source_target_pairs={{0,96},{32,0},{64,32},{96,64},{1,97},{33,1},{65,33},{97,65},{2,98}... | collective-permute-start | bytes 835592 | tf_op jit(solution)/shard_map/ppermute | solution.py:524
  231.5 2.7 collective-permute-start.15
  236.3 3.4 %collective-permute-done.13 = bf16[4,304,128]{2,1,0:T(8,128)(2,1)} collective-permute-done((bf16[4,304,128]{2,1,0:T(8,128)(2,1)}, bf16[4,304,128]{2,1,0:T(8,128)(2,1)}, u32[]{:S(2)}, u32[]{:S(2)}) %collective-permute-start.13) | collective-permute-done | bytes 311328 | tf_op jit(solution)/shard_map/ppermute | solution.py:524
  239.8 1.2 fusion.11
  241.2 15.6 %all_to_all.30 = bf16[4,2,576,128]{3,2,1,0:T(8,128)(2,1)S(1)} all-to-all(bf16[4,2,576,128]{3,2,1,0:T(8,128)(2,1)S(1)} %bitcast.90), channel_id=1, replica_groups=mesh['z'=4,'x'=4,'yl'=2,'yh'=2,'c'=2] {'yl','yh'}, dimensions={0} | all-to-all | bytes 2359296 | tf_op jit(solution)/shard_map/all_to_all | solution.py:625
  257.2 4.1 %collective-permute-start.23 = (bf16[2,768,128]{2,1,0:T(8,128)(2,1)S(1)}, bf16[2,768,128]{2,1,0:T(8,128)(2,1)S(1)}, u32[]{:S(2)}, u32[]{:S(2)}) collective-permute-start(bf16[2,768,128]{2,1,0:T(8,128)(2,1)S(1)} %get-tuple-element.100), channel_id=1, source_target_pairs={{0,1},{1,0},{2,3},{3,2},{4,5},{5,4},{6,7},{7,6},{8,9},{9,8},{10,11... | collective-permute-start | bytes 1179656 | tf_op jit(solution)/shard_map/ppermute | solution.py:628
  266.1 6.0 %update.1 = (f32[192,2048]{1,0:T(8,128)}, f32[1,2048]{1,0:T(1,128)}) custom-call(s32[1,2048]{1,0:T(1,128)} %bitcast.103, bf16[2,2,768,128]{3,2,1,0:T(8,128)(2,1)} %maximum_select_fusion.sum_ref, f32[192,2048]{1,0:T(8,128)} %bitcast.104, f32[1,2048]{1,0:T(1,128)} %bitcast.105), custom_call_target="tpu_custom_call" | custom-call | flops 4000000000 | bytes 4718592 | tf_op jit(solution)/shard_map/update/pallas_call | solution.py:495
  (116 shorter events, 22.6 us)
Async XLA Ops:
  4.7 40.4 %all-to-all-start = ((bf16[32,272,128]{2,1,0:T(8,128)(2,1)}), bf16[32,272,128]{2,1,0:T(8,128)(2,1)S(1)}, u32[]{:S(2)}, u32[]{:S(2)}) async-start(bf16[32,272,128]{2,1,0:T(8,128)(2,1)} %broadcast_in_dim.28), calls=%async_computation | async-start | bytes 4456448 | tf_op jit(solution)/shard_map/all_to_all | solution.py:519
  45.1 19.9 %copy-start.6 = (bf16[32,272,128]{2,1,0:T(8,128)(2,1)}, bf16[32,272,128]{2,1,0:T(8,128)(2,1)S(1)}, u32[]{:S(2)}) copy-start(bf16[32,272,128]{2,1,0:T(8,128)(2,1)S(1)} %all-to-all-done.nraw_ref.near_ref) | copy-start | bytes 6684676
  45.1 19.9 %collective-permute-start = (bf16[32,272,128]{2,1,0:T(8,128)(2,1)S(1)}, bf16[32,272,128]{2,1,0:T(8,128)(2,1)}, u32[]{:S(2)}, u32[]{:S(2)}) collective-permute-start(bf16[32,272,128]{2,1,0:T(8,128)(2,1)S(1)} %all-to-all-done.nraw_ref.near_ref), channel_id=1, source_target_pairs={{0,1},{1,0},{2,3},{3,2},{4,5},{5,4},{6,7},{7,6},{8,9},{9,8},{10,11... | collective-permute-start | bytes 6684680 | tf_op jit(solution)/shard_map/ppermute | solution.py:572
  65.0 15.7 %copy-start.13 = (s32[256]{0:T(256)S(1)}, s32[256]{0:T(256)}, u32[]{:S(2)}) copy-start(s32[256]{0:T(256)} %param.15) | copy-start | bytes 3076
  80.6 5.8 %copy-start.7 = (bf16[32,256,128]{2,1,0:T(8,128)(2,1)S(1)}, bf16[32,256,128]{2,1,0:T(8,128)(2,1)}, u32[]{:S(2)}) copy-start(bf16[32,256,128]{2,1,0:T(8,128)(2,1)} %get-tuple-element.53) | copy-start | bytes 6291460
  80.6 4.4 %collective-permute-start.1 = (bf16[32,256,128]{2,1,0:T(8,128)(2,1)}, bf16[32,256,128]{2,1,0:T(8,128)(2,1)S(1)}, u32[]{:S(2)}, u32[]{:S(2)}) collective-permute-start(bf16[32,256,128]{2,1,0:T(8,128)(2,1)} %get-tuple-element.54), channel_id=1, source_target_pairs={{0,1},{1,0},{2,3},{3,2},{4,5},{5,4},{6,7},{7,6},{8,9},{9,8},{10,11... | collective-permute-start | bytes 6291464 | tf_op jit(solution)/shard_map/ppermute | solution.py:585
  87.8 30.3 %all-to-all-start.1 = ((bf16[32,160,128]{2,1,0:T(8,128)(2,1)}), bf16[32,160,128]{2,1,0:T(8,128)(2,1)S(1)}, u32[]{:S(2)}, u32[]{:S(2)}) async-start(bf16[32,160,128]{2,1,0:T(8,128)(2,1)} %add_convert_fusion), calls=%async_computation.1 | async-start | bytes 2621440 | tf_op jit(solution)/shard_map/all_to_all | solution.py:590
  91.8 27.6 %copy-start.9 = (s32[128,256]{1,0:T(8,128)S(1)}, s32[128,256]{1,0:T(8,128)}, u32[]{:S(2)}) copy-start(s32[128,256]{1,0:T(8,128)} %param.14) | copy-start | bytes 393220
  118.1 5.2 %copy-start.10 = (f32[96,256]{1,0:T(8,128)S(1)}, f32[96,256]{1,0:T(8,128)}, u32[]{:S(2)}) copy-start(f32[96,256]{1,0:T(8,128)} %get-tuple-element.69) | copy-start | bytes 294916
  118.1 5.2 %copy-start.11 = (f32[16,256]{1,0:T(8,128)S(1)}, f32[16,256]{1,0:T(8,128)}, u32[]{:S(2)}) copy-start(f32[16,256]{1,0:T(8,128)} %get-tuple-element.70) | copy-start | bytes 49156
  118.1 1.1 copy-start
  119.2 13.1 %collective-permute-start.2 = (bf16[128,4,48,128]{3,2,1,0:T(8,128)(2,1)}, bf16[128,4,48,128]{3,2,1,0:T(8,128)(2,1)}, u32[]{:S(2)}, u32[]{:S(2)}) collective-permute-start(bf16[128,4,48,128]{3,2,1,0:T(8,128)(2,1)} %get-tuple-element.60), channel_id=1, source_target_pairs={{0,1},{1,0},{2,3},{3,2},{4,5},{5,4},{6,7},{7,6},{8,9},{9,8},{10,11... | collective-permute-start | bytes 18874376 | tf_op jit(solution)/shard_map/ppermute | solution.py:598
  122.4 9.9 %collective-permute-start.3 = (s32[64,2,128]{2,1,0:T(2,128)S(1)}, s32[64,2,128]{2,1,0:T(2,128)S(1)}, u32[]{:S(2)}, u32[]{:S(2)}) collective-permute-start(s32[64,2,128]{2,1,0:T(2,128)S(1)} %bitcast.100), channel_id=1, source_target_pairs={{0,1},{1,0},{2,3},{3,2},{4,5},{5,4},{6,7},{7,6},{8,9},{9,8},{10,11... | collective-permute-start | bytes 196616 | tf_op jit(solution)/shard_map/ppermute | solution.py:579
  124.5 28.3 %all-to-all-start.2 = ((bf16[32,112,128]{2,1,0:T(8,128)(2,1)}), bf16[32,112,128]{2,1,0:T(8,128)(2,1)S(1)}, u32[]{:S(2)}, u32[]{:S(2)}) async-start(bf16[32,112,128]{2,1,0:T(8,128)(2,1)} %pad_maximum_fusion), calls=%async_computation.2 | async-start | bytes 1835008 | tf_op jit(solution)/shard_map/all_to_all | solution.py:596
  132.2 0.6 copy-start.14
  147.6 13.8 %collective-permute-start.10 = (bf16[2,4,272,128]{3,2,1,0:T(8,128)(2,1)}, bf16[2,4,272,128]{3,2,1,0:T(8,128)(2,1)}, u32[]{:S(2)}, u32[]{:S(2)}) collective-permute-start(bf16[2,4,272,128]{3,2,1,0:T(8,128)(2,1)} %get-tuple-element.66), channel_id=1, source_target_pairs={{0,24},{8,0},{16,8},{24,16},{1,25},{9,1},{17,9},{25,17},{2,26},{10... | collective-permute-start | bytes 1671176 | tf_op jit(solution)/shard_map/ppermute | solution.py:524
  150.1 14.3 %collective-permute-start.8 = (bf16[2,4,272,128]{3,2,1,0:T(8,128)(2,1)}, bf16[2,4,272,128]{3,2,1,0:T(8,128)(2,1)}, u32[]{:S(2)}, u32[]{:S(2)}) collective-permute-start(bf16[2,4,272,128]{3,2,1,0:T(8,128)(2,1)} %get-tuple-element.65), channel_id=1, source_target_pairs={{0,8},{8,16},{16,24},{24,0},{1,9},{9,17},{17,25},{25,1},{2,10},{10... | collective-permute-start | bytes 1671176 | tf_op jit(solution)/shard_map/ppermute | solution.py:524
  150.1 19.6 %collective-permute-start.4 = (bf16[2,4,304,128]{3,2,1,0:T(8,128)(2,1)}, bf16[2,4,304,128]{3,2,1,0:T(8,128)(2,1)}, u32[]{:S(2)}, u32[]{:S(2)}) collective-permute-start(bf16[2,4,304,128]{3,2,1,0:T(8,128)(2,1)} %get-tuple-element.62), channel_id=1, source_target_pairs={{0,32},{32,64},{64,96},{96,0},{1,33},{33,65},{65,97},{97,1},{2,34}... | collective-permute-start | bytes 1867784 | tf_op jit(solution)/shard_map/ppermute | solution.py:524
  151.3 18.4 %collective-permute-start.6 = (bf16[2,4,304,128]{3,2,1,0:T(8,128)(2,1)}, bf16[2,4,304,128]{3,2,1,0:T(8,128)(2,1)}, u32[]{:S(2)}, u32[]{:S(2)}) collective-permute-start(bf16[2,4,304,128]{3,2,1,0:T(8,128)(2,1)} %get-tuple-element.63), channel_id=1, source_target_pairs={{0,96},{32,0},{64,32},{96,64},{1,97},{33,1},{65,33},{97,65},{2,98}... | collective-permute-start | bytes 1867784 | tf_op jit(solution)/shard_map/ppermute | solution.py:524
  152.8 0.9 copy-start.3
  153.7 50.2 %all-to-all-start.3 = ((bf16[4,4,4,192,128]{4,3,2,1,0:T(8,128)(2,1)}), bf16[4,4,4,192,128]{4,3,2,1,0:T(8,128)(2,1)S(1)}, u32[]{:S(2)}, u32[]{:S(2)}) async-start(bf16[4,4,4,192,128]{4,3,2,1,0:T(8,128)(2,1)} %get-tuple-element.71), calls=%async_computation.3 | async-start | bytes 6291456 | tf_op jit(solution)/shard_map/all_to_all | solution.py:603
  164.4 5.2 %copy-start.5 = (bf16[4,4,4,304,128]{4,3,2,1,0:T(8,128)(2,1)S(1)}, bf16[4,4,4,304,128]{4,3,2,1,0:T(8,128)(2,1)}, u32[]{:S(2)}) copy-start(bf16[4,4,4,304,128]{4,3,2,1,0:T(8,128)(2,1)} %get-tuple-element.61) | copy-start | bytes 14942212
  168.2 24.1 %collective-permute-start.11 = (bf16[4,4,272,128]{3,2,1,0:T(8,128)(2,1)}, bf16[4,4,272,128]{3,2,1,0:T(8,128)(2,1)}, u32[]{:S(2)}, u32[]{:S(2)}) collective-permute-start(bf16[4,4,272,128]{3,2,1,0:T(8,128)(2,1)} %get-tuple-element.90), channel_id=1, source_target_pairs={{0,24},{8,0},{16,8},{24,16},{1,25},{9,1},{17,9},{25,17},{2,26},{10... | collective-permute-start | bytes 3342344 | tf_op jit(solution)/shard_map/ppermute | solution.py:524
  168.5 25.4 %collective-permute-start.9 = (bf16[4,4,272,128]{3,2,1,0:T(8,128)(2,1)}, bf16[4,4,272,128]{3,2,1,0:T(8,128)(2,1)}, u32[]{:S(2)}, u32[]{:S(2)}) collective-permute-start(bf16[4,4,272,128]{3,2,1,0:T(8,128)(2,1)} %get-tuple-element.89), channel_id=1, source_target_pairs={{0,8},{8,16},{16,24},{24,0},{1,9},{9,17},{17,25},{25,1},{2,10},{10... | collective-permute-start | bytes 3342344 | tf_op jit(solution)/shard_map/ppermute | solution.py:524
  172.7 27.6 %collective-permute-start.5 = (bf16[4,4,304,128]{3,2,1,0:T(8,128)(2,1)}, bf16[4,4,304,128]{3,2,1,0:T(8,128)(2,1)}, u32[]{:S(2)}, u32[]{:S(2)}) collective-permute-start(bf16[4,4,304,128]{3,2,1,0:T(8,128)(2,1)} %get-tuple-element.87), channel_id=1, source_target_pairs={{0,32},{32,64},{64,96},{96,0},{1,33},{33,65},{65,97},{97,1},{2,34}... | collective-permute-start | bytes 3735560 | tf_op jit(solution)/shard_map/ppermute | solution.py:524
  173.9 26.4 %collective-permute-start.7 = (bf16[4,4,304,128]{3,2,1,0:T(8,128)(2,1)}, bf16[4,4,304,128]{3,2,1,0:T(8,128)(2,1)}, u32[]{:S(2)}, u32[]{:S(2)}) collective-permute-start(bf16[4,4,304,128]{3,2,1,0:T(8,128)(2,1)} %get-tuple-element.88), channel_id=1, source_target_pairs={{0,96},{32,0},{64,32},{96,64},{1,97},{33,1},{65,33},{97,65},{2,98}... | collective-permute-start | bytes 3735560 | tf_op jit(solution)/shard_map/ppermute | solution.py:524
  175.4 1.6 copy-start.4
  205.5 11.6 %copy-start.1 = (bf16[4,4,304,128]{3,2,1,0:T(8,128)(2,1)S(1)}, bf16[4,4,304,128]{3,2,1,0:T(8,128)(2,1)}, u32[]{:S(2)}) copy-start(bf16[4,4,304,128]{3,2,1,0:T(8,128)(2,1)} %fusion.3) | copy-start | bytes 3735556
  205.5 22.1 %copy-start.2 = (bf16[4,4,272,128]{3,2,1,0:T(8,128)(2,1)S(1)}, bf16[4,4,272,128]{3,2,1,0:T(8,128)(2,1)}, u32[]{:S(2)}) copy-start(bf16[4,4,272,128]{3,2,1,0:T(8,128)(2,1)} %fusion.7) | copy-start | bytes 3342340
  205.5 14.4 %collective-permute-start.21 = (f32[264,128]{1,0:T(8,128)S(1)}, f32[264,128]{1,0:T(8,128)S(1)}, u32[]{:S(2)}, u32[]{:S(2)}) collective-permute-start(f32[264,128]{1,0:T(8,128)S(1)} %fusion.16), channel_id=1, source_target_pairs={{0,2},{2,0},{1,3},{3,1},{4,6},{6,4},{5,7},{7,5},{8,10},{10,8},{9,1... | collective-permute-start | bytes 405512 | tf_op jit(solution)/shard_map/ppermute | solution.py:613
  208.1 27.5 %all-to-all-start.4 = ((bf16[16,192,128]{2,1,0:T(8,128)(2,1)}), bf16[16,192,128]{2,1,0:T(8,128)(2,1)S(1)}, u32[]{:S(2)}, u32[]{:S(2)}) async-start(bf16[16,192,128]{2,1,0:T(8,128)(2,1)} %bitcast.91), calls=%async_computation.4 | async-start | bytes 1572864 | tf_op jit(solution)/shard_map/all_to_all | solution.py:610
  214.4 11.0 %collective-permute-start.16 = (bf16[2,272,128]{2,1,0:T(8,128)(2,1)S(1)}, bf16[2,272,128]{2,1,0:T(8,128)(2,1)S(1)}, u32[]{:S(2)}, u32[]{:S(2)}) collective-permute-start(bf16[2,272,128]{2,1,0:T(8,128)(2,1)S(1)} %get-tuple-element.97), channel_id=1, source_target_pairs={{0,32},{32,64},{64,96},{96,0},{1,33},{33,65},{65,97},{97,1},{2,34}... | collective-permute-start | bytes 417800 | tf_op jit(solution)/shard_map/ppermute | solution.py:524
  215.8 11.8 %collective-permute-start.18 = (bf16[2,272,128]{2,1,0:T(8,128)(2,1)S(1)}, bf16[2,272,128]{2,1,0:T(8,128)(2,1)S(1)}, u32[]{:S(2)}, u32[]{:S(2)}) collective-permute-start(bf16[2,272,128]{2,1,0:T(8,128)(2,1)S(1)} %get-tuple-element.98), channel_id=1, source_target_pairs={{0,96},{32,0},{64,32},{96,64},{1,97},{33,1},{65,33},{97,65},{2,98}... | collective-permute-start | bytes 417800 | tf_op jit(solution)/shard_map/ppermute | solution.py:524
  217.2 13.4 %collective-permute-start.12 = (bf16[2,304,128]{2,1,0:T(8,128)(2,1)S(1)}, bf16[2,304,128]{2,1,0:T(8,128)(2,1)S(1)}, u32[]{:S(2)}, u32[]{:S(2)}) collective-permute-start(bf16[2,304,128]{2,1,0:T(8,128)(2,1)S(1)} %get-tuple-element.93), channel_id=1, source_target_pairs={{0,8},{8,16},{16,24},{24,0},{1,9},{9,17},{17,25},{25,1},{2,10},{10... | collective-permute-start | bytes 466952 | tf_op jit(solution)/shard_map/ppermute | solution.py:524
  218.6 12.0 %collective-permute-start.14 = (bf16[2,304,128]{2,1,0:T(8,128)(2,1)S(1)}, bf16[2,304,128]{2,1,0:T(8,128)(2,1)S(1)}, u32[]{:S(2)}, u32[]{:S(2)}) collective-permute-start(bf16[2,304,128]{2,1,0:T(8,128)(2,1)S(1)} %get-tuple-element.94), channel_id=1, source_target_pairs={{0,24},{8,0},{16,8},{24,16},{1,25},{9,1},{17,9},{25,17},{2,26},{10... | collective-permute-start | bytes 466952 | tf_op jit(solution)/shard_map/ppermute | solution.py:524
  220.0 14.2 %collective-permute-start.22 = (f32[264,128]{1,0:T(8,128)S(1)}, f32[264,128]{1,0:T(8,128)S(1)}, u32[]{:S(2)}, u32[]{:S(2)}) collective-permute-start(f32[264,128]{1,0:T(8,128)S(1)} %add.151), channel_id=1, source_target_pairs={{0,1},{1,0},{2,3},{3,2},{4,5},{5,4},{6,7},{7,6},{8,9},{9,8},{10,11... | collective-permute-start | bytes 405512 | tf_op jit(solution)/shard_map/ppermute | solution.py:614
  227.7 7.8 %collective-permute-start.17 = (bf16[4,272,128]{2,1,0:T(8,128)(2,1)S(1)}, bf16[4,272,128]{2,1,0:T(8,128)(2,1)S(1)}, u32[]{:S(2)}, u32[]{:S(2)}) collective-permute-start(bf16[4,272,128]{2,1,0:T(8,128)(2,1)S(1)} %get-tuple-element.95), channel_id=1, source_target_pairs={{0,32},{32,64},{64,96},{96,0},{1,33},{33,65},{65,97},{97,1},{2,34}... | collective-permute-start | bytes 835592 | tf_op jit(solution)/shard_map/ppermute | solution.py:524
  227.8 7.7 %collective-permute-start.19 = (bf16[4,272,128]{2,1,0:T(8,128)(2,1)S(1)}, bf16[4,272,128]{2,1,0:T(8,128)(2,1)S(1)}, u32[]{:S(2)}, u32[]{:S(2)}) collective-permute-start(bf16[4,272,128]{2,1,0:T(8,128)(2,1)S(1)} %get-tuple-element.96), channel_id=1, source_target_pairs={{0,96},{32,0},{64,32},{96,64},{1,97},{33,1},{65,33},{97,65},{2,98}... | collective-permute-start | bytes 835592 | tf_op jit(solution)/shard_map/ppermute | solution.py:524
  231.5 8.3 %collective-permute-start.13 = (bf16[4,304,128]{2,1,0:T(8,128)(2,1)}, bf16[4,304,128]{2,1,0:T(8,128)(2,1)}, u32[]{:S(2)}, u32[]{:S(2)}) collective-permute-start(bf16[4,304,128]{2,1,0:T(8,128)(2,1)} %get-tuple-element.91), channel_id=1, source_target_pairs={{0,8},{8,16},{16,24},{24,0},{1,9},{9,17},{17,25},{25,1},{2,10},{10... | collective-permute-start | bytes 933896 | tf_op jit(solution)/shard_map/ppermute | solution.py:524
  231.5 8.3 %collective-permute-start.15 = (bf16[4,304,128]{2,1,0:T(8,128)(2,1)}, bf16[4,304,128]{2,1,0:T(8,128)(2,1)}, u32[]{:S(2)}, u32[]{:S(2)}) collective-permute-start(bf16[4,304,128]{2,1,0:T(8,128)(2,1)} %get-tuple-element.92), channel_id=1, source_target_pairs={{0,24},{8,0},{16,8},{24,16},{1,25},{9,1},{17,9},{25,17},{2,26},{10... | collective-permute-start | bytes 933896 | tf_op jit(solution)/shard_map/ppermute | solution.py:524
  235.7 5.2 %collective-permute-start.20 = (bf16[192,128]{1,0:T(8,128)(2,1)S(1)}, bf16[192,128]{1,0:T(8,128)(2,1)S(1)}, u32[]{:S(2)}, u32[]{:S(2)}) collective-permute-start(bf16[192,128]{1,0:T(8,128)(2,1)S(1)} %reduce_sum.57), channel_id=1, source_target_pairs={{0,2},{2,0},{1,3},{3,1},{4,6},{6,4},{5,7},{7,5},{8,10},{10,8},{9,1... | collective-permute-start | bytes 147464 | tf_op jit(solution)/shard_map/ppermute | solution.py:618
  256.8 4.5 %copy-start.12 = (s32[8,256]{1,0:T(8,128)S(1)}, s32[8,256]{1,0:T(8,128)}, u32[]{:S(2)}) copy-start(s32[8,256]{1,0:T(8,128)} %param.16) | copy-start | bytes 24580
  256.8 5.1 %copy-start.8 = (f32[2,256,128]{2,1,0:T(8,128)S(1)}, f32[2,256,128]{2,1,0:T(8,128)}, u32[]{:S(2)}) copy-start(f32[2,256,128]{2,1,0:T(8,128)} %reverse_select_fusion) | copy-start | bytes 786436
  257.2 7.9 %collective-permute-start.23 = (bf16[2,768,128]{2,1,0:T(8,128)(2,1)S(1)}, bf16[2,768,128]{2,1,0:T(8,128)(2,1)S(1)}, u32[]{:S(2)}, u32[]{:S(2)}) collective-permute-start(bf16[2,768,128]{2,1,0:T(8,128)(2,1)S(1)} %get-tuple-element.100), channel_id=1, source_target_pairs={{0,1},{1,0},{2,3},{3,2},{4,5},{5,4},{6,7},{7,6},{8,9},{9,8},{10,11... | collective-permute-start | bytes 1179656 | tf_op jit(solution)/shard_map/ppermute | solution.py:628

commit v9 on v8

--- a/solution.py
+++ b/solution.py
@@ -564,19 +564,22 @@
     near = jnp.concatenate([lax.dynamic_slice_in_dim(shard, core * rows, rows, 0), small], axis=0)
     x3 = unfold(samples, n, 0)
     g2 = unfold(out_grad, nl, out_grad.shape[1] // D // nl - 1)
-    near, x3, g2 = lax.optimization_barrier((gather(near), x3, g2))
-    small = near[:, rows : rows + per].reshape(n, 128)
-    proj_f = small[:, :K]
-    gain_t = small[:, K : 2 * K].T.astype(F32)
-    w_lcb_f = small[:, 2 * K : 2 * K + nl]
-    far = lax.ppermute(near, "c", SWAP)
-
     quad = per // 2
     spot = table_owner // per * quad + table_owner % quad
     spot = jnp.where((table_owner % per) // quad == core, spot, spot + n // 2)
     order = jnp.zeros((n,), jnp.int32).at[spot].set(jnp.arange(n, dtype=jnp.int32))
     ids = jnp.take(row_ids.T, order, axis=0).reshape(2, n // 4, 2, count)
     other_ids = lax.ppermute(ids[1], "c", SWAP)
+    mine_ids = ids[0]
+    near, x3, g2, mine_ids, other_ids = lax.optimization_barrier(
+        (gather(near), x3, g2, mine_ids, other_ids)
+    )
+    small = near[:, rows : rows + per].reshape(n, 128)
+    proj_f = small[:, :K]
+    gain_t = small[:, K : 2 * K].T.astype(F32)
+    w_lcb_f = small[:, 2 * K : 2 * K + nl]
+    far = lax.ppermute(near, "c", SWAP)
+
 
     wt, score, dl, xh, inv = forward(x3, g2, proj_f, w_lcb_f)
     w_keep, w_send, g_gain, dfm = batch(
@@ -597,7 +600,7 @@
 
     other = lax.ppermute(send, "c", SWAP)
     at = jnp.stack([lax.axis_index("z"), lax.axis_index("x")]).astype(jnp.int32)
-    a, b, c, af, ab, bf, bb = sums(at, keep, other, ids[0], other_ids)
+    a, b, c, af, ab, bf, bb = sums(at, keep, other, mine_ids, other_ids)
     c, w_second = lax.optimization_barrier((c, w_second))
     a, b = ring_sums([("z", a), ("x", b)], [(af, ab), (bf, bb)])
     c = lax.all_to_all(c, ("yl", "yh"), 0, 0, tiled=True)

time: 273 us -> 272 us (level)
  waiting for transfers between devices: 43.1 us -> 40 us
    all_to_all x1, waiting for transfers between devices: 6.68 us -> 2.16 us  [gather(): lax.all_to_all(jnp.broadcast_to(a[None], (n,) + a.shape), WIDE, 0, 0, til...]
  transfers between devices with their start and end apart: 29 -> 29, of which waited for: 10 -> 10; matrix products, arithmetic and copies ran while one was open for 11% -> 12% of each run, Pallas kernels for 30% -> 30%
where the time goes in v9:
time: 272 us; the launch traced here: 270 us
  Pallas kernels  102 us (38%)
  starting transfers between devices  68.1 us (25%)
  waiting for transfers between devices  40 us (15%)
  other arithmetic  30.6 us (11%)
  blocking collectives  15.7 us (6%)
  local copies, waits for them, and re-layouts  12.6 us (5%)
    ppermute x16, waiting for transfers between devices, ring_step(): return lax.ppermute(v, axis, [(i, (i + by) % n) for i in range(n)])  33.7 us
    pallas_call x1, Pallas kernels, last(): pl.pallas_call(last_kernel, grid_spec=grid, out_shape=[half, half, jax.Sh...  26.1 us
    pallas_call x2, Pallas kernels, unfold(): pl.pallas_call(unfold_kernel, grid=(count // rows,), in_specs=[pl.BlockSp...  24 us
    ppermute x16, starting transfers between devices, ring_step(): return lax.ppermute(v, axis, [(i, (i + by) % n) for i in range(n)])  20.5 us
    convert_element_type x10, other arithmetic, add(): return total.astype(BF16)  18.9 us
    pallas_call x1, Pallas kernels, first(): pl.pallas_call(first_kernel, grid=(count // rows,), in_specs=[pl.BlockSpe...  16.1 us
    all_to_all x1, blocking collectives, body(): ab = lax.all_to_all(ab, ('yl', 'yh'), 0, 0, tiled=True)  15.7 us
    pallas_call x1, Pallas kernels, batch(): pl.pallas_call(batch_kernel, grid=(total // rows,), in_specs=[pl.BlockSpe...  15.6 us
  transfers between devices with their start and end apart: 29, of which 10 were waited for; matrix products, arithmetic and copies ran while one was open for 12% of the time, Pallas kernels for 30%

profile of v9, /device:TPU:1, one launch (start us, length us, event | category | flops | bytes accessed | tf_op | source)
XLA Modules:
  0.0 270.4 jit_solution(16253754250871234166)
XLA Ops:
  3.0 1.7 broadcast_in_dim.28
  4.7 9.9 %all-to-all-start = ((bf16[32,272,128]{2,1,0:T(8,128)(2,1)}), bf16[32,272,128]{2,1,0:T(8,128)(2,1)S(1)}, u32[]{:S(2)}, u32[]{:S(2)}) async-start(bf16[32,272,128]{2,1,0:T(8,128)(2,1)} %broadcast_in_dim.28), calls=%async_computation | async-start | bytes 4456448 | tf_op jit(solution)/shard_map/all_to_all | solution.py:519
  15.3 1.4 scatter_custom_fusion
  19.1 17.7 %unfold.2.x_ref = bf16[128,256,256]{2,1,0:T(8,128)(2,1)} custom-call(bf16[128,49152]{1,0:T(8,128)(2,1)} %x_ref.2), custom_call_target="tpu_custom_call" | custom-call | flops 1000000000 | bytes 29491200 | tf_op jit(solution)/shard_map/unfold/pallas_call | solution.py:67
  36.8 6.3 %unfold.3.g_ref = bf16[128,64,256]{2,1,0:T(8,128)(2,1)} custom-call(bf16[128,24576]{1,0:T(8,128)(2,1)} %g_ref.1), custom_call_target="tpu_custom_call" | custom-call | flops 1000000000 | bytes 7372800 | tf_op jit(solution)/shard_map/unfold/pallas_call | solution.py:67
  43.1 2.2 all-to-all-done.nraw_ref.near_ref
  45.3 2.1 collective-permute-start.1
  49.1 16.1 %first.1 = (bf16[128,32,256]{2,1,0:T(8,128)(2,1)}, bf16[128,64,256]{2,1,0:T(8,128)(2,1)}, f32[16,128,256]{2,1,0:T(8,128)}, f32[128,128]{1,0:T(8,128)}) custom-call(bf16[128,256,256]{2,1,0:T(8,128)(2,1)} %unfold.2.x_ref, bf16[128,64,256]{2,1,0:T(8,128)(2,1)} %unfold.3.g_ref, bf16[80,256]{1,0:T(8,128)(2,1)} %pad_maximum_fusion.6.w_ref.wt_ref), custom_call_target="tpu_custom_call" | custom-call | flops 20000000000 | bytes 16777216 | tf_op jit(solution)/shard_map/first/pallas_call | solution.py:122
  65.2 15.6 %batch.1 = (bf16[32,256,128]{2,1,0:T(8,128)(2,1)}, bf16[32,256,128]{2,1,0:T(8,128)(2,1)}, f32[16,256]{1,0:T(8,128)}, f32[16,128,256]{2,1,0:T(8,128)}) custom-call(s32[1]{0:T(128)} %bitcast.8.core_ref, f32[16,128,256]{2,1,0:T(8,128)} %get-tuple-element.53.xh_ref, f32[128,128]{1,0:T(8,128)} %get-tuple-element.54.inv_ref, ...), custom_call_target="tpu_custom_call" | custom-call | flops 20000000000 | bytes 20000000 | tf_op jit(solution)/shard_map/batch/pallas_call | solution.py:239
  81.0 4.1 %collective-permute-done.2 = bf16[32,256,128]{2,1,0:T(8,128)(2,1)S(1)} collective-permute-done((bf16[32,256,128]{2,1,0:T(8,128)(2,1)}, bf16[32,256,128]{2,1,0:T(8,128)(2,1)S(1)}, u32[]{:S(2)}, u32[]{:S(2)}) %collective-permute-start.2) | collective-permute-done | bytes 2097184 | tf_op jit(solution)/shard_map/ppermute | solution.py:588
  85.1 1.4 add_convert_fusion.1
  86.5 1.5 add_convert_fusion
  88.0 4.3 %all-to-all-start.1 = ((bf16[32,160,128]{2,1,0:T(8,128)(2,1)}), bf16[32,160,128]{2,1,0:T(8,128)(2,1)S(1)}, u32[]{:S(2)}, u32[]{:S(2)}) async-start(bf16[32,160,128]{2,1,0:T(8,128)(2,1)} %add_convert_fusion), calls=%async_computation.1 | async-start | bytes 2621440 | tf_op jit(solution)/shard_map/all_to_all | solution.py:593
  92.3 26.1 %last.1 = (bf16[128,4,48,128]{3,2,1,0:T(8,128)(2,1)}, bf16[128,4,48,128]{3,2,1,0:T(8,128)(2,1)}, f32[96,256]{1,0:T(8,128)}) custom-call(s32[256]{0:T(256)} %get-tuple-element.90.at_ref, bf16[128,256,256]{2,1,0:T(8,128)(2,1)} %unfold.2.x_ref, bf16[128,32,256]{2,1,0:T(8,128)(2,1)} %get-tuple-element.51.s_ref, bf16[128,64,256]{2,1,0:T(8,128)(2,1)} %get-tuple-element.52.dl_ref, ...), custom_call_target="tpu_custom_call" | custom-call | flops 20000000000 | bytes 33554432 | tf_op jit(solution)/shard_map/last/pallas_call | solution.py:357
  122.4 7.8 %all-to-all-start.2 = ((bf16[32,112,128]{2,1,0:T(8,128)(2,1)}), bf16[32,112,128]{2,1,0:T(8,128)(2,1)S(1)}, u32[]{:S(2)}, u32[]{:S(2)}) async-start(bf16[32,112,128]{2,1,0:T(8,128)(2,1)} %pad_maximum_fusion), calls=%async_computation.2 | async-start | bytes 1835008 | tf_op jit(solution)/shard_map/all_to_all | solution.py:599
  130.2 14.7 %sums.1 = (bf16[4,4,4,304,128]{4,3,2,1,0:T(8,128)(2,1)}, bf16[4,4,4,272,128]{4,3,2,1,0:T(8,128)(2,1)}, bf16[4,4,4,192,128]{4,3,2,1,0:T(8,128)(2,1)}, bf16[2,4,30...) custom-call(s32[2]{0:T(128)} %pad_add_fusion.at_ref, ...), custom_call_target="tpu_custom_call" | custom-call | flops 10000000000 | bytes 25165824 | tf_op jit(solution)/shard_map/sums/pallas_call | solution.py:450
  144.9 2.5 collective-permute-start.10
  147.4 1.2 collective-permute-start.4
  148.7 1.4 collective-permute-start.6
  151.0 3.9 %all-to-all-start.3 = ((bf16[4,4,4,192,128]{4,3,2,1,0:T(8,128)(2,1)}), bf16[4,4,4,192,128]{4,3,2,1,0:T(8,128)(2,1)S(1)}, u32[]{:S(2)}, u32[]{:S(2)}) async-start(bf16[4,4,4,192,128]{4,3,2,1,0:T(8,128)(2,1)} %get-tuple-element.75), calls=%async_computation.3 | async-start | bytes 6291456 | tf_op jit(solution)/shard_map/all_to_all | solution.py:606
  154.9 4.1 %collective-permute-done.10 = bf16[2,4,272,128]{3,2,1,0:T(8,128)(2,1)} collective-permute-done((bf16[2,4,272,128]{3,2,1,0:T(8,128)(2,1)}, bf16[2,4,272,128]{3,2,1,0:T(8,128)(2,1)}, u32[]{:S(2)}, u32[]{:S(2)}) %collective-permute-start.10) | collective-permute-done | bytes 557088 | tf_op jit(solution)/shard_map/ppermute | solution.py:524
  159.0 3.0 %collective-permute-done.8 = bf16[2,4,272,128]{3,2,1,0:T(8,128)(2,1)} collective-permute-done((bf16[2,4,272,128]{3,2,1,0:T(8,128)(2,1)}, bf16[2,4,272,128]{3,2,1,0:T(8,128)(2,1)}, u32[]{:S(2)}, u32[]{:S(2)}) %collective-permute-start.8) | collective-permute-done | bytes 557088 | tf_op jit(solution)/shard_map/ppermute | solution.py:524
  162.0 3.7 %fusion.5 = (bf16[4,4,272,128]{3,2,1,0:T(8,128)(2,1)}, bf16[4,4,272,128]{3,2,1,0:T(8,128)(2,1)}) fusion(bf16[2,4,272,128]{3,2,1,0:T(8,128)(2,1)} %collective-permute-done.8, bf16[4,4,4,272,128]{4,3,2,1,0:T(8,128)(2,1)} %get-tuple-element.68, bf16[2,4,272,128]{3,2,1,0:T(8,128)(2,1)} %collective-permute-done.10), kind=kLoop, calls=%fused_computation.14 | loop fusion | flops 4456448 | bytes 5570560 | tf_op jit(solution)/shard_map/convert_element_type | solution.py:531
  167.2 3.0 %fusion.1 = (bf16[4,4,304,128]{3,2,1,0:T(8,128)(2,1)}, bf16[4,4,304,128]{3,2,1,0:T(8,128)(2,1)}) fusion(bf16[2,4,304,128]{3,2,1,0:T(8,128)(2,1)} %collective-permute-done.4, bf16[4,4,4,304,128]{4,3,2,1,0:T(8,128)(2,1)S(1)} %copy-done.5, bf16[2,4,304,128]{3,2,1,0:T(8,128)(2,1)} %collective-permute-done.6), kind=kLoop, calls=%fused_computation.7 | loop fusion | flops 4980736 | bytes 6225920 | tf_op jit(solution)/shard_map/convert_element_type | solution.py:531
  170.3 1.3 collective-permute-start.5
  171.5 1.4 collective-permute-start.7
  173.0 1.6 convert_reduce_fusion
  174.7 15.5 %collective-permute-done.11 = bf16[4,4,272,128]{3,2,1,0:T(8,128)(2,1)} collective-permute-done((bf16[4,4,272,128]{3,2,1,0:T(8,128)(2,1)}, bf16[4,4,272,128]{3,2,1,0:T(8,128)(2,1)}, u32[]{:S(2)}, u32[]{:S(2)}) %collective-permute-start.11) | collective-permute-done | bytes 1114144 | tf_op jit(solution)/shard_map/ppermute | solution.py:524
  190.2 1.6 collective-permute-done.9
  191.8 3.4 %fusion.7 = bf16[4,4,272,128]{3,2,1,0:T(8,128)(2,1)} fusion(bf16[4,4,272,128]{3,2,1,0:T(8,128)(2,1)} %collective-permute-done.11, bf16[4,4,272,128]{3,2,1,0:T(8,128)(2,1)} %collective-permute-done.9, bf16[4,4,4,272,128]{4,3,2,1,0:T(8,128)(2,1)} %get-tuple-element.68), kind=kLoop, calls=%fused_computation.17 | loop fusion | flops 3342336 | bytes 4456448 | tf_op jit(solution)/shard_map/convert_element_type | solution.py:531
  195.1 3.0 %collective-permute-done.5 = bf16[4,4,304,128]{3,2,1,0:T(8,128)(2,1)} collective-permute-done((bf16[4,4,304,128]{3,2,1,0:T(8,128)(2,1)}, bf16[4,4,304,128]{3,2,1,0:T(8,128)(2,1)}, u32[]{:S(2)}, u32[]{:S(2)}) %collective-permute-start.5) | collective-permute-done | bytes 1245216 | tf_op jit(solution)/shard_map/ppermute | solution.py:524
  198.2 3.6 %fusion.3 = bf16[4,4,304,128]{3,2,1,0:T(8,128)(2,1)} fusion(bf16[4,4,304,128]{3,2,1,0:T(8,128)(2,1)} %collective-permute-done.7, bf16[4,4,304,128]{3,2,1,0:T(8,128)(2,1)} %collective-permute-done.5, bf16[4,4,4,304,128]{4,3,2,1,0:T(8,128)(2,1)} %get-tuple-element.65), kind=kLoop, calls=%fused_computation.10 | loop fusion | flops 3735552 | bytes 4980736 | tf_op jit(solution)/shard_map/convert_element_type | solution.py:531
  201.7 1.7 reduce_sum.54
  203.4 2.6 collective-permute-start.21
  206.0 5.3 %all-to-all-start.4 = ((bf16[16,192,128]{2,1,0:T(8,128)(2,1)}), bf16[16,192,128]{2,1,0:T(8,128)(2,1)S(1)}, u32[]{:S(2)}, u32[]{:S(2)}) async-start(bf16[16,192,128]{2,1,0:T(8,128)(2,1)} %bitcast.91), calls=%async_computation.4 | async-start | bytes 1572864 | tf_op jit(solution)/shard_map/all_to_all | solution.py:613
  212.4 1.4 collective-permute-start.16
  213.8 1.3 collective-permute-start.18
  215.2 1.4 collective-permute-start.12
  216.6 1.3 collective-permute-start.14
  217.9 5.4 %collective-permute-start.22 = (f32[264,128]{1,0:T(8,128)S(1)}, f32[264,128]{1,0:T(8,128)S(1)}, u32[]{:S(2)}, u32[]{:S(2)}) collective-permute-start(f32[264,128]{1,0:T(8,128)S(1)} %add.151), channel_id=1, source_target_pairs={{0,1},{1,0},{2,3},{3,2},{4,5},{5,4},{6,7},{7,6},{8,9},{9,8},{10,11... | collective-permute-start | bytes 405512 | tf_op jit(solution)/shard_map/ppermute | solution.py:617
  223.3 2.3 collective-permute-done.18
  225.8 3.0 %collective-permute-start.19 = (bf16[4,272,128]{2,1,0:T(8,128)(2,1)S(1)}, bf16[4,272,128]{2,1,0:T(8,128)(2,1)S(1)}, u32[]{:S(2)}, u32[]{:S(2)}) collective-permute-start(bf16[4,272,128]{2,1,0:T(8,128)(2,1)S(1)} %get-tuple-element.100), channel_id=1, source_target_pairs={{0,96},{32,0},{64,32},{96,64},{1,97},{33,1},{65,33},{97,65},{2,98}... | collective-permute-start | bytes 835592 | tf_op jit(solution)/shard_map/ppermute | solution.py:524
  230.5 1.8 collective-permute-start.15
  234.7 3.4 %collective-permute-done.13 = bf16[4,304,128]{2,1,0:T(8,128)(2,1)} collective-permute-done((bf16[4,304,128]{2,1,0:T(8,128)(2,1)}, bf16[4,304,128]{2,1,0:T(8,128)(2,1)}, u32[]{:S(2)}, u32[]{:S(2)}) %collective-permute-start.13) | collective-permute-done | bytes 311328 | tf_op jit(solution)/shard_map/ppermute | solution.py:524
  238.1 1.2 fusion.11
  239.6 15.7 %all_to_all.30 = bf16[4,2,576,128]{3,2,1,0:T(8,128)(2,1)S(1)} all-to-all(bf16[4,2,576,128]{3,2,1,0:T(8,128)(2,1)S(1)} %bitcast.90), channel_id=1, replica_groups=mesh['z'=4,'x'=4,'yl'=2,'yh'=2,'c'=2] {'yl','yh'}, dimensions={0} | all-to-all | bytes 2359296 | tf_op jit(solution)/shard_map/all_to_all | solution.py:628
  255.6 4.0 %collective-permute-start.23 = (bf16[2,768,128]{2,1,0:T(8,128)(2,1)S(1)}, bf16[2,768,128]{2,1,0:T(8,128)(2,1)S(1)}, u32[]{:S(2)}, u32[]{:S(2)}) collective-permute-start(bf16[2,768,128]{2,1,0:T(8,128)(2,1)S(1)} %get-tuple-element.104), channel_id=1, source_target_pairs={{0,1},{1,0},{2,3},{3,2},{4,5},{5,4},{6,7},{7,6},{8,9},{9,8},{10,11... | collective-permute-start | bytes 1179656 | tf_op jit(solution)/shard_map/ppermute | solution.py:631
  264.5 6.0 %update.1 = (f32[192,2048]{1,0:T(8,128)}, f32[1,2048]{1,0:T(1,128)}) custom-call(s32[1,2048]{1,0:T(1,128)} %bitcast.103, bf16[2,2,768,128]{3,2,1,0:T(8,128)(2,1)} %maximum_select_fusion.sum_ref, f32[192,2048]{1,0:T(8,128)} %bitcast.104, f32[1,2048]{1,0:T(1,128)} %bitcast.105), custom_call_target="tpu_custom_call" | custom-call | flops 4000000000 | bytes 4718592 | tf_op jit(solution)/shard_map/update/pallas_call | solution.py:495
  (114 shorter events, 24.6 us)
Async XLA Ops:
  4.7 9.9 %copy-start.9 = (s32[128,256]{1,0:T(8,128)S(1)}, s32[128,256]{1,0:T(8,128)}, u32[]{:S(2)}) copy-start(s32[128,256]{1,0:T(8,128)} %param.14) | copy-start | bytes 393220
  4.7 10.0 %copy-start.12 = (s32[256]{0:T(256)S(1)}, s32[256]{0:T(256)}, u32[]{:S(2)}) copy-start(s32[256]{0:T(256)} %param.15) | copy-start | bytes 3076
  4.7 40.5 %all-to-all-start = ((bf16[32,272,128]{2,1,0:T(8,128)(2,1)}), bf16[32,272,128]{2,1,0:T(8,128)(2,1)S(1)}, u32[]{:S(2)}, u32[]{:S(2)}) async-start(bf16[32,272,128]{2,1,0:T(8,128)(2,1)} %broadcast_in_dim.28), calls=%async_computation | async-start | bytes 4456448 | tf_op jit(solution)/shard_map/all_to_all | solution.py:519
  18.2 24.9 %collective-permute-start = (s32[64,2,128]{2,1,0:T(2,128)S(1)}, s32[64,2,128]{2,1,0:T(2,128)S(1)}, u32[]{:S(2)}, u32[]{:S(2)}) collective-permute-start(s32[64,2,128]{2,1,0:T(2,128)S(1)} %bitcast.100), channel_id=1, source_target_pairs={{0,1},{1,0},{2,3},{3,2},{4,5},{5,4},{6,7},{7,6},{8,9},{9,8},{10,11... | collective-permute-start | bytes 196616 | tf_op jit(solution)/shard_map/ppermute | solution.py:572
  43.1 22.0 %copy-start.13 = (s32[64,2,128]{2,1,0:T(2,128)}, s32[64,2,128]{2,1,0:T(2,128)S(1)}, u32[]{:S(2)}) copy-start(s32[64,2,128]{2,1,0:T(2,128)S(1)} %collective-permute-done.oid_ref) | copy-start | bytes 196612
  45.3 19.9 %copy-start.6 = (bf16[32,272,128]{2,1,0:T(8,128)(2,1)}, bf16[32,272,128]{2,1,0:T(8,128)(2,1)S(1)}, u32[]{:S(2)}) copy-start(bf16[32,272,128]{2,1,0:T(8,128)(2,1)S(1)} %all-to-all-done.nraw_ref.near_ref) | copy-start | bytes 6684676
  45.3 19.9 %collective-permute-start.1 = (bf16[32,272,128]{2,1,0:T(8,128)(2,1)S(1)}, bf16[32,272,128]{2,1,0:T(8,128)(2,1)}, u32[]{:S(2)}, u32[]{:S(2)}) collective-permute-start(bf16[32,272,128]{2,1,0:T(8,128)(2,1)S(1)} %all-to-all-done.nraw_ref.near_ref), channel_id=1, source_target_pairs={{0,1},{1,0},{2,3},{3,2},{4,5},{5,4},{6,7},{7,6},{8,9},{9,8},{10,11... | collective-permute-start | bytes 6684680 | tf_op jit(solution)/shard_map/ppermute | solution.py:581
  80.7 5.8 %copy-start.7 = (bf16[32,256,128]{2,1,0:T(8,128)(2,1)S(1)}, bf16[32,256,128]{2,1,0:T(8,128)(2,1)}, u32[]{:S(2)}) copy-start(bf16[32,256,128]{2,1,0:T(8,128)(2,1)} %get-tuple-element.55) | copy-start | bytes 6291460
  80.7 4.4 %collective-permute-start.2 = (bf16[32,256,128]{2,1,0:T(8,128)(2,1)}, bf16[32,256,128]{2,1,0:T(8,128)(2,1)S(1)}, u32[]{:S(2)}, u32[]{:S(2)}) collective-permute-start(bf16[32,256,128]{2,1,0:T(8,128)(2,1)} %get-tuple-element.56), channel_id=1, source_target_pairs={{0,1},{1,0},{2,3},{3,2},{4,5},{5,4},{6,7},{7,6},{8,9},{9,8},{10,11... | collective-permute-start | bytes 6291464 | tf_op jit(solution)/shard_map/ppermute | solution.py:588
  88.0 30.4 %all-to-all-start.1 = ((bf16[32,160,128]{2,1,0:T(8,128)(2,1)}), bf16[32,160,128]{2,1,0:T(8,128)(2,1)S(1)}, u32[]{:S(2)}, u32[]{:S(2)}) async-start(bf16[32,160,128]{2,1,0:T(8,128)(2,1)} %add_convert_fusion), calls=%async_computation.1 | async-start | bytes 2621440 | tf_op jit(solution)/shard_map/all_to_all | solution.py:593
  92.3 28.9 %copy-start.10 = (f32[16,256]{1,0:T(8,128)S(1)}, f32[16,256]{1,0:T(8,128)}, u32[]{:S(2)}) copy-start(f32[16,256]{1,0:T(8,128)} %get-tuple-element.74) | copy-start | bytes 49156
  118.4 3.9 %copy-start = (bf16[32,160,128]{2,1,0:T(8,128)(2,1)}, bf16[32,160,128]{2,1,0:T(8,128)(2,1)S(1)}, u32[]{:S(2)}) copy-start(bf16[32,160,128]{2,1,0:T(8,128)(2,1)S(1)} %all-to-all-done.1) | copy-start | bytes 3932164
  118.4 11.8 %collective-permute-start.3 = (bf16[128,4,48,128]{3,2,1,0:T(8,128)(2,1)}, bf16[128,4,48,128]{3,2,1,0:T(8,128)(2,1)}, u32[]{:S(2)}, u32[]{:S(2)}) collective-permute-start(bf16[128,4,48,128]{3,2,1,0:T(8,128)(2,1)} %get-tuple-element.62), channel_id=1, source_target_pairs={{0,1},{1,0},{2,3},{3,2},{4,5},{5,4},{6,7},{7,6},{8,9},{9,8},{10,11... | collective-permute-start | bytes 18874376 | tf_op jit(solution)/shard_map/ppermute | solution.py:601
  122.4 27.7 %all-to-all-start.2 = ((bf16[32,112,128]{2,1,0:T(8,128)(2,1)}), bf16[32,112,128]{2,1,0:T(8,128)(2,1)S(1)}, u32[]{:S(2)}, u32[]{:S(2)}) async-start(bf16[32,112,128]{2,1,0:T(8,128)(2,1)} %pad_maximum_fusion), calls=%async_computation.2 | async-start | bytes 1835008 | tf_op jit(solution)/shard_map/all_to_all | solution.py:599
  144.9 14.1 %collective-permute-start.10 = (bf16[2,4,272,128]{3,2,1,0:T(8,128)(2,1)}, bf16[2,4,272,128]{3,2,1,0:T(8,128)(2,1)}, u32[]{:S(2)}, u32[]{:S(2)}) collective-permute-start(bf16[2,4,272,128]{3,2,1,0:T(8,128)(2,1)} %get-tuple-element.70), channel_id=1, source_target_pairs={{0,24},{8,0},{16,8},{24,16},{1,25},{9,1},{17,9},{25,17},{2,26},{10... | collective-permute-start | bytes 1671176 | tf_op jit(solution)/shard_map/ppermute | solution.py:524
  147.4 14.6 %collective-permute-start.8 = (bf16[2,4,272,128]{3,2,1,0:T(8,128)(2,1)}, bf16[2,4,272,128]{3,2,1,0:T(8,128)(2,1)}, u32[]{:S(2)}, u32[]{:S(2)}) collective-permute-start(bf16[2,4,272,128]{3,2,1,0:T(8,128)(2,1)} %get-tuple-element.69), channel_id=1, source_target_pairs={{0,8},{8,16},{16,24},{24,0},{1,9},{9,17},{17,25},{25,1},{2,10},{10... | collective-permute-start | bytes 1671176 | tf_op jit(solution)/shard_map/ppermute | solution.py:524
  147.4 19.8 %collective-permute-start.4 = (bf16[2,4,304,128]{3,2,1,0:T(8,128)(2,1)}, bf16[2,4,304,128]{3,2,1,0:T(8,128)(2,1)}, u32[]{:S(2)}, u32[]{:S(2)}) collective-permute-start(bf16[2,4,304,128]{3,2,1,0:T(8,128)(2,1)} %get-tuple-element.66), channel_id=1, source_target_pairs={{0,32},{32,64},{64,96},{96,0},{1,33},{33,65},{65,97},{97,1},{2,34}... | collective-permute-start | bytes 1867784 | tf_op jit(solution)/shard_map/ppermute | solution.py:524
  148.7 18.6 %collective-permute-start.6 = (bf16[2,4,304,128]{3,2,1,0:T(8,128)(2,1)}, bf16[2,4,304,128]{3,2,1,0:T(8,128)(2,1)}, u32[]{:S(2)}, u32[]{:S(2)}) collective-permute-start(bf16[2,4,304,128]{3,2,1,0:T(8,128)(2,1)} %get-tuple-element.67), channel_id=1, source_target_pairs={{0,96},{32,0},{64,32},{96,64},{1,97},{33,1},{65,33},{97,65},{2,98}... | collective-permute-start | bytes 1867784 | tf_op jit(solution)/shard_map/ppermute | solution.py:524
  150.1 0.9 copy-start.3
  151.0 50.7 %all-to-all-start.3 = ((bf16[4,4,4,192,128]{4,3,2,1,0:T(8,128)(2,1)}), bf16[4,4,4,192,128]{4,3,2,1,0:T(8,128)(2,1)S(1)}, u32[]{:S(2)}, u32[]{:S(2)}) async-start(bf16[4,4,4,192,128]{4,3,2,1,0:T(8,128)(2,1)} %get-tuple-element.75), calls=%async_computation.3 | async-start | bytes 6291456 | tf_op jit(solution)/shard_map/all_to_all | solution.py:606
  162.0 5.2 %copy-start.5 = (bf16[4,4,4,304,128]{4,3,2,1,0:T(8,128)(2,1)S(1)}, bf16[4,4,4,304,128]{4,3,2,1,0:T(8,128)(2,1)}, u32[]{:S(2)}) copy-start(bf16[4,4,4,304,128]{4,3,2,1,0:T(8,128)(2,1)} %get-tuple-element.65) | copy-start | bytes 14942212
  165.8 24.4 %collective-permute-start.11 = (bf16[4,4,272,128]{3,2,1,0:T(8,128)(2,1)}, bf16[4,4,272,128]{3,2,1,0:T(8,128)(2,1)}, u32[]{:S(2)}, u32[]{:S(2)}) collective-permute-start(bf16[4,4,272,128]{3,2,1,0:T(8,128)(2,1)} %get-tuple-element.94), channel_id=1, source_target_pairs={{0,24},{8,0},{16,8},{24,16},{1,25},{9,1},{17,9},{25,17},{2,26},{10... | collective-permute-start | bytes 3342344 | tf_op jit(solution)/shard_map/ppermute | solution.py:524
  166.1 25.7 %collective-permute-start.9 = (bf16[4,4,272,128]{3,2,1,0:T(8,128)(2,1)}, bf16[4,4,272,128]{3,2,1,0:T(8,128)(2,1)}, u32[]{:S(2)}, u32[]{:S(2)}) collective-permute-start(bf16[4,4,272,128]{3,2,1,0:T(8,128)(2,1)} %get-tuple-element.93), channel_id=1, source_target_pairs={{0,8},{8,16},{16,24},{24,0},{1,9},{9,17},{17,25},{25,1},{2,10},{10... | collective-permute-start | bytes 3342344 | tf_op jit(solution)/shard_map/ppermute | solution.py:524
  170.3 27.9 %collective-permute-start.5 = (bf16[4,4,304,128]{3,2,1,0:T(8,128)(2,1)}, bf16[4,4,304,128]{3,2,1,0:T(8,128)(2,1)}, u32[]{:S(2)}, u32[]{:S(2)}) collective-permute-start(bf16[4,4,304,128]{3,2,1,0:T(8,128)(2,1)} %get-tuple-element.91), channel_id=1, source_target_pairs={{0,32},{32,64},{64,96},{96,0},{1,33},{33,65},{65,97},{97,1},{2,34}... | collective-permute-start | bytes 3735560 | tf_op jit(solution)/shard_map/ppermute | solution.py:524
  171.5 26.6 %collective-permute-start.7 = (bf16[4,4,304,128]{3,2,1,0:T(8,128)(2,1)}, bf16[4,4,304,128]{3,2,1,0:T(8,128)(2,1)}, u32[]{:S(2)}, u32[]{:S(2)}) collective-permute-start(bf16[4,4,304,128]{3,2,1,0:T(8,128)(2,1)} %get-tuple-element.92), channel_id=1, source_target_pairs={{0,96},{32,0},{64,32},{96,64},{1,97},{33,1},{65,33},{97,65},{2,98}... | collective-permute-start | bytes 3735560 | tf_op jit(solution)/shard_map/ppermute | solution.py:524
  173.0 1.6 copy-start.4
  203.4 11.7 %copy-start.1 = (bf16[4,4,304,128]{3,2,1,0:T(8,128)(2,1)S(1)}, bf16[4,4,304,128]{3,2,1,0:T(8,128)(2,1)}, u32[]{:S(2)}) copy-start(bf16[4,4,304,128]{3,2,1,0:T(8,128)(2,1)} %fusion.3) | copy-start | bytes 3735556
  203.4 22.2 %copy-start.2 = (bf16[4,4,272,128]{3,2,1,0:T(8,128)(2,1)S(1)}, bf16[4,4,272,128]{3,2,1,0:T(8,128)(2,1)}, u32[]{:S(2)}) copy-start(bf16[4,4,272,128]{3,2,1,0:T(8,128)(2,1)} %fusion.7) | copy-start | bytes 3342340
  203.4 14.5 %collective-permute-start.21 = (f32[264,128]{1,0:T(8,128)S(1)}, f32[264,128]{1,0:T(8,128)S(1)}, u32[]{:S(2)}, u32[]{:S(2)}) collective-permute-start(f32[264,128]{1,0:T(8,128)S(1)} %fusion.16), channel_id=1, source_target_pairs={{0,2},{2,0},{1,3},{3,1},{4,6},{6,4},{5,7},{7,5},{8,10},{10,8},{9,1... | collective-permute-start | bytes 405512 | tf_op jit(solution)/shard_map/ppermute | solution.py:616
  206.0 28.0 %all-to-all-start.4 = ((bf16[16,192,128]{2,1,0:T(8,128)(2,1)}), bf16[16,192,128]{2,1,0:T(8,128)(2,1)S(1)}, u32[]{:S(2)}, u32[]{:S(2)}) async-start(bf16[16,192,128]{2,1,0:T(8,128)(2,1)} %bitcast.91), calls=%async_computation.4 | async-start | bytes 1572864 | tf_op jit(solution)/shard_map/all_to_all | solution.py:613
  212.4 10.9 %collective-permute-start.16 = (bf16[2,272,128]{2,1,0:T(8,128)(2,1)S(1)}, bf16[2,272,128]{2,1,0:T(8,128)(2,1)S(1)}, u32[]{:S(2)}, u32[]{:S(2)}) collective-permute-start(bf16[2,272,128]{2,1,0:T(8,128)(2,1)S(1)} %get-tuple-element.101), channel_id=1, source_target_pairs={{0,32},{32,64},{64,96},{96,0},{1,33},{33,65},{65,97},{97,1},{2,34}... | collective-permute-start | bytes 417800 | tf_op jit(solution)/shard_map/ppermute | solution.py:524
  213.8 11.8 %collective-permute-start.18 = (bf16[2,272,128]{2,1,0:T(8,128)(2,1)S(1)}, bf16[2,272,128]{2,1,0:T(8,128)(2,1)S(1)}, u32[]{:S(2)}, u32[]{:S(2)}) collective-permute-start(bf16[2,272,128]{2,1,0:T(8,128)(2,1)S(1)} %get-tuple-element.102), channel_id=1, source_target_pairs={{0,96},{32,0},{64,32},{96,64},{1,97},{33,1},{65,33},{97,65},{2,98}... | collective-permute-start | bytes 417800 | tf_op jit(solution)/shard_map/ppermute | solution.py:524
  215.2 13.6 %collective-permute-start.12 = (bf16[2,304,128]{2,1,0:T(8,128)(2,1)S(1)}, bf16[2,304,128]{2,1,0:T(8,128)(2,1)S(1)}, u32[]{:S(2)}, u32[]{:S(2)}) collective-permute-start(bf16[2,304,128]{2,1,0:T(8,128)(2,1)S(1)} %get-tuple-element.97), channel_id=1, source_target_pairs={{0,8},{8,16},{16,24},{24,0},{1,9},{9,17},{17,25},{25,1},{2,10},{10... | collective-permute-start | bytes 466952 | tf_op jit(solution)/shard_map/ppermute | solution.py:524
  216.6 12.2 %collective-permute-start.14 = (bf16[2,304,128]{2,1,0:T(8,128)(2,1)S(1)}, bf16[2,304,128]{2,1,0:T(8,128)(2,1)S(1)}, u32[]{:S(2)}, u32[]{:S(2)}) collective-permute-start(bf16[2,304,128]{2,1,0:T(8,128)(2,1)S(1)} %get-tuple-element.98), channel_id=1, source_target_pairs={{0,24},{8,0},{16,8},{24,16},{1,25},{9,1},{17,9},{25,17},{2,26},{10... | collective-permute-start | bytes 466952 | tf_op jit(solution)/shard_map/ppermute | solution.py:524
  217.9 14.4 %collective-permute-start.22 = (f32[264,128]{1,0:T(8,128)S(1)}, f32[264,128]{1,0:T(8,128)S(1)}, u32[]{:S(2)}, u32[]{:S(2)}) collective-permute-start(f32[264,128]{1,0:T(8,128)S(1)} %add.151), channel_id=1, source_target_pairs={{0,1},{1,0},{2,3},{3,2},{4,5},{5,4},{6,7},{7,6},{8,9},{9,8},{10,11... | collective-permute-start | bytes 405512 | tf_op jit(solution)/shard_map/ppermute | solution.py:617
  225.7 8.2 %collective-permute-start.17 = (bf16[4,272,128]{2,1,0:T(8,128)(2,1)S(1)}, bf16[4,272,128]{2,1,0:T(8,128)(2,1)S(1)}, u32[]{:S(2)}, u32[]{:S(2)}) collective-permute-start(bf16[4,272,128]{2,1,0:T(8,128)(2,1)S(1)} %get-tuple-element.99), channel_id=1, source_target_pairs={{0,32},{32,64},{64,96},{96,0},{1,33},{33,65},{65,97},{97,1},{2,34}... | collective-permute-start | bytes 835592 | tf_op jit(solution)/shard_map/ppermute | solution.py:524
  225.8 8.1 %collective-permute-start.19 = (bf16[4,272,128]{2,1,0:T(8,128)(2,1)S(1)}, bf16[4,272,128]{2,1,0:T(8,128)(2,1)S(1)}, u32[]{:S(2)}, u32[]{:S(2)}) collective-permute-start(bf16[4,272,128]{2,1,0:T(8,128)(2,1)S(1)} %get-tuple-element.100), channel_id=1, source_target_pairs={{0,96},{32,0},{64,32},{96,64},{1,97},{33,1},{65,33},{97,65},{2,98}... | collective-permute-start | bytes 835592 | tf_op jit(solution)/shard_map/ppermute | solution.py:524
  229.7 8.4 %collective-permute-start.13 = (bf16[4,304,128]{2,1,0:T(8,128)(2,1)}, bf16[4,304,128]{2,1,0:T(8,128)(2,1)}, u32[]{:S(2)}, u32[]{:S(2)}) collective-permute-start(bf16[4,304,128]{2,1,0:T(8,128)(2,1)} %get-tuple-element.95), channel_id=1, source_target_pairs={{0,8},{8,16},{16,24},{24,0},{1,9},{9,17},{17,25},{25,1},{2,10},{10... | collective-permute-start | bytes 933896 | tf_op jit(solution)/shard_map/ppermute | solution.py:524
  230.5 7.6 %collective-permute-start.15 = (bf16[4,304,128]{2,1,0:T(8,128)(2,1)}, bf16[4,304,128]{2,1,0:T(8,128)(2,1)}, u32[]{:S(2)}, u32[]{:S(2)}) collective-permute-start(bf16[4,304,128]{2,1,0:T(8,128)(2,1)} %get-tuple-element.96), channel_id=1, source_target_pairs={{0,24},{8,0},{16,8},{24,16},{1,25},{9,1},{17,9},{25,17},{2,26},{10... | collective-permute-start | bytes 933896 | tf_op jit(solution)/shard_map/ppermute | solution.py:524
  234.2 5.1 %collective-permute-start.20 = (bf16[192,128]{1,0:T(8,128)(2,1)S(1)}, bf16[192,128]{1,0:T(8,128)(2,1)S(1)}, u32[]{:S(2)}, u32[]{:S(2)}) collective-permute-start(bf16[192,128]{1,0:T(8,128)(2,1)S(1)} %reduce_sum.57), channel_id=1, source_target_pairs={{0,2},{2,0},{1,3},{3,1},{4,6},{6,4},{5,7},{7,5},{8,10},{10,8},{9,1... | collective-permute-start | bytes 147464 | tf_op jit(solution)/shard_map/ppermute | solution.py:621
  255.2 4.4 %copy-start.11 = (s32[8,256]{1,0:T(8,128)S(1)}, s32[8,256]{1,0:T(8,128)}, u32[]{:S(2)}) copy-start(s32[8,256]{1,0:T(8,128)} %param.16) | copy-start | bytes 24580
  255.2 5.0 %copy-start.8 = (f32[2,256,128]{2,1,0:T(8,128)S(1)}, f32[2,256,128]{2,1,0:T(8,128)}, u32[]{:S(2)}) copy-start(f32[2,256,128]{2,1,0:T(8,128)} %reverse_select_fusion) | copy-start | bytes 786436
  255.6 7.8 %collective-permute-start.23 = (bf16[2,768,128]{2,1,0:T(8,128)(2,1)S(1)}, bf16[2,768,128]{2,1,0:T(8,128)(2,1)S(1)}, u32[]{:S(2)}, u32[]{:S(2)}) collective-permute-start(bf16[2,768,128]{2,1,0:T(8,128)(2,1)S(1)} %get-tuple-element.104), channel_id=1, source_target_pairs={{0,1},{1,0},{2,3},{3,2},{4,5},{5,4},{6,7},{7,6},{8,9},{9,8},{10,11... | collective-permute-start | bytes 1179656 | tf_op jit(solution)/shard_map/ppermute | solution.py:631
